TPU v7x, 32 devices: a whole 2x2x4 slice. The times are simulated.
32 devices in a mesh: batch: 8 (over z, core), mp: 4 (over y, x).
Axes of the slice: x: 2, y: 2, z: 4, core: 2. Of those that a mesh axis runs over, the one named last changes fastest.
Arguments:
- hidden_states: bfloat16 [128, 4, 16384], P('batch', None, 'mp'), may hold values from -6 to 6
- accepted: int32 [128], P('batch'), may hold values from 1 to 4
- norm_gain: float32 [16384], replicated, may hold values from 0.25 to 1.75
- head_weight: bfloat16 [2, 16384, 16384], P(None, 'batch', 'mp'), may hold values from -0.046875 to 0.046875
- head_bias: float32 [2, 16384], P(None, 'mp'), may hold values from -4 to 4
- vocab_weight: bfloat16 [16384, 65536], P('mp', 'batch')
- cand_ids: int32 [128, 2, 10], P('mp'), may hold values from 0 to 65535
- tree_paths: int32 [64, 2], replicated, may hold values from 0 to 9
Outputs:
- log_probs: float32 [128, 2, 65536], P('mp', None, 'batch')
- path_scores: float32 [128, 64], P('mp')
All inputs are finite; a program needn't handle non-finite values.
Results may differ from a plain program's by a relative error of at most 0.0032.
Values may be sent and summed in bfloat16 or wider, within the bound.
No kernel may reach another device: no remote copies, remote signals or barrier semaphores. Data moves between devices by JAX's collectives and lax.ppermute only.
A program may use at most 256 MiB of HBM per device.

v0:
```python
import jax
import jax.numpy as jnp
from jax import lax
from jax.sharding import PartitionSpec as P

EPSILON = 1e-05


def joined(part, axis, combine):
    gathered = jax.tree.map(lambda a: lax.all_gather(a, axis), part)

    def take(source):
        return jax.tree.map(lambda a: lax.dynamic_index_in_dim(a, source, 0, False), gathered)

    return lax.fori_loop(
        1, lax.axis_size(axis), lambda source, state: combine(state, take(source)), take(0)
    )


def combine_stats(earlier, latter):
    row_peak = jnp.maximum(earlier[0], latter[0])
    row_total = earlier[1] * jnp.exp(earlier[0] - row_peak) + latter[1] * jnp.exp(
        latter[0] - row_peak
    )
    return (row_peak, row_total, earlier[2] + latter[2])


def shards(
    hidden_states, accepted, norm_gain, head_weight, head_bias, vocab_weight, cand_ids, tree_paths
):
    position = (accepted - 1)[:, None, None]
    chosen = jnp.take_along_axis(hidden_states, position, axis=1)[:, 0, :]
    full_rows = lax.all_gather(chosen, "mp", axis=1, tiled=True)
    widened = full_rows.astype(jnp.float32)
    mean_square = jnp.mean(widened * widened, axis=1, keepdims=True)
    normed = (widened * lax.rsqrt(mean_square + EPSILON) * norm_gain).astype(jnp.bfloat16)
    head_count = head_weight.shape[0]
    feat_width = head_weight.shape[2]
    vocab_width = vocab_weight.shape[1]
    local_rows = normed.shape[0]
    own_part = lax.dynamic_slice_in_dim(
        normed, lax.axis_index("mp") * feat_width, feat_width, 1
    ).astype(jnp.float32)
    spread = lax.all_to_all(normed, "batch", split_axis=1, concat_axis=0, tiled=True)
    all_rows = spread.shape[0]
    out_rows = all_rows // lax.axis_size("mp")
    logit_list = []
    for head_index in range(head_count):
        weight_now = head_weight[head_index]

        def head_terms(first_row, row_count, weight_now=weight_now):
            return jnp.dot(spread, weight_now, preferred_element_type=jnp.float32)

        before = lax.psum_scatter(
            head_terms(jnp.int32(0), local_rows * lax.axis_size("batch")),
            "batch",
            scatter_dimension=0,
            tiled=True,
        )
        residual = (own_part + jax.nn.silu(before + head_bias[head_index])).astype(jnp.bfloat16)
        gathered = lax.all_gather(residual, "batch", axis=0, tiled=True)

        def vocab_terms(first_row, row_count, gathered=gathered):
            return jnp.dot(gathered, vocab_weight, preferred_element_type=jnp.float32)

        logit_list.append(
            lax.psum_scatter(
                vocab_terms(jnp.int32(0), out_rows * lax.axis_size("mp")),
                "mp",
                scatter_dimension=0,
                tiled=True,
            )
        )
    logits = jnp.stack(logit_list, axis=1)
    vocab_offset = lax.axis_index("batch") * vocab_width
    relative = cand_ids - vocab_offset
    inside = (relative >= 0) & (relative < vocab_width)
    clipped = jnp.clip(relative, 0, vocab_width - 1)
    found_logit = jnp.take_along_axis(logits, clipped, axis=2)
    local_pick = jnp.where(inside, found_logit, 0.0)
    local_peak = jnp.max(logits, axis=2)
    local_total = jnp.sum(jnp.exp(logits - local_peak[:, :, None]), axis=2)
    row_peak, row_total, row_pick = joined(
        (local_peak, local_total, local_pick), "batch", combine_stats
    )
    normalizer = row_peak + jnp.log(row_total)
    log_probs = logits - normalizer[:, :, None]
    picked = row_pick - normalizer[:, :, None]
    choices_count = cand_ids.shape[2]
    path_scores = jnp.zeros((out_rows, tree_paths.shape[0]), jnp.float32)
    for head_index in range(head_count):
        selector = (
            tree_paths[:, head_index][None, :]
            == jnp.arange(choices_count, dtype=jnp.int32)[:, None]
        ).astype(jnp.float32)
        path_scores = path_scores + jnp.dot(
            picked[:, head_index, :], selector, precision=lax.Precision.HIGHEST
        )
    return (log_probs, path_scores)


def solution(mesh):
    return jax.shard_map(
        shards,
        mesh=mesh,
        in_specs=(
            P("batch", None, "mp"),
            P("batch"),
            P(),
            P(None, "batch", "mp"),
            P(None, "mp"),
            P("mp", "batch"),
            P("mp", None, None),
            P(),
        ),
        out_specs=(P("mp", None, "batch"), P("mp", None)),
        check_vma=False,
    )
```

profile of v0, /device:TPU:0, one launch (start us, length us, event | category | flops | bytes accessed | tf_op | source)
XLA Modules:
  0.0 336.9 jit_solution(18402874012525148372)
XLA Ops:
  7.2 0.7 fusion.16
  7.9 0.7 compare_and_fusion
  8.6 1.0 gather_fusion
  9.7 11.5 %all_gather.27 = bf16[16,16384]{1,0:T(8,128)(2,1)S(1)} all-gather(bf16[16,4096]{1,0:T(8,128)(2,1)S(1)} %broadcast_select_fusion), channel_id=1, replica_groups=mesh['batch'=8,'mp'=4] {'mp'}, dimensions={1}, use_global_device_ids=true | all-gather | bytes 655360 | tf_op jit(solution)/shard_map/all_gather | solution.py:33
  21.2 0.2 fusion.8
  21.5 0.2 fusion.10
  21.7 20.0 %all_to_all.19 = bf16[16,8,2048]{2,0,1:T(8,128)(2,1)S(1)} all-to-all(bf16[16,8,2048]{2,0,1:T(8,128)(2,1)S(1)} %bitcast.75), channel_id=1, replica_groups=mesh['batch'=8,'mp'=4] {'batch'}, dimensions={1} | all-to-all | bytes 1048576 | tf_op jit(solution)/shard_map/all_to_all | solution.py:44
  41.7 9.4 %fusion.4 = f32[128,4096]{1,0:T(8,128)} fusion(bf16[128,2048]{1,0:T(8,128)(2,1)S(1)} %bitcast.77, bf16[2,2048,4096]{2,1,0:T(8,128)(2,1)} %param.13), kind=kOutput, calls=%fused_computation.11 | convolution fusion | flops 2147483648 | bytes 19398656 | tf_op jit(solution)/shard_map/dot_general | solution.py:52
  51.2 9.7 %fusion.2 = f32[128,4096]{1,0:T(8,128)} fusion(bf16[128,2048]{1,0:T(8,128)(2,1)S(1)} %bitcast.78, bf16[2,2048,4096]{2,1,0:T(8,128)(2,1)} %param.13), kind=kOutput, calls=%fused_computation.9 | convolution fusion | flops 2147483648 | bytes 19398656 | tf_op jit(solution)/shard_map/dot_general | solution.py:52
  61.0 0.7 copy-done.4
  61.7 23.4 %reduce-scatter.5.cloned.1.call-done = f32[16,4096]{1,0:T(8,128)} async-done(((f32[128,4096]{1,0:T(8,128)}), f32[16,4096]{1,0:T(8,128)}) %reduce-scatter.5.cloned.1.call-update) | async-done | bytes 262160 | tf_op jit(solution)/shard_map/reduce_scatter | solution.py:54
  85.1 36.8 %reduce-scatter.9.cloned.1.call-done = f32[16,4096]{1,0:T(8,128)} async-done(((f32[128,4096]{1,0:T(8,128)}), f32[16,4096]{1,0:T(8,128)}) %reduce-scatter.9.cloned.1.call-update) | async-done | bytes 262160 | tf_op jit(solution)/shard_map/reduce_scatter | solution.py:54
  122.0 1.9 fusion.11
  123.9 0.5 all-gather.10.cloned.1.call-update
  124.5 20.4 %all-gather.8.cloned.1.call-done = bf16[128,4096]{1,0:T(8,128)(2,1)} async-done(((bf16[16,4096]{1,0:T(8,128)(2,1)}), bf16[128,4096]{1,0:T(8,128)(2,1)}) %all-gather.8.cloned.1.call-update) | async-done | bytes 1048592 | tf_op jit(solution)/shard_map/all_gather | solution.py:61
  144.9 26.3 %fusion.19 = f32[128,8192]{1,0:T(8,128)} fusion(bf16[128,4096]{1,0:T(8,128)(2,1)} %all-gather.8.cloned.1.call-done, bf16[4096,8192]{1,0:T(8,128)(2,1)} %param.15), kind=kOutput, calls=%fused_computation.55 | convolution fusion | flops 8589934592 | bytes 72351744 | tf_op jit(solution)/shard_map/dot_general | solution.py:64
  171.2 0.2 reduce-scatter.11.cloned.1.call-start
  171.5 27.5 %fusion.20 = f32[128,8192]{1,0:T(8,128)} fusion(bf16[128,4096]{1,0:T(8,128)(2,1)} %all-gather.10.cloned.1.call-done, bf16[4096,8192]{1,0:T(8,128)(2,1)} %param.15), kind=kOutput, calls=%fused_computation.56 | convolution fusion | flops 8589934592 | bytes 72351744 | tf_op jit(solution)/shard_map/dot_general | solution.py:64
  199.0 0.7 copy-done.5
  200.1 23.7 %reduce-scatter.7.cloned.1.call-done = f32[32,8192]{1,0:T(8,128)} async-done(((f32[128,8192]{1,0:T(8,128)}), f32[32,8192]{1,0:T(8,128)}) %reduce-scatter.7.cloned.1.call-update) | async-done | bytes 1048592 | tf_op jit(solution)/shard_map/reduce_scatter | solution.py:67
  223.7 55.8 %reduce-scatter.11.cloned.1.call-done = f32[32,8192]{1,0:T(8,128)} async-done(((f32[128,8192]{1,0:T(8,128)}), f32[32,8192]{1,0:T(8,128)}) %reduce-scatter.11.cloned.1.call-update) | async-done | bytes 1048592 | tf_op jit(solution)/shard_map/reduce_scatter | solution.py:67
  279.5 2.0 pad_maximum_fusion
  281.7 0.5 exponential_reduce_fusion
  282.2 11.7 %all-gather.4 = f32[8,32,2]{1,2,0:T(2,128)S(1)} all-gather(f32[1,32,2]{1,2,0:T(2,128)S(1)} %bitcast.82), channel_id=3, replica_groups=mesh['batch'=8,'mp'=4] {'batch'}, dimensions={0}, use_global_device_ids=true | all-gather | bytes 2304 | tf_op jit(solution)/shard_map/all_gather | solution.py:10
  293.9 6.5 %gather_fusion.1 = f32[640]{0:T(1024)S(1)} fusion(f32[32,2,8192]{2,0,1:T(8,128)S(1)} %get-tuple-element.219, s32[640]{0:T(1024)S(1)} %reshape.57), kind=kCustom, calls=%fused_computation.1 | custom fusion | bytes 12800 | tf_op jit(solution)/shard_map/jit(take_along_axis)/gather | solution.py:79
  300.6 14.2 %all-gather.2 = f32[256,2,10]{2,1,0:T(2,128)S(1)} all-gather(f32[32,2,10]{2,1,0:T(2,128)S(1)} %and_select_fusion.1), channel_id=4, replica_groups=mesh['batch'=8,'mp'=4] {'batch'}, dimensions={0}, use_global_device_ids=true | all-gather | bytes 23040 | tf_op jit(solution)/shard_map/all_gather | solution.py:10
  315.1 8.8 %all-gather.3 = f32[8,32,2]{1,2,0:T(2,128)S(1)} all-gather(f32[1,32,2]{1,2,0:T(2,128)S(1)} %bitcast.81), channel_id=2, replica_groups=mesh['batch'=8,'mp'=4] {'batch'}, dimensions={0}, use_global_device_ids=true | all-gather | bytes 2304 | tf_op jit(solution)/shard_map/all_gather | solution.py:10
  323.8 0.4 while.19
  324.3 1.7 broadcast_subtract_fusion
  326.1 2.9 copy.24
  329.0 0.2 fusion.13
  329.2 0.8 convolution_add_fusion
  (57 shorter events, 1.8 us)
Async XLA Ops:
  7.2 1.5 copy-start
  7.2 14.3 %copy-start.3 = (f32[16384]{0:T(1024)S(1)}, f32[16384]{0:T(1024)}, u32[]{:S(2)}) copy-start(f32[16384]{0:T(1024)} %param.12) | copy-start | bytes 196612
  7.2 77.9 %reduce-scatter.5.cloned.1.call-start = ((), (), s32[]{:S(2)}) async-start(), calls=%async_computation.5 | async-start | bytes 2359296 | tf_op jit(solution)/shard_map/reduce_scatter | solution.py:54
  51.2 70.8 %reduce-scatter.9.cloned.1.call-start = ((), (), s32[]{:S(2)}) async-start(), calls=%async_computation.8 | async-start | bytes 2359296 | tf_op jit(solution)/shard_map/reduce_scatter | solution.py:54
  60.9 0.8 copy-start.4
  60.9 84.0 %all-gather.8.cloned.1.call-start = ((), (), s32[]{:S(2)}) async-start(), calls=%async_computation.6 | async-start | bytes 1179648 | tf_op jit(solution)/shard_map/all_gather | solution.py:61
  123.8 47.6 %all-gather.10.cloned.1.call-start = ((), (), s32[]{:S(2)}) async-start(), calls=%async_computation.9 | async-start | bytes 1179648 | tf_op jit(solution)/shard_map/all_gather | solution.py:61
  124.4 99.3 %reduce-scatter.7.cloned.1.call-start = ((), (), s32[]{:S(2)}) async-start(), calls=%async_computation.7 | async-start | bytes 5242880 | tf_op jit(solution)/shard_map/reduce_scatter | solution.py:67
  171.2 108.3 %reduce-scatter.11.cloned.1.call-start = ((), (), s32[]{:S(2)}) async-start(), calls=%async_computation.10 | async-start | bytes 5242880 | tf_op jit(solution)/shard_map/reduce_scatter | solution.py:67
  199.0 0.7 copy-start.5
  199.0 1.0 copy-start.6
  279.5 2.0 copy-start.1
  279.5 2.2 copy-start.2
Sparse Core Ops, SparseCore 0:
  51.3 33.7 reduce-scatter.4
  87.4 34.4 reduce-scatter.8
  124.1 20.7 all-gather.7
  146.4 21.7 all-gather.9
  171.3 52.3 reduce-scatter.6
  226.8 52.6 reduce-scatter.10
where the time goes:
time: 337 us
  waiting for transfers between devices  161 us (48%)
  matrix products  73.9 us (22%)
  blocking collectives  66.2 us (20%)
  between operations  14.3 us (4%)
  local copies, waits for them, and re-layouts  12.6 us (4%)
  other arithmetic  8.45 us (3%)
    reduce_scatter x2, waiting for transfers between devices, shards(): lax.psum_scatter(vocab_terms(jnp.int32(0), out_rows * lax.axis_size('mp')...  79.5 us
    reduce_scatter x2, waiting for transfers between devices, shards(): lax.psum_scatter(head_terms(jnp.int32(0), local_rows * lax.axis_size('bat...  60.3 us
    dot_general x2, matrix products, vocab_terms(): return jnp.dot(gathered, vocab_weight, preferred_element_type=jnp.float32)  53.8 us
    all_gather x3, blocking collectives, joined(): gathered = jax.tree.map(lambda a: lax.all_gather(a, axis), part)  34.7 us
    all_gather x2, waiting for transfers between devices, shards(): gathered = lax.all_gather(residual, 'batch', axis=0, tiled=True)  20.5 us
    all_to_all x1, blocking collectives, shards(): lax.all_to_all(normed, 'batch', split_axis=1, concat_axis=0, tiled=True)  20 us
    dot_general x2, matrix products, head_terms(): return jnp.dot(spread, weight_now, preferred_element_type=jnp.float32)  19.1 us
    all_gather x1, blocking collectives, shards(): full_rows = lax.all_gather(chosen, 'mp', axis=1, tiled=True)  11.5 us
  transfers between devices with their start and end apart: 6, of which 5 were waited for; matrix products, arithmetic and copies ran while one was open for 19% of the time, Pallas kernels for 0%

commit v1 on v0

v1 whole, which is shorter than its diff:
```python
import functools

import jax
import jax.numpy as jnp
from jax import lax
from jax.experimental import pallas as pl
from jax.experimental.pallas import tpu as pltpu
from jax.sharding import PartitionSpec as P

EPSILON = 1e-05
MIB = 1024 * 1024


def bits_of(count):
    return [1 << i for i in range(count.bit_length() - 1)]


def exchange(array, axis, bit):
    size = lax.axis_size(axis)
    return lax.ppermute(array, axis, [(i, i ^ bit) for i in range(size)])


def place(index, stages):
    spot = 0
    for bit in stages:
        spot = 2 * spot + (index & bit) // bit
    return spot


def widest(limit, size):
    tile = min(limit, size)
    while size % tile:
        tile //= 2
    return tile


def head_body(spots, *refs, count):
    received, (weight, keep, send, rows) = refs[:count], refs[count:]
    height = received[0].shape[0]

    @pl.when(pl.program_id(0) == 0)
    def _():
        for k in range(count):
            start = pl.multiple_of(spots[k] * height, height)
            rows[pl.ds(start, height), :] = received[k][...]

    total = jnp.dot(rows[...], weight[0], preferred_element_type=jnp.float32)
    half = total.shape[0] // 2
    keep[...] = total[:half]
    send[...] = total[half:].astype(jnp.bfloat16)


def head_matmul(spots, received, head_weight, head):
    count = len(received)
    height, depth = received[0].shape
    width = head_weight.shape[2]
    tile = widest(512, width)
    half = count * height // 2
    return pl.pallas_call(
        functools.partial(head_body, count=count),
        grid_spec=pltpu.PrefetchScalarGridSpec(
            num_scalar_prefetch=1,
            grid=(width // tile,),
            in_specs=[pl.BlockSpec((height, depth), lambda n, s: (0, 0))] * count
            + [pl.BlockSpec((1, depth, tile), lambda n, s: (head, 0, n))],
            out_specs=[pl.BlockSpec((half, tile), lambda n, s: (0, n))] * 2,
            scratch_shapes=[pltpu.VMEM((count * height, depth), jnp.bfloat16)],
        ),
        out_shape=[
            jax.ShapeDtypeStruct((half, width), jnp.float32),
            jax.ShapeDtypeStruct((half, width), jnp.bfloat16),
        ],
        compiler_params=pltpu.CompilerParams(vmem_limit_bytes=32 * MIB),
        cost_estimate=pl.CostEstimate(
            flops=2 * count * height * depth * width,
            bytes_accessed=2 * depth * width,
            transcendentals=0,
        ),
    )(spots, *received, head_weight)


def vocab_body(spots, *refs, heads, height):
    parts, (weight, keep, send, rows) = refs[:heads], refs[heads:]
    blocks = parts[0].shape[0] // height

    @pl.when(pl.program_id(0) == 0)
    def _():
        for head in range(heads):
            for block in range(blocks):
                start = pl.multiple_of(spots[head * blocks + block] * height, height)
                rows[pl.ds(start, height), :] = parts[head][block * height : (block + 1) * height, :]

    total = jnp.dot(rows[...], weight[...], preferred_element_type=jnp.float32)
    half = total.shape[0] // 2
    keep[...] = total[:half]
    send[...] = total[half:].astype(jnp.bfloat16)


def vocab_matmul(spots, parts, height, vocab_weight, first, width):
    heads = len(parts)
    depth = vocab_weight.shape[0]
    all_rows = sum(p.shape[0] for p in parts)
    half = all_rows // 2
    tile = widest(256, width)
    base = first // tile
    return pl.pallas_call(
        functools.partial(vocab_body, heads=heads, height=height),
        grid_spec=pltpu.PrefetchScalarGridSpec(
            num_scalar_prefetch=1,
            grid=(width // tile,),
            in_specs=[pl.BlockSpec(p.shape, lambda n, s: (0, 0)) for p in parts]
            + [pl.BlockSpec((depth, tile), lambda n, s: (0, base + n))],
            out_specs=[pl.BlockSpec((half, tile), lambda n, s: (0, n))] * 2,
            scratch_shapes=[pltpu.VMEM((all_rows, depth), jnp.bfloat16)],
        ),
        out_shape=[
            jax.ShapeDtypeStruct((half, width), jnp.float32),
            jax.ShapeDtypeStruct((half, width), jnp.bfloat16),
        ],
        compiler_params=pltpu.CompilerParams(vmem_limit_bytes=32 * MIB),
        cost_estimate=pl.CostEstimate(
            flops=2 * all_rows * depth * width,
            bytes_accessed=2 * depth * width,
            transcendentals=0,
        ),
    )(spots, *parts, vocab_weight)


def stats_body(wanted, *refs, chunks, choices):
    kept, came, (logits, stats) = refs[:chunks], refs[chunks : 2 * chunks], refs[2 * chunks :]
    width = kept[0].shape[1]
    block = 16

    def one(step, carry):
        here = pl.ds(pl.multiple_of(step * block, block), block)
        ids = wanted[here, :]
        peak = jnp.full((block, 1), -jnp.inf, jnp.float32)
        for c in range(chunks):
            value = kept[c][here, :] + came[c][here, :].astype(jnp.float32)
            logits[here, c * width : (c + 1) * width] = value
            peak = jnp.maximum(peak, jnp.max(value, axis=1, keepdims=True))
        total = jnp.zeros((block, 1), jnp.float32)
        picks = [jnp.zeros((block, 1), jnp.float32) for _ in range(choices)]
        columns = lax.broadcasted_iota(jnp.int32, (block, width), 1)
        for c in range(chunks):
            value = logits[here, c * width : (c + 1) * width]
            total = total + jnp.sum(jnp.exp(value - peak), axis=1, keepdims=True)
            for k in range(choices):
                hit = columns == ids[:, k : k + 1] - c * width
                picks[k] = picks[k] + jnp.sum(jnp.where(hit, value, 0.0), axis=1, keepdims=True)
        lane = lax.broadcasted_iota(jnp.int32, (block, stats.shape[1]), 1)
        out = jnp.where(lane == 0, peak, 0.0)
        for k, item in enumerate([total] + picks):
            out = jnp.where(lane == k + 1, item, out)
        stats[here, :] = out
        return carry

    lax.fori_loop(0, logits.shape[0] // block, one, 0)


def row_stats(wanted, kept, came, choices):
    chunks = len(kept)
    rows, width = kept[0].shape
    lanes = wanted.shape[1]
    vmem = pl.BlockSpec(memory_space=pltpu.VMEM)
    return pl.pallas_call(
        functools.partial(stats_body, chunks=chunks, choices=choices),
        in_specs=[vmem] * (1 + 2 * chunks),
        out_specs=[vmem] * 2,
        out_shape=[
            jax.ShapeDtypeStruct((rows, chunks * width), jnp.float32),
            jax.ShapeDtypeStruct((rows, lanes), jnp.float32),
        ],
        compiler_params=pltpu.CompilerParams(vmem_limit_bytes=32 * MIB),
    )(wanted, *kept, *came)


def shards(
    hidden_states, accepted, norm_gain, head_weight, head_bias, vocab_weight, cand_ids, tree_paths
):
    batch, mp = lax.axis_size("batch"), lax.axis_size("mp")
    b, m = lax.axis_index("batch"), lax.axis_index("mp")
    rows, positions, feat = hidden_states.shape
    heads, inner, _ = head_weight.shape
    vocab_width = vocab_weight.shape[1]
    out_rows = cand_ids.shape[0]
    choices = cand_ids.shape[2]
    pieces = feat // inner
    ratio = out_rows // rows
    batch_bits, mp_bits = bits_of(batch), bits_of(mp)

    chosen = hidden_states[:, 0, :]
    for position in range(1, positions):
        chosen = jnp.where((accepted == position + 1)[:, None], hidden_states[:, position, :], chosen)
    chosen = chosen.astype(jnp.float32)
    square_sum = jnp.sum(chosen * chosen, axis=1, keepdims=True)
    gain = lax.dynamic_slice_in_dim(norm_gain, m * feat, feat, 0)
    scaled = (chosen * gain).astype(jnp.bfloat16)

    outgoing = [
        lax.dynamic_slice_in_dim(scaled, ((b // mp) ^ q) * inner, inner, 1) for q in range(pieces)
    ]
    received = []
    for k in range(batch):
        perm = []
        for src in range(batch):
            target = src ^ k
            for col in range(mp):
                perm.append((src * mp + col, (col * pieces + target // mp) * mp + target % mp))
        received.append(lax.ppermute(outgoing[k // mp], ("batch", "mp"), perm))
    turn = ((b % pieces) * mp + m) ^ b

    for bit in mp_bits:
        square_sum = square_sum + exchange(square_sum, "mp", bit)
    row_scale = lax.rsqrt(square_sum / (mp * feat) + EPSILON)
    own_normed = (chosen * row_scale * gain).astype(jnp.bfloat16).astype(jnp.float32)

    spots = jnp.stack([place(turn ^ k, batch_bits) for k in range(batch)]).astype(jnp.int32)
    gathered, orders = [], []
    for head in range(heads):
        outer = batch_bits[1:]
        stages = batch_bits[:1] + (outer if head % 2 == 0 else outer[::-1])
        keep, send = head_matmul(spots, received, head_weight, head)
        order = sorted(range(batch), key=lambda j: place(j, batch_bits))
        order = order[: batch // 2]
        total = keep + exchange(send, "batch", stages[0]).astype(jnp.float32)
        for bit in stages[1:]:
            blocks = total.reshape(len(order), rows, feat)
            stay = [i for i, j in enumerate(order) if not j & bit]
            leave = [i for i, j in enumerate(order) if j & bit]
            outbound = jnp.concatenate([blocks[i] for i in leave], axis=0).astype(jnp.bfloat16)
            home = jnp.concatenate([blocks[i] for i in stay], axis=0)
            total = home + exchange(outbound, "batch", bit).astype(jnp.float32)
            order = [order[i] for i in stay]
        before = total * row_scale + head_bias[head][None, :]
        block = (own_normed + jax.nn.silu(before)).astype(jnp.bfloat16)
        order = [0]
        for bit in stages[::-1]:
            block = jnp.concatenate([block, exchange(block, "batch", bit)], axis=0)
            order = order + [j ^ bit for j in order]
        gathered.append(block)
        orders.append(order)

    width = widest(1024, vocab_width)
    chunks = vocab_width // width
    kept, came = [], []
    spots_by_stage = []
    for stages in (mp_bits, mp_bits[::-1]):
        table = []
        for head in range(heads):
            for j in orders[head]:
                source = b ^ j
                spot = place((source // ratio) ^ m, stages)
                table.append((spot * ratio + source % ratio) * heads + head)
        spots_by_stage.append(jnp.stack(table).astype(jnp.int32))
    for chunk in range(chunks):
        stages = mp_bits if chunk % 2 == 0 else mp_bits[::-1]
        keep, send = vocab_matmul(
            spots_by_stage[chunk % 2], gathered, rows, vocab_weight, chunk * width, width
        )
        for index, bit in enumerate(stages):
            arrived = exchange(send, "mp", bit)
            if index + 1 < len(stages):
                total = keep + arrived.astype(jnp.float32)
                half = total.shape[0] // 2
                keep, send = total[:half], total[half:].astype(jnp.bfloat16)
        kept.append(keep)
        came.append(arrived)

    wanted = (cand_ids - b * vocab_width).reshape(ratio, rows, heads, choices)
    wanted = wanted.transpose(0, 2, 1, 3).reshape(out_rows * heads, choices)
    wanted = jnp.pad(wanted, ((0, 0), (0, 128 - choices)), constant_values=-1)
    logits, stats = row_stats(wanted, kept, came, choices)

    level = [stats] + [
        lax.ppermute(stats, "batch", [(i, i ^ j) for i in range(batch)]) for j in range(1, batch)
    ]
    peak = functools.reduce(jnp.maximum, [s[:, :1] for s in level])
    sums = [
        jnp.concatenate([s[:, 1:2] * jnp.exp(s[:, :1] - peak), s[:, 2 : 2 + choices]], axis=1)
        for s in level
    ]
    while len(sums) > 1:
        sums = [x + y for x, y in zip(sums[::2], sums[1::2])]
    normalizer = peak + jnp.log(sums[0][:, :1])
    picked = sums[0][:, 1:] - normalizer

    def natural(array):
        array = array.reshape(ratio, heads, rows, array.shape[1])
        return array.transpose(0, 2, 1, 3).reshape(out_rows, heads, array.shape[3])

    log_probs = natural(logits - normalizer)
    picked = natural(picked)
    path_scores = jnp.zeros((out_rows, tree_paths.shape[0]), jnp.float32)
    for head in range(heads):
        found = jnp.zeros_like(path_scores)
        for choice in range(choices):
            taken = tree_paths[:, head][None, :] == choice
            found = jnp.where(taken, picked[:, head, choice : choice + 1], found)
        path_scores = path_scores + found
    return (log_probs, path_scores)


def solution(mesh):
    return jax.shard_map(
        shards,
        mesh=mesh,
        in_specs=(
            P("batch", None, "mp"),
            P("batch"),
            P(),
            P(None, "batch", "mp"),
            P(None, "mp"),
            P("mp", "batch"),
            P("mp", None, None),
            P(),
        ),
        out_specs=(P("mp", None, "batch"), P("mp", None)),
        check_vma=False,
    )
```

time: 337 us -> 246 us (0.73)
  waiting for transfers between devices: 161 us -> 61.3 us
  Pallas kernels: 0 us -> 95.3 us
  matrix products: 73.9 us -> 0 us
  starting transfers between devices: 0.43 us -> 73.1 us
  blocking collectives: 66.2 us -> 0 us
  between operations: 14.3 us -> 1.9 us
  other arithmetic: 8.45 us -> 3.64 us
    reduce_scatter x4 -> x0, waiting for transfers between devices: 140 us -> none  [the longest x2 79.5 us: shards(): lax.psum_scatter(vocab_terms(jnp.int32(0), out_rows * lax.axis_size('mp')...]
    pallas_call x0 -> x11, Pallas kernels: none -> 95.3 us  [the longest x8 49.8 us: vocab_matmul(): pl.pallas_call(functools.partial(vocab_body, heads=heads, height=height),...]
    dot_general x6 -> x0, matrix products: 73.9 us -> none  [the longest x2 53.8 us: vocab_terms(): return jnp.dot(gathered, vocab_weight, preferred_element_type=jnp.float32)]
    ppermute x0 -> x45, starting transfers between devices: none -> 73.1 us  [the longest x30 40.6 us: exchange(): return lax.ppermute(array, axis, [(i, i ^ bit) for i in range(size)])]
    ppermute x0 -> x45, waiting for transfers between devices: none -> 61.3 us  [the longest x30 51.3 us: exchange(): return lax.ppermute(array, axis, [(i, i ^ bit) for i in range(size)])]
    all_gather x4 -> x0, blocking collectives: 46.2 us -> none  [the longest x3 34.7 us: joined(): gathered = jax.tree.map(lambda a: lax.all_gather(a, axis), part)]
    all_gather x2 -> x0, waiting for transfers between devices: 20.5 us -> none  [shards(): gathered = lax.all_gather(residual, 'batch', axis=0, tiled=True)]
    all_to_all x1 -> x0, blocking collectives: 20 us -> none  [shards(): lax.all_to_all(normed, 'batch', split_axis=1, concat_axis=0, tiled=True)]
  transfers between devices with their start and end apart: 6 -> 45, of which waited for: 5 -> 23; matrix products, arithmetic and copies ran while one was open for 19% -> 1% of each run, Pallas kernels for 0% -> 13%
where the time goes in v1:
time: 246 us; the launch traced here: 245 us
  Pallas kernels  95.3 us (39%)
  starting transfers between devices  73.1 us (30%)
  waiting for transfers between devices  61.3 us (25%)
  local copies, waits for them, and re-layouts  9.62 us (4%)
  other arithmetic  3.64 us (1%)
    ppermute x30, waiting for transfers between devices, exchange(): return lax.ppermute(array, axis, [(i, i ^ bit) for i in range(size)])  51.3 us
    pallas_call x8, Pallas kernels, vocab_matmul(): pl.pallas_call(functools.partial(vocab_body, heads=heads, height=height),...  49.8 us
    ppermute x30, starting transfers between devices, exchange(): return lax.ppermute(array, axis, [(i, i ^ bit) for i in range(size)])  40.6 us
    pallas_call x1, Pallas kernels, row_stats(): pl.pallas_call(functools.partial(stats_body, chunks=chunks, choices=choic...  25.6 us
    ppermute x8, starting transfers between devices, shards(): received.append(lax.ppermute(outgoing[k // mp], ('batch', 'mp'), perm))  24.3 us
    pallas_call x2, Pallas kernels, head_matmul(): pl.pallas_call(functools.partial(head_body, count=count), grid_spec=pltpu...  19.9 us
    ppermute x7, starting transfers between devices, shards(): lax.ppermute(stats, 'batch', [(i, i ^ j) for i in range(batch)])  8.16 us
    ppermute x8, waiting for transfers between devices, shards(): received.append(lax.ppermute(outgoing[k // mp], ('batch', 'mp'), perm))  6.03 us
  transfers between devices with their start and end apart: 45, of which 23 were waited for; matrix products, arithmetic and copies ran while one was open for 1% of the time, Pallas kernels for 13%

profile of v1, /device:TPU:0, one launch (start us, length us, event | category | flops | bytes accessed | tf_op | source)
XLA Modules:
  0.0 244.9 jit_solution(187482341946484413)
XLA Ops:
  0.7 2.8 %fusion.22 = (bf16[16,1,4096]{2,1,0:T(2,128)(2,1)S(1)}, bf16[16,1,4096]{2,1,0:T(2,128)(2,1)S(1)}, bf16[16,1,4096]{2,1,0:T(2,128)(2,1)S(1)}, bf16[16,1,4096]{2,1,0:T(2,128)(2,1)S(1)}) fusion(bf16[16,4,4096]{2,1,0:T(4,128)(2,1)} %param.8), kind=kLoop, calls=%fused_computation.127 | loop fusion | bytes 1048576 | tf_op jit(solution)/shard_map/slice | solution.py:194
  5.7 5.8 %collective-permute-start.3 = (bf16[16,2048]{1,0:T(8,128)(2,1)S(1)}, bf16[16,2048]{1,0:T(8,128)(2,1)S(1)}, u32[]{:S(2)}, u32[]{:S(2)}) collective-permute-start(bf16[16,2048]{1,0:T(8,128)(2,1)S(1)} %get-tuple-element.63), channel_id=1, source_target_pairs={{0,1},{1,9},{2,17},{3,25},{4,0},{5,8},{6,16},{7,24},{8,3},{9,11},{... | collective-permute-start | bytes 196616 | tf_op jit(solution)/shard_map/ppermute | solution.py:210
  13.4 5.0 %collective-permute-start.5 = (bf16[16,2048]{1,0:T(8,128)(2,1)S(1)}, bf16[16,2048]{1,0:T(8,128)(2,1)S(1)}, u32[]{:S(2)}, u32[]{:S(2)}) collective-permute-start(bf16[16,2048]{1,0:T(8,128)(2,1)S(1)} %get-tuple-element.63), channel_id=1, source_target_pairs={{0,3},{1,11},{2,19},{3,27},{4,2},{5,10},{6,18},{7,26},{8,1},{9,9},... | collective-permute-start | bytes 196616 | tf_op jit(solution)/shard_map/ppermute | solution.py:210
  18.5 2.7 %collective-permute-start.7 = (bf16[16,2048]{1,0:T(8,128)(2,1)S(1)}, bf16[16,2048]{1,0:T(8,128)(2,1)S(1)}, u32[]{:S(2)}, u32[]{:S(2)}) collective-permute-start(bf16[16,2048]{1,0:T(8,128)(2,1)S(1)} %get-tuple-element.62), channel_id=1, source_target_pairs={{0,5},{1,13},{2,21},{3,29},{4,4},{5,12},{6,20},{7,28},{8,7},{9,15}... | collective-permute-start | bytes 196616 | tf_op jit(solution)/shard_map/ppermute | solution.py:210
  21.2 8.2 %collective-permute-start.8 = (bf16[16,2048]{1,0:T(8,128)(2,1)S(1)}, bf16[16,2048]{1,0:T(8,128)(2,1)S(1)}, u32[]{:S(2)}, u32[]{:S(2)}) collective-permute-start(bf16[16,2048]{1,0:T(8,128)(2,1)S(1)} %get-tuple-element.62), channel_id=1, source_target_pairs={{0,6},{1,14},{2,22},{3,30},{4,7},{5,15},{6,23},{7,31},{8,4},{9,12}... | collective-permute-start | bytes 196616 | tf_op jit(solution)/shard_map/ppermute | solution.py:210
  29.4 2.7 %collective-permute-done.4.refs_2_ = bf16[16,2048]{1,0:T(8,128)(2,1)S(1)} collective-permute-done((bf16[16,2048]{1,0:T(8,128)(2,1)S(1)}, bf16[16,2048]{1,0:T(8,128)(2,1)S(1)}, u32[]{:S(2)}, u32[]{:S(2)}) %collective-permute-start.4) | collective-permute-done | bytes 65568 | tf_op jit(solution)/shard_map/ppermute | solution.py:210
  33.6 5.9 %collective-permute-start = (f32[16,1]{0,1:T(1,128)S(1)}, f32[16,1]{0,1:T(1,128)S(1)}, u32[]{:S(2)}, u32[]{:S(2)}) collective-permute-start(f32[16,1]{0,1:T(1,128)S(1)} %bitcast.170), channel_id=1, source_target_pairs={{0,1},{1,0},{2,3},{3,2},{4,5},{5,4},{6,7},{7,6},{8,9},{9,8},{10,11... | collective-permute-start | bytes 200 | tf_op jit(solution)/shard_map/ppermute | solution.py:20
  41.4 9.9 %shard_map.95 = (f32[64,4096]{1,0:T(8,128)S(1)}, bf16[64,4096]{1,0:T(8,128)(2,1)S(1)}) custom-call(s32[8]{0:T(128)S(1)} %stack.154.spots, bf16[16,2048]{1,0:T(8,128)(2,1)S(1)} %collective-permute-done.2.refs_0_, bf16[16,2048]{1,0:T(8,128)(2,1)S(1)} %collective-permute-done.3.refs_1_, bf16[16,2048]{1,0:T(8,128)(2,1)S(1)} %collective-permute-done.4.refs_2_, ...), custom_call_target="tpu_custom_call" | custom-call | flops 2147483648 | bytes 16777216 | tf_op jit(solution)/shard_map/pallas_call | solution.py:59
  51.4 4.7 %collective-permute-start.10 = (bf16[64,4096]{1,0:T(8,128)(2,1)S(1)}, bf16[64,4096]{1,0:T(8,128)(2,1)S(1)}, u32[]{:S(2)}, u32[]{:S(2)}) collective-permute-start(bf16[64,4096]{1,0:T(8,128)(2,1)S(1)} %get-tuple-element.25), channel_id=1, source_target_pairs={{0,4},{4,0},{8,12},{12,8},{16,20},{20,16},{24,28},{28,24},{1,5},{5... | collective-permute-start | bytes 1572872 | tf_op jit(solution)/shard_map/ppermute | solution.py:20
  56.5 9.9 %shard_map.96 = (f32[64,4096]{1,0:T(8,128)S(1)}, bf16[64,4096]{1,0:T(8,128)(2,1)S(1)}) custom-call(s32[8]{0:T(128)S(1)} %stack.154.spots, bf16[16,2048]{1,0:T(8,128)(2,1)S(1)} %collective-permute-done.2.refs_0_, bf16[16,2048]{1,0:T(8,128)(2,1)S(1)} %collective-permute-done.3.refs_1_, bf16[16,2048]{1,0:T(8,128)(2,1)S(1)} %collective-permute-done.4.refs_2_, ...), custom_call_target="tpu_custom_call" | custom-call | flops 2147483648 | bytes 16777216 | tf_op jit(solution)/shard_map/pallas_call | solution.py:59
  68.6 3.5 %collective-permute-start.17 = (bf16[32,4096]{1,0:T(8,128)(2,1)S(1)}, bf16[32,4096]{1,0:T(8,128)(2,1)S(1)}, u32[]{:S(2)}, u32[]{:S(2)}) collective-permute-start(bf16[32,4096]{1,0:T(8,128)(2,1)S(1)} %pad_maximum_fusion.5), channel_id=1, source_target_pairs={{0,16},{4,20},{8,24},{12,28},{16,0},{20,4},{24,8},{28,12},{1,17},{... | collective-permute-start | bytes 786440 | tf_op jit(solution)/shard_map/ppermute | solution.py:20
  72.1 8.4 %collective-permute-done.11 = bf16[32,4096]{1,0:T(8,128)(2,1)S(1)} collective-permute-done((bf16[32,4096]{1,0:T(8,128)(2,1)S(1)}, bf16[32,4096]{1,0:T(8,128)(2,1)S(1)}, u32[]{:S(2)}, u32[]{:S(2)}) %collective-permute-start.11) | collective-permute-done | bytes 262176 | tf_op jit(solution)/shard_map/ppermute | solution.py:20
  80.7 6.8 %collective-permute-done.17 = bf16[32,4096]{1,0:T(8,128)(2,1)S(1)} collective-permute-done((bf16[32,4096]{1,0:T(8,128)(2,1)S(1)}, bf16[32,4096]{1,0:T(8,128)(2,1)S(1)}, u32[]{:S(2)}, u32[]{:S(2)}) %collective-permute-start.17) | collective-permute-done | bytes 262176 | tf_op jit(solution)/shard_map/ppermute | solution.py:20
  89.9 2.7 %collective-permute-done.18 = bf16[16,4096]{1,0:T(8,128)(2,1)S(1)} collective-permute-done((bf16[16,4096]{1,0:T(8,128)(2,1)S(1)}, bf16[16,4096]{1,0:T(8,128)(2,1)S(1)}, u32[]{:S(2)}, u32[]{:S(2)}) %collective-permute-start.18) | collective-permute-done | bytes 131104 | tf_op jit(solution)/shard_map/ppermute | solution.py:20
  94.0 3.4 %collective-permute-start.13 = (bf16[16,4096]{1,0:T(8,128)(2,1)S(1)}, bf16[16,4096]{1,0:T(8,128)(2,1)S(1)}, u32[]{:S(2)}, u32[]{:S(2)}) collective-permute-start(bf16[16,4096]{1,0:T(8,128)(2,1)S(1)} %get-tuple-element.61), channel_id=1, source_target_pairs={{0,16},{4,20},{8,24},{12,28},{16,0},{20,4},{24,8},{28,12},{1,17},{... | collective-permute-start | bytes 393224 | tf_op jit(solution)/shard_map/ppermute | solution.py:20
  100.9 6.7 %collective-permute-done.13 = bf16[16,4096]{1,0:T(8,128)(2,1)S(1)} collective-permute-done((bf16[16,4096]{1,0:T(8,128)(2,1)S(1)}, bf16[16,4096]{1,0:T(8,128)(2,1)S(1)}, u32[]{:S(2)}, u32[]{:S(2)}) %collective-permute-start.13) | collective-permute-done | bytes 131104 | tf_op jit(solution)/shard_map/ppermute | solution.py:20
  107.6 5.6 %collective-permute-done.20 = bf16[32,4096]{1,0:T(8,128)(2,1)S(1)} collective-permute-done((bf16[32,4096]{1,0:T(8,128)(2,1)S(1)}, bf16[32,4096]{1,0:T(8,128)(2,1)S(1)}, u32[]{:S(2)}, u32[]{:S(2)}) %collective-permute-start.20) | collective-permute-done | bytes 262176 | tf_op jit(solution)/shard_map/ppermute | solution.py:20
  113.3 2.6 %collective-permute-done.14 = bf16[32,4096]{1,0:T(8,128)(2,1)S(1)} collective-permute-done((bf16[32,4096]{1,0:T(8,128)(2,1)S(1)}, bf16[32,4096]{1,0:T(8,128)(2,1)S(1)}, u32[]{:S(2)}, u32[]{:S(2)}) %collective-permute-start.14) | collective-permute-done | bytes 262176 | tf_op jit(solution)/shard_map/ppermute | solution.py:20
  118.0 6.2 %shard_map.104 = (f32[128,1024]{1,0:T(8,128)S(1)}, bf16[128,1024]{1,0:T(8,128)(2,1)S(1)}) custom-call(s32[16]{0:T(128)S(1)} %stack.171.spots, bf16[128,4096]{1,0:T(8,128)(2,1)S(1)} %pad_maximum_fusion.refs_0_, bf16[128,4096]{1,0:T(8,128)(2,1)S(1)} %pad_maximum_fusion.1.refs_1_, bf16[4096,8192]{1,0:T(8,128)(2,1)} %refs_2_.15), custom_call_target="tpu_custom_call" | custom-call | flops 2147483648 | bytes 8388608 | tf_op jit(solution)/shard_map/pallas_call | solution.py:106
  124.2 6.2 %shard_map.102 = (f32[128,1024]{1,0:T(8,128)S(1)}, bf16[128,1024]{1,0:T(8,128)(2,1)S(1)}) custom-call(s32[16]{0:T(128)S(1)} %stack.171.spots, bf16[128,4096]{1,0:T(8,128)(2,1)S(1)} %pad_maximum_fusion.refs_0_, bf16[128,4096]{1,0:T(8,128)(2,1)S(1)} %pad_maximum_fusion.1.refs_1_, bf16[4096,8192]{1,0:T(8,128)(2,1)} %refs_2_.15), custom_call_target="tpu_custom_call" | custom-call | flops 2147483648 | bytes 8388608 | tf_op jit(solution)/shard_map/pallas_call | solution.py:106
  130.5 6.2 %shard_map.103 = (f32[128,1024]{1,0:T(8,128)S(1)}, bf16[128,1024]{1,0:T(8,128)(2,1)S(1)}) custom-call(s32[16]{0:T(128)S(1)} %stack.145.spots, bf16[128,4096]{1,0:T(8,128)(2,1)S(1)} %pad_maximum_fusion.refs_0_, bf16[128,4096]{1,0:T(8,128)(2,1)S(1)} %pad_maximum_fusion.1.refs_1_, bf16[4096,8192]{1,0:T(8,128)(2,1)} %refs_2_.15), custom_call_target="tpu_custom_call" | custom-call | flops 2147483648 | bytes 8388608 | tf_op jit(solution)/shard_map/pallas_call | solution.py:106
  136.7 6.2 %shard_map.101 = (f32[128,1024]{1,0:T(8,128)S(1)}, bf16[128,1024]{1,0:T(8,128)(2,1)S(1)}) custom-call(s32[16]{0:T(128)S(1)} %stack.145.spots, bf16[128,4096]{1,0:T(8,128)(2,1)S(1)} %pad_maximum_fusion.refs_0_, bf16[128,4096]{1,0:T(8,128)(2,1)S(1)} %pad_maximum_fusion.1.refs_1_, bf16[4096,8192]{1,0:T(8,128)(2,1)} %refs_2_.15), custom_call_target="tpu_custom_call" | custom-call | flops 2147483648 | bytes 8388608 | tf_op jit(solution)/shard_map/pallas_call | solution.py:106
  142.9 6.2 %shard_map.100 = (f32[128,1024]{1,0:T(8,128)S(1)}, bf16[128,1024]{1,0:T(8,128)(2,1)S(1)}) custom-call(s32[16]{0:T(128)S(1)} %stack.171.spots, bf16[128,4096]{1,0:T(8,128)(2,1)S(1)} %pad_maximum_fusion.refs_0_, bf16[128,4096]{1,0:T(8,128)(2,1)S(1)} %pad_maximum_fusion.1.refs_1_, bf16[4096,8192]{1,0:T(8,128)(2,1)} %refs_2_.15), custom_call_target="tpu_custom_call" | custom-call | flops 2147483648 | bytes 8388608 | tf_op jit(solution)/shard_map/pallas_call | solution.py:106
  149.2 6.2 %shard_map.99 = (f32[128,1024]{1,0:T(8,128)S(1)}, bf16[128,1024]{1,0:T(8,128)(2,1)S(1)}) custom-call(s32[16]{0:T(128)S(1)} %stack.145.spots, bf16[128,4096]{1,0:T(8,128)(2,1)S(1)} %pad_maximum_fusion.refs_0_, bf16[128,4096]{1,0:T(8,128)(2,1)S(1)} %pad_maximum_fusion.1.refs_1_, bf16[4096,8192]{1,0:T(8,128)(2,1)} %refs_2_.15), custom_call_target="tpu_custom_call" | custom-call | flops 2147483648 | bytes 8388608 | tf_op jit(solution)/shard_map/pallas_call | solution.py:106
  155.8 6.2 %shard_map.98 = (f32[128,1024]{1,0:T(8,128)S(1)}, bf16[128,1024]{1,0:T(8,128)(2,1)S(1)}) custom-call(s32[16]{0:T(128)S(1)} %stack.171.spots, bf16[128,4096]{1,0:T(8,128)(2,1)S(1)} %pad_maximum_fusion.refs_0_, bf16[128,4096]{1,0:T(8,128)(2,1)S(1)} %pad_maximum_fusion.1.refs_1_, bf16[4096,8192]{1,0:T(8,128)(2,1)} %refs_2_.15), custom_call_target="tpu_custom_call" | custom-call | flops 2147483648 | bytes 8388608 | tf_op jit(solution)/shard_map/pallas_call | solution.py:106
  162.8 6.2 %shard_map.97 = (f32[128,1024]{1,0:T(8,128)S(1)}, bf16[128,1024]{1,0:T(8,128)(2,1)S(1)}) custom-call(s32[16]{0:T(128)S(1)} %stack.145.spots, bf16[128,4096]{1,0:T(8,128)(2,1)S(1)} %pad_maximum_fusion.refs_0_, bf16[128,4096]{1,0:T(8,128)(2,1)S(1)} %pad_maximum_fusion.1.refs_1_, bf16[4096,8192]{1,0:T(8,128)(2,1)} %refs_2_.15), custom_call_target="tpu_custom_call" | custom-call | flops 2147483648 | bytes 8388608 | tf_op jit(solution)/shard_map/pallas_call | solution.py:106
  175.0 3.3 %collective-permute-done.27 = bf16[128,1024]{1,0:T(8,128)(2,1)S(1)} collective-permute-done((bf16[128,1024]{1,0:T(8,128)(2,1)S(1)}, bf16[128,1024]{1,0:T(8,128)(2,1)S(1)}, u32[]{:S(2)}, u32[]{:S(2)}) %collective-permute-start.27) | collective-permute-done | bytes 262176 | tf_op jit(solution)/shard_map/ppermute | solution.py:20
  181.4 2.5 %collective-permute-done.25 = bf16[128,1024]{1,0:T(8,128)(2,1)S(1)} collective-permute-done((bf16[128,1024]{1,0:T(8,128)(2,1)S(1)}, bf16[128,1024]{1,0:T(8,128)(2,1)S(1)}, u32[]{:S(2)}, u32[]{:S(2)}) %collective-permute-start.25) | collective-permute-done | bytes 262176 | tf_op jit(solution)/shard_map/ppermute | solution.py:20
  187.3 2.3 collective-permute-done.23
  201.7 25.6 %shard_map.105 = (f32[64,8192]{1,0:T(8,128)S(1)}, f32[64,128]{1,0:T(8,128)S(1)}) custom-call(s32[64,128]{1,0:T(8,128)S(1)} %pad.4.wanted, f32[64,1024]{1,0:T(8,128)S(1)} %slice.377.refs_0_, f32[64,1024]{1,0:T(8,128)S(1)} %slice.378.refs_1_, f32[64,1024]{1,0:T(8,128)S(1)} %slice.379.refs_2_, f32[64,1024]{1,0:T(8,128)S(1)} %slice.380.refs_3_, ...), custom_call_target="tpu_custom_call" | custom-call | tf_op jit(solution)/shard_map/pallas_call | solution.py:166
  232.0 3.0 %collective-permute-start.43 = (f32[64,128]{1,0:T(8,128)S(1)}, f32[64,128]{1,0:T(8,128)S(1)}, u32[]{:S(2)}, u32[]{:S(2)}) collective-permute-start(f32[64,128]{1,0:T(8,128)S(1)} %get-tuple-element.45), channel_id=1, source_target_pairs={{0,24},{4,28},{8,16},{12,20},{16,8},{20,12},{24,0},{28,4},{1,25},{... | collective-permute-start | bytes 98312 | tf_op jit(solution)/shard_map/ppermute | solution.py:276
  241.2 2.9 %copy.60 = f32[2,16,2,8192]{3,2,1,0:T(2,128)} copy(f32[2,16,2,8192]{3,1,2,0:T(8,128)S(1)} %bitcast.163) | data formatting | bytes 4194304 | tf_op jit(solution)/shard_map/transpose | solution.py:290
  (174 shorter events, 56.4 us)
Async XLA Ops:
  5.0 13.5 %collective-permute-start.2 = (bf16[16,2048]{1,0:T(8,128)(2,1)S(1)}, bf16[16,2048]{1,0:T(8,128)(2,1)S(1)}, u32[]{:S(2)}, u32[]{:S(2)}) collective-permute-start(bf16[16,2048]{1,0:T(8,128)(2,1)S(1)} %get-tuple-element.63), channel_id=1, source_target_pairs={{0,0},{1,8},{2,16},{3,24},{4,1},{5,9},{6,17},{7,25},{8,2},{9,10},{... | collective-permute-start | bytes 196616 | tf_op jit(solution)/shard_map/ppermute | solution.py:210
  5.7 15.5 %collective-permute-start.3 = (bf16[16,2048]{1,0:T(8,128)(2,1)S(1)}, bf16[16,2048]{1,0:T(8,128)(2,1)S(1)}, u32[]{:S(2)}, u32[]{:S(2)}) collective-permute-start(bf16[16,2048]{1,0:T(8,128)(2,1)S(1)} %get-tuple-element.63), channel_id=1, source_target_pairs={{0,1},{1,9},{2,17},{3,25},{4,0},{5,8},{6,16},{7,24},{8,3},{9,11},{... | collective-permute-start | bytes 196616 | tf_op jit(solution)/shard_map/ppermute | solution.py:210
  11.5 20.6 %collective-permute-start.4 = (bf16[16,2048]{1,0:T(8,128)(2,1)S(1)}, bf16[16,2048]{1,0:T(8,128)(2,1)S(1)}, u32[]{:S(2)}, u32[]{:S(2)}) collective-permute-start(bf16[16,2048]{1,0:T(8,128)(2,1)S(1)} %get-tuple-element.63), channel_id=1, source_target_pairs={{0,2},{1,10},{2,18},{3,26},{4,3},{5,11},{6,19},{7,27},{8,0},{9,8},... | collective-permute-start | bytes 196616 | tf_op jit(solution)/shard_map/ppermute | solution.py:210
  13.4 20.2 %collective-permute-start.5 = (bf16[16,2048]{1,0:T(8,128)(2,1)S(1)}, bf16[16,2048]{1,0:T(8,128)(2,1)S(1)}, u32[]{:S(2)}, u32[]{:S(2)}) collective-permute-start(bf16[16,2048]{1,0:T(8,128)(2,1)S(1)} %get-tuple-element.63), channel_id=1, source_target_pairs={{0,3},{1,11},{2,19},{3,27},{4,2},{5,10},{6,18},{7,26},{8,1},{9,9},... | collective-permute-start | bytes 196616 | tf_op jit(solution)/shard_map/ppermute | solution.py:210
  18.4 21.1 %collective-permute-start.6 = (bf16[16,2048]{1,0:T(8,128)(2,1)S(1)}, bf16[16,2048]{1,0:T(8,128)(2,1)S(1)}, u32[]{:S(2)}, u32[]{:S(2)}) collective-permute-start(bf16[16,2048]{1,0:T(8,128)(2,1)S(1)} %get-tuple-element.62), channel_id=1, source_target_pairs={{0,4},{1,12},{2,20},{3,28},{4,5},{5,13},{6,21},{7,29},{8,6},{9,14}... | collective-permute-start | bytes 196616 | tf_op jit(solution)/shard_map/ppermute | solution.py:210
  18.5 21.0 %collective-permute-start.7 = (bf16[16,2048]{1,0:T(8,128)(2,1)S(1)}, bf16[16,2048]{1,0:T(8,128)(2,1)S(1)}, u32[]{:S(2)}, u32[]{:S(2)}) collective-permute-start(bf16[16,2048]{1,0:T(8,128)(2,1)S(1)} %get-tuple-element.62), channel_id=1, source_target_pairs={{0,5},{1,13},{2,21},{3,29},{4,4},{5,12},{6,20},{7,28},{8,7},{9,15}... | collective-permute-start | bytes 196616 | tf_op jit(solution)/shard_map/ppermute | solution.py:210
  21.2 20.2 %collective-permute-start.8 = (bf16[16,2048]{1,0:T(8,128)(2,1)S(1)}, bf16[16,2048]{1,0:T(8,128)(2,1)S(1)}, u32[]{:S(2)}, u32[]{:S(2)}) collective-permute-start(bf16[16,2048]{1,0:T(8,128)(2,1)S(1)} %get-tuple-element.62), channel_id=1, source_target_pairs={{0,6},{1,14},{2,22},{3,30},{4,7},{5,15},{6,23},{7,31},{8,4},{9,12}... | collective-permute-start | bytes 196616 | tf_op jit(solution)/shard_map/ppermute | solution.py:210
  32.1 9.3 %collective-permute-start.9 = (bf16[16,2048]{1,0:T(8,128)(2,1)S(1)}, bf16[16,2048]{1,0:T(8,128)(2,1)S(1)}, u32[]{:S(2)}, u32[]{:S(2)}) collective-permute-start(bf16[16,2048]{1,0:T(8,128)(2,1)S(1)} %get-tuple-element.62), channel_id=1, source_target_pairs={{0,7},{1,15},{2,23},{3,31},{4,6},{5,14},{6,22},{7,30},{8,5},{9,13}... | collective-permute-start | bytes 196616 | tf_op jit(solution)/shard_map/ppermute | solution.py:210
  33.6 22.5 %collective-permute-start = (f32[16,1]{0,1:T(1,128)S(1)}, f32[16,1]{0,1:T(1,128)S(1)}, u32[]{:S(2)}, u32[]{:S(2)}) collective-permute-start(f32[16,1]{0,1:T(1,128)S(1)} %bitcast.170), channel_id=1, source_target_pairs={{0,1},{1,0},{2,3},{3,2},{4,5},{5,4},{6,7},{7,6},{8,9},{9,8},{10,11... | collective-permute-start | bytes 200 | tf_op jit(solution)/shard_map/ppermute | solution.py:20
  51.4 15.3 %collective-permute-start.10 = (bf16[64,4096]{1,0:T(8,128)(2,1)S(1)}, bf16[64,4096]{1,0:T(8,128)(2,1)S(1)}, u32[]{:S(2)}, u32[]{:S(2)}) collective-permute-start(bf16[64,4096]{1,0:T(8,128)(2,1)S(1)} %get-tuple-element.25), channel_id=1, source_target_pairs={{0,4},{4,0},{8,12},{12,8},{16,20},{20,16},{24,28},{28,24},{1,5},{5... | collective-permute-start | bytes 1572872 | tf_op jit(solution)/shard_map/ppermute | solution.py:20
  56.1 32.6 %collective-permute-start.1 = (f32[16,1]{0,1:T(1,128)S(1)}, f32[16,1]{0,1:T(1,128)S(1)}, u32[]{:S(2)}, u32[]{:S(2)}) collective-permute-start(f32[16,1]{0,1:T(1,128)S(1)} %bitcast_add_fusion), channel_id=1, source_target_pairs={{0,2},{1,3},{2,0},{3,1},{4,6},{5,7},{6,4},{7,5},{8,10},{9,11},{10,... | collective-permute-start | bytes 200 | tf_op jit(solution)/shard_map/ppermute | solution.py:20
  66.8 13.7 %collective-permute-start.11 = (bf16[32,4096]{1,0:T(8,128)(2,1)S(1)}, bf16[32,4096]{1,0:T(8,128)(2,1)S(1)}, u32[]{:S(2)}, u32[]{:S(2)}) collective-permute-start(bf16[32,4096]{1,0:T(8,128)(2,1)S(1)} %concatenate.81), channel_id=1, source_target_pairs={{0,8},{4,12},{8,0},{12,4},{16,24},{20,28},{24,16},{28,20},{1,9},{5... | collective-permute-start | bytes 786440 | tf_op jit(solution)/shard_map/ppermute | solution.py:20
  68.6 18.9 %collective-permute-start.17 = (bf16[32,4096]{1,0:T(8,128)(2,1)S(1)}, bf16[32,4096]{1,0:T(8,128)(2,1)S(1)}, u32[]{:S(2)}, u32[]{:S(2)}) collective-permute-start(bf16[32,4096]{1,0:T(8,128)(2,1)S(1)} %pad_maximum_fusion.5), channel_id=1, source_target_pairs={{0,16},{4,20},{8,24},{12,28},{16,0},{20,4},{24,8},{28,12},{1,17},{... | collective-permute-start | bytes 786440 | tf_op jit(solution)/shard_map/ppermute | solution.py:20
  80.6 9.3 %collective-permute-start.12 = (bf16[16,4096]{1,0:T(8,128)(2,1)S(1)}, bf16[16,4096]{1,0:T(8,128)(2,1)S(1)}, u32[]{:S(2)}, u32[]{:S(2)}) collective-permute-start(bf16[16,4096]{1,0:T(8,128)(2,1)S(1)} %slice.539), channel_id=1, source_target_pairs={{0,16},{4,20},{8,24},{12,28},{16,0},{20,4},{24,8},{28,12},{1,17},{... | collective-permute-start | bytes 393224 | tf_op jit(solution)/shard_map/ppermute | solution.py:20
  94.0 13.6 %collective-permute-start.13 = (bf16[16,4096]{1,0:T(8,128)(2,1)S(1)}, bf16[16,4096]{1,0:T(8,128)(2,1)S(1)}, u32[]{:S(2)}, u32[]{:S(2)}) collective-permute-start(bf16[16,4096]{1,0:T(8,128)(2,1)S(1)} %get-tuple-element.61), channel_id=1, source_target_pairs={{0,16},{4,20},{8,24},{12,28},{16,0},{20,4},{24,8},{28,12},{1,17},{... | collective-permute-start | bytes 393224 | tf_op jit(solution)/shard_map/ppermute | solution.py:20
  99.2 14.0 %collective-permute-start.20 = (bf16[32,4096]{1,0:T(8,128)(2,1)S(1)}, bf16[32,4096]{1,0:T(8,128)(2,1)S(1)}, u32[]{:S(2)}, u32[]{:S(2)}) collective-permute-start(bf16[32,4096]{1,0:T(8,128)(2,1)S(1)} %pad_maximum_fusion.6), channel_id=1, source_target_pairs={{0,16},{4,20},{8,24},{12,28},{16,0},{20,4},{24,8},{28,12},{1,17},{... | collective-permute-start | bytes 786440 | tf_op jit(solution)/shard_map/ppermute | solution.py:20
  107.5 8.4 %collective-permute-start.14 = (bf16[32,4096]{1,0:T(8,128)(2,1)S(1)}, bf16[32,4096]{1,0:T(8,128)(2,1)S(1)}, u32[]{:S(2)}, u32[]{:S(2)}) collective-permute-start(bf16[32,4096]{1,0:T(8,128)(2,1)S(1)} %pad_maximum_fusion.4), channel_id=1, source_target_pairs={{0,8},{4,12},{8,0},{12,4},{16,24},{20,28},{24,16},{28,20},{1,9},{5... | collective-permute-start | bytes 786440 | tf_op jit(solution)/shard_map/ppermute | solution.py:20
  155.4 17.1 %collective-permute-start.29 = (bf16[128,1024]{1,0:T(8,128)(2,1)S(1)}, bf16[128,1024]{1,0:T(8,128)(2,1)S(1)}, u32[]{:S(2)}, u32[]{:S(2)}) collective-permute-start(bf16[128,1024]{1,0:T(8,128)(2,1)S(1)} %get-tuple-element.43), channel_id=1, source_target_pairs={{0,2},{1,3},{2,0},{3,1},{4,6},{5,7},{6,4},{7,5},{8,10},{9,11},{10,... | collective-permute-start | bytes 786440 | tf_op jit(solution)/shard_map/ppermute | solution.py:20
  162.1 11.1 %collective-permute-start.28 = (bf16[128,1024]{1,0:T(8,128)(2,1)S(1)}, bf16[128,1024]{1,0:T(8,128)(2,1)S(1)}, u32[]{:S(2)}, u32[]{:S(2)}) collective-permute-start(bf16[128,1024]{1,0:T(8,128)(2,1)S(1)} %get-tuple-element.41), channel_id=1, source_target_pairs={{0,1},{1,0},{2,3},{3,2},{4,5},{5,4},{6,7},{7,6},{8,9},{9,8},{10,11... | collective-permute-start | bytes 786440 | tf_op jit(solution)/shard_map/ppermute | solution.py:20
  169.0 9.3 %collective-permute-start.27 = (bf16[128,1024]{1,0:T(8,128)(2,1)S(1)}, bf16[128,1024]{1,0:T(8,128)(2,1)S(1)}, u32[]{:S(2)}, u32[]{:S(2)}) collective-permute-start(bf16[128,1024]{1,0:T(8,128)(2,1)S(1)} %get-tuple-element.39), channel_id=1, source_target_pairs={{0,2},{1,3},{2,0},{3,1},{4,6},{5,7},{6,4},{7,5},{8,10},{9,11},{10,... | collective-permute-start | bytes 786440 | tf_op jit(solution)/shard_map/ppermute | solution.py:20
  170.7 9.2 %collective-permute-start.26 = (bf16[128,1024]{1,0:T(8,128)(2,1)S(1)}, bf16[128,1024]{1,0:T(8,128)(2,1)S(1)}, u32[]{:S(2)}, u32[]{:S(2)}) collective-permute-start(bf16[128,1024]{1,0:T(8,128)(2,1)S(1)} %get-tuple-element.37), channel_id=1, source_target_pairs={{0,1},{1,0},{2,3},{3,2},{4,5},{5,4},{6,7},{7,6},{8,9},{9,8},{10,11... | collective-permute-start | bytes 786440 | tf_op jit(solution)/shard_map/ppermute | solution.py:20
  172.1 11.8 %collective-permute-start.25 = (bf16[128,1024]{1,0:T(8,128)(2,1)S(1)}, bf16[128,1024]{1,0:T(8,128)(2,1)S(1)}, u32[]{:S(2)}, u32[]{:S(2)}) collective-permute-start(bf16[128,1024]{1,0:T(8,128)(2,1)S(1)} %get-tuple-element.35), channel_id=1, source_target_pairs={{0,2},{1,3},{2,0},{3,1},{4,6},{5,7},{6,4},{7,5},{8,10},{9,11},{10,... | collective-permute-start | bytes 786440 | tf_op jit(solution)/shard_map/ppermute | solution.py:20
  172.5 13.1 %collective-permute-start.24 = (bf16[128,1024]{1,0:T(8,128)(2,1)S(1)}, bf16[128,1024]{1,0:T(8,128)(2,1)S(1)}, u32[]{:S(2)}, u32[]{:S(2)}) collective-permute-start(bf16[128,1024]{1,0:T(8,128)(2,1)S(1)} %get-tuple-element.33), channel_id=1, source_target_pairs={{0,1},{1,0},{2,3},{3,2},{4,5},{5,4},{6,7},{7,6},{8,9},{9,8},{10,11... | collective-permute-start | bytes 786440 | tf_op jit(solution)/shard_map/ppermute | solution.py:20
  173.2 16.3 %collective-permute-start.23 = (bf16[128,1024]{1,0:T(8,128)(2,1)S(1)}, bf16[128,1024]{1,0:T(8,128)(2,1)S(1)}, u32[]{:S(2)}, u32[]{:S(2)}) collective-permute-start(bf16[128,1024]{1,0:T(8,128)(2,1)S(1)} %get-tuple-element.31), channel_id=1, source_target_pairs={{0,2},{1,3},{2,0},{3,1},{4,6},{5,7},{6,4},{7,5},{8,10},{9,11},{10,... | collective-permute-start | bytes 786440 | tf_op jit(solution)/shard_map/ppermute | solution.py:20
  178.3 12.9 %collective-permute-start.22 = (bf16[128,1024]{1,0:T(8,128)(2,1)S(1)}, bf16[128,1024]{1,0:T(8,128)(2,1)S(1)}, u32[]{:S(2)}, u32[]{:S(2)}) collective-permute-start(bf16[128,1024]{1,0:T(8,128)(2,1)S(1)} %get-tuple-element.29), channel_id=1, source_target_pairs={{0,1},{1,0},{2,3},{3,2},{4,5},{5,4},{6,7},{7,6},{8,9},{9,8},{10,11... | collective-permute-start | bytes 786440 | tf_op jit(solution)/shard_map/ppermute | solution.py:20
  179.9 14.0 %collective-permute-start.37 = (bf16[64,1024]{1,0:T(8,128)(2,1)S(1)}, bf16[64,1024]{1,0:T(8,128)(2,1)S(1)}, u32[]{:S(2)}, u32[]{:S(2)}) collective-permute-start(bf16[64,1024]{1,0:T(8,128)(2,1)S(1)} %slice.530), channel_id=1, source_target_pairs={{0,1},{1,0},{2,3},{3,2},{4,5},{5,4},{6,7},{7,6},{8,9},{9,8},{10,11... | collective-permute-start | bytes 393224 | tf_op jit(solution)/shard_map/ppermute | solution.py:20
  183.9 10.5 %collective-permute-start.36 = (bf16[64,1024]{1,0:T(8,128)(2,1)S(1)}, bf16[64,1024]{1,0:T(8,128)(2,1)S(1)}, u32[]{:S(2)}, u32[]{:S(2)}) collective-permute-start(bf16[64,1024]{1,0:T(8,128)(2,1)S(1)} %slice.531), channel_id=1, source_target_pairs={{0,2},{1,3},{2,0},{3,1},{4,6},{5,7},{6,4},{7,5},{8,10},{9,11},{10,... | collective-permute-start | bytes 393224 | tf_op jit(solution)/shard_map/ppermute | solution.py:20
  185.6 11.1 %collective-permute-start.35 = (bf16[64,1024]{1,0:T(8,128)(2,1)S(1)}, bf16[64,1024]{1,0:T(8,128)(2,1)S(1)}, u32[]{:S(2)}, u32[]{:S(2)}) collective-permute-start(bf16[64,1024]{1,0:T(8,128)(2,1)S(1)} %slice.532), channel_id=1, source_target_pairs={{0,1},{1,0},{2,3},{3,2},{4,5},{5,4},{6,7},{7,6},{8,9},{9,8},{10,11... | collective-permute-start | bytes 393224 | tf_op jit(solution)/shard_map/ppermute | solution.py:20
  189.5 9.7 %collective-permute-start.34 = (bf16[64,1024]{1,0:T(8,128)(2,1)S(1)}, bf16[64,1024]{1,0:T(8,128)(2,1)S(1)}, u32[]{:S(2)}, u32[]{:S(2)}) collective-permute-start(bf16[64,1024]{1,0:T(8,128)(2,1)S(1)} %slice.533), channel_id=1, source_target_pairs={{0,2},{1,3},{2,0},{3,1},{4,6},{5,7},{6,4},{7,5},{8,10},{9,11},{10,... | collective-permute-start | bytes 393224 | tf_op jit(solution)/shard_map/ppermute | solution.py:20
  191.3 8.0 %collective-permute-start.33 = (bf16[64,1024]{1,0:T(8,128)(2,1)S(1)}, bf16[64,1024]{1,0:T(8,128)(2,1)S(1)}, u32[]{:S(2)}, u32[]{:S(2)}) collective-permute-start(bf16[64,1024]{1,0:T(8,128)(2,1)S(1)} %slice.534), channel_id=1, source_target_pairs={{0,1},{1,0},{2,3},{3,2},{4,5},{5,4},{6,7},{7,6},{8,9},{9,8},{10,11... | collective-permute-start | bytes 393224 | tf_op jit(solution)/shard_map/ppermute | solution.py:20
  227.4 7.5 %collective-permute-start.39 = (f32[64,128]{1,0:T(8,128)S(1)}, f32[64,128]{1,0:T(8,128)S(1)}, u32[]{:S(2)}, u32[]{:S(2)}) collective-permute-start(f32[64,128]{1,0:T(8,128)S(1)} %get-tuple-element.45), channel_id=1, source_target_pairs={{0,8},{4,12},{8,0},{12,4},{16,24},{20,28},{24,16},{28,20},{1,9},{5... | collective-permute-start | bytes 98312 | tf_op jit(solution)/shard_map/ppermute | solution.py:276
  227.6 8.3 %collective-permute-start.40 = (f32[64,128]{1,0:T(8,128)S(1)}, f32[64,128]{1,0:T(8,128)S(1)}, u32[]{:S(2)}, u32[]{:S(2)}) collective-permute-start(f32[64,128]{1,0:T(8,128)S(1)} %get-tuple-element.45), channel_id=1, source_target_pairs={{0,12},{4,8},{8,4},{12,0},{16,28},{20,24},{24,20},{28,16},{1,13},{... | collective-permute-start | bytes 98312 | tf_op jit(solution)/shard_map/ppermute | solution.py:276
  (26 other events, 175.3 us)

commit v2 on v0

v2 whole, which is shorter than its diff:
```python
import functools

import jax
import jax.numpy as jnp
from jax import lax
from jax.experimental import pallas as pl
from jax.experimental.pallas import tpu as pltpu
from jax.sharding import PartitionSpec as P

EPSILON = 1e-05
MIB = 1024 * 1024
LANES = 128
CODE_BITS = 14


def bits_of(count):
    return [1 << i for i in range(count.bit_length() - 1)]


def swap(array, axis, partner):
    return lax.ppermute(array, axis, [(i, partner(i)) for i in range(lax.axis_size(axis))])


def place(index, stages):
    spot = 0
    for bit in stages:
        spot = 2 * spot + (index & bit) // bit
    return spot


def unplace(spot, stages):
    index = 0
    for step, bit in enumerate(stages[::-1]):
        index = index + ((spot >> step) & 1) * bit
    return index


def widest(limit, size):
    tile = min(limit, size)
    while size % tile:
        tile //= 2
    return tile


def weight_specs(ways, depth, tile, index):
    share = depth // ways
    return [pl.BlockSpec((share, tile), functools.partial(index, way)) for way in range(ways)]


def head_body(info, came, *refs, ways, height):
    weights, (out, rows) = refs[:ways], refs[ways:]

    @pl.when(pl.program_id(0) == 0)
    def _():
        for unit in range(came.shape[0] // height):
            start = pl.multiple_of(info[1 + unit] * height, height)
            rows[pl.ds(start, height), :] = came[unit * height : (unit + 1) * height, :]

    share = rows.shape[1] // ways
    total = None
    for way in range(ways):
        term = jnp.dot(
            rows[:, way * share : (way + 1) * share],
            weights[way][0],
            preferred_element_type=jnp.float32,
        )
        total = term if total is None else total + term
    out[...] = total.astype(out.dtype)


def head_matmul(info, came, head_weight, height, out_type):
    count, depth = came.shape
    width = head_weight.shape[2]
    tile = widest(512, width)
    ways = 4
    share = depth // ways
    specs = [
        pl.BlockSpec(
            (1, share, tile),
            functools.partial(lambda way, n, s: (s[0], way, n), way),
        )
        for way in range(ways)
    ]
    return pl.pallas_call(
        functools.partial(head_body, ways=ways, height=height),
        grid_spec=pltpu.PrefetchScalarGridSpec(
            num_scalar_prefetch=1,
            grid=(width // tile,),
            in_specs=[pl.BlockSpec((count, depth), lambda n, s: (0, 0))] + specs,
            out_specs=pl.BlockSpec((count, tile), lambda n, s: (0, n)),
            scratch_shapes=[pltpu.VMEM((count, depth), jnp.bfloat16)],
        ),
        out_shape=jax.ShapeDtypeStruct((count, width), out_type),
        compiler_params=pltpu.CompilerParams(vmem_limit_bytes=32 * MIB),
        cost_estimate=pl.CostEstimate(
            flops=2 * count * depth * width, bytes_accessed=2 * depth * width, transcendentals=0
        ),
    )(info, came, *[head_weight] * ways)


def encode(value):
    top = jnp.max(jnp.abs(value), axis=1, keepdims=True)
    power = jnp.floor(jnp.log2(jnp.maximum(top, 1e-30))) + 1.0
    code = jnp.floor(value * jnp.exp2(CODE_BITS - power) + 0.5)
    return code.astype(jnp.int32).astype(jnp.int16), power


def decode(code, power):
    return code.astype(jnp.int32).astype(jnp.float32) * jnp.exp2(power - CODE_BITS)


def marks_of(powers, height):
    lane = lax.broadcasted_iota(jnp.int32, (height, LANES), 1)
    marks = jnp.zeros((height, LANES), jnp.float32)
    for index, power in enumerate(powers):
        marks = jnp.where(lane == index, power, marks)
    return marks.astype(jnp.int32).astype(jnp.int16)


def vocab_body(spots, *refs, heads, height, ways, tile, waits):
    parts, refs = refs[:heads], refs[heads:]
    weights, (keep, send, rows, powers) = refs[:ways], refs[ways + waits :]
    blocks = parts[0].shape[0] // height
    step = pl.program_id(0)

    @pl.when(step == 0)
    def _():
        powers[...] = jnp.zeros_like(powers)
        for head in range(heads):
            for block in range(blocks):
                start = pl.multiple_of(spots[head * blocks + block] * height, height)
                rows[pl.ds(start, height), :] = parts[head][block * height : (block + 1) * height, :]

    share = rows.shape[1] // ways
    total = None
    for way in range(ways):
        term = jnp.dot(
            rows[:, way * share : (way + 1) * share],
            weights[way][...],
            preferred_element_type=jnp.float32,
        )
        total = term if total is None else total + term
    half = total.shape[0] // 2
    keep[...] = total[:half]
    code, power = encode(total[half:])
    send[:, pl.ds(pl.multiple_of(step * tile, tile), tile)] = code
    lane = lax.broadcasted_iota(jnp.int32, powers.shape, 1)
    powers[...] = jnp.where(lane == step, power, powers[...])

    @pl.when(step == pl.num_programs(0) - 1)
    def _():
        width = send.shape[1] - LANES
        send[:, width:] = powers[...].astype(jnp.int32).astype(jnp.int16)


def vocab_matmul(spots, parts, height, vocab_weight, first, width, tile, after):
    heads = len(parts)
    depth = vocab_weight.shape[0]
    all_rows = sum(p.shape[0] for p in parts)
    half = all_rows // 2
    base = first // tile
    ways = 4
    return pl.pallas_call(
        functools.partial(
            vocab_body, heads=heads, height=height, ways=ways, tile=tile, waits=len(after)
        ),
        grid_spec=pltpu.PrefetchScalarGridSpec(
            num_scalar_prefetch=1,
            grid=(width // tile,),
            in_specs=[pl.BlockSpec(p.shape, lambda n, s: (0, 0)) for p in parts]
            + weight_specs(ways, depth, tile, lambda way, n, s: (way, base + n))
            + [pl.BlockSpec(memory_space=pl.ANY)] * len(after),
            out_specs=[
                pl.BlockSpec((half, tile), lambda n, s: (0, n)),
                pl.BlockSpec((half, width + LANES), lambda n, s: (0, 0)),
            ],
            scratch_shapes=[
                pltpu.VMEM((all_rows, depth), jnp.bfloat16),
                pltpu.VMEM((half, LANES), jnp.float32),
            ],
        ),
        out_shape=[
            jax.ShapeDtypeStruct((half, width), jnp.float32),
            jax.ShapeDtypeStruct((half, width + LANES), jnp.int16),
        ],
        compiler_params=pltpu.CompilerParams(vmem_limit_bytes=40 * MIB),
        cost_estimate=pl.CostEstimate(
            flops=2 * all_rows * depth * width, bytes_accessed=2 * depth * width, transcendentals=0
        ),
    )(spots, *parts, *[vocab_weight] * ways, *after)


def fold_body(keep, came, stay, send, *, tile):
    half, width = stay.shape
    for row in range(0, 2 * half, 16):
        here = slice(row, row + 16)
        marks = came[here, width:].astype(jnp.int32).astype(jnp.float32)
        powers = []
        for step in range(width // tile):
            block = slice(step * tile, (step + 1) * tile)
            value = keep[here, block] + decode(came[here, block], marks[:, step : step + 1])
            if row < half:
                stay[here, block] = value
            else:
                there = slice(row - half, row - half + 16)
                code, power = encode(value)
                send[there, block] = code
                powers.append(power)
        if row >= half:
            send[row - half : row - half + 16, width:] = marks_of(powers, 16)


def fold(keep, came, tile):
    rows, width = keep.shape
    half = rows // 2
    vmem = pl.BlockSpec(memory_space=pltpu.VMEM)
    return pl.pallas_call(
        functools.partial(fold_body, tile=tile),
        in_specs=[vmem] * 2,
        out_specs=[vmem] * 2,
        out_shape=[
            jax.ShapeDtypeStruct((half, width), jnp.float32),
            jax.ShapeDtypeStruct((half, width + LANES), jnp.int16),
        ],
        compiler_params=pltpu.CompilerParams(vmem_limit_bytes=16 * MIB),
    )(keep, came)


def finish_body(wanted, keep, came, logits, stats, *, tile, choices, first):
    rows, width = keep.shape
    height = 16
    lane = lax.broadcasted_iota(jnp.int32, (height, LANES), 1)
    for row in range(0, rows, height):
        here = slice(row, row + height)
        marks = came[here, width:].astype(jnp.int32).astype(jnp.float32)
        ids = wanted[here, :] - first
        columns = [jnp.broadcast_to(ids[:, k : k + 1], (height, LANES)) for k in range(choices)]
        peak = None
        picks = [None] * choices
        for step in range(width // tile):
            scale = marks[:, step : step + 1]
            block = slice(step * tile, (step + 1) * tile)
            value = keep[here, block] + decode(came[here, block], scale)
            logits[here, block] = value
            for part in range(tile // LANES):
                piece = value[:, part * LANES : (part + 1) * LANES]
                at = lane + (step * tile + part * LANES)
                peak = piece if peak is None else jnp.maximum(peak, piece)
                for k in range(choices):
                    term = jnp.where(at == columns[k], piece, 0.0)
                    picks[k] = term if picks[k] is None else picks[k] + term
        peak = jnp.max(peak, axis=1, keepdims=True)
        total = None
        for part in range(width // LANES):
            term = jnp.exp(logits[here, part * LANES : (part + 1) * LANES] - peak)
            total = term if total is None else total + term
        out = jnp.where(lane == 0, peak, jnp.zeros((height, LANES), jnp.float32))
        for k, item in enumerate([total] + picks):
            out = jnp.where(lane == k + 1, jnp.sum(item, axis=1, keepdims=True), out)
        stats[here, :] = out


def finish(wanted, keep, came, tile, choices, first):
    rows, width = keep.shape
    vmem = pl.BlockSpec(memory_space=pltpu.VMEM)
    return pl.pallas_call(
        functools.partial(finish_body, tile=tile, choices=choices, first=first),
        in_specs=[vmem] * 3,
        out_specs=[vmem] * 2,
        out_shape=[
            jax.ShapeDtypeStruct((rows, width), jnp.float32),
            jax.ShapeDtypeStruct((rows, LANES), jnp.float32),
        ],
        compiler_params=pltpu.CompilerParams(vmem_limit_bytes=16 * MIB),
    )(wanted, keep, came)


def merge(one, two):
    peak = jnp.maximum(one[:, :1], two[:, :1])
    lane = lax.broadcasted_iota(jnp.int32, one.shape, 1)
    factor_one = jnp.where(lane == 1, jnp.exp(one[:, :1] - peak), 1.0)
    factor_two = jnp.where(lane == 1, jnp.exp(two[:, :1] - peak), 1.0)
    return jnp.where(lane == 0, peak, one * factor_one + two * factor_two)


def shards(
    hidden_states, accepted, norm_gain, head_weight, head_bias, vocab_weight, cand_ids, tree_paths
):
    batch, mp = lax.axis_size("batch"), lax.axis_size("mp")
    b, m = lax.axis_index("batch"), lax.axis_index("mp")
    rows, positions, feat = hidden_states.shape
    heads, inner, _ = head_weight.shape
    vocab_width = vocab_weight.shape[1]
    out_rows, _, choices = cand_ids.shape
    pieces = feat // inner
    ratio = out_rows // rows
    mp_bits = bits_of(mp)
    pair, core = b // 2, b % 2
    pair_bits = [bits_of(batch // 2), bits_of(batch // 2)[::-1]]

    chosen = hidden_states[:, 0, :]
    for position in range(1, positions):
        chosen = jnp.where((accepted == position + 1)[:, None], hidden_states[:, position, :], chosen)
    other = swap(chosen, "batch", lambda i: i ^ 1)
    chosen = jnp.concatenate(
        [jnp.where(core == 0, chosen, other), jnp.where(core == 0, other, chosen)], axis=0
    ).astype(jnp.float32)
    gain = lax.dynamic_slice_in_dim(norm_gain, m * feat, feat, 0)

    if pieces == 2:
        sent = lax.dynamic_slice_in_dim(chosen, core * inner, inner, 1)
        sent_gain = lax.dynamic_slice_in_dim(gain, core * inner, inner, 0)
    else:
        sent = lax.dynamic_slice_in_dim(chosen, core * rows, rows, 0)
        sent_gain = gain
    sent = (sent * sent_gain).astype(jnp.bfloat16)
    perm = []
    for i in range(batch):
        for j in range(mp):
            perm.append((i * mp + j, (j * pieces + i % pieces) * mp + i // pieces))
    block = lax.ppermute(sent, ("batch", "mp"), perm)
    for bit in mp_bits:
        block = jnp.concatenate([block, swap(block, "mp", lambda i: i ^ bit)], axis=0)

    square_sum = jnp.sum(chosen * chosen, axis=1, keepdims=True)
    for bit in mp_bits:
        square_sum = square_sum + swap(square_sum, "mp", lambda i: i ^ bit)
    row_scale = lax.rsqrt(square_sum / (mp * feat) + EPSILON)
    own_normed = (chosen * row_scale * gain).astype(jnp.bfloat16).astype(jnp.float32)

    spots = []
    for unit in range(batch):
        source = (m ^ (unit // pieces)) * pieces + unit % pieces
        apart = (source // 2) ^ pair
        spot = jnp.where(core == 0, place(apart, pair_bits[0]), place(apart, pair_bits[1]))
        spots.append(spot * 2 + source % 2)
    send = head_matmul(
        jnp.stack([1 - core] + spots).astype(jnp.int32), block, head_weight, rows, jnp.bfloat16
    )
    came = swap(send, "batch", lambda i: i ^ 1)
    keep = head_matmul(
        jnp.stack([core] + spots).astype(jnp.int32), block, head_weight, rows, jnp.float32
    )
    units = batch // 2
    turned = [place(unplace(u, pair_bits[0]), pair_bits[1]) for u in range(units)]
    came = came.reshape(units, 2 * rows, feat)
    came = jnp.concatenate([came[u] for u in turned], axis=0)
    total = keep + came.astype(jnp.float32)
    for step in range(len(pair_bits[0])):
        half = total.shape[0] // 2
        outbound = total[half:].astype(jnp.bfloat16)
        came = swap(outbound, "batch", lambda i: i ^ (2 * pair_bits[i % 2][step]))
        total = total[:half] + came.astype(jnp.float32)
    bias = lax.dynamic_slice_in_dim(head_bias, core, 1, 0)
    before = total * row_scale + bias
    residual = (own_normed + jax.nn.silu(before)).astype(jnp.bfloat16)
    for step in reversed(range(len(pair_bits[0]))):
        came = swap(residual, "batch", lambda i: i ^ (2 * pair_bits[i % 2][step]))
        residual = jnp.concatenate([residual, came], axis=0)
    parts = [residual, swap(residual, "batch", lambda i: i ^ 1)]

    orders = (mp_bits, mp_bits[::-1])
    spot_tables = []
    for stages in orders:
        table = []
        for whose in (core, 1 - core):
            for unit in range(batch):
                apart = jnp.where(
                    whose == 0, unplace(unit // 2, pair_bits[0]), unplace(unit // 2, pair_bits[1])
                )
                source = (pair ^ apart) * 2 + unit % 2
                spot = place((source // ratio) ^ m, stages)
                table.append((spot * ratio + source % ratio) * heads + whose)
        spot_tables.append(jnp.stack(table).astype(jnp.int32))
    wanted = (cand_ids - b * vocab_width).reshape(ratio, rows, heads, choices)
    wanted = wanted.transpose(0, 2, 1, 3).reshape(out_rows * heads, choices)
    wanted = jnp.pad(wanted, ((0, 0), (0, LANES - choices)), constant_values=-1)

    quarter = vocab_width // 4
    widths = [quarter, quarter, quarter, quarter // 2, quarter // 2]
    tile = widest(512, quarter // 2)
    first = 0
    arrivals, logits, stats = [], [], None
    for chunk, width in enumerate(widths):
        stages = orders[chunk % 2]
        after = []
        if chunk == 2:
            after = [arrivals[0]]
        elif chunk > 2:
            after = [arrivals[1], previous]
        keep, send = vocab_matmul(
            spot_tables[chunk % 2], parts, rows, vocab_weight, first, width, tile, after
        )
        previous = send
        for index, bit in enumerate(stages):
            came = swap(send, "mp", lambda i: i ^ bit)
            if index == 0:
                arrivals.append(came)
            if index + 1 < len(stages):
                keep, send = fold(keep, came, tile)
        block, part = finish(wanted, keep, came, tile, choices, first)
        logits.append(block)
        stats = part if stats is None else merge(stats, part)
        first += width

    for bit in bits_of(batch):
        came = swap(stats, "batch", lambda i: i ^ bit)
        low = (b & bit) == 0
        stats = merge(jnp.where(low, stats, came), jnp.where(low, came, stats))
    normalizer = stats[:, :1] + jnp.log(stats[:, 1:2])
    picked = stats[:, 2 : 2 + choices] - normalizer

    def natural(array):
        array = array.reshape(ratio, heads, rows, array.shape[1])
        return array.transpose(0, 2, 1, 3).reshape(out_rows, heads, array.shape[3])

    log_probs = natural(jnp.concatenate(logits, axis=1) - normalizer)
    picked = natural(picked)
    path_scores = jnp.zeros((out_rows, tree_paths.shape[0]), jnp.float32)
    for head in range(heads):
        found = jnp.zeros_like(path_scores)
        for choice in range(choices):
            taken = tree_paths[:, head][None, :] == choice
            found = jnp.where(taken, picked[:, head, choice : choice + 1], found)
        path_scores = path_scores + found
    return (log_probs, path_scores)


def solution(mesh):
    return jax.shard_map(
        shards,
        mesh=mesh,
        in_specs=(
            P("batch", None, "mp"),
            P("batch"),
            P(),
            P(None, "batch", "mp"),
            P(None, "mp"),
            P("mp", "batch"),
            P("mp", None, None),
            P(),
        ),
        out_specs=(P("mp", None, "batch"), P("mp", None)),
        check_vma=False,
    )
```

time: 337 us -> 208 us (0.62)
  waiting for transfers between devices: 161 us -> 72.5 us
  Pallas kernels: 0 us -> 74.5 us
  matrix products: 73.9 us -> 0 us
  blocking collectives: 66.2 us -> 0 us
  starting transfers between devices: 0.43 us -> 38.8 us
  between operations: 14.3 us -> 2.26 us
    reduce_scatter x4 -> x0, waiting for transfers between devices: 140 us -> none  [the longest x2 79.5 us: shards(): lax.psum_scatter(vocab_terms(jnp.int32(0), out_rows * lax.axis_size('mp')...]
    pallas_call x0 -> x17, Pallas kernels: none -> 74.5 us  [the longest x5 41.1 us: vocab_matmul(): pl.pallas_call(functools.partial(vocab_body, heads=heads, height=height,...]
    dot_general x6 -> x0, matrix products: 73.9 us -> none  [the longest x2 53.8 us: vocab_terms(): return jnp.dot(gathered, vocab_weight, preferred_element_type=jnp.float32)]
    ppermute x0 -> x25, waiting for transfers between devices: none -> 72.5 us  [the longest x24 72.5 us: swap(): lax.ppermute(array, axis, [(i, partner(i)) for i in range(lax.axis_size(a...]
    all_gather x4 -> x0, blocking collectives: 46.2 us -> none  [the longest x3 34.7 us: joined(): gathered = jax.tree.map(lambda a: lax.all_gather(a, axis), part)]
    ppermute x0 -> x25, starting transfers between devices: none -> 38.8 us  [the longest x24 38.1 us: swap(): lax.ppermute(array, axis, [(i, partner(i)) for i in range(lax.axis_size(a...]
    all_gather x2 -> x0, waiting for transfers between devices: 20.5 us -> none  [shards(): gathered = lax.all_gather(residual, 'batch', axis=0, tiled=True)]
    all_to_all x1 -> x0, blocking collectives: 20 us -> none  [shards(): lax.all_to_all(normed, 'batch', split_axis=1, concat_axis=0, tiled=True)]
  transfers between devices with their start and end apart: 6 -> 25, of which waited for: 5 -> 16; matrix products, arithmetic and copies ran while one was open for 19% -> 4% of each run, Pallas kernels for 0% -> 26%
where the time goes in v2:
time: 208 us
  Pallas kernels  74.5 us (36%)
  waiting for transfers between devices  72.5 us (35%)
  starting transfers between devices  38.8 us (19%)
  local copies, waits for them, and re-layouts  11.1 us (5%)
  other arithmetic  8.53 us (4%)
  between operations  2.26 us (1%)
    ppermute x24, waiting for transfers between devices, swap(): lax.ppermute(array, axis, [(i, partner(i)) for i in range(lax.axis_size(a...  72.5 us
    pallas_call x5, Pallas kernels, vocab_matmul(): pl.pallas_call(functools.partial(vocab_body, heads=heads, height=height,...  41.1 us
    ppermute x24, starting transfers between devices, swap(): lax.ppermute(array, axis, [(i, partner(i)) for i in range(lax.axis_size(a...  38.1 us
    pallas_call x2, Pallas kernels, head_matmul(): pl.pallas_call(functools.partial(head_body, ways=ways, height=height), gr...  19.5 us
    pallas_call x5, Pallas kernels, finish(): pl.pallas_call(functools.partial(finish_body, tile=tile, choices=choices,...  7.21 us
    pallas_call x5, Pallas kernels, fold(): pl.pallas_call(functools.partial(fold_body, tile=tile), in_specs=[vmem] *...  6.72 us
  transfers between devices with their start and end apart: 25, of which 16 were waited for; matrix products, arithmetic and copies ran while one was open for 4% of the time, Pallas kernels for 26%

profile of v2, /device:TPU:0, one launch (start us, length us, event | category | flops | bytes accessed | tf_op | source)
XLA Modules:
  0.0 207.8 jit_solution(12355869352478147536)
XLA Ops:
  0.7 3.0 %fusion.15 = (bf16[16,1,4096]{2,1,0:T(2,128)(2,1)S(1)}, bf16[16,1,4096]{2,1,0:T(2,128)(2,1)S(1)}, bf16[16,1,4096]{2,1,0:T(2,128)(2,1)S(1)}, bf16[16,1,4096]{2,1,0:T(2,128)(2,1)S(1)}) fusion(bf16[16,4,4096]{2,1,0:T(4,128)(2,1)} %param.8), kind=kLoop, calls=%fused_computation.129 | loop fusion | bytes 1048576 | tf_op jit(solution)/shard_map/slice | solution.py:303
  6.5 16.1 %collective-permute-start.4 = (bf16[32,2048]{1,0:T(8,128)(2,1)S(1)}, bf16[32,2048]{1,0:T(8,128)(2,1)S(1)}, u32[]{:S(2)}, u32[]{:S(2)}) collective-permute-start(bf16[32,2048]{1,0:T(8,128)(2,1)S(1)} %collective-permute-done.3), channel_id=1, source_target_pairs={{0,1},{1,0},{2,3},{3,2},{4,5},{5,4},{6,7},{7,6},{8,9},{9,8},{10,11... | collective-permute-start | bytes 393224 | tf_op jit(solution)/shard_map/ppermute | solution.py:21
  22.7 2.9 %collective-permute-done.4 = bf16[32,2048]{1,0:T(8,128)(2,1)S(1)} collective-permute-done((bf16[32,2048]{1,0:T(8,128)(2,1)S(1)}, bf16[32,2048]{1,0:T(8,128)(2,1)S(1)}, u32[]{:S(2)}, u32[]{:S(2)}) %collective-permute-start.4) | collective-permute-done | bytes 131104 | tf_op jit(solution)/shard_map/ppermute | solution.py:21
  26.0 6.4 %collective-permute-done.5 = bf16[64,2048]{1,0:T(8,128)(2,1)S(1)} collective-permute-done((bf16[64,2048]{1,0:T(8,128)(2,1)S(1)}, bf16[64,2048]{1,0:T(8,128)(2,1)S(1)}, u32[]{:S(2)}, u32[]{:S(2)}) %collective-permute-start.5) | collective-permute-done | bytes 262176 | tf_op jit(solution)/shard_map/ppermute | solution.py:21
  32.4 9.8 %shard_map.96 = bf16[128,4096]{1,0:T(8,128)(2,1)S(1)} custom-call(s32[9]{0:T(128)S(1)} %stack.174.info, bf16[128,2048]{1,0:T(8,128)(2,1)S(1)} %constant_dynamic-update-slice_fusion.came, bf16[2,2048,4096]{2,1,0:T(8,128)(2,1)} %refs_3_.8, bf16[2,2048,4096]{2,1,0:T(8,128)(2,1)} %refs_3_.8, bf16[2,2048,4096]{2,1,0:T(8,128)(2,1)} %refs_3_.8, ...), custom_call_target="tpu_custom_call" | custom-call | flops 2147483648 | bytes 16777216 | tf_op jit(solution)/shard_map/pallas_call | solution.py:84
  42.3 9.8 %shard_map.95 = f32[128,4096]{1,0:T(8,128)S(1)} custom-call(s32[9]{0:T(128)S(1)} %stack.172.info, bf16[128,2048]{1,0:T(8,128)(2,1)S(1)} %constant_dynamic-update-slice_fusion.came, bf16[2,2048,4096]{2,1,0:T(8,128)(2,1)} %refs_3_.8, bf16[2,2048,4096]{2,1,0:T(8,128)(2,1)} %refs_3_.8, bf16[2,2048,4096]{2,1,0:T(8,128)(2,1)} %refs_3_.8, ...), custom_call_target="tpu_custom_call" | custom-call | flops 2147483648 | bytes 16777216 | tf_op jit(solution)/shard_map/pallas_call | solution.py:84
  52.7 1.8 collective-permute-start.1
  54.5 1.8 collective-permute-done.1
  57.7 9.6 %collective-permute-done.7 = bf16[64,4096]{1,0:T(8,128)(2,1)S(1)} collective-permute-done((bf16[64,4096]{1,0:T(8,128)(2,1)S(1)}, bf16[64,4096]{1,0:T(8,128)(2,1)S(1)}, u32[]{:S(2)}, u32[]{:S(2)}) %collective-permute-start.7) | collective-permute-done | bytes 524320 | tf_op jit(solution)/shard_map/ppermute | solution.py:21
  67.5 2.0 collective-permute-start.8
  69.6 7.0 %collective-permute-done.8 = bf16[32,4096]{1,0:T(8,128)(2,1)S(1)} collective-permute-done((bf16[32,4096]{1,0:T(8,128)(2,1)S(1)}, bf16[32,4096]{1,0:T(8,128)(2,1)S(1)}, u32[]{:S(2)}, u32[]{:S(2)}) %collective-permute-start.8) | collective-permute-done | bytes 262176 | tf_op jit(solution)/shard_map/ppermute | solution.py:21
  76.9 1.6 collective-permute-start.9
  78.5 14.6 %collective-permute-done.9 = bf16[32,4096]{1,0:T(8,128)(2,1)S(1)} collective-permute-done((bf16[32,4096]{1,0:T(8,128)(2,1)S(1)}, bf16[32,4096]{1,0:T(8,128)(2,1)S(1)}, u32[]{:S(2)}, u32[]{:S(2)}) %collective-permute-start.9) | collective-permute-done | bytes 262176 | tf_op jit(solution)/shard_map/ppermute | solution.py:21
  93.3 10.4 %collective-permute-done.10 = bf16[64,4096]{1,0:T(8,128)(2,1)S(1)} collective-permute-done((bf16[64,4096]{1,0:T(8,128)(2,1)S(1)}, bf16[64,4096]{1,0:T(8,128)(2,1)S(1)}, u32[]{:S(2)}, u32[]{:S(2)}) %collective-permute-start.10) | collective-permute-done | bytes 524320 | tf_op jit(solution)/shard_map/ppermute | solution.py:21
  106.5 9.5 %shard_map.100 = (f32[128,2048]{1,0:T(8,128)S(1)}, s16[128,2176]{1,0:T(8,128)(2,1)S(1)}) custom-call(s32[16]{0:T(128)S(1)} %stack.191.spots, bf16[128,4096]{1,0:T(8,128)(2,1)S(1)} %pad_maximum_fusion.refs_0_, bf16[128,4096]{1,0:T(8,128)(2,1)S(1)} %collective-permute-done.11.refs_1_, bf16[4096,8192]{1,0:T(8,128)(2,1)} %refs_5_.9, bf16[4096,8192]{1,0:T(8,128)(2,1)} %refs_5_.9, ...), custom_call_target="tpu_custom_call" | custom-call | flops 4294967296 | bytes 16777216 | tf_op jit(solution)/shard_map/pallas_call | solution.py:163
  116.1 1.5 collective-permute-start.14
  117.6 9.5 %shard_map.97 = (f32[128,2048]{1,0:T(8,128)S(1)}, s16[128,2176]{1,0:T(8,128)(2,1)S(1)}) custom-call(s32[16]{0:T(128)S(1)} %stack.162.spots, bf16[128,4096]{1,0:T(8,128)(2,1)S(1)} %pad_maximum_fusion.refs_0_, bf16[128,4096]{1,0:T(8,128)(2,1)S(1)} %collective-permute-done.11.refs_1_, bf16[4096,8192]{1,0:T(8,128)(2,1)} %refs_5_.9, bf16[4096,8192]{1,0:T(8,128)(2,1)} %refs_5_.9, ...), custom_call_target="tpu_custom_call" | custom-call | flops 4294967296 | bytes 16777216 | tf_op jit(solution)/shard_map/pallas_call | solution.py:163
  130.8 1.8 shard_map.101
  133.9 8.8 %collective-permute-done.12.came.refs_6_ = s16[128,2176]{1,0:T(8,128)(2,1)S(1)} collective-permute-done((s16[128,2176]{1,0:T(8,128)(2,1)S(1)}, s16[128,2176]{1,0:T(8,128)(2,1)S(1)}, u32[]{:S(2)}, u32[]{:S(2)}) %collective-permute-start.12) | collective-permute-done | bytes 557088 | tf_op jit(solution)/shard_map/ppermute | solution.py:21
  142.7 1.8 shard_map.98
  145.1 10.3 %shard_map.103 = (f32[128,2048]{1,0:T(8,128)S(1)}, s16[128,2176]{1,0:T(8,128)(2,1)}) custom-call(s32[16]{0:T(128)S(1)} %stack.162.spots, bf16[128,4096]{1,0:T(8,128)(2,1)S(1)} %pad_maximum_fusion.refs_0_, bf16[128,4096]{1,0:T(8,128)(2,1)S(1)} %collective-permute-done.11.refs_1_, bf16[4096,8192]{1,0:T(8,128)(2,1)} %refs_5_.9, bf16[4096,8192]{1,0:T(8,128)(2,1)} %refs_5_.9, ...), custom_call_target="tpu_custom_call" | custom-call | flops 4294967296 | bytes 16777216 | tf_op jit(solution)/shard_map/pallas_call | solution.py:163
  156.7 5.8 %shard_map.106 = (f32[128,1024]{1,0:T(8,128)S(1)}, s16[128,1152]{1,0:T(8,128)(2,1)S(1)}) custom-call(s32[16]{0:T(128)S(1)} %stack.191.spots, bf16[128,4096]{1,0:T(8,128)(2,1)S(1)} %pad_maximum_fusion.refs_0_, bf16[128,4096]{1,0:T(8,128)(2,1)S(1)} %collective-permute-done.11.refs_1_, bf16[4096,8192]{1,0:T(8,128)(2,1)} %refs_5_.9, bf16[4096,8192]{1,0:T(8,128)(2,1)} %refs_5_.9, ...), custom_call_target="tpu_custom_call" | custom-call | flops 2147483648 | bytes 8388608 | tf_op jit(solution)/shard_map/pallas_call | solution.py:163
  163.4 5.9 %shard_map.109 = (f32[128,1024]{1,0:T(8,128)S(1)}, s16[128,1152]{1,0:T(8,128)(2,1)S(1)}) custom-call(s32[16]{0:T(128)S(1)} %stack.162.spots, bf16[128,4096]{1,0:T(8,128)(2,1)S(1)} %pad_maximum_fusion.refs_0_, bf16[128,4096]{1,0:T(8,128)(2,1)S(1)} %collective-permute-done.11.refs_1_, bf16[4096,8192]{1,0:T(8,128)(2,1)} %refs_5_.9, bf16[4096,8192]{1,0:T(8,128)(2,1)} %refs_5_.9, ...), custom_call_target="tpu_custom_call" | custom-call | flops 2147483648 | bytes 8388608 | tf_op jit(solution)/shard_map/pallas_call | solution.py:163
  170.8 2.2 %shard_map.102 = (f32[64,2048]{1,0:T(8,128)S(1)}, f32[64,128]{1,0:T(8,128)S(1)}) custom-call(s32[64,128]{1,0:T(8,128)S(1)} %pad.4.wanted, f32[64,2048]{1,0:T(8,128)S(1)} %get-tuple-element.39.keep, s16[64,2176]{1,0:T(8,128)(2,1)} %collective-permute-done.15.came), custom_call_target="tpu_custom_call" | custom-call | tf_op jit(solution)/shard_map/pallas_call | solution.py:266
  173.0 2.2 %shard_map.99 = (f32[64,2048]{1,0:T(8,128)S(1)}, f32[64,128]{1,0:T(8,128)S(1)}) custom-call(s32[64,128]{1,0:T(8,128)S(1)} %pad.4.wanted, f32[64,2048]{1,0:T(8,128)S(1)} %get-tuple-element.34.keep, s16[64,2176]{1,0:T(8,128)(2,1)} %collective-permute-done.13.came), custom_call_target="tpu_custom_call" | custom-call | tf_op jit(solution)/shard_map/pallas_call | solution.py:266
  176.8 2.2 %shard_map.104 = (f32[64,2048]{1,0:T(8,128)S(1)}, s16[64,2176]{1,0:T(8,128)(2,1)S(1)}) custom-call(f32[128,2048]{1,0:T(8,128)S(1)} %get-tuple-element.42.keep, s16[128,2176]{1,0:T(8,128)(2,1)} %collective-permute-done.16.came), custom_call_target="tpu_custom_call" | custom-call | tf_op jit(solution)/shard_map/pallas_call | solution.py:217
  183.1 2.3 %collective-permute-done.19.came = s16[64,1152]{1,0:T(8,128)(2,1)S(1)} collective-permute-done((s16[64,1152]{1,0:T(8,128)(2,1)S(1)}, s16[64,1152]{1,0:T(8,128)(2,1)S(1)}, u32[]{:S(2)}, u32[]{:S(2)}) %collective-permute-start.19) | collective-permute-done | bytes 147488 | tf_op jit(solution)/shard_map/ppermute | solution.py:21
  193.6 2.3 %collective-permute-done.23 = f32[64,128]{1,0:T(8,128)S(1)} collective-permute-done((f32[64,128]{1,0:T(8,128)S(1)}, f32[64,128]{1,0:T(8,128)S(1)}, u32[]{:S(2)}, u32[]{:S(2)}) %collective-permute-start.23) | collective-permute-done | bytes 32800 | tf_op jit(solution)/shard_map/ppermute | solution.py:21
  196.1 2.3 %collective-permute-start.24 = (f32[64,128]{1,0:T(8,128)S(1)}, f32[64,128]{1,0:T(8,128)S(1)}, u32[]{:S(2)}, u32[]{:S(2)}) collective-permute-start(f32[64,128]{1,0:T(8,128)S(1)} %add_select_fusion.1), channel_id=1, source_target_pairs={{0,16},{4,20},{8,24},{12,28},{16,0},{20,4},{24,8},{28,12},{1,17},{... | collective-permute-start | bytes 98312 | tf_op jit(solution)/shard_map/ppermute | solution.py:21
  199.2 1.8 collective-permute-done.24
  201.8 1.8 subtract_bitcast_fusion
  203.9 2.9 %copy.22 = f32[2,16,2,8192]{3,2,1,0:T(2,128)} copy(f32[2,16,2,8192]{3,1,2,0:T(8,128)S(1)} %subtract_bitcast_fusion) | data formatting | bytes 4194304 | tf_op jit(solution)/shard_map/transpose | solution.py:415
  (160 shorter events, 33.6 us)
Async XLA Ops:
  0.6 68.9 %copy-start = (f32[2,4096]{1,0:T(2,128)S(1)}, f32[2,4096]{1,0:T(2,128)}, u32[]{:S(2)}) copy-start(f32[2,4096]{1,0:T(2,128)} %param.12) | copy-start | bytes 98308
  4.2 1.5 collective-permute-start
  5.8 0.7 collective-permute-start.3
  6.5 19.1 %collective-permute-start.4 = (bf16[32,2048]{1,0:T(8,128)(2,1)S(1)}, bf16[32,2048]{1,0:T(8,128)(2,1)S(1)}, u32[]{:S(2)}, u32[]{:S(2)}) collective-permute-start(bf16[32,2048]{1,0:T(8,128)(2,1)S(1)} %collective-permute-done.3), channel_id=1, source_target_pairs={{0,1},{1,0},{2,3},{3,2},{4,5},{5,4},{6,7},{7,6},{8,9},{9,8},{10,11... | collective-permute-start | bytes 393224 | tf_op jit(solution)/shard_map/ppermute | solution.py:21
  25.7 6.7 %collective-permute-start.5 = (bf16[64,2048]{1,0:T(8,128)(2,1)S(1)}, bf16[64,2048]{1,0:T(8,128)(2,1)S(1)}, u32[]{:S(2)}, u32[]{:S(2)}) collective-permute-start(bf16[64,2048]{1,0:T(8,128)(2,1)S(1)} %pad_maximum_fusion.2), channel_id=1, source_target_pairs={{0,2},{1,3},{2,0},{3,1},{4,6},{5,7},{6,4},{7,5},{8,10},{9,11},{10,... | collective-permute-start | bytes 786440 | tf_op jit(solution)/shard_map/ppermute | solution.py:21
  42.1 9.9 %collective-permute-start.6 = (bf16[128,4096]{1,0:T(8,128)(2,1)S(1)}, bf16[128,4096]{1,0:T(8,128)(2,1)S(1)}, u32[]{:S(2)}, u32[]{:S(2)}) collective-permute-start(bf16[128,4096]{1,0:T(8,128)(2,1)S(1)} %shard_map.96), channel_id=1, source_target_pairs={{0,4},{4,0},{8,12},{12,8},{16,20},{20,16},{24,28},{28,24},{1,5},{5... | collective-permute-start | bytes 3145736 | tf_op jit(solution)/shard_map/ppermute | solution.py:21
  52.4 24.2 %dynamic-slice-start = ((f32[16384]{0:T(1024)}, s32[]{:T(128)}), f32[4096]{0:T(1024)S(1)}, s32[]{:S(2)}) async-start(f32[16384]{0:T(1024)} %param.10, s32[]{:T(128)} %select_n.654), calls=%async_computation | async-start | bytes 33280 | tf_op jit(solution)/shard_map/dynamic_slice | solution.py:308
  52.5 14.9 %collective-permute-start.7 = (bf16[64,4096]{1,0:T(8,128)(2,1)S(1)}, bf16[64,4096]{1,0:T(8,128)(2,1)S(1)}, u32[]{:S(2)}, u32[]{:S(2)}) collective-permute-start(bf16[64,4096]{1,0:T(8,128)(2,1)S(1)} %slice.451), channel_id=1, source_target_pairs={{0,8},{4,20},{8,0},{12,28},{16,24},{20,4},{24,16},{28,12},{1,9},{5... | collective-permute-start | bytes 1572872 | tf_op jit(solution)/shard_map/ppermute | solution.py:21
  52.7 3.6 %collective-permute-start.1 = (f32[32,1]{0,1:T(1,128)S(1)}, f32[32,1]{0,1:T(1,128)S(1)}, u32[]{:S(2)}, u32[]{:S(2)}) collective-permute-start(f32[32,1]{0,1:T(1,128)S(1)} %bitcast.174), channel_id=1, source_target_pairs={{0,1},{1,0},{2,3},{3,2},{4,5},{5,4},{6,7},{7,6},{8,9},{9,8},{10,11... | collective-permute-start | bytes 392 | tf_op jit(solution)/shard_map/ppermute | solution.py:21
  56.3 13.2 %collective-permute-start.2 = (f32[32,1]{0,1:T(1,128)S(1)}, f32[32,1]{0,1:T(1,128)S(1)}, u32[]{:S(2)}, u32[]{:S(2)}) collective-permute-start(f32[32,1]{0,1:T(1,128)S(1)} %bitcast_add_fusion), channel_id=1, source_target_pairs={{0,2},{1,3},{2,0},{3,1},{4,6},{5,7},{6,4},{7,5},{8,10},{9,11},{10,... | collective-permute-start | bytes 392 | tf_op jit(solution)/shard_map/ppermute | solution.py:21
  67.5 9.1 %collective-permute-start.8 = (bf16[32,4096]{1,0:T(8,128)(2,1)S(1)}, bf16[32,4096]{1,0:T(8,128)(2,1)S(1)}, u32[]{:S(2)}, u32[]{:S(2)}) collective-permute-start(bf16[32,4096]{1,0:T(8,128)(2,1)S(1)} %slice.452), channel_id=1, source_target_pairs={{0,16},{4,12},{8,24},{12,4},{16,0},{20,28},{24,8},{28,20},{1,17},{... | collective-permute-start | bytes 786440 | tf_op jit(solution)/shard_map/ppermute | solution.py:21
  76.9 27.7 %copy-start.5 = (s32[32,2,10]{0,1,2:T(2,128)S(1)}, s32[32,2,10]{0,1,2:T(2,128)}, u32[]{:S(2)}) copy-start(s32[32,2,10]{0,1,2:T(2,128)} %param.14) | copy-start | bytes 7684
  76.9 16.3 %collective-permute-start.9 = (bf16[32,4096]{1,0:T(8,128)(2,1)S(1)}, bf16[32,4096]{1,0:T(8,128)(2,1)S(1)}, u32[]{:S(2)}, u32[]{:S(2)}) collective-permute-start(bf16[32,4096]{1,0:T(8,128)(2,1)S(1)} %add_convert_fusion), channel_id=1, source_target_pairs={{0,16},{4,12},{8,24},{12,4},{16,0},{20,28},{24,8},{28,20},{1,17},{... | collective-permute-start | bytes 786440 | tf_op jit(solution)/shard_map/ppermute | solution.py:21
  93.2 10.5 %collective-permute-start.10 = (bf16[64,4096]{1,0:T(8,128)(2,1)S(1)}, bf16[64,4096]{1,0:T(8,128)(2,1)S(1)}, u32[]{:S(2)}, u32[]{:S(2)}) collective-permute-start(bf16[64,4096]{1,0:T(8,128)(2,1)S(1)} %pad_maximum_fusion.1), channel_id=1, source_target_pairs={{0,8},{4,20},{8,0},{12,28},{16,24},{20,4},{24,16},{28,12},{1,9},{5... | collective-permute-start | bytes 1572872 | tf_op jit(solution)/shard_map/ppermute | solution.py:21
  103.8 2.7 %collective-permute-start.11 = (bf16[128,4096]{1,0:T(8,128)(2,1)S(1)}, bf16[128,4096]{1,0:T(8,128)(2,1)S(1)}, u32[]{:S(2)}, u32[]{:S(2)}) collective-permute-start(bf16[128,4096]{1,0:T(8,128)(2,1)S(1)} %pad_maximum_fusion.refs_0_), channel_id=1, source_target_pairs={{0,4},{4,0},{8,12},{12,8},{16,20},{20,16},{24,28},{28,24},{1,5},{5... | collective-permute-start | bytes 3145736 | tf_op jit(solution)/shard_map/ppermute | solution.py:21
  116.1 12.4 %copy-start.24 = (s32[64,2]{0,1:T(2,128)S(1)}, s32[64,2]{0,1:T(2,128)}, u32[]{:S(2)}) copy-start(s32[64,2]{0,1:T(2,128)} %param.15) | copy-start | bytes 1540
  116.1 14.7 %collective-permute-start.14 = (s16[128,2176]{1,0:T(8,128)(2,1)S(1)}, s16[128,2176]{1,0:T(8,128)(2,1)S(1)}, u32[]{:S(2)}, u32[]{:S(2)}) collective-permute-start(s16[128,2176]{1,0:T(8,128)(2,1)S(1)} %get-tuple-element.38), channel_id=1, source_target_pairs={{0,2},{1,3},{2,0},{3,1},{4,6},{5,7},{6,4},{7,5},{8,10},{9,11},{10,... | collective-permute-start | bytes 1671176 | tf_op jit(solution)/shard_map/ppermute | solution.py:21
  127.2 15.6 %collective-permute-start.12 = (s16[128,2176]{1,0:T(8,128)(2,1)S(1)}, s16[128,2176]{1,0:T(8,128)(2,1)S(1)}, u32[]{:S(2)}, u32[]{:S(2)}) collective-permute-start(s16[128,2176]{1,0:T(8,128)(2,1)S(1)} %get-tuple-element.33), channel_id=1, source_target_pairs={{0,1},{1,0},{2,3},{3,2},{4,5},{5,4},{6,7},{7,6},{8,9},{9,8},{10,11... | collective-permute-start | bytes 1671176 | tf_op jit(solution)/shard_map/ppermute | solution.py:21
  132.6 38.2 %collective-permute-start.15 = (s16[64,2176]{1,0:T(8,128)(2,1)}, s16[64,2176]{1,0:T(8,128)(2,1)}, u32[]{:S(2)}, u32[]{:S(2)}) collective-permute-start(s16[64,2176]{1,0:T(8,128)(2,1)} %get-tuple-element.40), channel_id=1, source_target_pairs={{0,1},{1,0},{2,3},{3,2},{4,5},{5,4},{6,7},{7,6},{8,9},{9,8},{10,11... | collective-permute-start | bytes 835592 | tf_op jit(solution)/shard_map/ppermute | solution.py:21
  144.6 28.4 %collective-permute-start.13 = (s16[64,2176]{1,0:T(8,128)(2,1)}, s16[64,2176]{1,0:T(8,128)(2,1)}, u32[]{:S(2)}, u32[]{:S(2)}) collective-permute-start(s16[64,2176]{1,0:T(8,128)(2,1)} %get-tuple-element.35), channel_id=1, source_target_pairs={{0,2},{1,3},{2,0},{3,1},{4,6},{5,7},{6,4},{7,5},{8,10},{9,11},{10,... | collective-permute-start | bytes 835592 | tf_op jit(solution)/shard_map/ppermute | solution.py:21
  155.4 21.4 %collective-permute-start.16 = (s16[128,2176]{1,0:T(8,128)(2,1)}, s16[128,2176]{1,0:T(8,128)(2,1)}, u32[]{:S(2)}, u32[]{:S(2)}) collective-permute-start(s16[128,2176]{1,0:T(8,128)(2,1)} %get-tuple-element.43.refs_7_), channel_id=1, source_target_pairs={{0,1},{1,0},{2,3},{3,2},{4,5},{5,4},{6,7},{7,6},{8,9},{9,8},{10,11... | collective-permute-start | bytes 1671176 | tf_op jit(solution)/shard_map/ppermute | solution.py:21
  162.5 17.3 %collective-permute-start.18 = (s16[128,1152]{1,0:T(8,128)(2,1)S(1)}, s16[128,1152]{1,0:T(8,128)(2,1)S(1)}, u32[]{:S(2)}, u32[]{:S(2)}) collective-permute-start(s16[128,1152]{1,0:T(8,128)(2,1)S(1)} %get-tuple-element.48.refs_7_), channel_id=1, source_target_pairs={{0,2},{1,3},{2,0},{3,1},{4,6},{5,7},{6,4},{7,5},{8,10},{9,11},{10,... | collective-permute-start | bytes 884744 | tf_op jit(solution)/shard_map/ppermute | solution.py:21
  169.4 12.2 %collective-permute-start.20 = (s16[128,1152]{1,0:T(8,128)(2,1)S(1)}, s16[128,1152]{1,0:T(8,128)(2,1)S(1)}, u32[]{:S(2)}, u32[]{:S(2)}) collective-permute-start(s16[128,1152]{1,0:T(8,128)(2,1)S(1)} %get-tuple-element.53), channel_id=1, source_target_pairs={{0,1},{1,0},{2,3},{3,2},{4,5},{5,4},{6,7},{7,6},{8,9},{9,8},{10,11... | collective-permute-start | bytes 884744 | tf_op jit(solution)/shard_map/ppermute | solution.py:21
  176.0 7.0 %copy-start.3 = (pred[128]{0:T(512)(128)(4,1)S(1)}, pred[128]{0:T(512)(128)(4,1)}, u32[]{:S(2)}) copy-start(pred[128]{0:T(512)(128)(4,1)} %iota_compare_fusion) | copy-start | bytes 388
  176.0 7.0 %copy-start.4 = (pred[128]{0:T(512)(128)(4,1)S(1)}, pred[128]{0:T(512)(128)(4,1)}, u32[]{:S(2)}) copy-start(pred[128]{0:T(512)(128)(4,1)} %iota_compare_fusion.1) | copy-start | bytes 388
  179.0 9.4 %collective-permute-start.17 = (s16[64,2176]{1,0:T(8,128)(2,1)S(1)}, s16[64,2176]{1,0:T(8,128)(2,1)S(1)}, u32[]{:S(2)}, u32[]{:S(2)}) collective-permute-start(s16[64,2176]{1,0:T(8,128)(2,1)S(1)} %get-tuple-element.45), channel_id=1, source_target_pairs={{0,2},{1,3},{2,0},{3,1},{4,6},{5,7},{6,4},{7,5},{8,10},{9,11},{10,... | collective-permute-start | bytes 835592 | tf_op jit(solution)/shard_map/ppermute | solution.py:21
  180.2 5.2 %collective-permute-start.19 = (s16[64,1152]{1,0:T(8,128)(2,1)S(1)}, s16[64,1152]{1,0:T(8,128)(2,1)S(1)}, u32[]{:S(2)}, u32[]{:S(2)}) collective-permute-start(s16[64,1152]{1,0:T(8,128)(2,1)S(1)} %get-tuple-element.50), channel_id=1, source_target_pairs={{0,1},{1,0},{2,3},{3,2},{4,5},{5,4},{6,7},{7,6},{8,9},{9,8},{10,11... | collective-permute-start | bytes 442376 | tf_op jit(solution)/shard_map/ppermute | solution.py:21
  182.1 5.4 %collective-permute-start.21 = (s16[64,1152]{1,0:T(8,128)(2,1)S(1)}, s16[64,1152]{1,0:T(8,128)(2,1)S(1)}, u32[]{:S(2)}, u32[]{:S(2)}) collective-permute-start(s16[64,1152]{1,0:T(8,128)(2,1)S(1)} %get-tuple-element.55), channel_id=1, source_target_pairs={{0,2},{1,3},{2,0},{3,1},{4,6},{5,7},{6,4},{7,5},{8,10},{9,11},{10,... | collective-permute-start | bytes 442376 | tf_op jit(solution)/shard_map/ppermute | solution.py:21
  190.3 1.3 collective-permute-start.22
  191.9 4.0 %collective-permute-start.23 = (f32[64,128]{1,0:T(8,128)S(1)}, f32[64,128]{1,0:T(8,128)S(1)}, u32[]{:S(2)}, u32[]{:S(2)}) collective-permute-start(f32[64,128]{1,0:T(8,128)S(1)} %add_select_fusion.2), channel_id=1, source_target_pairs={{0,8},{4,12},{8,0},{12,4},{16,24},{20,28},{24,16},{28,20},{1,9},{5... | collective-permute-start | bytes 98312 | tf_op jit(solution)/shard_map/ppermute | solution.py:21
  196.1 4.9 %collective-permute-start.24 = (f32[64,128]{1,0:T(8,128)S(1)}, f32[64,128]{1,0:T(8,128)S(1)}, u32[]{:S(2)}, u32[]{:S(2)}) collective-permute-start(f32[64,128]{1,0:T(8,128)S(1)} %add_select_fusion.1), channel_id=1, source_target_pairs={{0,16},{4,20},{8,24},{12,28},{16,0},{20,4},{24,8},{28,12},{1,17},{... | collective-permute-start | bytes 98312 | tf_op jit(solution)/shard_map/ppermute | solution.py:21
  201.8 5.9 %copy-start.1 = (f32[2,4096]{1,0:T(2,128)S(1)}, f32[2,4096]{1,0:T(2,128)}, u32[]{:S(2)}) copy-start(f32[2,4096]{1,0:T(2,128)} %param.12) | copy-start | bytes 98308
  (22 other events, 69.4 us)

commit v3 on v2

v3 whole, which is shorter than its diff:
```python
import functools

import jax
import jax.numpy as jnp
from jax import lax
from jax.experimental import pallas as pl
from jax.experimental.pallas import tpu as pltpu
from jax.sharding import PartitionSpec as P

EPSILON = 1e-05
MIB = 1024 * 1024
LANES = 128
CODE_BITS = 14
VMEM_LIMIT = 4 * MIB
HEAD_LIMIT = 24 * MIB


def together(*arrays):
    return lax.optimization_barrier(arrays)


def bits_of(count):
    return [1 << i for i in range(count.bit_length() - 1)]


def swap(array, axis, partner):
    return lax.ppermute(array, axis, [(i, partner(i)) for i in range(lax.axis_size(axis))])


def place(index, stages):
    spot = 0
    for bit in stages:
        spot = 2 * spot + (index & bit) // bit
    return spot


def unplace(spot, stages):
    index = 0
    for step, bit in enumerate(stages[::-1]):
        index = index + ((spot >> step) & 1) * bit
    return index


def widest(limit, size):
    tile = min(limit, size)
    while size % tile:
        tile //= 2
    return tile


VMEM = pl.BlockSpec(memory_space=pltpu.VMEM)
ANY = pl.BlockSpec(memory_space=pl.ANY)
WAYS = 4


def copies_in(source, target, sems, first):
    depth, width = target.shape
    share = depth // WAYS
    return [
        pltpu.make_async_copy(
            source.at[pl.ds(way * share, share), pl.ds(first, width)],
            target.at[pl.ds(way * share, share), :],
            sems.at[way],
        )
        for way in range(WAYS)
    ]


def fetch_body(info, weight, *refs, firsts):
    targets, sems = refs[-1 - len(firsts) : -1], refs[-1]
    source = weight.at[info[0]] if len(weight.shape) == 3 else weight
    copies = []
    for index, target in enumerate(targets):
        copies += copies_in(source, target, sems.at[index], firsts[index])
    for copy in copies:
        copy.start()
    for copy in copies:
        copy.wait()


def fetch(info, weight, firsts, width, after, limit=VMEM_LIMIT):
    depth = weight.shape[-2]
    return pl.pallas_call(
        functools.partial(fetch_body, firsts=firsts),
        in_specs=[pl.BlockSpec(memory_space=pltpu.SMEM), ANY] + [ANY] * len(after),
        out_specs=[VMEM] * len(firsts),
        out_shape=[jax.ShapeDtypeStruct((depth, width), weight.dtype)] * len(firsts),
        scratch_shapes=[pltpu.SemaphoreType.DMA((len(firsts), WAYS))],
        compiler_params=pltpu.CompilerParams(vmem_limit_bytes=limit),
        cost_estimate=pl.CostEstimate(
            flops=700 * depth * width * len(firsts), bytes_accessed=0, transcendentals=0
        ),
    )(info, weight, *after)


def head_body(info, came, source, *refs, height, held, firsts):
    weights, refs = refs[:held], refs[held:]
    out, targets, (rows, sems) = refs[0], refs[1:-2], refs[-2:]
    copies = []
    for index, target in enumerate(targets):
        copies += copies_in(source.at[info[0]], target, sems.at[index], firsts[index])
    for copy in copies:
        copy.start()
    for unit in range(came.shape[0] // height):
        start = pl.multiple_of(info[1 + unit] * height, height)
        rows[pl.ds(start, height), :] = came[unit * height : (unit + 1) * height, :]
    at = 0
    for weight in weights:
        width = weight.shape[1]
        tile = widest(512, width)
        for n in range(width // tile):
            total = jnp.dot(
                rows[...], weight[:, n * tile : (n + 1) * tile], preferred_element_type=jnp.float32
            )
            out[:, at : at + tile] = total.astype(out.dtype)
            at += tile
    for copy in copies:
        copy.wait()


def head_matmul(info, came, head_weight, weights, height, out_type, firsts):
    count, depth = came.shape
    wide = weights[0].shape[1]
    width = wide * len(weights)
    return pl.pallas_call(
        functools.partial(head_body, height=height, held=len(weights), firsts=firsts),
        in_specs=[pl.BlockSpec(memory_space=pltpu.SMEM), VMEM, ANY] + [VMEM] * len(weights),
        out_specs=[VMEM] * (1 + len(firsts)),
        out_shape=[jax.ShapeDtypeStruct((count, width), out_type)]
        + [jax.ShapeDtypeStruct((depth, wide), head_weight.dtype)] * len(firsts),
        scratch_shapes=[
            pltpu.VMEM((count, depth), jnp.bfloat16),
            pltpu.SemaphoreType.DMA((max(1, len(firsts)), WAYS)),
        ],
        compiler_params=pltpu.CompilerParams(vmem_limit_bytes=VMEM_LIMIT),
        cost_estimate=pl.CostEstimate(
            flops=2 * count * depth * width, bytes_accessed=count * width, transcendentals=0
        ),
    )(info, came, head_weight, *weights)


def encode(value):
    top = jnp.max(jnp.abs(value), axis=1, keepdims=True)
    power = jnp.floor(jnp.log2(jnp.maximum(top, 1e-30))) + 1.0
    code = jnp.floor(value * jnp.exp2(CODE_BITS - power) + 0.5)
    return code.astype(jnp.int32).astype(jnp.int16), power


def decode(code, power):
    return code.astype(jnp.int32).astype(jnp.float32) * jnp.exp2(power - CODE_BITS)


def marks_of(powers, height):
    lane = lax.broadcasted_iota(jnp.int32, (height, LANES), 1)
    marks = jnp.zeros((height, LANES), jnp.float32)
    for index, power in enumerate(powers):
        marks = jnp.where(lane == index, power, marks)
    return marks.astype(jnp.int32).astype(jnp.int16)


def gather_body(spots, *refs, height):
    parts, rows = refs[:-1], refs[-1]
    unit = 0
    for part in parts:
        for block in range(part.shape[0] // height):
            start = pl.multiple_of(spots[unit] * height, height)
            rows[pl.ds(start, height), :] = part[block * height : (block + 1) * height, :]
            unit += 1


def gather_rows(spots, parts, height):
    count = sum(p.shape[0] for p in parts)
    return pl.pallas_call(
        functools.partial(gather_body, height=height),
        in_specs=[pl.BlockSpec(memory_space=pltpu.SMEM)] + [VMEM] * len(parts),
        out_specs=VMEM,
        out_shape=jax.ShapeDtypeStruct((count, parts[0].shape[1]), parts[0].dtype),
        compiler_params=pltpu.CompilerParams(vmem_limit_bytes=VMEM_LIMIT),
    )(spots, *parts)


def vocab_body(rows, source, *refs, order, tile, counts, firsts):
    held, waits = counts
    weights, refs = refs[:held], refs[held + waits :]
    keep, send = refs[:2]
    targets, sems = refs[2:-1], refs[-1]
    copies = []
    for index, target in enumerate(targets):
        copies += copies_in(source, target, sems.at[index], firsts[index])
    for copy in copies:
        copy.start()
    groups = len(order)
    height = rows.shape[0] // groups
    half = groups // 2
    powers = []
    at = 0
    for weight in weights:
        for n in range(weight.shape[1] // tile):
            total = jnp.dot(
                rows[...], weight[:, n * tile : (n + 1) * tile], preferred_element_type=jnp.float32
            )
            sorted_rows = [total[g * height : (g + 1) * height] for g in order]
            for spot, value in enumerate(sorted_rows[:half]):
                keep[spot * height : (spot + 1) * height, at : at + tile] = value
            code, power = encode(jnp.concatenate(sorted_rows[half:], axis=0))
            send[:, at : at + tile] = code
            powers.append(power)
            at += tile
    send[:, at:] = marks_of(powers, send.shape[0])
    for copy in copies:
        copy.wait()


def vocab_matmul(rows, vocab_weight, weights, order, tile, coming, after):
    depth = vocab_weight.shape[0]
    count = rows.shape[0]
    half = count // 2
    width = sum(w.shape[1] for w in weights)
    return pl.pallas_call(
        functools.partial(
            vocab_body,
            order=order,
            tile=tile,
            counts=(len(weights), len(after)),
            firsts=[first for first, _ in coming],
        ),
        in_specs=[VMEM, ANY] + [VMEM] * len(weights) + [ANY] * len(after),
        out_specs=[VMEM] * (2 + len(coming)),
        out_shape=[
            jax.ShapeDtypeStruct((half, width), jnp.float32),
            jax.ShapeDtypeStruct((half, width + LANES), jnp.int16),
        ]
        + [jax.ShapeDtypeStruct((depth, wide), vocab_weight.dtype) for _, wide in coming],
        scratch_shapes=[pltpu.SemaphoreType.DMA((max(1, len(coming)), WAYS))],
        compiler_params=pltpu.CompilerParams(vmem_limit_bytes=VMEM_LIMIT),
        cost_estimate=pl.CostEstimate(
            flops=2 * count * depth * width, bytes_accessed=2 * depth * width, transcendentals=0
        ),
    )(rows, vocab_weight, *weights, *after)


def fold_body(keep, came, *refs, tile):
    send = refs[-1]
    half = send.shape[0]
    width = keep.shape[1]
    for row in range(half, 2 * half, 16):
        here, there = slice(row, row + 16), slice(row - half, row - half + 16)
        marks = came[here, width:].astype(jnp.int32).astype(jnp.float32)
        powers = []
        for step in range(width // tile):
            block = slice(step * tile, (step + 1) * tile)
            value = keep[here, block] + decode(came[here, block], marks[:, step : step + 1])
            code, power = encode(value)
            send[there, block] = code
            powers.append(power)
        send[there, width:] = marks_of(powers, 16)


def fold(keep, came, tile, after):
    rows, width = keep.shape
    return pl.pallas_call(
        functools.partial(fold_body, tile=tile),
        in_specs=[VMEM] * 2 + [ANY] * len(after),
        out_specs=VMEM,
        out_shape=jax.ShapeDtypeStruct((rows // 2, width + LANES), jnp.int16),
        compiler_params=pltpu.CompilerParams(vmem_limit_bytes=VMEM_LIMIT),
    )(keep, came, *after)


def add_body(keep, came, out, *, tile):
    half, width = out.shape
    for row in range(0, half, 16):
        here = slice(row, row + 16)
        marks = came[here, width:].astype(jnp.int32).astype(jnp.float32)
        for step in range(width // tile):
            block = slice(step * tile, (step + 1) * tile)
            out[here, block] = keep[here, block] + decode(came[here, block], marks[:, step : step + 1])


def add_kept(keep, came, tile):
    rows, width = keep.shape
    return pl.pallas_call(
        functools.partial(add_body, tile=tile),
        in_specs=[VMEM] * 2,
        out_specs=VMEM,
        out_shape=jax.ShapeDtypeStruct((rows // 2, width), jnp.float32),
        compiler_params=pltpu.CompilerParams(vmem_limit_bytes=VMEM_LIMIT),
    )(keep, came)


def finish_body(wanted, keep, *refs, tile, choices, first, arrived):
    arrivals, (logits, stats) = refs[:arrived], refs[-2:]
    rows, width = logits.shape
    height = 16
    lane = lax.broadcasted_iota(jnp.int32, (height, LANES), 1)
    for row in range(0, rows, height):
        here = slice(row, row + height)
        marks = [came[here, width:].astype(jnp.int32).astype(jnp.float32) for came in arrivals]
        ids = wanted[here, :] - first
        columns = [jnp.broadcast_to(ids[:, k : k + 1], (height, LANES)) for k in range(choices)]
        peak = None
        picks = [None] * choices
        for step in range(width // tile):
            block = slice(step * tile, (step + 1) * tile)
            value = keep[here, block]
            for came, mark in zip(arrivals, marks):
                value = value + decode(came[here, block], mark[:, step : step + 1])
            logits[here, block] = value
            for part in range(tile // LANES):
                piece = value[:, part * LANES : (part + 1) * LANES]
                at = lane + (step * tile + part * LANES)
                peak = piece if peak is None else jnp.maximum(peak, piece)
                for k in range(choices):
                    term = jnp.where(at == columns[k], piece, 0.0)
                    picks[k] = term if picks[k] is None else picks[k] + term
        peak = jnp.max(peak, axis=1, keepdims=True)
        total = None
        for part in range(width // LANES):
            term = jnp.exp(logits[here, part * LANES : (part + 1) * LANES] - peak)
            total = term if total is None else total + term
        out = jnp.where(lane == 0, peak, jnp.zeros((height, LANES), jnp.float32))
        for k, item in enumerate([total] + picks):
            out = jnp.where(lane == k + 1, jnp.sum(item, axis=1, keepdims=True), out)
        stats[here, :] = out


def finish(wanted, keep, arrivals, tile, choices, first, after):
    rows, width = wanted.shape[0], keep.shape[1]
    return pl.pallas_call(
        functools.partial(
            finish_body, tile=tile, choices=choices, first=first, arrived=len(arrivals)
        ),
        in_specs=[VMEM] * (2 + len(arrivals)) + [ANY] * len(after),
        out_specs=[VMEM] * 2,
        out_shape=[
            jax.ShapeDtypeStruct((rows, width), jnp.float32),
            jax.ShapeDtypeStruct((rows, LANES), jnp.float32),
        ],
        compiler_params=pltpu.CompilerParams(vmem_limit_bytes=VMEM_LIMIT),
    )(wanted, keep, *arrivals, *after)


def tail_body(stats, tree, *refs, heads, height, choices):
    logits, (log_probs, scores) = refs[:-2], refs[-2:]
    blocks = log_probs.shape[0] // height
    paths = scores.shape[1]
    for block in range(blocks):
        there = slice(block * height, (block + 1) * height)
        score = jnp.zeros((height, paths), jnp.float32)
        for head in range(heads):
            row = (block * heads + head) * height
            here = slice(row, row + height)
            normalizer = stats[here, 0:1] + jnp.log(stats[here, 1:2])
            first = 0
            for part in logits:
                width = part.shape[1]
                log_probs[there, head, first : first + width] = part[here, :] - normalizer
                first += width
            found = jnp.zeros((height, paths), jnp.float32)
            for k in range(choices):
                picked = stats[here, 2 + k : 3 + k] - normalizer
                found = jnp.where(tree[head : head + 1, :] == k, picked, found)
            score = score + found
        scores[there, :] = score


def tail(stats, tree, logits, out_rows, height, choices):
    heads, paths = tree.shape
    width = sum(part.shape[1] for part in logits)
    return pl.pallas_call(
        functools.partial(tail_body, heads=heads, height=height, choices=choices),
        in_specs=[VMEM] * (2 + len(logits)),
        out_specs=[VMEM] * 2,
        out_shape=[
            jax.ShapeDtypeStruct((out_rows, heads, width), jnp.float32),
            jax.ShapeDtypeStruct((out_rows, paths), jnp.float32),
        ],
        compiler_params=pltpu.CompilerParams(vmem_limit_bytes=VMEM_LIMIT),
    )(stats, tree, *logits)


def merge(one, two):
    peak = jnp.maximum(one[:, :1], two[:, :1])
    lane = lax.broadcasted_iota(jnp.int32, one.shape, 1)
    factor_one = jnp.where(lane == 1, jnp.exp(one[:, :1] - peak), 1.0)
    factor_two = jnp.where(lane == 1, jnp.exp(two[:, :1] - peak), 1.0)
    return jnp.where(lane == 0, peak, one * factor_one + two * factor_two)


def shards(
    hidden_states, accepted, norm_gain, head_weight, head_bias, vocab_weight, cand_ids, tree_paths
):
    batch, mp = lax.axis_size("batch"), lax.axis_size("mp")
    b, m = lax.axis_index("batch"), lax.axis_index("mp")
    rows, positions, feat = hidden_states.shape
    heads, inner, _ = head_weight.shape
    vocab_width = vocab_weight.shape[1]
    out_rows, _, choices = cand_ids.shape
    pieces = feat // inner
    ratio = out_rows // rows
    mp_bits = bits_of(mp)
    pair, core = b // 2, b % 2
    pair_bits = [bits_of(batch // 2), bits_of(batch // 2)[::-1]]

    chosen = hidden_states[:, 0, :]
    for position in range(1, positions):
        chosen = jnp.where((accepted == position + 1)[:, None], hidden_states[:, position, :], chosen)
    other = swap(chosen, "batch", lambda i: i ^ 1)
    chosen = jnp.concatenate(
        [jnp.where(core == 0, chosen, other), jnp.where(core == 0, other, chosen)], axis=0
    ).astype(jnp.float32)
    gain = lax.dynamic_slice_in_dim(norm_gain, m * feat, feat, 0)

    if pieces == 2:
        sent = lax.dynamic_slice_in_dim(chosen, core * inner, inner, 1)
        sent_gain = lax.dynamic_slice_in_dim(gain, core * inner, inner, 0)
    else:
        sent = lax.dynamic_slice_in_dim(chosen, core * rows, rows, 0)
        sent_gain = gain
    sent = (sent * sent_gain).astype(jnp.bfloat16)
    perm = []
    for i in range(batch):
        for j in range(mp):
            perm.append((i * mp + j, (j * pieces + i % pieces) * mp + ((i // pieces) ^ j)))
    head_first = (1 - core).astype(jnp.int32).reshape(1)
    head_then = core.astype(jnp.int32).reshape(1)
    part = feat // 2
    head_first = (1 - core).astype(jnp.int32).reshape(1)
    head_then = core.astype(jnp.int32).reshape(1)
    part = feat // 4
    firsts = [part * i for i in range(4)]
    weights_first = fetch(head_first, head_weight, firsts, part, [sent], HEAD_LIMIT)
    weights_then = []
    block = lax.ppermute(sent, ("batch", "mp"), perm)
    block, *weights_first = together(block, *weights_first)
    for bit in mp_bits:
        came = swap(block, "mp", lambda i: i ^ bit)
        if not weights_then:
            fetched = fetch(head_then, head_weight, firsts[:2], part, [block], HEAD_LIMIT)
            came, *weights_then = together(came, *fetched)
        block = jnp.concatenate([block, came], axis=0)

    square_sum = jnp.sum(chosen * chosen, axis=1, keepdims=True)
    for bit in mp_bits:
        square_sum = square_sum + swap(square_sum, "mp", lambda i: i ^ bit)
    row_scale = lax.rsqrt(square_sum / (mp * feat) + EPSILON)
    own_normed = (chosen * row_scale * gain).astype(jnp.bfloat16).astype(jnp.float32)

    spots = []
    for unit in range(batch):
        source = (m ^ (unit // pieces) ^ (b // pieces)) * pieces + unit % pieces
        apart = (source // 2) ^ pair
        spot = jnp.where(core == 0, place(apart, pair_bits[0]), place(apart, pair_bits[1]))
        spots.append(spot * 2 + source % 2)
    info = jnp.stack([core] + spots).astype(jnp.int32)
    send, *fetched = head_matmul(
        info, block, head_weight, weights_first, rows, jnp.bfloat16, firsts[2:]
    )
    weights_then = list(weights_then) + fetched
    came = swap(send, "batch", lambda i: i ^ 1)
    (keep,) = head_matmul(info, block, head_weight, weights_then, rows, jnp.float32, [])
    units = batch // 2
    turned = [place(unplace(u, pair_bits[0]), pair_bits[1]) for u in range(units)]
    came = came.reshape(units, 2 * rows, feat)
    came = jnp.concatenate([came[u] for u in turned], axis=0)
    total = keep + came.astype(jnp.float32)
    unit_width = vocab_width // 16
    held = {}

    def fetch_units(units, after):
        firsts = [unit * unit_width for unit in units]
        held.update(zip(units, fetch(head_then, vocab_weight, firsts, unit_width, after)))

    def wait_for(came, units):
        came, *fetched = together(came, *[held[unit] for unit in units])
        held.update(zip(units, fetched))
        return came

    for step in range(len(pair_bits[0])):
        half = total.shape[0] // 2
        outbound = total[half:].astype(jnp.bfloat16)
        units = (range(0, 4), range(4, 6))[step] if step < 2 else ()
        if units:
            fetch_units(units, [outbound])
        came = swap(outbound, "batch", lambda i: i ^ (2 * pair_bits[i % 2][step]))
        if units:
            came = wait_for(came, units)
        total = total[:half] + came.astype(jnp.float32)
    bias = lax.dynamic_slice_in_dim(head_bias, core, 1, 0)
    before = total * row_scale + bias
    residual = (own_normed + jax.nn.silu(before)).astype(jnp.bfloat16)
    for step in reversed(range(len(pair_bits[0]))):
        came = swap(residual, "batch", lambda i: i ^ (2 * pair_bits[i % 2][step]))
        if step:
            residual = jnp.concatenate([residual, came], axis=0)
    own = [residual, came]
    parts = own + [swap(part, "batch", lambda i: i ^ 1) for part in own]

    table = []
    for whose in (core, 1 - core):
        for unit in range(batch):
            apart = jnp.where(
                whose == 0, unplace(unit // 2, pair_bits[0]), unplace(unit // 2, pair_bits[1])
            )
            source = (pair ^ apart) * 2 + unit % 2
            table.append((((source // ratio) ^ m) * ratio + source % ratio) * heads + whose)
    all_rows = gather_rows(jnp.stack(table).astype(jnp.int32), parts, rows)
    wanted = (cand_ids - b * vocab_width).reshape(ratio, rows, heads, choices)
    wanted = wanted.transpose(0, 2, 1, 3).reshape(out_rows * heads, choices)
    wanted = jnp.pad(wanted, ((0, 0), (0, LANES - choices)), constant_values=-1)

    plan = [
        (range(0, 4), range(6, 8)),
        (range(4, 8), range(8, 12)),
        (range(8, 12), range(12, 16)),
        (range(12, 14), ()),
        (range(14, 16), ()),
    ]
    tile = widest(512, unit_width)
    blocks = len(plan)
    stages = [mp_bits if block % 2 == 0 else mp_bits[::-1] for block in range(blocks)]
    keeps, sends, arrivals = [], [], [[] for _ in plan]

    def begin(block, after):
        units, coming = plan[block]
        order = sorted(range(mp), key=lambda g: place(g, stages[block]))
        keep, send, *fetched = vocab_matmul(
            all_rows,
            vocab_weight,
            [held[u] for u in units],
            order,
            tile,
            [(u * unit_width, unit_width) for u in coming],
            after,
        )
        held.update(zip(coming, fetched))
        keeps.append(keep)
        sends.append(send)
        arrivals[block].append(swap(send, "mp", lambda i: i ^ stages[block][0]))

    def go_on(block, after):
        keep = keeps[block]
        for bit in stages[block][1:]:
            while len(arrivals[block]) > 1:
                rest = arrivals[block].pop(0)
                keep = add_kept(keep, rest, tile)
            send = fold(keep, arrivals[block][-1], tile, after)
            arrivals[block].append(swap(send, "mp", lambda i: i ^ bit))
        keeps[block] = keep
        return send

    begin(0, [])
    begin(1, [sends[0]])
    begin(2, [sends[1]])
    last = go_on(0, [sends[2]])
    begin(3, [last])
    last = go_on(1, [sends[3]])
    begin(4, [last])
    lasts = [go_on(block, [sends[4]]) for block in (2, 3, 4)]
    logits, stats = [], None
    for block, (units, _) in enumerate(plan):
        after = lasts[block : block + 1]
        part, part_stats = finish(
            wanted, keeps[block], arrivals[block], tile, choices, units[0] * unit_width, after
        )
        logits.append(part)
        stats = part_stats if stats is None else merge(stats, part_stats)

    for bit in bits_of(batch):
        came = swap(stats, "batch", lambda i: i ^ bit)
        low = (b & bit) == 0
        stats = merge(jnp.where(low, stats, came), jnp.where(low, came, stats))
    log_probs, path_scores = tail(stats, tree_paths.T, logits, out_rows, rows, choices)
    return (log_probs, path_scores)


def solution(mesh):
    return jax.shard_map(
        shards,
        mesh=mesh,
        in_specs=(
            P("batch", None, "mp"),
            P("batch"),
            P(),
            P(None, "batch", "mp"),
            P(None, "mp"),
            P("mp", "batch"),
            P("mp", None, None),
            P(),
        ),
        out_specs=(P("mp", None, "batch"), P("mp", None)),
        check_vma=False,
    )
```

time: 208 us -> 197 us (0.947)
  waiting for transfers between devices: 72.5 us -> 52.7 us
  local copies, waits for them, and re-layouts: 11.1 us -> 27.5 us
  starting transfers between devices: 38.8 us -> 29.1 us
  Pallas kernels: 74.5 us -> 82.2 us
  other arithmetic: 8.53 us -> 3.89 us
    ppermute x24 -> x25, waiting for transfers between devices: 72.5 us -> 52.7 us  [swap(): lax.ppermute(array, axis, [(i, partner(i)) for i in range(lax.axis_size(a...]
    unnamed x62 -> x70, local copies, waits for them, and re-layouts: 3.38 us -> 23.2 us
    ppermute x24 -> x25, starting transfers between devices: 38.1 us -> 28.3 us  [swap(): lax.ppermute(array, axis, [(i, partner(i)) for i in range(lax.axis_size(a...]
    pallas_call x12 -> x18, Pallas kernels: 67.3 us -> 73.2 us  [the longest x5 35.6 us: vocab_matmul(): pl.pallas_call(functools.partial(vocab_body, order=order, tile=tile, coun...]
    transpose x1 -> x0, local copies, waits for them, and re-layouts: 2.94 us -> none  [natural(): return array.transpose(0, 2, 1, 3).reshape(out_rows, heads, array.shape[3])]
  transfers between devices with their start and end apart: 25 -> 26, of which waited for: 16 -> 13; matrix products, arithmetic and copies ran while one was open for 4% -> 1% of each run, Pallas kernels for 26% -> 35%
where the time goes in v3:
time: 197 us
  Pallas kernels  82.2 us (42%)
  waiting for transfers between devices  52.7 us (27%)
  starting transfers between devices  29.1 us (15%)
  local copies, waits for them, and re-layouts  27.5 us (14%)
  other arithmetic  3.89 us (2%)
    ppermute x25, waiting for transfers between devices, swap(): lax.ppermute(array, axis, [(i, partner(i)) for i in range(lax.axis_size(a...  52.7 us
    pallas_call x5, Pallas kernels, vocab_matmul(): pl.pallas_call(functools.partial(vocab_body, order=order, tile=tile, coun...  35.6 us
    ppermute x25, starting transfers between devices, swap(): lax.ppermute(array, axis, [(i, partner(i)) for i in range(lax.axis_size(a...  28.3 us
    unnamed x70, local copies, waits for them, and re-layouts  23.2 us
    pallas_call x4, Pallas kernels, fetch(): pl.pallas_call(functools.partial(fetch_body, firsts=firsts), in_specs=[pl...  19.1 us
    pallas_call x2, Pallas kernels, head_matmul(): pl.pallas_call(functools.partial(head_body, height=height, held=len(weigh...  9.26 us
    pallas_call x5, Pallas kernels, finish(): pl.pallas_call(functools.partial(finish_body, tile=tile, choices=choices,...  8.95 us
    pallas_call x5, Pallas kernels, fold(): pl.pallas_call(functools.partial(fold_body, tile=tile), in_specs=[VMEM] *...  5.91 us
  transfers between devices with their start and end apart: 26, of which 13 were waited for; matrix products, arithmetic and copies ran while one was open for 1% of the time, Pallas kernels for 35%

profile of v3, /device:TPU:0, one launch (start us, length us, event | category | flops | bytes accessed | tf_op | source)
XLA Modules:
  0.0 196.8 jit_solution(17099281726248871568)
XLA Ops:
  0.6 3.0 %fusion.13 = (bf16[16,1,4096]{2,1,0:T(2,128)(2,1)S(1)}, bf16[16,1,4096]{2,1,0:T(2,128)(2,1)S(1)}, bf16[16,1,4096]{2,1,0:T(2,128)(2,1)S(1)}, bf16[16,1,4096]{2,1,0:T(2,128)(2,1)S(1)}) fusion(bf16[16,4,4096]{2,1,0:T(4,128)(2,1)} %param.8), kind=kLoop, calls=%fused_computation.77 | loop fusion | bytes 1048576 | tf_op jit(solution)/shard_map/slice | solution.py:407
  7.5 5.8 %collective-permute-start.1 = (f32[32,1]{0,1:T(1,128)S(1)}, f32[32,1]{0,1:T(1,128)S(1)}, u32[]{:S(2)}, u32[]{:S(2)}) collective-permute-start(f32[32,1]{0,1:T(1,128)S(1)} %bitcast.60), channel_id=1, source_target_pairs={{0,1},{1,0},{2,3},{3,2},{4,5},{5,4},{6,7},{7,6},{8,9},{9,8},{10,11... | collective-permute-start | bytes 392 | tf_op jit(solution)/shard_map/ppermute | solution.py:27
  13.2 6.0 %shard_map.95 = (bf16[2048,1024]{1,0:T(8,128)(2,1)S(1)}, bf16[2048,1024]{1,0:T(8,128)(2,1)S(1)}, bf16[2048,1024]{1,0:T(8,128)(2,1)S(1)}, bf16[2048,1024]{1,0:T(8,128)(2,1)S(1)}) custom-call(s32[1]{0:T(128)} %bitcast.33.info, bf16[2,2048,4096]{2,1,0:T(8,128)(2,1)} %source.8, bf16[32,2048]{1,0:T(8,128)(2,1)S(1)} %multiply_convert_fusion.1.refs_0_), custom_call_target="tpu_custom_call" | custom-call | flops 5872025600 | tf_op jit(solution)/shard_map/pallas_call | solution.py:83
  19.2 4.2 %collective-permute-start.4 = (bf16[32,2048]{1,0:T(8,128)(2,1)S(1)}, bf16[32,2048]{1,0:T(8,128)(2,1)S(1)}, u32[]{:S(2)}, u32[]{:S(2)}) collective-permute-start(bf16[32,2048]{1,0:T(8,128)(2,1)S(1)} %collective-permute-done.3.refs_0_), channel_id=1, source_target_pairs={{0,1},{1,0},{2,3},{3,2},{4,5},{5,4},{6,7},{7,6},{8,9},{9,8},{10,11... | collective-permute-start | bytes 393224 | tf_op jit(solution)/shard_map/ppermute | solution.py:27
  23.4 3.5 %shard_map.96 = (bf16[2048,1024]{1,0:T(8,128)(2,1)S(1)}, bf16[2048,1024]{1,0:T(8,128)(2,1)S(1)}) custom-call(s32[1]{0:T(128)} %bitcast.24.info, bf16[2,2048,4096]{2,1,0:T(8,128)(2,1)} %source.8, bf16[32,2048]{1,0:T(8,128)(2,1)S(1)} %collective-permute-done.3.refs_0_), custom_call_target="tpu_custom_call" | custom-call | flops 2936012800 | tf_op jit(solution)/shard_map/pallas_call | solution.py:83
  27.9 6.3 %collective-permute-done.5 = bf16[64,2048]{1,0:T(8,128)(2,1)S(1)} collective-permute-done((bf16[64,2048]{1,0:T(8,128)(2,1)S(1)}, bf16[64,2048]{1,0:T(8,128)(2,1)S(1)}, u32[]{:S(2)}, u32[]{:S(2)}) %collective-permute-start.5) | collective-permute-done | bytes 262176 | tf_op jit(solution)/shard_map/ppermute | solution.py:27
  34.3 6.3 %shard_map.97 = (bf16[128,4096]{1,0:T(8,128)(2,1)S(1)}, bf16[2048,1024]{1,0:T(8,128)(2,1)S(1)}, bf16[2048,1024]{1,0:T(8,128)(2,1)S(1)}) custom-call(s32[9]{0:T(128)S(1)} %stack.107.info, bf16[128,2048]{1,0:T(8,128)(2,1)S(1)} %constant_dynamic-update-slice_fusion.came, bf16[2,2048,4096]{2,1,0:T(8,128)(2,1)} %source.8, ...), custom_call_target="tpu_custom_call" | custom-call | flops 2147483648 | bytes 524288 | tf_op jit(solution)/shard_map/pallas_call | solution.py:125
  41.1 3.2 %collective-permute-done.2 = f32[32,1]{0,1:T(1,128)S(1)} collective-permute-done((f32[32,1]{0,1:T(1,128)S(1)}, f32[32,1]{0,1:T(1,128)S(1)}, u32[]{:S(2)}, u32[]{:S(2)}) %collective-permute-start.2) | collective-permute-done | bytes 160 | tf_op jit(solution)/shard_map/ppermute | solution.py:27
  44.3 3.0 %shard_map.98 = f32[128,4096]{1,0:T(8,128)S(1)} custom-call(s32[9]{0:T(128)S(1)} %stack.107.info, bf16[128,2048]{1,0:T(8,128)(2,1)S(1)} %constant_dynamic-update-slice_fusion.came, bf16[2,2048,4096]{2,1,0:T(8,128)(2,1)} %source.8, bf16[2048,1024]{1,0:T(8,128)(2,1)S(1)} %get-tuple-element.71.refs_0_, bf16[2048,1024]{1,0:T(8,128)(2,1)S(1)} %get-tuple-element.72.refs_1_, ...), custom_call_target="tpu_custom_call" | custom-call | flops 2147483648 | bytes 524288 | tf_op jit(solution)/shard_map/pallas_call | solution.py:125
  47.7 6.1 %shard_map.99 = (bf16[4096,512]{1,0:T(8,128)(2,1)S(1)}, bf16[4096,512]{1,0:T(8,128)(2,1)S(1)}, bf16[4096,512]{1,0:T(8,128)(2,1)S(1)}, bf16[4096,512]{1,0:T(8,128)(2,1)S(1)}) custom-call(s32[1]{0:T(128)} %bitcast.24.info, bf16[4096,8192]{1,0:T(8,128)(2,1)} %source.13, bf16[64,4096]{1,0:T(8,128)(2,1)S(1)} %slice.263.refs_0_), custom_call_target="tpu_custom_call" | custom-call | flops 5872025600 | tf_op jit(solution)/shard_map/pallas_call | solution.py:83
  61.5 2.6 %collective-permute-start.8 = (bf16[32,4096]{1,0:T(8,128)(2,1)S(1)}, bf16[32,4096]{1,0:T(8,128)(2,1)S(1)}, u32[]{:S(2)}, u32[]{:S(2)}) collective-permute-start(bf16[32,4096]{1,0:T(8,128)(2,1)S(1)} %slice.264.refs_0_), channel_id=1, source_target_pairs={{0,16},{4,12},{8,24},{12,4},{16,0},{20,28},{24,8},{28,20},{1,17},{... | collective-permute-start | bytes 786440 | tf_op jit(solution)/shard_map/ppermute | solution.py:27
  64.0 3.5 %shard_map.100 = (bf16[4096,512]{1,0:T(8,128)(2,1)S(1)}, bf16[4096,512]{1,0:T(8,128)(2,1)S(1)}) custom-call(s32[1]{0:T(128)} %bitcast.24.info, bf16[4096,8192]{1,0:T(8,128)(2,1)} %source.13, bf16[32,4096]{1,0:T(8,128)(2,1)S(1)} %slice.264.refs_0_), custom_call_target="tpu_custom_call" | custom-call | flops 2936012800 | tf_op jit(solution)/shard_map/pallas_call | solution.py:83
  69.5 2.0 %copy-done.4 = bf16[4096,512]{1,0:T(8,128)(2,1)} copy-done((bf16[4096,512]{1,0:T(8,128)(2,1)}, bf16[4096,512]{1,0:T(8,128)(2,1)S(1)}, u32[]{:S(2)}) %copy-start.4) | copy-done | bytes 4194328
  73.2 15.4 %collective-permute-done.9 = bf16[32,4096]{1,0:T(8,128)(2,1)S(1)} collective-permute-done((bf16[32,4096]{1,0:T(8,128)(2,1)S(1)}, bf16[32,4096]{1,0:T(8,128)(2,1)S(1)}, u32[]{:S(2)}, u32[]{:S(2)}) %collective-permute-start.9) | collective-permute-done | bytes 262176 | tf_op jit(solution)/shard_map/ppermute | solution.py:27
  88.6 2.0 %collective-permute-start.10 = (bf16[64,4096]{1,0:T(8,128)(2,1)S(1)}, bf16[64,4096]{1,0:T(8,128)(2,1)S(1)}, u32[]{:S(2)}, u32[]{:S(2)}) collective-permute-start(bf16[64,4096]{1,0:T(8,128)(2,1)S(1)} %pad_maximum_fusion.refs_0_), channel_id=1, source_target_pairs={{0,8},{4,20},{8,0},{12,28},{16,24},{20,4},{24,16},{28,12},{1,9},{5... | collective-permute-start | bytes 1572872 | tf_op jit(solution)/shard_map/ppermute | solution.py:27
  90.6 8.3 %collective-permute-done.10.refs_1_ = bf16[64,4096]{1,0:T(8,128)(2,1)S(1)} collective-permute-done((bf16[64,4096]{1,0:T(8,128)(2,1)S(1)}, bf16[64,4096]{1,0:T(8,128)(2,1)S(1)}, u32[]{:S(2)}, u32[]{:S(2)}) %collective-permute-start.10) | collective-permute-done | bytes 524320 | tf_op jit(solution)/shard_map/ppermute | solution.py:27
  102.2 2.2 %copy-done.13 = bf16[4096,512]{1,0:T(8,128)(2,1)S(1)} copy-done((bf16[4096,512]{1,0:T(8,128)(2,1)S(1)}, bf16[4096,512]{1,0:T(8,128)(2,1)}, u32[]{:S(2)}) %copy-start.13) | copy-done | bytes 4194328
  104.4 2.2 %copy-done.15 = bf16[4096,512]{1,0:T(8,128)(2,1)S(1)} copy-done((bf16[4096,512]{1,0:T(8,128)(2,1)S(1)}, bf16[4096,512]{1,0:T(8,128)(2,1)}, u32[]{:S(2)}) %copy-start.15) | copy-done | bytes 4194328
  106.6 2.2 %copy-done.17 = bf16[4096,512]{1,0:T(8,128)(2,1)S(1)} copy-done((bf16[4096,512]{1,0:T(8,128)(2,1)S(1)}, bf16[4096,512]{1,0:T(8,128)(2,1)}, u32[]{:S(2)}) %copy-start.17) | copy-done | bytes 4194328
  108.8 8.1 %shard_map.102 = (f32[128,2048]{1,0:T(8,128)S(1)}, s16[128,2176]{1,0:T(8,128)(2,1)}, bf16[4096,512]{1,0:T(8,128)(2,1)S(1)}, bf16[4096,512]{1,0:T(8,128)(2,1)S(1)}) custom-call(bf16[256,4096]{1,0:T(8,128)(2,1)S(1)} %shard_map.101.rows, bf16[4096,8192]{1,0:T(8,128)(2,1)} %source.13, bf16[4096,512]{1,0:T(8,128)(2,1)S(1)} %copy-done.11, ...), custom_call_target="tpu_custom_call" | custom-call | flops 4294967296 | bytes 16777216 | tf_op jit(solution)/shard_map/pallas_call | solution.py:219
  117.6 10.6 %shard_map.103 = (f32[128,2048]{1,0:T(8,128)S(1)}, s16[128,2176]{1,0:T(8,128)(2,1)S(1)}, bf16[4096,512]{1,0:T(8,128)(2,1)S(1)}, bf16[4096,512]{1,0:T(8,128)(2,1)...) custom-call(bf16[256,4096]{1,0:T(8,128)(2,1)S(1)} %shard_map.101.rows, bf16[4096,8192]{1,0:T(8,128)(2,1)} %source.13, ...), custom_call_target="tpu_custom_call" | custom-call | flops 4294967296 | bytes 16777216 | tf_op jit(solution)/shard_map/pallas_call | solution.py:219
  128.2 2.6 %collective-permute-start.16 = (s16[128,2176]{1,0:T(8,128)(2,1)S(1)}, s16[128,2176]{1,0:T(8,128)(2,1)S(1)}, u32[]{:S(2)}, u32[]{:S(2)}) collective-permute-start(s16[128,2176]{1,0:T(8,128)(2,1)S(1)} %get-tuple-element.102.refs_4_), channel_id=1, source_target_pairs={{0,2},{1,3},{2,0},{3,1},{4,6},{5,7},{6,4},{7,5},{8,10},{9,11},{10,... | collective-permute-start | bytes 1671176 | tf_op jit(solution)/shard_map/ppermute | solution.py:27
  130.8 11.2 %shard_map.104 = (f32[128,2048]{1,0:T(8,128)S(1)}, s16[128,2176]{1,0:T(8,128)(2,1)}, bf16[4096,512]{1,0:T(8,128)(2,1)S(1)}, bf16[4096,512]{1,0:T(8,128)(2,1)S(1)...) custom-call(bf16[256,4096]{1,0:T(8,128)(2,1)S(1)} %shard_map.101.rows, bf16[4096,8192]{1,0:T(8,128)(2,1)} %source.13, ...), custom_call_target="tpu_custom_call" | custom-call | flops 4294967296 | bytes 16777216 | tf_op jit(solution)/shard_map/pallas_call | solution.py:219
  144.6 3.2 %shard_map.106 = (f32[128,1024]{1,0:T(8,128)S(1)}, s16[128,1152]{1,0:T(8,128)(2,1)}) custom-call(bf16[256,4096]{1,0:T(8,128)(2,1)S(1)} %shard_map.101.rows, bf16[4096,8192]{1,0:T(8,128)(2,1)} %source.13, bf16[4096,512]{1,0:T(8,128)(2,1)S(1)} %get-tuple-element.108.refs_0_, bf16[4096,512]{1,0:T(8,128)(2,1)S(1)} %get-tuple-element.109.refs_1_, ...), custom_call_target="tpu_custom_call" | custom-call | flops 2147483648 | bytes 8388608 | tf_op jit(solution)/shard_map/pallas_call | solution.py:219
  150.7 2.0 %collective-permute-start.17 = (s16[64,2176]{1,0:T(8,128)(2,1)}, s16[64,2176]{1,0:T(8,128)(2,1)}, u32[]{:S(2)}, u32[]{:S(2)}) collective-permute-start(s16[64,2176]{1,0:T(8,128)(2,1)} %shard_map.107.refs_2_), channel_id=1, source_target_pairs={{0,1},{1,0},{2,3},{3,2},{4,5},{5,4},{6,7},{7,6},{8,9},{9,8},{10,11... | collective-permute-start | bytes 835592 | tf_op jit(solution)/shard_map/ppermute | solution.py:27
  152.7 2.5 %shard_map.108 = (f32[128,1024]{1,0:T(8,128)S(1)}, s16[128,1152]{1,0:T(8,128)(2,1)S(1)}) custom-call(bf16[256,4096]{1,0:T(8,128)(2,1)S(1)} %shard_map.101.rows, bf16[4096,8192]{1,0:T(8,128)(2,1)} %source.13, bf16[4096,512]{1,0:T(8,128)(2,1)S(1)} %get-tuple-element.105.refs_0_, bf16[4096,512]{1,0:T(8,128)(2,1)S(1)} %get-tuple-element.106.refs_1_, ...), custom_call_target="tpu_custom_call" | custom-call | flops 2147483648 | bytes 8388608 | tf_op jit(solution)/shard_map/pallas_call | solution.py:219
  159.9 2.2 %shard_map.110 = (f32[64,2048]{1,0:T(8,128)S(1)}, f32[64,128]{1,0:T(8,128)S(1)}) custom-call(s32[64,128]{1,0:T(8,128)S(1)} %pad.4.wanted, f32[128,2048]{1,0:T(8,128)S(1)} %get-tuple-element.92.keep, s16[128,2176]{1,0:T(8,128)(2,1)S(1)} %copy-done.21, s16[64,2176]{1,0:T(8,128)(2,1)} %collective-permute-done.14.refs_1_, s16[64,2176]{1,0:T(8,128)(2,1)S(1)} %shard_map.109.refs_2_), custom_call_target="tpu_custom_call" | custom-call | tf_op jit(solution)/shard_map/pallas_call | solution.py:329
  164.5 5.6 %collective-permute-done.20.came.refs_0_ = s16[128,1152]{1,0:T(8,128)(2,1)S(1)} collective-permute-done((s16[128,1152]{1,0:T(8,128)(2,1)S(1)}, s16[128,1152]{1,0:T(8,128)(2,1)S(1)}, u32[]{:S(2)}, u32[]{:S(2)}) %collective-permute-start.20) | collective-permute-done | bytes 294944 | tf_op jit(solution)/shard_map/ppermute | solution.py:27
  171.8 2.6 %shard_map.112 = (f32[64,2048]{1,0:T(8,128)S(1)}, f32[64,128]{1,0:T(8,128)S(1)}) custom-call(s32[64,128]{1,0:T(8,128)S(1)} %pad.4.wanted, f32[128,2048]{1,0:T(8,128)S(1)} %copy-done.9, s16[128,2176]{1,0:T(8,128)(2,1)S(1)} %copy-done.19, s16[64,2176]{1,0:T(8,128)(2,1)} %collective-permute-done.17.refs_1_, s16[64,1152]{1,0:T(8,128)(2,1)S(1)} %shard_map.111.refs_2_), custom_call_target="tpu_custom_call" | custom-call | tf_op jit(solution)/shard_map/pallas_call | solution.py:329
  183.0 3.7 %collective-permute-done.24 = f32[64,128]{1,0:T(8,128)S(1)} collective-permute-done((f32[64,128]{1,0:T(8,128)S(1)}, f32[64,128]{1,0:T(8,128)S(1)}, u32[]{:S(2)}, u32[]{:S(2)}) %collective-permute-start.24) | collective-permute-done | bytes 32800 | tf_op jit(solution)/shard_map/ppermute | solution.py:27
  188.6 3.6 %collective-permute-done.25 = f32[64,128]{1,0:T(8,128)S(1)} collective-permute-done((f32[64,128]{1,0:T(8,128)S(1)}, f32[64,128]{1,0:T(8,128)S(1)}, u32[]{:S(2)}, u32[]{:S(2)}) %collective-permute-start.25) | collective-permute-done | bytes 32800 | tf_op jit(solution)/shard_map/ppermute | solution.py:27
  194.6 2.2 %shard_map.117 = (f32[32,2,8192]{2,1,0:T(2,128)}, f32[32,64]{1,0:T(8,128)}) custom-call(f32[64,128]{1,0:T(8,128)S(1)} %add_select_fusion.stats, s32[2,64]{1,0:T(2,128)S(1)} %bitcast.57, f32[64,2048]{1,0:T(8,128)S(1)} %copy-done.27, f32[64,2048]{1,0:T(8,128)S(1)} %copy-done.29, f32[64,2048]{1,0:T(8,128)S(1)} %copy-done.31, ...), custom_call_target="tpu_custom_call" | custom-call | tf_op jit(solution)/shard_map/pallas_call | solution.py:370
  (160 shorter events, 47.7 us)
Async XLA Ops:
  0.6 40.4 %copy-start = (f32[2,4096]{1,0:T(2,128)S(1)}, f32[2,4096]{1,0:T(2,128)}, u32[]{:S(2)}) copy-start(f32[2,4096]{1,0:T(2,128)} %param.12) | copy-start | bytes 98308
  4.8 1.5 collective-permute-start
  6.6 12.6 %collective-permute-start.3 = (bf16[32,2048]{1,0:T(8,128)(2,1)S(1)}, bf16[32,2048]{1,0:T(8,128)(2,1)S(1)}, u32[]{:S(2)}, u32[]{:S(2)}) collective-permute-start(bf16[32,2048]{1,0:T(8,128)(2,1)S(1)} %multiply_convert_fusion.1.refs_0_), channel_id=1, source_target_pairs={{0,0},{1,9},{2,18},{3,27},{4,4},{5,13},{6,22},{7,31},{8,1},{9,8},{... | collective-permute-start | bytes 393224 | tf_op jit(solution)/shard_map/ppermute | solution.py:434
  7.5 33.2 %collective-permute-start.1 = (f32[32,1]{0,1:T(1,128)S(1)}, f32[32,1]{0,1:T(1,128)S(1)}, u32[]{:S(2)}, u32[]{:S(2)}) collective-permute-start(f32[32,1]{0,1:T(1,128)S(1)} %bitcast.60), channel_id=1, source_target_pairs={{0,1},{1,0},{2,3},{3,2},{4,5},{5,4},{6,7},{7,6},{8,9},{9,8},{10,11... | collective-permute-start | bytes 392 | tf_op jit(solution)/shard_map/ppermute | solution.py:27
  19.2 7.7 %collective-permute-start.4 = (bf16[32,2048]{1,0:T(8,128)(2,1)S(1)}, bf16[32,2048]{1,0:T(8,128)(2,1)S(1)}, u32[]{:S(2)}, u32[]{:S(2)}) collective-permute-start(bf16[32,2048]{1,0:T(8,128)(2,1)S(1)} %collective-permute-done.3.refs_0_), channel_id=1, source_target_pairs={{0,1},{1,0},{2,3},{3,2},{4,5},{5,4},{6,7},{7,6},{8,9},{9,8},{10,11... | collective-permute-start | bytes 393224 | tf_op jit(solution)/shard_map/ppermute | solution.py:27
  27.0 7.3 %collective-permute-start.5 = (bf16[64,2048]{1,0:T(8,128)(2,1)S(1)}, bf16[64,2048]{1,0:T(8,128)(2,1)S(1)}, u32[]{:S(2)}, u32[]{:S(2)}) collective-permute-start(bf16[64,2048]{1,0:T(8,128)(2,1)S(1)} %pad_maximum_fusion.1), channel_id=1, source_target_pairs={{0,2},{1,3},{2,0},{3,1},{4,6},{5,7},{6,4},{7,5},{8,10},{9,11},{10,... | collective-permute-start | bytes 786440 | tf_op jit(solution)/shard_map/ppermute | solution.py:27
  40.6 6.7 %collective-permute-start.6 = (bf16[128,4096]{1,0:T(8,128)(2,1)S(1)}, bf16[128,4096]{1,0:T(8,128)(2,1)S(1)}, u32[]{:S(2)}, u32[]{:S(2)}) collective-permute-start(bf16[128,4096]{1,0:T(8,128)(2,1)S(1)} %get-tuple-element.79), channel_id=1, source_target_pairs={{0,4},{4,0},{8,12},{12,8},{16,20},{20,16},{24,28},{28,24},{1,5},{5... | collective-permute-start | bytes 3145736 | tf_op jit(solution)/shard_map/ppermute | solution.py:27
  40.7 3.6 %collective-permute-start.2 = (f32[32,1]{0,1:T(1,128)S(1)}, f32[32,1]{0,1:T(1,128)S(1)}, u32[]{:S(2)}, u32[]{:S(2)}) collective-permute-start(f32[32,1]{0,1:T(1,128)S(1)} %bitcast_add_fusion), channel_id=1, source_target_pairs={{0,2},{1,3},{2,0},{3,1},{4,6},{5,7},{6,4},{7,5},{8,10},{9,11},{10,... | collective-permute-start | bytes 392 | tf_op jit(solution)/shard_map/ppermute | solution.py:27
  47.6 13.7 %collective-permute-start.7 = (bf16[64,4096]{1,0:T(8,128)(2,1)S(1)}, bf16[64,4096]{1,0:T(8,128)(2,1)S(1)}, u32[]{:S(2)}, u32[]{:S(2)}) collective-permute-start(bf16[64,4096]{1,0:T(8,128)(2,1)S(1)} %slice.263.refs_0_), channel_id=1, source_target_pairs={{0,8},{4,20},{8,0},{12,28},{16,24},{20,4},{24,16},{28,12},{1,9},{5... | collective-permute-start | bytes 1572872 | tf_op jit(solution)/shard_map/ppermute | solution.py:27
  61.5 10.2 %collective-permute-start.8 = (bf16[32,4096]{1,0:T(8,128)(2,1)S(1)}, bf16[32,4096]{1,0:T(8,128)(2,1)S(1)}, u32[]{:S(2)}, u32[]{:S(2)}) collective-permute-start(bf16[32,4096]{1,0:T(8,128)(2,1)S(1)} %slice.264.refs_0_), channel_id=1, source_target_pairs={{0,16},{4,12},{8,24},{12,4},{16,0},{20,28},{24,8},{28,20},{1,17},{... | collective-permute-start | bytes 786440 | tf_op jit(solution)/shard_map/ppermute | solution.py:27
  72.0 16.6 %collective-permute-start.9 = (bf16[32,4096]{1,0:T(8,128)(2,1)S(1)}, bf16[32,4096]{1,0:T(8,128)(2,1)S(1)}, u32[]{:S(2)}, u32[]{:S(2)}) collective-permute-start(bf16[32,4096]{1,0:T(8,128)(2,1)S(1)} %add_convert_fusion), channel_id=1, source_target_pairs={{0,16},{4,12},{8,24},{12,4},{16,0},{20,28},{24,8},{28,20},{1,17},{... | collective-permute-start | bytes 786440 | tf_op jit(solution)/shard_map/ppermute | solution.py:27
  88.6 10.3 %collective-permute-start.10 = (bf16[64,4096]{1,0:T(8,128)(2,1)S(1)}, bf16[64,4096]{1,0:T(8,128)(2,1)S(1)}, u32[]{:S(2)}, u32[]{:S(2)}) collective-permute-start(bf16[64,4096]{1,0:T(8,128)(2,1)S(1)} %pad_maximum_fusion.refs_0_), channel_id=1, source_target_pairs={{0,8},{4,20},{8,0},{12,28},{16,24},{20,4},{24,16},{28,12},{1,9},{5... | collective-permute-start | bytes 1572872 | tf_op jit(solution)/shard_map/ppermute | solution.py:27
  90.6 8.5 %collective-permute-start.11 = (bf16[64,4096]{1,0:T(8,128)(2,1)S(1)}, bf16[64,4096]{1,0:T(8,128)(2,1)S(1)}, u32[]{:S(2)}, u32[]{:S(2)}) collective-permute-start(bf16[64,4096]{1,0:T(8,128)(2,1)S(1)} %pad_maximum_fusion.refs_0_), channel_id=1, source_target_pairs={{0,4},{4,0},{8,12},{12,8},{16,20},{20,16},{24,28},{28,24},{1,5},{5... | collective-permute-start | bytes 1572872 | tf_op jit(solution)/shard_map/ppermute | solution.py:27
  99.0 2.0 %collective-permute-start.12 = (bf16[64,4096]{1,0:T(8,128)(2,1)S(1)}, bf16[64,4096]{1,0:T(8,128)(2,1)}, u32[]{:S(2)}, u32[]{:S(2)}) collective-permute-start(bf16[64,4096]{1,0:T(8,128)(2,1)S(1)} %collective-permute-done.10.refs_1_), channel_id=1, source_target_pairs={{0,4},{4,0},{8,12},{12,8},{16,20},{20,16},{24,28},{28,24},{1,5},{5... | collective-permute-start | bytes 1572872 | tf_op jit(solution)/shard_map/ppermute | solution.py:27
  116.9 25.2 %collective-permute-start.13 = (s16[128,2176]{1,0:T(8,128)(2,1)}, s16[128,2176]{1,0:T(8,128)(2,1)S(1)}, u32[]{:S(2)}, u32[]{:S(2)}) collective-permute-start(s16[128,2176]{1,0:T(8,128)(2,1)} %get-tuple-element.93.refs_4_), channel_id=1, source_target_pairs={{0,1},{1,0},{2,3},{3,2},{4,5},{5,4},{6,7},{7,6},{8,9},{9,8},{10,11... | collective-permute-start | bytes 1671176 | tf_op jit(solution)/shard_map/ppermute | solution.py:27
  128.2 20.9 %copy-start.8 = (f32[128,2048]{1,0:T(8,128)}, f32[128,2048]{1,0:T(8,128)S(1)}, u32[]{:S(2)}) copy-start(f32[128,2048]{1,0:T(8,128)S(1)} %get-tuple-element.107.keep) | copy-start | bytes 3145732
  128.2 20.9 %collective-permute-start.16 = (s16[128,2176]{1,0:T(8,128)(2,1)S(1)}, s16[128,2176]{1,0:T(8,128)(2,1)S(1)}, u32[]{:S(2)}, u32[]{:S(2)}) collective-permute-start(s16[128,2176]{1,0:T(8,128)(2,1)S(1)} %get-tuple-element.102.refs_4_), channel_id=1, source_target_pairs={{0,2},{1,3},{2,0},{3,1},{4,6},{5,7},{6,4},{7,5},{8,10},{9,11},{10,... | collective-permute-start | bytes 1671176 | tf_op jit(solution)/shard_map/ppermute | solution.py:27
  142.0 15.8 %collective-permute-start.15 = (s16[128,2176]{1,0:T(8,128)(2,1)}, s16[128,2176]{1,0:T(8,128)(2,1)S(1)}, u32[]{:S(2)}, u32[]{:S(2)}) collective-permute-start(s16[128,2176]{1,0:T(8,128)(2,1)} %get-tuple-element.103.refs_0_), channel_id=1, source_target_pairs={{0,1},{1,0},{2,3},{3,2},{4,5},{5,4},{6,7},{7,6},{8,9},{9,8},{10,11... | collective-permute-start | bytes 1671176 | tf_op jit(solution)/shard_map/ppermute | solution.py:27
  143.7 15.1 %collective-permute-start.14 = (s16[64,2176]{1,0:T(8,128)(2,1)}, s16[64,2176]{1,0:T(8,128)(2,1)}, u32[]{:S(2)}, u32[]{:S(2)}) collective-permute-start(s16[64,2176]{1,0:T(8,128)(2,1)} %shard_map.105.refs_2_), channel_id=1, source_target_pairs={{0,2},{1,3},{2,0},{3,1},{4,6},{5,7},{6,4},{7,5},{8,10},{9,11},{10,... | collective-permute-start | bytes 835592 | tf_op jit(solution)/shard_map/ppermute | solution.py:27
  147.8 14.3 %collective-permute-start.18 = (s16[128,1152]{1,0:T(8,128)(2,1)}, s16[128,1152]{1,0:T(8,128)(2,1)}, u32[]{:S(2)}, u32[]{:S(2)}) collective-permute-start(s16[128,1152]{1,0:T(8,128)(2,1)} %get-tuple-element.110.refs_0_), channel_id=1, source_target_pairs={{0,2},{1,3},{2,0},{3,1},{4,6},{5,7},{6,4},{7,5},{8,10},{9,11},{10,... | collective-permute-start | bytes 884744 | tf_op jit(solution)/shard_map/ppermute | solution.py:27
  150.7 19.9 %collective-permute-start.17 = (s16[64,2176]{1,0:T(8,128)(2,1)}, s16[64,2176]{1,0:T(8,128)(2,1)}, u32[]{:S(2)}, u32[]{:S(2)}) collective-permute-start(s16[64,2176]{1,0:T(8,128)(2,1)} %shard_map.107.refs_2_), channel_id=1, source_target_pairs={{0,1},{1,0},{2,3},{3,2},{4,5},{5,4},{6,7},{7,6},{8,9},{9,8},{10,11... | collective-permute-start | bytes 835592 | tf_op jit(solution)/shard_map/ppermute | solution.py:27
  156.0 14.1 %collective-permute-start.20 = (s16[128,1152]{1,0:T(8,128)(2,1)S(1)}, s16[128,1152]{1,0:T(8,128)(2,1)S(1)}, u32[]{:S(2)}, u32[]{:S(2)}) collective-permute-start(s16[128,1152]{1,0:T(8,128)(2,1)S(1)} %get-tuple-element.111.refs_0_), channel_id=1, source_target_pairs={{0,1},{1,0},{2,3},{3,2},{4,5},{5,4},{6,7},{7,6},{8,9},{9,8},{10,11... | collective-permute-start | bytes 884744 | tf_op jit(solution)/shard_map/ppermute | solution.py:27
  156.3 14.3 %copy-start.19 = (s16[128,2176]{1,0:T(8,128)(2,1)S(1)}, s16[128,2176]{1,0:T(8,128)(2,1)}, u32[]{:S(2)}) copy-start(s16[128,2176]{1,0:T(8,128)(2,1)} %copy-done.18) | copy-start | bytes 1671172
  158.7 16.7 %collective-permute-start.19 = (s16[64,2176]{1,0:T(8,128)(2,1)S(1)}, s16[64,2176]{1,0:T(8,128)(2,1)S(1)}, u32[]{:S(2)}, u32[]{:S(2)}) collective-permute-start(s16[64,2176]{1,0:T(8,128)(2,1)S(1)} %shard_map.109.refs_2_), channel_id=1, source_target_pairs={{0,2},{1,3},{2,0},{3,1},{4,6},{5,7},{6,4},{7,5},{8,10},{9,11},{10,... | collective-permute-start | bytes 835592 | tf_op jit(solution)/shard_map/ppermute | solution.py:27
  163.6 14.2 %collective-permute-start.21 = (s16[64,1152]{1,0:T(8,128)(2,1)S(1)}, s16[64,1152]{1,0:T(8,128)(2,1)S(1)}, u32[]{:S(2)}, u32[]{:S(2)}) collective-permute-start(s16[64,1152]{1,0:T(8,128)(2,1)S(1)} %shard_map.111.refs_2_), channel_id=1, source_target_pairs={{0,1},{1,0},{2,3},{3,2},{4,5},{5,4},{6,7},{7,6},{8,9},{9,8},{10,11... | collective-permute-start | bytes 442376 | tf_op jit(solution)/shard_map/ppermute | solution.py:27
  170.1 22.3 %copy-start.32 = (s32[64,2]{0,1:T(2,128)S(1)}, s32[64,2]{0,1:T(2,128)}, u32[]{:S(2)}) copy-start(s32[64,2]{0,1:T(2,128)} %param.15) | copy-start | bytes 1540
  170.5 9.5 %collective-permute-start.22 = (s16[64,1152]{1,0:T(8,128)(2,1)S(1)}, s16[64,1152]{1,0:T(8,128)(2,1)S(1)}, u32[]{:S(2)}, u32[]{:S(2)}) collective-permute-start(s16[64,1152]{1,0:T(8,128)(2,1)S(1)} %shard_map.113.refs_2_), channel_id=1, source_target_pairs={{0,2},{1,3},{2,0},{3,1},{4,6},{5,7},{6,4},{7,5},{8,10},{9,11},{10,... | collective-permute-start | bytes 442376 | tf_op jit(solution)/shard_map/ppermute | solution.py:27
  171.8 20.7 %copy-start.27 = (f32[64,2048]{1,0:T(8,128)S(1)}, f32[64,2048]{1,0:T(8,128)}, u32[]{:S(2)}) copy-start(f32[64,2048]{1,0:T(8,128)} %copy-done.26) | copy-start | bytes 1572868
  171.8 25.0 %copy-start.1 = (f32[2,4096]{1,0:T(2,128)S(1)}, f32[2,4096]{1,0:T(2,128)}, u32[]{:S(2)}) copy-start(f32[2,4096]{1,0:T(2,128)} %param.12) | copy-start | bytes 98308
  181.2 1.3 collective-permute-start.23
  182.7 4.0 %collective-permute-start.24 = (f32[64,128]{1,0:T(8,128)S(1)}, f32[64,128]{1,0:T(8,128)S(1)}, u32[]{:S(2)}, u32[]{:S(2)}) collective-permute-start(f32[64,128]{1,0:T(8,128)S(1)} %add_select_fusion.2), channel_id=1, source_target_pairs={{0,8},{4,12},{8,0},{12,4},{16,24},{20,28},{24,16},{28,20},{1,9},{5... | collective-permute-start | bytes 98312 | tf_op jit(solution)/shard_map/ppermute | solution.py:27
  187.0 5.2 %collective-permute-start.25 = (f32[64,128]{1,0:T(8,128)S(1)}, f32[64,128]{1,0:T(8,128)S(1)}, u32[]{:S(2)}, u32[]{:S(2)}) collective-permute-start(f32[64,128]{1,0:T(8,128)S(1)} %add_select_fusion.1), channel_id=1, source_target_pairs={{0,16},{4,20},{8,24},{12,28},{16,0},{20,4},{24,8},{28,12},{1,17},{... | collective-permute-start | bytes 98312 | tf_op jit(solution)/shard_map/ppermute | solution.py:27
  (29 other events, 123.7 us)

commit v4 on v3

--- a/solution.py
+++ b/solution.py
@@ -53,29 +53,47 @@
 WAYS = 4
 
 
-def copies_in(source, target, sems, first):
-    depth, width = target.shape
-    share = depth // WAYS
-    return [
-        pltpu.make_async_copy(
-            source.at[pl.ds(way * share, share), pl.ds(first, width)],
-            target.at[pl.ds(way * share, share), :],
-            sems.at[way],
-        )
-        for way in range(WAYS)
-    ]
+def copy_groups(source, targets, sems, firsts):
+    groups = []
+    for index, target in enumerate(targets):
+        depth, width = target.shape
+        share, tile = depth // WAYS, widest(512, width)
+        for step in range(width // tile):
+            groups.append(
+                [
+                    pltpu.make_async_copy(
+                        source.at[pl.ds(way * share, share), pl.ds(firsts[index] + step * tile, tile)],
+                        target.at[pl.ds(way * share, share), pl.ds(step * tile, tile)],
+                        sems.at[index, step, way],
+                    )
+                    for way in range(WAYS)
+                ]
+            )
+    return groups
+
+
+def group_sems(count, width):
+    return pltpu.SemaphoreType.DMA((max(1, count), width // widest(512, width), WAYS))
+
+
+def start_group(group):
+    for copy in group:
+        copy.start()
+
+
+def wait_groups(groups):
+    for group in groups:
+        for copy in group:
+            copy.wait()
 
 
 def fetch_body(info, weight, *refs, firsts):
     targets, sems = refs[-1 - len(firsts) : -1], refs[-1]
     source = weight.at[info[0]] if len(weight.shape) == 3 else weight
-    copies = []
-    for index, target in enumerate(targets):
-        copies += copies_in(source, target, sems.at[index], firsts[index])
-    for copy in copies:
-        copy.start()
-    for copy in copies:
-        copy.wait()
+    groups = copy_groups(source, targets, sems, firsts)
+    for group in groups:
+        start_group(group)
+    wait_groups(groups)
 
 
 def fetch(info, weight, firsts, width, after, limit=VMEM_LIMIT):
@@ -85,7 +103,7 @@
         in_specs=[pl.BlockSpec(memory_space=pltpu.SMEM), ANY] + [ANY] * len(after),
         out_specs=[VMEM] * len(firsts),
         out_shape=[jax.ShapeDtypeStruct((depth, width), weight.dtype)] * len(firsts),
-        scratch_shapes=[pltpu.SemaphoreType.DMA((len(firsts), WAYS))],
+        scratch_shapes=[group_sems(len(firsts), width)],
         compiler_params=pltpu.CompilerParams(vmem_limit_bytes=limit),
         cost_estimate=pl.CostEstimate(
             flops=700 * depth * width * len(firsts), bytes_accessed=0, transcendentals=0
@@ -96,11 +114,8 @@
 def head_body(info, came, source, *refs, height, held, firsts):
     weights, refs = refs[:held], refs[held:]
     out, targets, (rows, sems) = refs[0], refs[1:-2], refs[-2:]
-    copies = []
-    for index, target in enumerate(targets):
-        copies += copies_in(source.at[info[0]], target, sems.at[index], firsts[index])
-    for copy in copies:
-        copy.start()
+    groups = copy_groups(source.at[info[0]], targets, sems, firsts)
+    waiting = list(groups)
     for unit in range(came.shape[0] // height):
         start = pl.multiple_of(info[1 + unit] * height, height)
         rows[pl.ds(start, height), :] = came[unit * height : (unit + 1) * height, :]
@@ -109,13 +124,14 @@
         width = weight.shape[1]
         tile = widest(512, width)
         for n in range(width // tile):
+            if waiting:
+                start_group(waiting.pop(0))
             total = jnp.dot(
                 rows[...], weight[:, n * tile : (n + 1) * tile], preferred_element_type=jnp.float32
             )
             out[:, at : at + tile] = total.astype(out.dtype)
             at += tile
-    for copy in copies:
-        copy.wait()
+    wait_groups(groups)
 
 
 def head_matmul(info, came, head_weight, weights, height, out_type, firsts):
@@ -130,7 +146,7 @@
         + [jax.ShapeDtypeStruct((depth, wide), head_weight.dtype)] * len(firsts),
         scratch_shapes=[
             pltpu.VMEM((count, depth), jnp.bfloat16),
-            pltpu.SemaphoreType.DMA((max(1, len(firsts)), WAYS)),
+            group_sems(len(firsts), wide),
         ],
         compiler_params=pltpu.CompilerParams(vmem_limit_bytes=VMEM_LIMIT),
         cost_estimate=pl.CostEstimate(
@@ -184,18 +200,16 @@
     weights, refs = refs[:held], refs[held + waits :]
     keep, send = refs[:2]
     targets, sems = refs[2:-1], refs[-1]
-    copies = []
-    for index, target in enumerate(targets):
-        copies += copies_in(source, target, sems.at[index], firsts[index])
-    for copy in copies:
-        copy.start()
-    groups = len(order)
-    height = rows.shape[0] // groups
-    half = groups // 2
+    groups = copy_groups(source, targets, sems, firsts)
+    waiting = list(groups)
+    height = rows.shape[0] // len(order)
+    half = len(order) // 2
     powers = []
     at = 0
     for weight in weights:
         for n in range(weight.shape[1] // tile):
+            if waiting:
+                start_group(waiting.pop(0))
             total = jnp.dot(
                 rows[...], weight[:, n * tile : (n + 1) * tile], preferred_element_type=jnp.float32
             )
@@ -207,8 +221,7 @@
             powers.append(power)
             at += tile
     send[:, at:] = marks_of(powers, send.shape[0])
-    for copy in copies:
-        copy.wait()
+    wait_groups(groups)
 
 
 def vocab_matmul(rows, vocab_weight, weights, order, tile, coming, after):
@@ -231,7 +244,7 @@
             jax.ShapeDtypeStruct((half, width + LANES), jnp.int16),
         ]
         + [jax.ShapeDtypeStruct((depth, wide), vocab_weight.dtype) for _, wide in coming],
-        scratch_shapes=[pltpu.SemaphoreType.DMA((max(1, len(coming)), WAYS))],
+        scratch_shapes=[group_sems(len(coming), coming[0][1] if coming else width)],
         compiler_params=pltpu.CompilerParams(vmem_limit_bytes=VMEM_LIMIT),
         cost_estimate=pl.CostEstimate(
             flops=2 * count * depth * width, bytes_accessed=2 * depth * width, transcendentals=0
@@ -288,8 +301,17 @@
     )(keep, came)
 
 
-def finish_body(wanted, keep, *refs, tile, choices, first, arrived):
-    arrivals, (logits, stats) = refs[:arrived], refs[-2:]
+def merge_rows(one, two):
+    peak = jnp.maximum(one[:, :1], two[:, :1])
+    lane = lax.broadcasted_iota(jnp.int32, one.shape, 1)
+    factor_one = jnp.where(lane == 1, jnp.exp(one[:, :1] - peak), 1.0)
+    factor_two = jnp.where(lane == 1, jnp.exp(two[:, :1] - peak), 1.0)
+    return jnp.where(lane == 0, peak, one * factor_one + two * factor_two)
+
+
+def finish_body(wanted, keep, *refs, tile, choices, first, arrived, earlier):
+    arrivals, (total_logits, stats, logits, sem) = refs[:arrived], refs[-4:]
+    before = refs[arrived] if earlier else None
     rows, width = logits.shape
     height = 16
     lane = lax.broadcasted_iota(jnp.int32, (height, LANES), 1)
@@ -321,29 +343,59 @@
         out = jnp.where(lane == 0, peak, jnp.zeros((height, LANES), jnp.float32))
         for k, item in enumerate([total] + picks):
             out = jnp.where(lane == k + 1, jnp.sum(item, axis=1, keepdims=True), out)
-        stats[here, :] = out
-
-
-def finish(wanted, keep, arrivals, tile, choices, first, after):
+        stats[here, :] = out if before is None else merge_rows(before[here, :], out)
+    copy = pltpu.make_async_copy(logits, total_logits.at[:, pl.ds(first, width)], sem)
+    copy.start()
+    copy.wait()
+
+
+def finish(wanted, keep, arrivals, tile, choices, first, vocab_width, earlier, after):
     rows, width = wanted.shape[0], keep.shape[1]
+    operands = [wanted, keep, *arrivals] + ([earlier[1]] if earlier else [])
+    buffer = [earlier[0]] if earlier else []
     return pl.pallas_call(
         functools.partial(
-            finish_body, tile=tile, choices=choices, first=first, arrived=len(arrivals)
+            finish_body,
+            tile=tile,
+            choices=choices,
+            first=first,
+            arrived=len(arrivals),
+            earlier=bool(earlier),
         ),
-        in_specs=[VMEM] * (2 + len(arrivals)) + [ANY] * len(after),
-        out_specs=[VMEM] * 2,
+        in_specs=[VMEM] * len(operands) + [ANY] * len(buffer + after),
+        out_specs=[ANY, VMEM],
         out_shape=[
-            jax.ShapeDtypeStruct((rows, width), jnp.float32),
+            jax.ShapeDtypeStruct((rows, vocab_width), jnp.float32),
             jax.ShapeDtypeStruct((rows, LANES), jnp.float32),
         ],
-        compiler_params=pltpu.CompilerParams(vmem_limit_bytes=VMEM_LIMIT),
-    )(wanted, keep, *arrivals, *after)
-
-
-def tail_body(stats, tree, *refs, heads, height, choices):
-    logits, (log_probs, scores) = refs[:-2], refs[-2:]
+        scratch_shapes=[pltpu.VMEM((rows, width), jnp.float32), pltpu.SemaphoreType.DMA],
+        input_output_aliases={len(operands): 0} if earlier else {},
+        compiler_params=pltpu.CompilerParams(vmem_limit_bytes=VMEM_LIMIT),
+    )(*operands, *buffer, *after)
+
+
+def merge_body(low, own, came, out):
+    first = jnp.where(low[0] == 1, own[...], came[...])
+    second = jnp.where(low[0] == 1, came[...], own[...])
+    out[...] = merge_rows(first, second)
+
+
+def merge(low, own, came):
+    return pl.pallas_call(
+        merge_body,
+        in_specs=[pl.BlockSpec(memory_space=pltpu.SMEM), VMEM, VMEM],
+        out_specs=VMEM,
+        out_shape=jax.ShapeDtypeStruct(own.shape, own.dtype),
+        compiler_params=pltpu.CompilerParams(vmem_limit_bytes=VMEM_LIMIT),
+    )(low, own, came)
+
+
+def tail_body(low, own, came, tree, logits, log_probs, scores, stats, *, heads, height, choices):
+    merge_body(low, own, came, stats)
     blocks = log_probs.shape[0] // height
     paths = scores.shape[1]
+    width = logits.shape[1]
+    tile = widest(1024, width)
     for block in range(blocks):
         there = slice(block * height, (block + 1) * height)
         score = jnp.zeros((height, paths), jnp.float32)
@@ -351,11 +403,8 @@
             row = (block * heads + head) * height
             here = slice(row, row + height)
             normalizer = stats[here, 0:1] + jnp.log(stats[here, 1:2])
-            first = 0
-            for part in logits:
-                width = part.shape[1]
-                log_probs[there, head, first : first + width] = part[here, :] - normalizer
-                first += width
+            for at in range(0, width, tile):
+                log_probs[there, head, at : at + tile] = logits[here, at : at + tile] - normalizer
             found = jnp.zeros((height, paths), jnp.float32)
             for k in range(choices):
                 picked = stats[here, 2 + k : 3 + k] - normalizer
@@ -364,27 +413,19 @@
         scores[there, :] = score
 
 
-def tail(stats, tree, logits, out_rows, height, choices):
+def tail(low, own, came, tree, logits, out_rows, height, choices):
     heads, paths = tree.shape
-    width = sum(part.shape[1] for part in logits)
     return pl.pallas_call(
         functools.partial(tail_body, heads=heads, height=height, choices=choices),
-        in_specs=[VMEM] * (2 + len(logits)),
+        in_specs=[pl.BlockSpec(memory_space=pltpu.SMEM)] + [VMEM] * 4,
         out_specs=[VMEM] * 2,
         out_shape=[
-            jax.ShapeDtypeStruct((out_rows, heads, width), jnp.float32),
+            jax.ShapeDtypeStruct((out_rows, heads, logits.shape[1]), jnp.float32),
             jax.ShapeDtypeStruct((out_rows, paths), jnp.float32),
         ],
-        compiler_params=pltpu.CompilerParams(vmem_limit_bytes=VMEM_LIMIT),
-    )(stats, tree, *logits)
-
-
-def merge(one, two):
-    peak = jnp.maximum(one[:, :1], two[:, :1])
-    lane = lax.broadcasted_iota(jnp.int32, one.shape, 1)
-    factor_one = jnp.where(lane == 1, jnp.exp(one[:, :1] - peak), 1.0)
-    factor_two = jnp.where(lane == 1, jnp.exp(two[:, :1] - peak), 1.0)
-    return jnp.where(lane == 0, peak, one * factor_one + two * factor_two)
+        scratch_shapes=[pltpu.VMEM(own.shape, own.dtype)],
+        compiler_params=pltpu.CompilerParams(vmem_limit_bytes=VMEM_LIMIT),
+    )(low, own, came, tree, logits)
 
 
 def shards(
@@ -402,9 +443,9 @@
     pair, core = b // 2, b % 2
     pair_bits = [bits_of(batch // 2), bits_of(batch // 2)[::-1]]
 
-    chosen = hidden_states[:, 0, :]
-    for position in range(1, positions):
-        chosen = jnp.where((accepted == position + 1)[:, None], hidden_states[:, position, :], chosen)
+    taken = lax.broadcasted_iota(jnp.int32, (rows, positions, 1), 1) == (accepted - 1)[:, None, None]
+    chosen = jnp.sum(jnp.where(taken, hidden_states, 0).astype(jnp.float32), axis=1)
+    chosen = chosen.astype(jnp.bfloat16)
     other = swap(chosen, "batch", lambda i: i ^ 1)
     chosen = jnp.concatenate(
         [jnp.where(core == 0, chosen, other), jnp.where(core == 0, other, chosen)], axis=0
@@ -464,33 +505,21 @@
     came = came.reshape(units, 2 * rows, feat)
     came = jnp.concatenate([came[u] for u in turned], axis=0)
     total = keep + came.astype(jnp.float32)
-    unit_width = vocab_width // 16
-    held = {}
-
-    def fetch_units(units, after):
-        firsts = [unit * unit_width for unit in units]
-        held.update(zip(units, fetch(head_then, vocab_weight, firsts, unit_width, after)))
-
-    def wait_for(came, units):
-        came, *fetched = together(came, *[held[unit] for unit in units])
-        held.update(zip(units, fetched))
-        return came
+    unit_width = vocab_width // 8
 
     for step in range(len(pair_bits[0])):
         half = total.shape[0] // 2
         outbound = total[half:].astype(jnp.bfloat16)
-        units = (range(0, 4), range(4, 6))[step] if step < 2 else ()
-        if units:
-            fetch_units(units, [outbound])
         came = swap(outbound, "batch", lambda i: i ^ (2 * pair_bits[i % 2][step]))
-        if units:
-            came = wait_for(came, units)
         total = total[:half] + came.astype(jnp.float32)
     bias = lax.dynamic_slice_in_dim(head_bias, core, 1, 0)
     before = total * row_scale + bias
     residual = (own_normed + jax.nn.silu(before)).astype(jnp.bfloat16)
+    (ahead,) = fetch(head_then, vocab_weight, [0], 2 * unit_width, [residual])
     for step in reversed(range(len(pair_bits[0]))):
         came = swap(residual, "batch", lambda i: i ^ (2 * pair_bits[i % 2][step]))
+        if step == len(pair_bits[0]) - 1:
+            came, ahead = together(came, ahead)
         if step:
             residual = jnp.concatenate([residual, came], axis=0)
     own = [residual, came]
@@ -509,13 +538,8 @@
     wanted = wanted.transpose(0, 2, 1, 3).reshape(out_rows * heads, choices)
     wanted = jnp.pad(wanted, ((0, 0), (0, LANES - choices)), constant_values=-1)
 
-    plan = [
-        (range(0, 4), range(6, 8)),
-        (range(4, 8), range(8, 12)),
-        (range(8, 12), range(12, 16)),
-        (range(12, 14), ()),
-        (range(14, 16), ()),
-    ]
+    held = {(0, 1): ahead}
+    plan = [((0, 1), (2, 3)), ((2, 3), (4, 5)), ((4, 5), (6, 7)), ((6,), ()), ((7,), ())]
     tile = widest(512, unit_width)
     blocks = len(plan)
     stages = [mp_bits if block % 2 == 0 else mp_bits[::-1] for block in range(blocks)]
@@ -527,7 +551,7 @@
         keep, send, *fetched = vocab_matmul(
             all_rows,
             vocab_weight,
-            [held[u] for u in units],
+            [held[units]] if units in held else [held[u] for u in units],
             order,
             tile,
             [(u * unit_width, unit_width) for u in coming],
@@ -557,20 +581,30 @@
     last = go_on(1, [sends[3]])
     begin(4, [last])
     lasts = [go_on(block, [sends[4]]) for block in (2, 3, 4)]
-    logits, stats = [], None
+    joined = None
     for block, (units, _) in enumerate(plan):
-        after = lasts[block : block + 1]
-        part, part_stats = finish(
-            wanted, keeps[block], arrivals[block], tile, choices, units[0] * unit_width, after
+        first = units[0] * unit_width
+        joined = finish(
+            wanted,
+            keeps[block],
+            arrivals[block],
+            tile,
+            choices,
+            first,
+            vocab_width,
+            joined,
+            lasts[block : block + 1],
         )
-        logits.append(part)
-        stats = part_stats if stats is None else merge(stats, part_stats)
+    logits, stats = joined
 
     for bit in bits_of(batch):
         came = swap(stats, "batch", lambda i: i ^ bit)
-        low = (b & bit) == 0
-        stats = merge(jnp.where(low, stats, came), jnp.where(low, came, stats))
-    log_probs, path_scores = tail(stats, tree_paths.T, logits, out_rows, rows, choices)
+        low = (1 - (b & bit) // bit).astype(jnp.int32).reshape(1)
+        if 2 * bit < batch:
+            stats = merge(low, stats, came)
+    log_probs, path_scores = tail(
+        low, stats, came, tree_paths.T, logits, out_rows, rows, choices
+    )
     return (log_probs, path_scores)
 
 

time: 197 us -> 196 us (level)
  local copies, waits for them, and re-layouts: 27.5 us -> 23 us
    pallas_call x4 -> x3, Pallas kernels: 19.1 us -> 15.8 us  [fetch(): pl.pallas_call(functools.partial(fetch_body, firsts=firsts), in_specs=[pl...]
    slice x1 -> x0, local copies, waits for them, and re-layouts: 2.96 us -> none  [shards(): hidden_states[:, position, :]]
    pallas_call x5, Pallas kernels: 8.95 us -> 11.2 us  [finish(): pl.pallas_call(functools.partial(finish_body, tile=tile, choices=choices,...]
    ppermute x25, waiting for transfers between devices: 52.7 us -> 54.6 us  [swap(): lax.ppermute(array, axis, [(i, partner(i)) for i in range(lax.axis_size(a...]
    unnamed x70 -> x50, local copies, waits for them, and re-layouts: 23.2 us -> 21.7 us
  transfers between devices with their start and end apart: 26 -> 26, of which waited for: 13 -> 12; matrix products, arithmetic and copies ran while one was open for 1% -> 1% of each run, Pallas kernels for 35% -> 31%
where the time goes in v4:
time: 196 us
  Pallas kernels  82.7 us (42%)
  waiting for transfers between devices  54.6 us (28%)
  starting transfers between devices  30.8 us (16%)
  local copies, waits for them, and re-layouts  23 us (12%)
  other arithmetic  3.27 us (2%)
    ppermute x25, waiting for transfers between devices, swap(): lax.ppermute(array, axis, [(i, partner(i)) for i in range(lax.axis_size(a...  54.6 us
    pallas_call x5, Pallas kernels, vocab_matmul(): pl.pallas_call(functools.partial(vocab_body, order=order, tile=tile, coun...  37.1 us
    ppermute x25, starting transfers between devices, swap(): lax.ppermute(array, axis, [(i, partner(i)) for i in range(lax.axis_size(a...  30.2 us
    unnamed x50, local copies, waits for them, and re-layouts  21.7 us
    pallas_call x3, Pallas kernels, fetch(): pl.pallas_call(functools.partial(fetch_body, firsts=firsts), in_specs=[pl...  15.8 us
    pallas_call x5, Pallas kernels, finish(): pl.pallas_call(functools.partial(finish_body, tile=tile, choices=choices,...  11.2 us
    pallas_call x2, Pallas kernels, head_matmul(): pl.pallas_call(functools.partial(head_body, height=height, held=len(weigh...  9.38 us
    pallas_call x5, Pallas kernels, fold(): pl.pallas_call(functools.partial(fold_body, tile=tile), in_specs=[VMEM] *...  6.31 us
  transfers between devices with their start and end apart: 26, of which 12 were waited for; matrix products, arithmetic and copies ran while one was open for 1% of the time, Pallas kernels for 31%

profile of v4, /device:TPU:0, one launch (start us, length us, event | category | flops | bytes accessed | tf_op | source)
XLA Modules:
  0.0 195.8 jit_solution(10769035081715896051)
XLA Ops:
  5.3 6.2 %shard_map.95 = (bf16[2048,1024]{1,0:T(8,128)(2,1)S(1)}, bf16[2048,1024]{1,0:T(8,128)(2,1)S(1)}, bf16[2048,1024]{1,0:T(8,128)(2,1)S(1)}, bf16[2048,1024]{1,0:T(8,128)(2,1)S(1)}) custom-call(s32[1]{0:T(128)} %bitcast.32.info, bf16[2,2048,4096]{2,1,0:T(8,128)(2,1)} %source.8, bf16[32,2048]{1,0:T(8,128)(2,1)S(1)} %multiply_convert_fusion.1.refs_0_), custom_call_target="tpu_custom_call" | custom-call | flops 5872025600 | tf_op jit(solution)/shard_map/pallas_call | solution.py:101
  11.5 9.9 %collective-permute-start.4 = (bf16[32,2048]{1,0:T(8,128)(2,1)S(1)}, bf16[32,2048]{1,0:T(8,128)(2,1)S(1)}, u32[]{:S(2)}, u32[]{:S(2)}) collective-permute-start(bf16[32,2048]{1,0:T(8,128)(2,1)S(1)} %collective-permute-done.3.refs_0_), channel_id=1, source_target_pairs={{0,1},{1,0},{2,3},{3,2},{4,5},{5,4},{6,7},{7,6},{8,9},{9,8},{10,11... | collective-permute-start | bytes 393224 | tf_op jit(solution)/shard_map/ppermute | solution.py:27
  21.4 3.6 %shard_map.96 = (bf16[2048,1024]{1,0:T(8,128)(2,1)S(1)}, bf16[2048,1024]{1,0:T(8,128)(2,1)S(1)}) custom-call(s32[1]{0:T(128)} %bitcast.23.info, bf16[2,2048,4096]{2,1,0:T(8,128)(2,1)} %source.8, bf16[32,2048]{1,0:T(8,128)(2,1)S(1)} %collective-permute-done.3.refs_0_), custom_call_target="tpu_custom_call" | custom-call | flops 2936012800 | tf_op jit(solution)/shard_map/pallas_call | solution.py:101
  25.2 7.2 %collective-permute-done.5 = bf16[64,2048]{1,0:T(8,128)(2,1)S(1)} collective-permute-done((bf16[64,2048]{1,0:T(8,128)(2,1)S(1)}, bf16[64,2048]{1,0:T(8,128)(2,1)S(1)}, u32[]{:S(2)}, u32[]{:S(2)}) %collective-permute-start.5) | collective-permute-done | bytes 262176 | tf_op jit(solution)/shard_map/ppermute | solution.py:27
  32.3 6.4 %shard_map.97 = (bf16[128,4096]{1,0:T(8,128)(2,1)S(1)}, bf16[2048,1024]{1,0:T(8,128)(2,1)S(1)}, bf16[2048,1024]{1,0:T(8,128)(2,1)S(1)}) custom-call(s32[9]{0:T(128)S(1)} %stack.107.info, bf16[128,2048]{1,0:T(8,128)(2,1)S(1)} %constant_dynamic-update-slice_fusion.came, bf16[2,2048,4096]{2,1,0:T(8,128)(2,1)} %source.8, ...), custom_call_target="tpu_custom_call" | custom-call | flops 2147483648 | bytes 524288 | tf_op jit(solution)/shard_map/pallas_call | solution.py:141
  38.8 3.0 %shard_map.98 = f32[128,4096]{1,0:T(8,128)S(1)} custom-call(s32[9]{0:T(128)S(1)} %stack.107.info, bf16[128,2048]{1,0:T(8,128)(2,1)S(1)} %constant_dynamic-update-slice_fusion.came, bf16[2,2048,4096]{2,1,0:T(8,128)(2,1)} %source.8, bf16[2048,1024]{1,0:T(8,128)(2,1)S(1)} %get-tuple-element.55.refs_0_, bf16[2048,1024]{1,0:T(8,128)(2,1)S(1)} %get-tuple-element.56.refs_1_, ...), custom_call_target="tpu_custom_call" | custom-call | flops 2147483648 | bytes 524288 | tf_op jit(solution)/shard_map/pallas_call | solution.py:141
  43.1 3.0 %collective-permute-done.1 = f32[32,1]{0,1:T(1,128)S(1)} collective-permute-done((f32[32,1]{0,1:T(1,128)S(1)}, f32[32,1]{0,1:T(1,128)S(1)}, u32[]{:S(2)}, u32[]{:S(2)}) %collective-permute-start.1) | collective-permute-done | bytes 160 | tf_op jit(solution)/shard_map/ppermute | solution.py:27
  46.5 10.6 %collective-permute-done.7 = bf16[64,4096]{1,0:T(8,128)(2,1)S(1)} collective-permute-done((bf16[64,4096]{1,0:T(8,128)(2,1)S(1)}, bf16[64,4096]{1,0:T(8,128)(2,1)S(1)}, u32[]{:S(2)}, u32[]{:S(2)}) %collective-permute-start.7) | collective-permute-done | bytes 524320 | tf_op jit(solution)/shard_map/ppermute | solution.py:27
  57.2 2.0 %collective-permute-start.8 = (bf16[32,4096]{1,0:T(8,128)(2,1)S(1)}, bf16[32,4096]{1,0:T(8,128)(2,1)S(1)}, u32[]{:S(2)}, u32[]{:S(2)}) collective-permute-start(bf16[32,4096]{1,0:T(8,128)(2,1)S(1)} %slice.57), channel_id=1, source_target_pairs={{0,16},{4,12},{8,24},{12,4},{16,0},{20,28},{24,8},{28,20},{1,17},{... | collective-permute-start | bytes 786440 | tf_op jit(solution)/shard_map/ppermute | solution.py:27
  59.3 8.1 %collective-permute-done.8 = bf16[32,4096]{1,0:T(8,128)(2,1)S(1)} collective-permute-done((bf16[32,4096]{1,0:T(8,128)(2,1)S(1)}, bf16[32,4096]{1,0:T(8,128)(2,1)S(1)}, u32[]{:S(2)}, u32[]{:S(2)}) %collective-permute-start.8) | collective-permute-done | bytes 262176 | tf_op jit(solution)/shard_map/ppermute | solution.py:27
  68.4 6.1 %shard_map.99.refs_0_ = bf16[4096,2048]{1,0:T(8,128)(2,1)S(1)} custom-call(s32[1]{0:T(128)} %bitcast.23.info, bf16[4096,8192]{1,0:T(8,128)(2,1)} %source.13, bf16[32,4096]{1,0:T(8,128)(2,1)S(1)} %add_convert_fusion.refs_0_), custom_call_target="tpu_custom_call" | custom-call | flops 5872025600 | tf_op jit(solution)/shard_map/pallas_call | solution.py:101
  74.5 5.8 %copy-done.2 = bf16[4096,2048]{1,0:T(8,128)(2,1)} copy-done((bf16[4096,2048]{1,0:T(8,128)(2,1)}, bf16[4096,2048]{1,0:T(8,128)(2,1)S(1)}, u32[]{:S(2)}) %copy-start.2) | copy-done | bytes 16777240
  80.3 3.3 %collective-permute-start.10 = (bf16[64,4096]{1,0:T(8,128)(2,1)S(1)}, bf16[64,4096]{1,0:T(8,128)(2,1)S(1)}, u32[]{:S(2)}, u32[]{:S(2)}) collective-permute-start(bf16[64,4096]{1,0:T(8,128)(2,1)S(1)} %pad_maximum_fusion.refs_0_), channel_id=1, source_target_pairs={{0,8},{4,20},{8,0},{12,28},{16,24},{20,4},{24,16},{28,12},{1,9},{5... | collective-permute-start | bytes 1572872 | tf_op jit(solution)/shard_map/ppermute | solution.py:27
  83.6 12.7 %collective-permute-done.10.refs_1_ = bf16[64,4096]{1,0:T(8,128)(2,1)S(1)} collective-permute-done((bf16[64,4096]{1,0:T(8,128)(2,1)S(1)}, bf16[64,4096]{1,0:T(8,128)(2,1)S(1)}, u32[]{:S(2)}, u32[]{:S(2)}) %collective-permute-start.10) | collective-permute-done | bytes 524320 | tf_op jit(solution)/shard_map/ppermute | solution.py:27
  98.9 5.8 %copy-done.3 = bf16[4096,2048]{1,0:T(8,128)(2,1)S(1)} copy-done((bf16[4096,2048]{1,0:T(8,128)(2,1)S(1)}, bf16[4096,2048]{1,0:T(8,128)(2,1)}, u32[]{:S(2)}) %copy-start.3) | copy-done | bytes 16777240
  104.7 10.4 %shard_map.101 = (f32[128,2048]{1,0:T(8,128)S(1)}, s16[128,2176]{1,0:T(8,128)(2,1)S(1)}, bf16[4096,1024]{1,0:T(8,128)(2,1)S(1)}, bf16[4096,1024]{1,0:T(8,128)(2,1)S(1)}) custom-call(bf16[256,4096]{1,0:T(8,128)(2,1)S(1)} %shard_map.100.rows, bf16[4096,8192]{1,0:T(8,128)(2,1)} %source.13, bf16[4096,2048]{1,0:T(8,128)(2,1)S(1)} %copy-done.3), custom_call_target="tpu_custom_call" | custom-call | flops 4294967296 | bytes 16777216 | tf_op jit(solution)/shard_map/pallas_call | solution.py:232
  115.1 3.3 %copy-done.4 = bf16[4096,1024]{1,0:T(8,128)(2,1)} copy-done((bf16[4096,1024]{1,0:T(8,128)(2,1)}, bf16[4096,1024]{1,0:T(8,128)(2,1)S(1)}, u32[]{:S(2)}) %copy-start.4) | copy-done | bytes 8388632
  118.9 3.4 %copy-done.5 = bf16[4096,1024]{1,0:T(8,128)(2,1)S(1)} copy-done((bf16[4096,1024]{1,0:T(8,128)(2,1)S(1)}, bf16[4096,1024]{1,0:T(8,128)(2,1)}, u32[]{:S(2)}) %copy-start.5) | copy-done | bytes 8388632
  122.2 10.6 %shard_map.102 = (f32[128,2048]{1,0:T(8,128)S(1)}, s16[128,2176]{1,0:T(8,128)(2,1)S(1)}, bf16[4096,1024]{1,0:T(8,128)(2,1)S(1)}, bf16[4096,1024]{1,0:T(8,128)(2,1)S(1)}) custom-call(bf16[256,4096]{1,0:T(8,128)(2,1)S(1)} %shard_map.100.rows, bf16[4096,8192]{1,0:T(8,128)(2,1)} %source.13, bf16[4096,1024]{1,0:T(8,128)(2,1)S(1)} %copy-done.5, ...), custom_call_target="tpu_custom_call" | custom-call | flops 4294967296 | bytes 16777216 | tf_op jit(solution)/shard_map/pallas_call | solution.py:232
  132.9 10.4 %shard_map.103 = (f32[128,2048]{1,0:T(8,128)S(1)}, s16[128,2176]{1,0:T(8,128)(2,1)S(1)}, bf16[4096,1024]{1,0:T(8,128)(2,1)S(1)}, bf16[4096,1024]{1,0:T(8,128)(2,1)S(1)}) custom-call(bf16[256,4096]{1,0:T(8,128)(2,1)S(1)} %shard_map.100.rows, bf16[4096,8192]{1,0:T(8,128)(2,1)} %source.13, bf16[4096,1024]{1,0:T(8,128)(2,1)S(1)} %get-tuple-element.69.refs_0_, ...), custom_call_target="tpu_custom_call" | custom-call | flops 4294967296 | bytes 16777216 | tf_op jit(solution)/shard_map/pallas_call | solution.py:232
  145.8 3.3 %shard_map.105 = (f32[128,1024]{1,0:T(8,128)S(1)}, s16[128,1152]{1,0:T(8,128)(2,1)}) custom-call(bf16[256,4096]{1,0:T(8,128)(2,1)S(1)} %shard_map.100.rows, bf16[4096,8192]{1,0:T(8,128)(2,1)} %source.13, bf16[4096,1024]{1,0:T(8,128)(2,1)S(1)} %get-tuple-element.74.refs_0_, s16[64,2176]{1,0:T(8,128)(2,1)S(1)} %shard_map.104.refs_1_), custom_call_target="tpu_custom_call" | custom-call | flops 2147483648 | bytes 8388608 | tf_op jit(solution)/shard_map/pallas_call | solution.py:232
  149.1 2.1 %collective-permute-start.17 = (s16[128,1152]{1,0:T(8,128)(2,1)}, s16[128,1152]{1,0:T(8,128)(2,1)S(1)}, u32[]{:S(2)}, u32[]{:S(2)}) collective-permute-start(s16[128,1152]{1,0:T(8,128)(2,1)} %get-tuple-element.77.refs_0_), channel_id=1, source_target_pairs={{0,2},{1,3},{2,0},{3,1},{4,6},{5,7},{6,4},{7,5},{8,10},{9,11},{10,... | collective-permute-start | bytes 884744 | tf_op jit(solution)/shard_map/ppermute | solution.py:27
  152.8 2.5 %shard_map.107 = (f32[128,1024]{1,0:T(8,128)S(1)}, s16[128,1152]{1,0:T(8,128)(2,1)S(1)}) custom-call(bf16[256,4096]{1,0:T(8,128)(2,1)S(1)} %shard_map.100.rows, bf16[4096,8192]{1,0:T(8,128)(2,1)} %source.13, bf16[4096,1024]{1,0:T(8,128)(2,1)S(1)} %get-tuple-element.72.refs_0_, s16[64,2176]{1,0:T(8,128)(2,1)} %shard_map.106.refs_1_), custom_call_target="tpu_custom_call" | custom-call | flops 2147483648 | bytes 8388608 | tf_op jit(solution)/shard_map/pallas_call | solution.py:232
  160.1 2.5 %collective-permute-start.20 = (s16[64,2176]{1,0:T(8,128)(2,1)}, s16[64,2176]{1,0:T(8,128)(2,1)}, u32[]{:S(2)}, u32[]{:S(2)}) collective-permute-start(s16[64,2176]{1,0:T(8,128)(2,1)} %shard_map.110.refs_2_), channel_id=1, source_target_pairs={{0,2},{1,3},{2,0},{3,1},{4,6},{5,7},{6,4},{7,5},{8,10},{9,11},{10,... | collective-permute-start | bytes 835592 | tf_op jit(solution)/shard_map/ppermute | solution.py:27
  169.7 2.3 %shard_map.111 = (f32[64,8192]{1,0:T(8,128)S(1)}, f32[64,128]{1,0:T(8,128)S(1)}) custom-call(s32[64,128]{1,0:T(8,128)S(1)} %pad.4.wanted, f32[128,2048]{1,0:T(8,128)S(1)} %get-tuple-element.75.keep, s16[128,2176]{1,0:T(8,128)(2,1)S(1)} %copy-done.11, s16[64,2176]{1,0:T(8,128)(2,1)} %collective-permute-done.22.refs_1_, s16[64,2176]{1,0:T(8,128)(2,1)} %shard_map.110.refs_2_), custom_call_target="tpu_custom_call" | custom-call | tf_op jit(solution)/shard_map/pallas_call | solution.py:356
  174.3 2.5 %shard_map.112 = (f32[64,8192]{1,0:T(8,128)S(1)}, f32[64,128]{1,0:T(8,128)S(1)}) custom-call(s32[64,128]{1,0:T(8,128)S(1)} %pad.4.wanted, f32[128,2048]{1,0:T(8,128)S(1)} %copy-done.9, s16[128,2176]{1,0:T(8,128)(2,1)S(1)} %copy-done.15, s16[64,2176]{1,0:T(8,128)(2,1)} %collective-permute-done.21.refs_1_, ...), custom_call_target="tpu_custom_call", output_to_operand_aliasing={{0}: (5, {})} | custom-call | tf_op jit(solution)/shard_map/pallas_call | solution.py:356
  176.9 2.4 %shard_map.113 = (f32[64,8192]{1,0:T(8,128)S(1)}, f32[64,128]{1,0:T(8,128)S(1)}) custom-call(s32[64,128]{1,0:T(8,128)S(1)} %pad.4.wanted, f32[128,2048]{1,0:T(8,128)S(1)} %copy-done.7, s16[128,2176]{1,0:T(8,128)(2,1)S(1)} %copy-done.13, s16[64,2176]{1,0:T(8,128)(2,1)} %collective-permute-done.20.refs_1_, ...), custom_call_target="tpu_custom_call", output_to_operand_aliasing={{0}: (5, {})} | custom-call | tf_op jit(solution)/shard_map/pallas_call | solution.py:356
  179.3 2.0 %shard_map.114 = (f32[64,8192]{1,0:T(8,128)S(1)}, f32[64,128]{1,0:T(8,128)S(1)}) custom-call(s32[64,128]{1,0:T(8,128)S(1)} %pad.4.wanted, f32[128,1024]{1,0:T(8,128)S(1)} %copy-done.17, s16[128,1152]{1,0:T(8,128)(2,1)S(1)} %collective-permute-done.17.came.refs_0_, s16[64,1152]{1,0:T(8,128)(2,1)} %collective-permute-done.18.refs_1_, ...), custom_call_target="tpu_custom_call", output_to_operand_aliasing={{0}: (5, {})} | custom-call | tf_op jit(solution)/shard_map/pallas_call | solution.py:356
  181.4 2.0 %shard_map.115 = (f32[64,8192]{1,0:T(8,128)S(1)}, f32[64,128]{1,0:T(8,128)S(1)}) custom-call(s32[64,128]{1,0:T(8,128)S(1)} %pad.4.wanted, f32[128,1024]{1,0:T(8,128)S(1)} %copy-done.19, s16[128,1152]{1,0:T(8,128)(2,1)S(1)} %copy-done.21, s16[64,1152]{1,0:T(8,128)(2,1)} %collective-permute-done.16.refs_1_, ...), custom_call_target="tpu_custom_call", output_to_operand_aliasing={{0}: (5, {})} | custom-call | tf_op jit(solution)/shard_map/pallas_call | solution.py:356
  184.9 3.9 %collective-permute-done.24.came = f32[64,128]{1,0:T(8,128)S(1)} collective-permute-done((f32[64,128]{1,0:T(8,128)S(1)}, f32[64,128]{1,0:T(8,128)S(1)}, u32[]{:S(2)}, u32[]{:S(2)}) %collective-permute-start.24) | collective-permute-done | bytes 32800 | tf_op jit(solution)/shard_map/ppermute | solution.py:27
  189.0 4.8 %collective-permute-done.25.came = f32[64,128]{1,0:T(8,128)S(1)} collective-permute-done((f32[64,128]{1,0:T(8,128)S(1)}, f32[64,128]{1,0:T(8,128)S(1)}, u32[]{:S(2)}, u32[]{:S(2)}) %collective-permute-start.25) | collective-permute-done | bytes 32800 | tf_op jit(solution)/shard_map/ppermute | solution.py:27
  193.8 2.0 %shard_map.118 = (f32[32,2,8192]{2,1,0:T(2,128)}, f32[32,64]{1,0:T(8,128)}) custom-call(s32[1]{0:T(128)} %bitcast.low, f32[64,128]{1,0:T(8,128)S(1)} %shard_map.117.own, f32[64,128]{1,0:T(8,128)S(1)} %collective-permute-done.25.came, s32[2,64]{1,0:T(2,128)S(1)} %bitcast.40, f32[64,8192]{1,0:T(8,128)S(1)} %get-tuple-element.91.logits), custom_call_target="tpu_custom_call" | custom-call | tf_op jit(solution)/shard_map/pallas_call | solution.py:418
  (122 shorter events, 30.7 us)
Async XLA Ops:
  0.6 58.6 %copy-start = (f32[2,4096]{1,0:T(2,128)S(1)}, f32[2,4096]{1,0:T(2,128)}, u32[]{:S(2)}) copy-start(f32[2,4096]{1,0:T(2,128)} %param.12) | copy-start | bytes 98308
  3.0 1.5 collective-permute-start
  4.6 6.9 %collective-permute-start.3 = (bf16[32,2048]{1,0:T(8,128)(2,1)S(1)}, bf16[32,2048]{1,0:T(8,128)(2,1)S(1)}, u32[]{:S(2)}, u32[]{:S(2)}) collective-permute-start(bf16[32,2048]{1,0:T(8,128)(2,1)S(1)} %multiply_convert_fusion.1.refs_0_), channel_id=1, source_target_pairs={{0,0},{1,9},{2,18},{3,27},{4,4},{5,13},{6,22},{7,31},{8,1},{9,8},{... | collective-permute-start | bytes 393224 | tf_op jit(solution)/shard_map/ppermute | solution.py:475
  11.5 13.5 %collective-permute-start.4 = (bf16[32,2048]{1,0:T(8,128)(2,1)S(1)}, bf16[32,2048]{1,0:T(8,128)(2,1)S(1)}, u32[]{:S(2)}, u32[]{:S(2)}) collective-permute-start(bf16[32,2048]{1,0:T(8,128)(2,1)S(1)} %collective-permute-done.3.refs_0_), channel_id=1, source_target_pairs={{0,1},{1,0},{2,3},{3,2},{4,5},{5,4},{6,7},{7,6},{8,9},{9,8},{10,11... | collective-permute-start | bytes 393224 | tf_op jit(solution)/shard_map/ppermute | solution.py:27
  25.0 7.3 %collective-permute-start.5 = (bf16[64,2048]{1,0:T(8,128)(2,1)S(1)}, bf16[64,2048]{1,0:T(8,128)(2,1)S(1)}, u32[]{:S(2)}, u32[]{:S(2)}) collective-permute-start(bf16[64,2048]{1,0:T(8,128)(2,1)S(1)} %pad_maximum_fusion.1), channel_id=1, source_target_pairs={{0,2},{1,3},{2,0},{3,1},{4,6},{5,7},{6,4},{7,5},{8,10},{9,11},{10,... | collective-permute-start | bytes 786440 | tf_op jit(solution)/shard_map/ppermute | solution.py:27
  38.7 3.1 %collective-permute-start.6 = (bf16[128,4096]{1,0:T(8,128)(2,1)S(1)}, bf16[128,4096]{1,0:T(8,128)(2,1)S(1)}, u32[]{:S(2)}, u32[]{:S(2)}) collective-permute-start(bf16[128,4096]{1,0:T(8,128)(2,1)S(1)} %get-tuple-element.63), channel_id=1, source_target_pairs={{0,4},{4,0},{8,12},{12,8},{16,20},{20,16},{24,28},{28,24},{1,5},{5... | collective-permute-start | bytes 3145736 | tf_op jit(solution)/shard_map/ppermute | solution.py:27
  42.1 25.3 %dynamic-slice-start = ((f32[16384]{0:T(1024)}, s32[]{:T(128)}), f32[4096]{0:T(1024)S(1)}, s32[]{:S(2)}) async-start(f32[16384]{0:T(1024)} %param.10, s32[]{:T(128)} %select_n.341), calls=%async_computation | async-start | bytes 33280 | tf_op jit(solution)/shard_map/dynamic_slice | solution.py:453
  42.2 14.9 %collective-permute-start.7 = (bf16[64,4096]{1,0:T(8,128)(2,1)S(1)}, bf16[64,4096]{1,0:T(8,128)(2,1)S(1)}, u32[]{:S(2)}, u32[]{:S(2)}) collective-permute-start(bf16[64,4096]{1,0:T(8,128)(2,1)S(1)} %slice.56), channel_id=1, source_target_pairs={{0,8},{4,20},{8,0},{12,28},{16,24},{20,4},{24,16},{28,12},{1,9},{5... | collective-permute-start | bytes 1572872 | tf_op jit(solution)/shard_map/ppermute | solution.py:27
  42.5 3.6 %collective-permute-start.1 = (f32[32,1]{0,1:T(1,128)S(1)}, f32[32,1]{0,1:T(1,128)S(1)}, u32[]{:S(2)}, u32[]{:S(2)}) collective-permute-start(f32[32,1]{0,1:T(1,128)S(1)} %bitcast.43), channel_id=1, source_target_pairs={{0,1},{1,0},{2,3},{3,2},{4,5},{5,4},{6,7},{7,6},{8,9},{9,8},{10,11... | collective-permute-start | bytes 392 | tf_op jit(solution)/shard_map/ppermute | solution.py:27
  46.1 13.2 %collective-permute-start.2 = (f32[32,1]{0,1:T(1,128)S(1)}, f32[32,1]{0,1:T(1,128)S(1)}, u32[]{:S(2)}, u32[]{:S(2)}) collective-permute-start(f32[32,1]{0,1:T(1,128)S(1)} %bitcast_add_fusion), channel_id=1, source_target_pairs={{0,2},{1,3},{2,0},{3,1},{4,6},{5,7},{6,4},{7,5},{8,10},{9,11},{10,... | collective-permute-start | bytes 392 | tf_op jit(solution)/shard_map/ppermute | solution.py:27
  57.2 10.2 %collective-permute-start.8 = (bf16[32,4096]{1,0:T(8,128)(2,1)S(1)}, bf16[32,4096]{1,0:T(8,128)(2,1)S(1)}, u32[]{:S(2)}, u32[]{:S(2)}) collective-permute-start(bf16[32,4096]{1,0:T(8,128)(2,1)S(1)} %slice.57), channel_id=1, source_target_pairs={{0,16},{4,12},{8,24},{12,4},{16,0},{20,28},{24,8},{28,20},{1,17},{... | collective-permute-start | bytes 786440 | tf_op jit(solution)/shard_map/ppermute | solution.py:27
  67.7 12.6 %collective-permute-start.9 = (bf16[32,4096]{1,0:T(8,128)(2,1)S(1)}, bf16[32,4096]{1,0:T(8,128)(2,1)S(1)}, u32[]{:S(2)}, u32[]{:S(2)}) collective-permute-start(bf16[32,4096]{1,0:T(8,128)(2,1)S(1)} %add_convert_fusion.refs_0_), channel_id=1, source_target_pairs={{0,16},{4,12},{8,24},{12,4},{16,0},{20,28},{24,8},{28,20},{1,17},{... | collective-permute-start | bytes 786440 | tf_op jit(solution)/shard_map/ppermute | solution.py:27
  80.3 16.0 %collective-permute-start.10 = (bf16[64,4096]{1,0:T(8,128)(2,1)S(1)}, bf16[64,4096]{1,0:T(8,128)(2,1)S(1)}, u32[]{:S(2)}, u32[]{:S(2)}) collective-permute-start(bf16[64,4096]{1,0:T(8,128)(2,1)S(1)} %pad_maximum_fusion.refs_0_), channel_id=1, source_target_pairs={{0,8},{4,20},{8,0},{12,28},{16,24},{20,4},{24,16},{28,12},{1,9},{5... | collective-permute-start | bytes 1572872 | tf_op jit(solution)/shard_map/ppermute | solution.py:27
  83.6 12.8 %collective-permute-start.11 = (bf16[64,4096]{1,0:T(8,128)(2,1)S(1)}, bf16[64,4096]{1,0:T(8,128)(2,1)S(1)}, u32[]{:S(2)}, u32[]{:S(2)}) collective-permute-start(bf16[64,4096]{1,0:T(8,128)(2,1)S(1)} %pad_maximum_fusion.refs_0_), channel_id=1, source_target_pairs={{0,4},{4,0},{8,12},{12,8},{16,20},{20,16},{24,28},{28,24},{1,5},{5... | collective-permute-start | bytes 1572872 | tf_op jit(solution)/shard_map/ppermute | solution.py:27
  96.3 1.9 collective-permute-start.12
  118.3 26.5 %collective-permute-start.14 = (s16[128,2176]{1,0:T(8,128)(2,1)S(1)}, s16[128,2176]{1,0:T(8,128)(2,1)S(1)}, u32[]{:S(2)}, u32[]{:S(2)}) collective-permute-start(s16[128,2176]{1,0:T(8,128)(2,1)S(1)} %get-tuple-element.68.refs_2_), channel_id=1, source_target_pairs={{0,1},{1,0},{2,3},{3,2},{4,5},{5,4},{6,7},{7,6},{8,9},{9,8},{10,11... | collective-permute-start | bytes 1671176 | tf_op jit(solution)/shard_map/ppermute | solution.py:27
  132.8 18.3 %copy-start.8 = (f32[128,2048]{1,0:T(8,128)}, f32[128,2048]{1,0:T(8,128)S(1)}, u32[]{:S(2)}) copy-start(f32[128,2048]{1,0:T(8,128)S(1)} %get-tuple-element.73.keep) | copy-start | bytes 3145732
  132.8 18.3 %collective-permute-start.13 = (s16[128,2176]{1,0:T(8,128)(2,1)S(1)}, s16[128,2176]{1,0:T(8,128)(2,1)S(1)}, u32[]{:S(2)}, u32[]{:S(2)}) collective-permute-start(s16[128,2176]{1,0:T(8,128)(2,1)S(1)} %get-tuple-element.71.refs_2_), channel_id=1, source_target_pairs={{0,2},{1,3},{2,0},{3,1},{4,6},{5,7},{6,4},{7,5},{8,10},{9,11},{10,... | collective-permute-start | bytes 1671176 | tf_op jit(solution)/shard_map/ppermute | solution.py:27
  143.3 15.2 %copy-start.6 = (f32[128,2048]{1,0:T(8,128)}, f32[128,2048]{1,0:T(8,128)S(1)}, u32[]{:S(2)}) copy-start(f32[128,2048]{1,0:T(8,128)S(1)} %get-tuple-element.81.keep) | copy-start | bytes 3145732
  143.3 15.2 %collective-permute-start.19 = (s16[128,2176]{1,0:T(8,128)(2,1)S(1)}, s16[128,2176]{1,0:T(8,128)(2,1)S(1)}, u32[]{:S(2)}, u32[]{:S(2)}) collective-permute-start(s16[128,2176]{1,0:T(8,128)(2,1)S(1)} %get-tuple-element.76.refs_0_), channel_id=1, source_target_pairs={{0,1},{1,0},{2,3},{3,2},{4,5},{5,4},{6,7},{7,6},{8,9},{9,8},{10,11... | collective-permute-start | bytes 1671176 | tf_op jit(solution)/shard_map/ppermute | solution.py:27
  149.1 13.5 %copy-start.16 = (f32[128,1024]{1,0:T(8,128)}, f32[128,1024]{1,0:T(8,128)S(1)}, u32[]{:S(2)}) copy-start(f32[128,1024]{1,0:T(8,128)S(1)} %get-tuple-element.80.keep) | copy-start | bytes 1572868
  149.1 13.5 %collective-permute-start.17 = (s16[128,1152]{1,0:T(8,128)(2,1)}, s16[128,1152]{1,0:T(8,128)(2,1)S(1)}, u32[]{:S(2)}, u32[]{:S(2)}) collective-permute-start(s16[128,1152]{1,0:T(8,128)(2,1)} %get-tuple-element.77.refs_0_), channel_id=1, source_target_pairs={{0,2},{1,3},{2,0},{3,1},{4,6},{5,7},{6,4},{7,5},{8,10},{9,11},{10,... | collective-permute-start | bytes 884744 | tf_op jit(solution)/shard_map/ppermute | solution.py:27
  155.3 10.0 %collective-permute-start.15 = (s16[128,1152]{1,0:T(8,128)(2,1)S(1)}, s16[128,1152]{1,0:T(8,128)(2,1)S(1)}, u32[]{:S(2)}, u32[]{:S(2)}) collective-permute-start(s16[128,1152]{1,0:T(8,128)(2,1)S(1)} %get-tuple-element.79.refs_0_), channel_id=1, source_target_pairs={{0,1},{1,0},{2,3},{3,2},{4,5},{5,4},{6,7},{7,6},{8,9},{9,8},{10,11... | collective-permute-start | bytes 884744 | tf_op jit(solution)/shard_map/ppermute | solution.py:27
  155.9 12.8 %collective-permute-start.22 = (s16[64,2176]{1,0:T(8,128)(2,1)S(1)}, s16[64,2176]{1,0:T(8,128)(2,1)}, u32[]{:S(2)}, u32[]{:S(2)}) collective-permute-start(s16[64,2176]{1,0:T(8,128)(2,1)S(1)} %shard_map.104.refs_1_), channel_id=1, source_target_pairs={{0,2},{1,3},{2,0},{3,1},{4,6},{5,7},{6,4},{7,5},{8,10},{9,11},{10,... | collective-permute-start | bytes 835592 | tf_op jit(solution)/shard_map/ppermute | solution.py:27
  155.9 16.1 %collective-permute-start.21 = (s16[64,2176]{1,0:T(8,128)(2,1)}, s16[64,2176]{1,0:T(8,128)(2,1)}, u32[]{:S(2)}, u32[]{:S(2)}) collective-permute-start(s16[64,2176]{1,0:T(8,128)(2,1)} %shard_map.106.refs_1_), channel_id=1, source_target_pairs={{0,1},{1,0},{2,3},{3,2},{4,5},{5,4},{6,7},{7,6},{8,9},{9,8},{10,11... | collective-permute-start | bytes 835592 | tf_op jit(solution)/shard_map/ppermute | solution.py:27
  160.1 16.7 %collective-permute-start.20 = (s16[64,2176]{1,0:T(8,128)(2,1)}, s16[64,2176]{1,0:T(8,128)(2,1)}, u32[]{:S(2)}, u32[]{:S(2)}) collective-permute-start(s16[64,2176]{1,0:T(8,128)(2,1)} %shard_map.110.refs_2_), channel_id=1, source_target_pairs={{0,2},{1,3},{2,0},{3,1},{4,6},{5,7},{6,4},{7,5},{8,10},{9,11},{10,... | collective-permute-start | bytes 835592 | tf_op jit(solution)/shard_map/ppermute | solution.py:27
  163.5 15.7 %collective-permute-start.18 = (s16[64,1152]{1,0:T(8,128)(2,1)}, s16[64,1152]{1,0:T(8,128)(2,1)}, u32[]{:S(2)}, u32[]{:S(2)}) collective-permute-start(s16[64,1152]{1,0:T(8,128)(2,1)} %shard_map.109.refs_4_), channel_id=1, source_target_pairs={{0,1},{1,0},{2,3},{3,2},{4,5},{5,4},{6,7},{7,6},{8,9},{9,8},{10,11... | collective-permute-start | bytes 442376 | tf_op jit(solution)/shard_map/ppermute | solution.py:27
  166.5 14.9 %collective-permute-start.16 = (s16[64,1152]{1,0:T(8,128)(2,1)}, s16[64,1152]{1,0:T(8,128)(2,1)}, u32[]{:S(2)}, u32[]{:S(2)}) collective-permute-start(s16[64,1152]{1,0:T(8,128)(2,1)} %shard_map.108.refs_4_), channel_id=1, source_target_pairs={{0,2},{1,3},{2,0},{3,1},{4,6},{5,7},{6,4},{7,5},{8,10},{9,11},{10,... | collective-permute-start | bytes 442376 | tf_op jit(solution)/shard_map/ppermute | solution.py:27
  181.4 14.4 %copy-start.1 = (f32[2,4096]{1,0:T(2,128)S(1)}, f32[2,4096]{1,0:T(2,128)}, u32[]{:S(2)}) copy-start(f32[2,4096]{1,0:T(2,128)} %param.12) | copy-start | bytes 98308
  183.4 1.3 collective-permute-start.23
  184.8 4.0 %collective-permute-start.24 = (f32[64,128]{1,0:T(8,128)S(1)}, f32[64,128]{1,0:T(8,128)S(1)}, u32[]{:S(2)}, u32[]{:S(2)}) collective-permute-start(f32[64,128]{1,0:T(8,128)S(1)} %shard_map.116.own), channel_id=1, source_target_pairs={{0,8},{4,12},{8,0},{12,4},{16,24},{20,28},{24,16},{28,20},{1,9},{5... | collective-permute-start | bytes 98312 | tf_op jit(solution)/shard_map/ppermute | solution.py:27
  188.9 4.9 %collective-permute-start.25 = (f32[64,128]{1,0:T(8,128)S(1)}, f32[64,128]{1,0:T(8,128)S(1)}, u32[]{:S(2)}, u32[]{:S(2)}) collective-permute-start(f32[64,128]{1,0:T(8,128)S(1)} %shard_map.117.own), channel_id=1, source_target_pairs={{0,16},{4,20},{8,24},{12,28},{16,0},{20,4},{24,8},{28,12},{1,17},{... | collective-permute-start | bytes 98312 | tf_op jit(solution)/shard_map/ppermute | solution.py:27
  (19 other events, 77.7 us)

commit v5 on v4

--- a/solution.py
+++ b/solution.py
@@ -13,6 +13,7 @@
 CODE_BITS = 14
 VMEM_LIMIT = 4 * MIB
 HEAD_LIMIT = 24 * MIB
+VOCAB_LIMIT = 20 * MIB
 
 
 def together(*arrays):
@@ -115,22 +116,28 @@
     weights, refs = refs[:held], refs[held:]
     out, targets, (rows, sems) = refs[0], refs[1:-2], refs[-2:]
     groups = copy_groups(source.at[info[0]], targets, sems, firsts)
-    waiting = list(groups)
     for unit in range(came.shape[0] // height):
         start = pl.multiple_of(info[1 + unit] * height, height)
         rows[pl.ds(start, height), :] = came[unit * height : (unit + 1) * height, :]
-    at = 0
+    waiting = list(groups)
+    first = 0
     for weight in weights:
         width = weight.shape[1]
         tile = widest(512, width)
-        for n in range(width // tile):
-            if waiting:
-                start_group(waiting.pop(0))
+        for group in waiting[: width // tile]:
+            start_group(group)
+        waiting = waiting[width // tile :]
+
+        def step(n, carry, weight=weight, tile=tile, first=first):
+            at = pl.multiple_of(n * tile, tile)
             total = jnp.dot(
-                rows[...], weight[:, n * tile : (n + 1) * tile], preferred_element_type=jnp.float32
+                rows[...], weight[:, pl.ds(at, tile)], preferred_element_type=jnp.float32
             )
-            out[:, at : at + tile] = total.astype(out.dtype)
-            at += tile
+            out[:, pl.ds(pl.multiple_of(first + at, tile), tile)] = total.astype(out.dtype)
+            return carry
+
+        lax.fori_loop(0, width // tile, step, 0)
+        first += width
     wait_groups(groups)
 
 
@@ -174,20 +181,25 @@
     return marks.astype(jnp.int32).astype(jnp.int16)
 
 
-def gather_body(spots, *refs, height):
+def gather_body(spots, *refs, height, halves):
     parts, rows = refs[:-1], refs[-1]
+    share = rows.shape[1] // halves
     unit = 0
     for part in parts:
         for block in range(part.shape[0] // height):
-            start = pl.multiple_of(spots[unit] * height, height)
-            rows[pl.ds(start, height), :] = part[block * height : (block + 1) * height, :]
-            unit += 1
-
-
-def gather_rows(spots, parts, height):
+            for half in range(halves):
+                start = pl.multiple_of(spots[unit] * height, height)
+                columns = slice(half * share, (half + 1) * share)
+                rows[pl.ds(start, height), columns] = part[
+                    block * height : (block + 1) * height, columns
+                ]
+                unit += 1
+
+
+def gather_rows(spots, parts, height, halves):
     count = sum(p.shape[0] for p in parts)
     return pl.pallas_call(
-        functools.partial(gather_body, height=height),
+        functools.partial(gather_body, height=height, halves=halves),
         in_specs=[pl.BlockSpec(memory_space=pltpu.SMEM)] + [VMEM] * len(parts),
         out_specs=VMEM,
         out_shape=jax.ShapeDtypeStruct((count, parts[0].shape[1]), parts[0].dtype),
@@ -195,61 +207,68 @@
     )(spots, *parts)
 
 
-def vocab_body(rows, source, *refs, order, tile, counts, firsts):
-    held, waits = counts
-    weights, refs = refs[:held], refs[held + waits :]
-    keep, send = refs[:2]
-    targets, sems = refs[2:-1], refs[-1]
-    groups = copy_groups(source, targets, sems, firsts)
-    waiting = list(groups)
+def vocab_body(rows, *refs, order, tile, waits):
+    weights, (keep, send, powers) = refs[:WAYS], refs[WAYS + waits :]
+    step = pl.program_id(0)
+    share = rows.shape[1] // WAYS
+    total = None
+    for way in range(WAYS):
+        term = jnp.dot(
+            rows[:, way * share : (way + 1) * share],
+            weights[way][...],
+            preferred_element_type=jnp.float32,
+        )
+        total = term if total is None else total + term
     height = rows.shape[0] // len(order)
     half = len(order) // 2
-    powers = []
-    at = 0
-    for weight in weights:
-        for n in range(weight.shape[1] // tile):
-            if waiting:
-                start_group(waiting.pop(0))
-            total = jnp.dot(
-                rows[...], weight[:, n * tile : (n + 1) * tile], preferred_element_type=jnp.float32
-            )
-            sorted_rows = [total[g * height : (g + 1) * height] for g in order]
-            for spot, value in enumerate(sorted_rows[:half]):
-                keep[spot * height : (spot + 1) * height, at : at + tile] = value
-            code, power = encode(jnp.concatenate(sorted_rows[half:], axis=0))
-            send[:, at : at + tile] = code
-            powers.append(power)
-            at += tile
-    send[:, at:] = marks_of(powers, send.shape[0])
-    wait_groups(groups)
-
-
-def vocab_matmul(rows, vocab_weight, weights, order, tile, coming, after):
+    sorted_rows = [total[g * height : (g + 1) * height] for g in order]
+    for spot, value in enumerate(sorted_rows[:half]):
+        keep[spot * height : (spot + 1) * height, :] = value
+    code, power = encode(jnp.concatenate(sorted_rows[half:], axis=0))
+    send[:, pl.ds(pl.multiple_of(step * tile, tile), tile)] = code
+    lane = lax.broadcasted_iota(jnp.int32, powers.shape, 1)
+
+    @pl.when(step == 0)
+    def _():
+        powers[...] = jnp.where(lane == 0, power, jnp.zeros_like(powers))
+
+    @pl.when(step > 0)
+    def _():
+        powers[...] = jnp.where(lane == step, power, powers[...])
+
+    @pl.when(step == pl.num_programs(0) - 1)
+    def _():
+        send[:, send.shape[1] - LANES :] = powers[...].astype(jnp.int32).astype(jnp.int16)
+
+
+def vocab_matmul(rows, vocab_weight, first, width, order, tile, after):
     depth = vocab_weight.shape[0]
     count = rows.shape[0]
     half = count // 2
-    width = sum(w.shape[1] for w in weights)
-    return pl.pallas_call(
-        functools.partial(
-            vocab_body,
-            order=order,
-            tile=tile,
-            counts=(len(weights), len(after)),
-            firsts=[first for first, _ in coming],
-        ),
-        in_specs=[VMEM, ANY] + [VMEM] * len(weights) + [ANY] * len(after),
-        out_specs=[VMEM] * (2 + len(coming)),
+    base = first // tile
+    share = depth // WAYS
+    weight_specs = [
+        pl.BlockSpec((share, tile), functools.partial(lambda way, n: (way, base + n), way))
+        for way in range(WAYS)
+    ]
+    return pl.pallas_call(
+        functools.partial(vocab_body, order=order, tile=tile, waits=len(after)),
+        grid=(width // tile,),
+        in_specs=[VMEM] + weight_specs + [ANY] * len(after),
+        out_specs=[
+            pl.BlockSpec((half, tile), lambda n: (0, n)),
+            pl.BlockSpec((half, width + LANES), lambda n: (0, 0)),
+        ],
         out_shape=[
             jax.ShapeDtypeStruct((half, width), jnp.float32),
             jax.ShapeDtypeStruct((half, width + LANES), jnp.int16),
-        ]
-        + [jax.ShapeDtypeStruct((depth, wide), vocab_weight.dtype) for _, wide in coming],
-        scratch_shapes=[group_sems(len(coming), coming[0][1] if coming else width)],
-        compiler_params=pltpu.CompilerParams(vmem_limit_bytes=VMEM_LIMIT),
+        ],
+        scratch_shapes=[pltpu.VMEM((half, LANES), jnp.float32)],
+        compiler_params=pltpu.CompilerParams(vmem_limit_bytes=VOCAB_LIMIT),
         cost_estimate=pl.CostEstimate(
             flops=2 * count * depth * width, bytes_accessed=2 * depth * width, transcendentals=0
         ),
-    )(rows, vocab_weight, *weights, *after)
+    )(rows, *[vocab_weight] * WAYS, *after)
 
 
 def fold_body(keep, came, *refs, tile):
@@ -309,32 +328,49 @@
     return jnp.where(lane == 0, peak, one * factor_one + two * factor_two)
 
 
-def finish_body(wanted, keep, *refs, tile, choices, first, arrived, earlier):
-    arrivals, (total_logits, stats, logits, sem) = refs[:arrived], refs[-4:]
-    before = refs[arrived] if earlier else None
+def finish_body(wanted, *refs, tile, choices, first, counts, earlier):
+    blocks = []
+    for count in counts:
+        blocks.append((refs[0], refs[1 : 1 + count]))
+        refs = refs[1 + count :]
+    before = refs[0] if earlier else None
+    total_logits, stats, logits, sems = refs[-4:]
     rows, width = logits.shape
     height = 16
     lane = lax.broadcasted_iota(jnp.int32, (height, LANES), 1)
-    for row in range(0, rows, height):
+    copies = []
+    for index, row in enumerate(range(0, rows, height)):
         here = slice(row, row + height)
-        marks = [came[here, width:].astype(jnp.int32).astype(jnp.float32) for came in arrivals]
         ids = wanted[here, :] - first
         columns = [jnp.broadcast_to(ids[:, k : k + 1], (height, LANES)) for k in range(choices)]
         peak = None
         picks = [None] * choices
-        for step in range(width // tile):
-            block = slice(step * tile, (step + 1) * tile)
-            value = keep[here, block]
-            for came, mark in zip(arrivals, marks):
-                value = value + decode(came[here, block], mark[:, step : step + 1])
-            logits[here, block] = value
-            for part in range(tile // LANES):
-                piece = value[:, part * LANES : (part + 1) * LANES]
-                at = lane + (step * tile + part * LANES)
-                peak = piece if peak is None else jnp.maximum(peak, piece)
-                for k in range(choices):
-                    term = jnp.where(at == columns[k], piece, 0.0)
-                    picks[k] = term if picks[k] is None else picks[k] + term
+        start = 0
+        for keep, arrivals in blocks:
+            wide = keep.shape[1]
+            marks = [came[here, wide:].astype(jnp.int32).astype(jnp.float32) for came in arrivals]
+            for step in range(wide // tile):
+                block = slice(step * tile, (step + 1) * tile)
+                value = keep[here, block]
+                for came, mark in zip(arrivals, marks):
+                    value = value + decode(came[here, block], mark[:, step : step + 1])
+                logits[here, start : start + tile] = value
+                for part in range(tile // LANES):
+                    piece = value[:, part * LANES : (part + 1) * LANES]
+                    at = lane + (start + part * LANES)
+                    peak = piece if peak is None else jnp.maximum(peak, piece)
+                    for k in range(choices):
+                        term = jnp.where(at == columns[k], piece, 0.0)
+                        picks[k] = term if picks[k] is None else picks[k] + term
+                start += tile
+        copies.append(
+            pltpu.make_async_copy(
+                logits.at[pl.ds(row, height), :],
+                total_logits.at[pl.ds(row, height), pl.ds(first, width)],
+                sems.at[index],
+            )
+        )
+        copies[-1].start()
         peak = jnp.max(peak, axis=1, keepdims=True)
         total = None
         for part in range(width // LANES):
@@ -344,14 +380,17 @@
         for k, item in enumerate([total] + picks):
             out = jnp.where(lane == k + 1, jnp.sum(item, axis=1, keepdims=True), out)
         stats[here, :] = out if before is None else merge_rows(before[here, :], out)
-    copy = pltpu.make_async_copy(logits, total_logits.at[:, pl.ds(first, width)], sem)
-    copy.start()
-    copy.wait()
-
-
-def finish(wanted, keep, arrivals, tile, choices, first, vocab_width, earlier, after):
-    rows, width = wanted.shape[0], keep.shape[1]
-    operands = [wanted, keep, *arrivals] + ([earlier[1]] if earlier else [])
+    for copy in copies:
+        copy.wait()
+
+
+def finish(wanted, blocks, tile, choices, first, vocab_width, earlier, after):
+    rows = wanted.shape[0]
+    width = sum(keep.shape[1] for keep, _ in blocks)
+    operands = [wanted]
+    for keep, arrivals in blocks:
+        operands += [keep, *arrivals]
+    operands += [earlier[1]] if earlier else []
     buffer = [earlier[0]] if earlier else []
     return pl.pallas_call(
         functools.partial(
@@ -359,7 +398,7 @@
             tile=tile,
             choices=choices,
             first=first,
-            arrived=len(arrivals),
+            counts=[len(arrivals) for _, arrivals in blocks],
             earlier=bool(earlier),
         ),
         in_specs=[VMEM] * len(operands) + [ANY] * len(buffer + after),
@@ -368,9 +407,12 @@
             jax.ShapeDtypeStruct((rows, vocab_width), jnp.float32),
             jax.ShapeDtypeStruct((rows, LANES), jnp.float32),
         ],
-        scratch_shapes=[pltpu.VMEM((rows, width), jnp.float32), pltpu.SemaphoreType.DMA],
+        scratch_shapes=[
+            pltpu.VMEM((rows, width), jnp.float32),
+            pltpu.SemaphoreType.DMA((rows // 16,)),
+        ],
         input_output_aliases={len(operands): 0} if earlier else {},
-        compiler_params=pltpu.CompilerParams(vmem_limit_bytes=VMEM_LIMIT),
+        compiler_params=pltpu.CompilerParams(vmem_limit_bytes=VOCAB_LIMIT),
     )(*operands, *buffer, *after)
 
 
@@ -441,7 +483,7 @@
     ratio = out_rows // rows
     mp_bits = bits_of(mp)
     pair, core = b // 2, b % 2
-    pair_bits = [bits_of(batch // 2), bits_of(batch // 2)[::-1]]
+    pair_bits = bits_of(batch // 2)
 
     taken = lax.broadcasted_iota(jnp.int32, (rows, positions, 1), 1) == (accepted - 1)[:, None, None]
     chosen = jnp.sum(jnp.where(taken, hidden_states, 0).astype(jnp.float32), axis=1)
@@ -490,9 +532,7 @@
     spots = []
     for unit in range(batch):
         source = (m ^ (unit // pieces) ^ (b // pieces)) * pieces + unit % pieces
-        apart = (source // 2) ^ pair
-        spot = jnp.where(core == 0, place(apart, pair_bits[0]), place(apart, pair_bits[1]))
-        spots.append(spot * 2 + source % 2)
+        spots.append(((source // 2) ^ pair) * 2 + source % 2)
     info = jnp.stack([core] + spots).astype(jnp.int32)
     send, *fetched = head_matmul(
         info, block, head_weight, weights_first, rows, jnp.bfloat16, firsts[2:]
@@ -501,63 +541,73 @@
     came = swap(send, "batch", lambda i: i ^ 1)
     (keep,) = head_matmul(info, block, head_weight, weights_then, rows, jnp.float32, [])
     units = batch // 2
-    turned = [place(unplace(u, pair_bits[0]), pair_bits[1]) for u in range(units)]
-    came = came.reshape(units, 2 * rows, feat)
-    came = jnp.concatenate([came[u] for u in turned], axis=0)
+    share = feat // 2
+    tall = 2 * rows
+    orders = (pair_bits, pair_bits[::-1])
     total = keep + came.astype(jnp.float32)
-    unit_width = vocab_width // 8
-
-    for step in range(len(pair_bits[0])):
-        half = total.shape[0] // 2
-        outbound = total[half:].astype(jnp.bfloat16)
-        came = swap(outbound, "batch", lambda i: i ^ (2 * pair_bits[i % 2][step]))
-        total = total[:half] + came.astype(jnp.float32)
+    halves = [
+        {u: total[u * tall : (u + 1) * tall, h * share : (h + 1) * share] for u in range(units)}
+        for h in range(2)
+    ]
+    for step in range(len(pair_bits)):
+        arrived = []
+        for half, order in zip(halves, orders):
+            leave = [u for u in half if u & order[step]]
+            outbound = jnp.concatenate([half[u] for u in leave], axis=0).astype(jnp.bfloat16)
+            arrived.append(swap(outbound, "batch", lambda i: i ^ (2 * order[step])))
+        for h, order in enumerate(orders):
+            stay = [u for u in halves[h] if not u & order[step]]
+            halves[h] = {
+                u: halves[h][u] + arrived[h][i * tall : (i + 1) * tall].astype(jnp.float32)
+                for i, u in enumerate(stay)
+            }
     bias = lax.dynamic_slice_in_dim(head_bias, core, 1, 0)
-    before = total * row_scale + bias
+    before = jnp.concatenate([half[0] for half in halves], axis=1) * row_scale + bias
     residual = (own_normed + jax.nn.silu(before)).astype(jnp.bfloat16)
-    (ahead,) = fetch(head_then, vocab_weight, [0], 2 * unit_width, [residual])
-    for step in reversed(range(len(pair_bits[0]))):
-        came = swap(residual, "batch", lambda i: i ^ (2 * pair_bits[i % 2][step]))
-        if step == len(pair_bits[0]) - 1:
-            came, ahead = together(came, ahead)
-        if step:
-            residual = jnp.concatenate([residual, came], axis=0)
-    own = [residual, came]
-    parts = own + [swap(part, "batch", lambda i: i ^ 1) for part in own]
+    filled = [residual[:, :share], residual[:, share:]]
+    held = [[0], [0]]
+    parts, others = [], []
+    block = residual
+    for step in reversed(range(len(pair_bits))):
+        arrived = [
+            swap(filled[h], "batch", lambda i: i ^ (2 * orders[h][step])) for h in range(2)
+        ]
+        for h in range(2):
+            held[h] = held[h] + [u ^ orders[h][step] for u in held[h]]
+        came = jnp.concatenate(arrived, axis=1)
+        if step == 0:
+            parts.append(block)
+            others.append(swap(block, "batch", lambda i: i ^ 1))
+            block = came
+        else:
+            block = jnp.concatenate([block, came], axis=0)
+            filled = [block[:, :share], block[:, share:]]
+    parts.append(block)
+    others.append(swap(block, "batch", lambda i: i ^ 1))
 
     table = []
     for whose in (core, 1 - core):
         for unit in range(batch):
-            apart = jnp.where(
-                whose == 0, unplace(unit // 2, pair_bits[0]), unplace(unit // 2, pair_bits[1])
-            )
-            source = (pair ^ apart) * 2 + unit % 2
-            table.append((((source // ratio) ^ m) * ratio + source % ratio) * heads + whose)
-    all_rows = gather_rows(jnp.stack(table).astype(jnp.int32), parts, rows)
+            for h in range(2):
+                source = (pair ^ held[h][unit // 2]) * 2 + unit % 2
+                table.append((((source // ratio) ^ m) * ratio + source % ratio) * heads + whose)
+    all_rows = gather_rows(jnp.stack(table).astype(jnp.int32), parts + others, rows, 2)
     wanted = (cand_ids - b * vocab_width).reshape(ratio, rows, heads, choices)
     wanted = wanted.transpose(0, 2, 1, 3).reshape(out_rows * heads, choices)
     wanted = jnp.pad(wanted, ((0, 0), (0, LANES - choices)), constant_values=-1)
 
-    held = {(0, 1): ahead}
-    plan = [((0, 1), (2, 3)), ((2, 3), (4, 5)), ((4, 5), (6, 7)), ((6,), ()), ((7,), ())]
+    unit_width = vocab_width // 8
+    plan = [(0, 2), (2, 2), (4, 2), (6, 1), (7, 1)]
+    plan = [(first * unit_width, count * unit_width) for first, count in plan]
     tile = widest(512, unit_width)
     blocks = len(plan)
     stages = [mp_bits if block % 2 == 0 else mp_bits[::-1] for block in range(blocks)]
     keeps, sends, arrivals = [], [], [[] for _ in plan]
 
     def begin(block, after):
-        units, coming = plan[block]
+        first, width = plan[block]
         order = sorted(range(mp), key=lambda g: place(g, stages[block]))
-        keep, send, *fetched = vocab_matmul(
-            all_rows,
-            vocab_weight,
-            [held[units]] if units in held else [held[u] for u in units],
-            order,
-            tile,
-            [(u * unit_width, unit_width) for u in coming],
-            after,
-        )
-        held.update(zip(coming, fetched))
+        keep, send = vocab_matmul(all_rows, vocab_weight, first, width, order, tile, after)
         keeps.append(keep)
         sends.append(send)
         arrivals[block].append(swap(send, "mp", lambda i: i ^ stages[block][0]))
@@ -582,18 +632,16 @@
     begin(4, [last])
     lasts = [go_on(block, [sends[4]]) for block in (2, 3, 4)]
     joined = None
-    for block, (units, _) in enumerate(plan):
-        first = units[0] * unit_width
+    for group in (range(0, 3), range(3, 5)):
         joined = finish(
             wanted,
-            keeps[block],
-            arrivals[block],
+            [(keeps[block], arrivals[block]) for block in group],
             tile,
             choices,
-            first,
+            plan[group[0]][0],
             vocab_width,
             joined,
-            lasts[block : block + 1],
+            lasts[2:] if joined is None else [],
         )
     logits, stats = joined
 

time: 196 us -> 203 us (1.036)
  starting transfers between devices: 30.8 us -> 36.8 us
  waiting for transfers between devices: 54.6 us -> 60.2 us
  Pallas kernels: 82.7 us -> 80.1 us
  local copies, waits for them, and re-layouts: 23 us -> 20.6 us
    pallas_call x3 -> x2, Pallas kernels: 15.8 us -> 9.75 us  [fetch(): pl.pallas_call(functools.partial(fetch_body, firsts=firsts), in_specs=[pl...]
    ppermute x25 -> x29, starting transfers between devices: 30.2 us -> 36.1 us  [swap(): lax.ppermute(array, axis, [(i, partner(i)) for i in range(lax.axis_size(a...]
    ppermute x25 -> x29, waiting for transfers between devices: 54.6 us -> 60.2 us  [swap(): lax.ppermute(array, axis, [(i, partner(i)) for i in range(lax.axis_size(a...]
    pallas_call x5, Pallas kernels: 6.31 us -> 9.5 us  [fold(): pl.pallas_call(functools.partial(fold_body, tile=tile), in_specs=[VMEM] *...]
    pallas_call x6, Pallas kernels: 37.8 us -> 40.7 us  [the longest x5 40 us: vocab_matmul(): pl.pallas_call(functools.partial(vocab_body, order=order, tile=tile, wait...]
    unnamed x50 -> x51, local copies, waits for them, and re-layouts: 21.7 us -> 19.3 us
    pallas_call x5 -> x2, Pallas kernels: 11.2 us -> 9.02 us  [finish(): pl.pallas_call(functools.partial(finish_body, tile=tile, choices=choices,...]
  transfers between devices with their start and end apart: 26 -> 30, of which waited for: 12 -> 16; matrix products, arithmetic and copies ran while one was open for 1% -> 1% of each run, Pallas kernels for 31% -> 30%
where the time goes in v5:
time: 203 us
  Pallas kernels  80.1 us (39%)
  waiting for transfers between devices  60.2 us (30%)
  starting transfers between devices  36.8 us (18%)
  local copies, waits for them, and re-layouts  20.6 us (10%)
  other arithmetic  3.45 us (2%)
    ppermute x29, waiting for transfers between devices, swap(): lax.ppermute(array, axis, [(i, partner(i)) for i in range(lax.axis_size(a...  60.2 us
    pallas_call x5, Pallas kernels, vocab_matmul(): pl.pallas_call(functools.partial(vocab_body, order=order, tile=tile, wait...  40 us
    ppermute x29, starting transfers between devices, swap(): lax.ppermute(array, axis, [(i, partner(i)) for i in range(lax.axis_size(a...  36.1 us
    unnamed x51, local copies, waits for them, and re-layouts  19.3 us
    pallas_call x2, Pallas kernels, fetch(): pl.pallas_call(functools.partial(fetch_body, firsts=firsts), in_specs=[pl...  9.75 us
    pallas_call x5, Pallas kernels, fold(): pl.pallas_call(functools.partial(fold_body, tile=tile), in_specs=[VMEM] *...  9.5 us
    pallas_call x2, Pallas kernels, finish(): pl.pallas_call(functools.partial(finish_body, tile=tile, choices=choices,...  9.02 us
    pallas_call x2, Pallas kernels, head_matmul(): pl.pallas_call(functools.partial(head_body, height=height, held=len(weigh...  8.9 us
  transfers between devices with their start and end apart: 30, of which 16 were waited for; matrix products, arithmetic and copies ran while one was open for 1% of the time, Pallas kernels for 30%

profile of v5, /device:TPU:0, one launch (start us, length us, event | category | flops | bytes accessed | tf_op | source)
XLA Modules:
  0.0 202.6 jit_solution(13607216014004876046)
XLA Ops:
  5.3 6.2 %shard_map.95 = (bf16[2048,1024]{1,0:T(8,128)(2,1)S(1)}, bf16[2048,1024]{1,0:T(8,128)(2,1)S(1)}, bf16[2048,1024]{1,0:T(8,128)(2,1)S(1)}, bf16[2048,1024]{1,0:T(8,128)(2,1)S(1)}) custom-call(s32[1]{0:T(128)} %bitcast.32.info, bf16[2,2048,4096]{2,1,0:T(8,128)(2,1)} %source.3, bf16[32,2048]{1,0:T(8,128)(2,1)S(1)} %multiply_convert_fusion.1.refs_0_), custom_call_target="tpu_custom_call" | custom-call | flops 5872025600 | tf_op jit(solution)/shard_map/pallas_call | solution.py:102
  11.5 9.9 %collective-permute-start.4 = (bf16[32,2048]{1,0:T(8,128)(2,1)S(1)}, bf16[32,2048]{1,0:T(8,128)(2,1)S(1)}, u32[]{:S(2)}, u32[]{:S(2)}) collective-permute-start(bf16[32,2048]{1,0:T(8,128)(2,1)S(1)} %collective-permute-done.3.refs_0_), channel_id=1, source_target_pairs={{0,1},{1,0},{2,3},{3,2},{4,5},{5,4},{6,7},{7,6},{8,9},{9,8},{10,11... | collective-permute-start | bytes 393224 | tf_op jit(solution)/shard_map/ppermute | solution.py:28
  21.4 3.6 %shard_map.96 = (bf16[2048,1024]{1,0:T(8,128)(2,1)S(1)}, bf16[2048,1024]{1,0:T(8,128)(2,1)S(1)}) custom-call(s32[1]{0:T(128)} %bitcast.23.info, bf16[2,2048,4096]{2,1,0:T(8,128)(2,1)} %source.3, bf16[32,2048]{1,0:T(8,128)(2,1)S(1)} %collective-permute-done.3.refs_0_), custom_call_target="tpu_custom_call" | custom-call | flops 2936012800 | tf_op jit(solution)/shard_map/pallas_call | solution.py:102
  29.1 7.2 %collective-permute-done.5 = bf16[64,2048]{1,0:T(8,128)(2,1)S(1)} collective-permute-done((bf16[64,2048]{1,0:T(8,128)(2,1)S(1)}, bf16[64,2048]{1,0:T(8,128)(2,1)S(1)}, u32[]{:S(2)}, u32[]{:S(2)}) %collective-permute-start.5) | collective-permute-done | bytes 262176 | tf_op jit(solution)/shard_map/ppermute | solution.py:28
  36.4 4.5 %shard_map.97 = (bf16[128,4096]{1,0:T(8,128)(2,1)S(1)}, bf16[2048,1024]{1,0:T(8,128)(2,1)S(1)}, bf16[2048,1024]{1,0:T(8,128)(2,1)S(1)}) custom-call(s32[9]{0:T(128)S(1)} %stack.123.info, bf16[128,2048]{1,0:T(8,128)(2,1)S(1)} %constant_dynamic-update-slice_fusion.came, bf16[2,2048,4096]{2,1,0:T(8,128)(2,1)} %source.3, ...), custom_call_target="tpu_custom_call" | custom-call | flops 2147483648 | bytes 524288 | tf_op jit(solution)/shard_map/pallas_call | solution.py:148
  45.4 2.2 %copy-done.9 = bf16[2048,1024]{1,0:T(8,128)(2,1)S(1)} copy-done((bf16[2048,1024]{1,0:T(8,128)(2,1)S(1)}, bf16[2048,1024]{1,0:T(8,128)(2,1)}, u32[]{:S(2)}) %copy-start.9) | copy-done | bytes 4194328
  47.6 2.2 %copy-done.11 = bf16[2048,1024]{1,0:T(8,128)(2,1)S(1)} copy-done((bf16[2048,1024]{1,0:T(8,128)(2,1)S(1)}, bf16[2048,1024]{1,0:T(8,128)(2,1)}, u32[]{:S(2)}) %copy-start.11) | copy-done | bytes 4194328
  49.8 2.2 %copy-done.13 = bf16[2048,1024]{1,0:T(8,128)(2,1)S(1)} copy-done((bf16[2048,1024]{1,0:T(8,128)(2,1)S(1)}, bf16[2048,1024]{1,0:T(8,128)(2,1)}, u32[]{:S(2)}) %copy-start.13) | copy-done | bytes 4194328
  52.0 2.2 %copy-done.15 = bf16[2048,1024]{1,0:T(8,128)(2,1)S(1)} copy-done((bf16[2048,1024]{1,0:T(8,128)(2,1)S(1)}, bf16[2048,1024]{1,0:T(8,128)(2,1)}, u32[]{:S(2)}) %copy-start.15) | copy-done | bytes 4194328
  54.2 4.4 %shard_map.98 = f32[128,4096]{1,0:T(8,128)S(1)} custom-call(s32[9]{0:T(128)S(1)} %stack.123.info, bf16[128,2048]{1,0:T(8,128)(2,1)S(1)} %constant_dynamic-update-slice_fusion.came, bf16[2,2048,4096]{2,1,0:T(8,128)(2,1)} %source.3, bf16[2048,1024]{1,0:T(8,128)(2,1)S(1)} %copy-done.9, bf16[2048,1024]{1,0:T(8,128)(2,1)S(1)} %copy-done.11, ...), custom_call_target="tpu_custom_call" | custom-call | flops 2147483648 | bytes 524288 | tf_op jit(solution)/shard_map/pallas_call | solution.py:148
  59.1 4.1 %collective-permute-start.9 = (bf16[64,2048]{1,0:T(8,128)(2,1)S(1)}, bf16[64,2048]{1,0:T(8,128)(2,1)S(1)}, u32[]{:S(2)}, u32[]{:S(2)}) collective-permute-start(bf16[64,2048]{1,0:T(8,128)(2,1)S(1)} %concatenate.38), channel_id=1, source_target_pairs={{0,16},{4,20},{8,24},{12,28},{16,0},{20,4},{24,8},{28,12},{1,17},{... | collective-permute-start | bytes 786440 | tf_op jit(solution)/shard_map/ppermute | solution.py:28
  63.6 9.2 %collective-permute-done.7 = bf16[64,2048]{1,0:T(8,128)(2,1)S(1)} collective-permute-done((bf16[64,2048]{1,0:T(8,128)(2,1)S(1)}, bf16[64,2048]{1,0:T(8,128)(2,1)S(1)}, u32[]{:S(2)}, u32[]{:S(2)}) %collective-permute-start.7) | collective-permute-done | bytes 262176 | tf_op jit(solution)/shard_map/ppermute | solution.py:28
  72.9 2.4 %collective-permute-done.9 = bf16[64,2048]{1,0:T(8,128)(2,1)S(1)} collective-permute-done((bf16[64,2048]{1,0:T(8,128)(2,1)S(1)}, bf16[64,2048]{1,0:T(8,128)(2,1)S(1)}, u32[]{:S(2)}, u32[]{:S(2)}) %collective-permute-start.9) | collective-permute-done | bytes 262176 | tf_op jit(solution)/shard_map/ppermute | solution.py:28
  75.8 2.7 %collective-permute-start.8 = (bf16[32,2048]{1,0:T(8,128)(2,1)S(1)}, bf16[32,2048]{1,0:T(8,128)(2,1)S(1)}, u32[]{:S(2)}, u32[]{:S(2)}) collective-permute-start(bf16[32,2048]{1,0:T(8,128)(2,1)S(1)} %get-tuple-element.68), channel_id=1, source_target_pairs={{0,16},{4,20},{8,24},{12,28},{16,0},{20,4},{24,8},{28,12},{1,17},{... | collective-permute-start | bytes 393224 | tf_op jit(solution)/shard_map/ppermute | solution.py:28
  78.4 4.0 %collective-permute-done.10 = bf16[32,2048]{1,0:T(8,128)(2,1)S(1)} collective-permute-done((bf16[32,2048]{1,0:T(8,128)(2,1)S(1)}, bf16[32,2048]{1,0:T(8,128)(2,1)S(1)}, u32[]{:S(2)}, u32[]{:S(2)}) %collective-permute-start.10) | collective-permute-done | bytes 131104 | tf_op jit(solution)/shard_map/ppermute | solution.py:28
  85.0 2.5 %collective-permute-start.12 = (bf16[32,2048]{1,0:T(8,128)(2,1)S(1)}, bf16[32,2048]{1,0:T(8,128)(2,1)S(1)}, u32[]{:S(2)}, u32[]{:S(2)}) collective-permute-start(bf16[32,2048]{1,0:T(8,128)(2,1)S(1)} %get-tuple-element.75), channel_id=1, source_target_pairs={{0,8},{4,12},{8,0},{12,4},{16,24},{20,28},{24,16},{28,20},{1,9},{5... | collective-permute-start | bytes 393224 | tf_op jit(solution)/shard_map/ppermute | solution.py:28
  87.6 4.4 %collective-permute-done.11 = bf16[32,2048]{1,0:T(8,128)(2,1)S(1)} collective-permute-done((bf16[32,2048]{1,0:T(8,128)(2,1)S(1)}, bf16[32,2048]{1,0:T(8,128)(2,1)S(1)}, u32[]{:S(2)}, u32[]{:S(2)}) %collective-permute-start.11) | collective-permute-done | bytes 131104 | tf_op jit(solution)/shard_map/ppermute | solution.py:28
  94.6 7.7 %collective-permute-done.13 = bf16[64,2048]{1,0:T(8,128)(2,1)S(1)} collective-permute-done((bf16[64,2048]{1,0:T(8,128)(2,1)S(1)}, bf16[64,2048]{1,0:T(8,128)(2,1)S(1)}, u32[]{:S(2)}, u32[]{:S(2)}) %collective-permute-start.13) | collective-permute-done | bytes 262176 | tf_op jit(solution)/shard_map/ppermute | solution.py:28
  102.3 2.5 %collective-permute-done.14 = bf16[64,2048]{1,0:T(8,128)(2,1)S(1)} collective-permute-done((bf16[64,2048]{1,0:T(8,128)(2,1)S(1)}, bf16[64,2048]{1,0:T(8,128)(2,1)S(1)}, u32[]{:S(2)}, u32[]{:S(2)}) %collective-permute-start.14) | collective-permute-done | bytes 262176 | tf_op jit(solution)/shard_map/ppermute | solution.py:28
  107.5 9.6 %shard_map.100 = (f32[128,2048]{1,0:T(8,128)S(1)}, s16[128,2176]{1,0:T(8,128)(2,1)}) custom-call(bf16[256,4096]{1,0:T(8,128)(2,1)S(1)} %shard_map.99.rows, bf16[4096,8192]{1,0:T(8,128)(2,1)} %refs_3_.9, bf16[4096,8192]{1,0:T(8,128)(2,1)} %refs_3_.9, bf16[4096,8192]{1,0:T(8,128)(2,1)} %refs_3_.9, bf16[4096,8192]{1,0:T(8,128)(2,1)} %refs_3_.9), custom_call_target="tpu_custom_call" | custom-call | flops 4294967296 | bytes 16777216 | tf_op jit(solution)/shard_map/pallas_call | solution.py:254
  118.9 9.7 %shard_map.101 = (f32[128,2048]{1,0:T(8,128)S(1)}, s16[128,2176]{1,0:T(8,128)(2,1)}) custom-call(bf16[256,4096]{1,0:T(8,128)(2,1)S(1)} %shard_map.99.rows, bf16[4096,8192]{1,0:T(8,128)(2,1)} %refs_3_.9, bf16[4096,8192]{1,0:T(8,128)(2,1)} %refs_3_.9, bf16[4096,8192]{1,0:T(8,128)(2,1)} %refs_3_.9, bf16[4096,8192]{1,0:T(8,128)(2,1)} %refs_3_.9, ...), custom_call_target="tpu_custom_call" | custom-call | flops 4294967296 | bytes 16777216 | tf_op jit(solution)/shard_map/pallas_call | solution.py:254
  128.8 9.7 %shard_map.102 = (f32[128,2048]{1,0:T(8,128)S(1)}, s16[128,2176]{1,0:T(8,128)(2,1)}) custom-call(bf16[256,4096]{1,0:T(8,128)(2,1)S(1)} %shard_map.99.rows, bf16[4096,8192]{1,0:T(8,128)(2,1)} %refs_3_.9, bf16[4096,8192]{1,0:T(8,128)(2,1)} %refs_3_.9, bf16[4096,8192]{1,0:T(8,128)(2,1)} %refs_3_.9, bf16[4096,8192]{1,0:T(8,128)(2,1)} %refs_3_.9, ...), custom_call_target="tpu_custom_call" | custom-call | flops 4294967296 | bytes 16777216 | tf_op jit(solution)/shard_map/pallas_call | solution.py:254
  140.9 5.8 %shard_map.104 = (f32[128,1024]{1,0:T(8,128)S(1)}, s16[128,1152]{1,0:T(8,128)(2,1)}) custom-call(bf16[256,4096]{1,0:T(8,128)(2,1)S(1)} %shard_map.99.rows, bf16[4096,8192]{1,0:T(8,128)(2,1)} %refs_3_.9, bf16[4096,8192]{1,0:T(8,128)(2,1)} %refs_3_.9, bf16[4096,8192]{1,0:T(8,128)(2,1)} %refs_3_.9, bf16[4096,8192]{1,0:T(8,128)(2,1)} %refs_3_.9, ...), custom_call_target="tpu_custom_call" | custom-call | flops 2147483648 | bytes 8388608 | tf_op jit(solution)/shard_map/pallas_call | solution.py:254
  146.7 2.8 %shard_map.105.refs_4_ = s16[64,2176]{1,0:T(8,128)(2,1)} custom-call(f32[128,2048]{1,0:T(8,128)S(1)} %get-tuple-element.56.keep.refs_3_, s16[128,2176]{1,0:T(8,128)(2,1)} %collective-permute-done.19.came.refs_4_, s16[128,1152]{1,0:T(8,128)(2,1)} %get-tuple-element.55.refs_0_), custom_call_target="tpu_custom_call" | custom-call | tf_op jit(solution)/shard_map/pallas_call | solution.py:293
  149.6 5.2 %shard_map.106 = (f32[128,1024]{1,0:T(8,128)S(1)}, s16[128,1152]{1,0:T(8,128)(2,1)S(1)}) custom-call(bf16[256,4096]{1,0:T(8,128)(2,1)S(1)} %shard_map.99.rows, bf16[4096,8192]{1,0:T(8,128)(2,1)} %refs_3_.9, bf16[4096,8192]{1,0:T(8,128)(2,1)} %refs_3_.9, bf16[4096,8192]{1,0:T(8,128)(2,1)} %refs_3_.9, bf16[4096,8192]{1,0:T(8,128)(2,1)} %refs_3_.9, ...), custom_call_target="tpu_custom_call" | custom-call | flops 2147483648 | bytes 8388608 | tf_op jit(solution)/shard_map/pallas_call | solution.py:254
  158.2 2.8 %shard_map.109 = s16[64,2176]{1,0:T(8,128)(2,1)} custom-call(f32[128,2048]{1,0:T(8,128)S(1)} %get-tuple-element.59.keep.refs_6_, s16[128,2176]{1,0:T(8,128)(2,1)} %collective-permute-done.25.came.refs_7_, s16[128,1152]{1,0:T(8,128)(2,1)S(1)} %get-tuple-element.57.refs_0_), custom_call_target="tpu_custom_call" | custom-call | tf_op jit(solution)/shard_map/pallas_call | solution.py:293
  170.0 2.8 %collective-permute-done.26.refs_8_ = s16[64,2176]{1,0:T(8,128)(2,1)} collective-permute-done((s16[64,2176]{1,0:T(8,128)(2,1)}, s16[64,2176]{1,0:T(8,128)(2,1)}, u32[]{:S(2)}, u32[]{:S(2)}) %collective-permute-start.26) | collective-permute-done | bytes 278560 | tf_op jit(solution)/shard_map/ppermute | solution.py:28
  172.8 5.8 %collective-permute-done.23.refs_2_ = s16[64,2176]{1,0:T(8,128)(2,1)} collective-permute-done((s16[64,2176]{1,0:T(8,128)(2,1)S(1)}, s16[64,2176]{1,0:T(8,128)(2,1)}, u32[]{:S(2)}, u32[]{:S(2)}) %collective-permute-start.23) | collective-permute-done | bytes 278560 | tf_op jit(solution)/shard_map/ppermute | solution.py:28
  181.1 5.8 %shard_map.110 = (f32[64,8192]{1,0:T(8,128)S(1)}, f32[64,128]{1,0:T(8,128)S(1)}) custom-call(s32[64,128]{1,0:T(8,128)S(1)} %pad.4.wanted, f32[128,2048]{1,0:T(8,128)S(1)} %copy-done.3, s16[128,2176]{1,0:T(8,128)(2,1)} %collective-permute-done.17.came.refs_1_, s16[64,2176]{1,0:T(8,128)(2,1)} %collective-permute-done.23.refs_2_, f32[128,2048]{1,0:T(8,128)S(1)} %copy-done.5, ...), custom_call_target="tpu_custom_call" | custom-call | tf_op jit(solution)/shard_map/pallas_call | solution.py:395
  187.0 3.2 %shard_map.111 = (f32[64,8192]{1,0:T(8,128)S(1)}, f32[64,128]{1,0:T(8,128)S(1)}) custom-call(s32[64,128]{1,0:T(8,128)S(1)} %pad.4.wanted, f32[128,1024]{1,0:T(8,128)S(1)} %copy-done.17, s16[128,1152]{1,0:T(8,128)(2,1)S(1)} %copy-done.21, s16[64,1152]{1,0:T(8,128)(2,1)} %collective-permute-done.20.refs_2_, ...), custom_call_target="tpu_custom_call", output_to_operand_aliasing={{0}: (8, {})} | custom-call | tf_op jit(solution)/shard_map/pallas_call | solution.py:395
  191.6 3.9 %collective-permute-done.28.came = f32[64,128]{1,0:T(8,128)S(1)} collective-permute-done((f32[64,128]{1,0:T(8,128)S(1)}, f32[64,128]{1,0:T(8,128)S(1)}, u32[]{:S(2)}, u32[]{:S(2)}) %collective-permute-start.28) | collective-permute-done | bytes 32800 | tf_op jit(solution)/shard_map/ppermute | solution.py:28
  196.0 4.5 %collective-permute-done.29.came = f32[64,128]{1,0:T(8,128)S(1)} collective-permute-done((f32[64,128]{1,0:T(8,128)S(1)}, f32[64,128]{1,0:T(8,128)S(1)}, u32[]{:S(2)}, u32[]{:S(2)}) %collective-permute-start.29) | collective-permute-done | bytes 32800 | tf_op jit(solution)/shard_map/ppermute | solution.py:28
  (131 shorter events, 45.4 us)
Async XLA Ops:
  0.6 62.6 %copy-start = (f32[2,4096]{1,0:T(2,128)S(1)}, f32[2,4096]{1,0:T(2,128)}, u32[]{:S(2)}) copy-start(f32[2,4096]{1,0:T(2,128)} %param.12) | copy-start | bytes 98308
  3.0 1.5 collective-permute-start
  4.6 6.9 %collective-permute-start.3 = (bf16[32,2048]{1,0:T(8,128)(2,1)S(1)}, bf16[32,2048]{1,0:T(8,128)(2,1)S(1)}, u32[]{:S(2)}, u32[]{:S(2)}) collective-permute-start(bf16[32,2048]{1,0:T(8,128)(2,1)S(1)} %multiply_convert_fusion.1.refs_0_), channel_id=1, source_target_pairs={{0,0},{1,9},{2,18},{3,27},{4,4},{5,13},{6,22},{7,31},{8,1},{9,8},{... | collective-permute-start | bytes 393224 | tf_op jit(solution)/shard_map/ppermute | solution.py:517
  11.5 17.5 %collective-permute-start.4 = (bf16[32,2048]{1,0:T(8,128)(2,1)S(1)}, bf16[32,2048]{1,0:T(8,128)(2,1)S(1)}, u32[]{:S(2)}, u32[]{:S(2)}) collective-permute-start(bf16[32,2048]{1,0:T(8,128)(2,1)S(1)} %collective-permute-done.3.refs_0_), channel_id=1, source_target_pairs={{0,1},{1,0},{2,3},{3,2},{4,5},{5,4},{6,7},{7,6},{8,9},{9,8},{10,11... | collective-permute-start | bytes 393224 | tf_op jit(solution)/shard_map/ppermute | solution.py:28
  29.0 7.3 %collective-permute-start.5 = (bf16[64,2048]{1,0:T(8,128)(2,1)S(1)}, bf16[64,2048]{1,0:T(8,128)(2,1)S(1)}, u32[]{:S(2)}, u32[]{:S(2)}) collective-permute-start(bf16[64,2048]{1,0:T(8,128)(2,1)S(1)} %pad_maximum_fusion), channel_id=1, source_target_pairs={{0,2},{1,3},{2,0},{3,1},{4,6},{5,7},{6,4},{7,5},{8,10},{9,11},{10,... | collective-permute-start | bytes 786440 | tf_op jit(solution)/shard_map/ppermute | solution.py:28
  44.9 13.7 %collective-permute-start.6 = (bf16[128,4096]{1,0:T(8,128)(2,1)S(1)}, bf16[128,4096]{1,0:T(8,128)(2,1)S(1)}, u32[]{:S(2)}, u32[]{:S(2)}) collective-permute-start(bf16[128,4096]{1,0:T(8,128)(2,1)S(1)} %get-tuple-element.49), channel_id=1, source_target_pairs={{0,4},{4,0},{8,12},{12,8},{16,20},{20,16},{24,28},{28,24},{1,5},{5... | collective-permute-start | bytes 3145736 | tf_op jit(solution)/shard_map/ppermute | solution.py:28
  45.1 18.2 %collective-permute-start.1 = (f32[32,1]{0,1:T(1,128)S(1)}, f32[32,1]{0,1:T(1,128)S(1)}, u32[]{:S(2)}, u32[]{:S(2)}) collective-permute-start(f32[32,1]{0,1:T(1,128)S(1)} %bitcast.43), channel_id=1, source_target_pairs={{0,1},{1,0},{2,3},{3,2},{4,5},{5,4},{6,7},{7,6},{8,9},{9,8},{10,11... | collective-permute-start | bytes 392 | tf_op jit(solution)/shard_map/ppermute | solution.py:28
  58.9 25.5 %dynamic-slice-start = ((f32[16384]{0:T(1024)}, s32[]{:T(128)}), f32[4096]{0:T(1024)S(1)}, s32[]{:S(2)}) async-start(f32[16384]{0:T(1024)} %param.10, s32[]{:T(128)} %select_n.264), calls=%async_computation | async-start | bytes 33280 | tf_op jit(solution)/shard_map/dynamic_slice | solution.py:495
  59.0 13.9 %collective-permute-start.7 = (bf16[64,2048]{1,0:T(8,128)(2,1)S(1)}, bf16[64,2048]{1,0:T(8,128)(2,1)S(1)}, u32[]{:S(2)}, u32[]{:S(2)}) collective-permute-start(bf16[64,2048]{1,0:T(8,128)(2,1)S(1)} %pad_maximum_fusion.1), channel_id=1, source_target_pairs={{0,8},{4,12},{8,0},{12,4},{16,24},{20,28},{24,16},{28,20},{1,9},{5... | collective-permute-start | bytes 786440 | tf_op jit(solution)/shard_map/ppermute | solution.py:28
  59.1 16.2 %collective-permute-start.9 = (bf16[64,2048]{1,0:T(8,128)(2,1)S(1)}, bf16[64,2048]{1,0:T(8,128)(2,1)S(1)}, u32[]{:S(2)}, u32[]{:S(2)}) collective-permute-start(bf16[64,2048]{1,0:T(8,128)(2,1)S(1)} %concatenate.38), channel_id=1, source_target_pairs={{0,16},{4,20},{8,24},{12,28},{16,0},{20,4},{24,8},{28,12},{1,17},{... | collective-permute-start | bytes 786440 | tf_op jit(solution)/shard_map/ppermute | solution.py:28
  63.3 15.2 %collective-permute-start.2 = (f32[32,1]{0,1:T(1,128)S(1)}, f32[32,1]{0,1:T(1,128)S(1)}, u32[]{:S(2)}, u32[]{:S(2)}) collective-permute-start(f32[32,1]{0,1:T(1,128)S(1)} %bitcast_add_fusion), channel_id=1, source_target_pairs={{0,2},{1,3},{2,0},{3,1},{4,6},{5,7},{6,4},{7,5},{8,10},{9,11},{10,... | collective-permute-start | bytes 392 | tf_op jit(solution)/shard_map/ppermute | solution.py:28
  75.4 7.1 %collective-permute-start.10 = (bf16[32,2048]{1,0:T(8,128)(2,1)S(1)}, bf16[32,2048]{1,0:T(8,128)(2,1)S(1)}, u32[]{:S(2)}, u32[]{:S(2)}) collective-permute-start(bf16[32,2048]{1,0:T(8,128)(2,1)S(1)} %get-tuple-element.69), channel_id=1, source_target_pairs={{0,8},{4,12},{8,0},{12,4},{16,24},{20,28},{24,16},{28,20},{1,9},{5... | collective-permute-start | bytes 393224 | tf_op jit(solution)/shard_map/ppermute | solution.py:28
  75.8 8.5 %collective-permute-start.8 = (bf16[32,2048]{1,0:T(8,128)(2,1)S(1)}, bf16[32,2048]{1,0:T(8,128)(2,1)S(1)}, u32[]{:S(2)}, u32[]{:S(2)}) collective-permute-start(bf16[32,2048]{1,0:T(8,128)(2,1)S(1)} %get-tuple-element.68), channel_id=1, source_target_pairs={{0,16},{4,20},{8,24},{12,28},{16,0},{20,4},{24,8},{28,12},{1,17},{... | collective-permute-start | bytes 393224 | tf_op jit(solution)/shard_map/ppermute | solution.py:28
  84.7 7.3 %collective-permute-start.11 = (bf16[32,2048]{1,0:T(8,128)(2,1)S(1)}, bf16[32,2048]{1,0:T(8,128)(2,1)S(1)}, u32[]{:S(2)}, u32[]{:S(2)}) collective-permute-start(bf16[32,2048]{1,0:T(8,128)(2,1)S(1)} %get-tuple-element.74), channel_id=1, source_target_pairs={{0,16},{4,20},{8,24},{12,28},{16,0},{20,4},{24,8},{28,12},{1,17},{... | collective-permute-start | bytes 393224 | tf_op jit(solution)/shard_map/ppermute | solution.py:28
  85.0 6.9 %collective-permute-start.12 = (bf16[32,2048]{1,0:T(8,128)(2,1)S(1)}, bf16[32,2048]{1,0:T(8,128)(2,1)S(1)}, u32[]{:S(2)}, u32[]{:S(2)}) collective-permute-start(bf16[32,2048]{1,0:T(8,128)(2,1)S(1)} %get-tuple-element.75), channel_id=1, source_target_pairs={{0,8},{4,12},{8,0},{12,4},{16,24},{20,28},{24,16},{28,20},{1,9},{5... | collective-permute-start | bytes 393224 | tf_op jit(solution)/shard_map/ppermute | solution.py:28
  92.0 10.2 %collective-permute-start.13 = (bf16[64,2048]{1,0:T(8,128)(2,1)S(1)}, bf16[64,2048]{1,0:T(8,128)(2,1)S(1)}, u32[]{:S(2)}, u32[]{:S(2)}) collective-permute-start(bf16[64,2048]{1,0:T(8,128)(2,1)S(1)} %get-tuple-element.73), channel_id=1, source_target_pairs={{0,8},{4,12},{8,0},{12,4},{16,24},{20,28},{24,16},{28,20},{1,9},{5... | collective-permute-start | bytes 786440 | tf_op jit(solution)/shard_map/ppermute | solution.py:28
  92.7 12.2 %collective-permute-start.14 = (bf16[64,2048]{1,0:T(8,128)(2,1)S(1)}, bf16[64,2048]{1,0:T(8,128)(2,1)S(1)}, u32[]{:S(2)}, u32[]{:S(2)}) collective-permute-start(bf16[64,2048]{1,0:T(8,128)(2,1)S(1)} %get-tuple-element.72), channel_id=1, source_target_pairs={{0,16},{4,20},{8,24},{12,28},{16,0},{20,4},{24,8},{28,12},{1,17},{... | collective-permute-start | bytes 786440 | tf_op jit(solution)/shard_map/ppermute | solution.py:28
  94.6 10.8 %collective-permute-start.15 = (bf16[64,4096]{1,0:T(8,128)(2,1)S(1)}, bf16[64,4096]{1,0:T(8,128)(2,1)S(1)}, u32[]{:S(2)}, u32[]{:S(2)}) collective-permute-start(bf16[64,4096]{1,0:T(8,128)(2,1)S(1)} %maximum_maximum_fusion.refs_0_), channel_id=1, source_target_pairs={{0,4},{4,0},{8,12},{12,8},{16,20},{20,16},{24,28},{28,24},{1,5},{5... | collective-permute-start | bytes 1572872 | tf_op jit(solution)/shard_map/ppermute | solution.py:28
  104.8 2.0 collective-permute-start.16
  117.1 21.8 %collective-permute-start.17 = (s16[128,2176]{1,0:T(8,128)(2,1)}, s16[128,2176]{1,0:T(8,128)(2,1)}, u32[]{:S(2)}, u32[]{:S(2)}) collective-permute-start(s16[128,2176]{1,0:T(8,128)(2,1)} %get-tuple-element.51.refs_4_), channel_id=1, source_target_pairs={{0,1},{1,0},{2,3},{3,2},{4,5},{5,4},{6,7},{7,6},{8,9},{9,8},{10,11... | collective-permute-start | bytes 1671176 | tf_op jit(solution)/shard_map/ppermute | solution.py:28
  128.6 18.1 %collective-permute-start.19 = (s16[128,2176]{1,0:T(8,128)(2,1)}, s16[128,2176]{1,0:T(8,128)(2,1)}, u32[]{:S(2)}, u32[]{:S(2)}) collective-permute-start(s16[128,2176]{1,0:T(8,128)(2,1)} %get-tuple-element.52.refs_4_), channel_id=1, source_target_pairs={{0,2},{1,3},{2,0},{3,1},{4,6},{5,7},{6,4},{7,5},{8,10},{9,11},{10,... | collective-permute-start | bytes 1671176 | tf_op jit(solution)/shard_map/ppermute | solution.py:28
  138.6 19.6 %collective-permute-start.25 = (s16[128,2176]{1,0:T(8,128)(2,1)}, s16[128,2176]{1,0:T(8,128)(2,1)}, u32[]{:S(2)}, u32[]{:S(2)}) collective-permute-start(s16[128,2176]{1,0:T(8,128)(2,1)} %get-tuple-element.53.refs_0_), channel_id=1, source_target_pairs={{0,1},{1,0},{2,3},{3,2},{4,5},{5,4},{6,7},{7,6},{8,9},{9,8},{10,11... | collective-permute-start | bytes 1671176 | tf_op jit(solution)/shard_map/ppermute | solution.py:28
  154.8 9.6 %collective-permute-start.21 = (s16[128,1152]{1,0:T(8,128)(2,1)S(1)}, s16[128,1152]{1,0:T(8,128)(2,1)S(1)}, u32[]{:S(2)}, u32[]{:S(2)}) collective-permute-start(s16[128,1152]{1,0:T(8,128)(2,1)S(1)} %get-tuple-element.57.refs_0_), channel_id=1, source_target_pairs={{0,1},{1,0},{2,3},{3,2},{4,5},{5,4},{6,7},{7,6},{8,9},{9,8},{10,11... | collective-permute-start | bytes 884744 | tf_op jit(solution)/shard_map/ppermute | solution.py:28
  156.5 10.2 %collective-permute-start.18 = (s16[128,1152]{1,0:T(8,128)(2,1)}, s16[128,1152]{1,0:T(8,128)(2,1)S(1)}, u32[]{:S(2)}, u32[]{:S(2)}) collective-permute-start(s16[128,1152]{1,0:T(8,128)(2,1)} %get-tuple-element.55.refs_0_), channel_id=1, source_target_pairs={{0,2},{1,3},{2,0},{3,1},{4,6},{5,7},{6,4},{7,5},{8,10},{9,11},{10,... | collective-permute-start | bytes 884744 | tf_op jit(solution)/shard_map/ppermute | solution.py:28
  161.0 11.8 %collective-permute-start.26 = (s16[64,2176]{1,0:T(8,128)(2,1)}, s16[64,2176]{1,0:T(8,128)(2,1)}, u32[]{:S(2)}, u32[]{:S(2)}) collective-permute-start(s16[64,2176]{1,0:T(8,128)(2,1)} %shard_map.109), channel_id=1, source_target_pairs={{0,2},{1,3},{2,0},{3,1},{4,6},{5,7},{6,4},{7,5},{8,10},{9,11},{10,... | collective-permute-start | bytes 835592 | tf_op jit(solution)/shard_map/ppermute | solution.py:28
  161.3 11.4 %collective-permute-start.24 = (s16[64,2176]{1,0:T(8,128)(2,1)}, s16[64,2176]{1,0:T(8,128)(2,1)}, u32[]{:S(2)}, u32[]{:S(2)}) collective-permute-start(s16[64,2176]{1,0:T(8,128)(2,1)} %shard_map.105.refs_4_), channel_id=1, source_target_pairs={{0,1},{1,0},{2,3},{3,2},{4,5},{5,4},{6,7},{7,6},{8,9},{9,8},{10,11... | collective-permute-start | bytes 835592 | tf_op jit(solution)/shard_map/ppermute | solution.py:28
  161.7 16.9 %collective-permute-start.23 = (s16[64,2176]{1,0:T(8,128)(2,1)S(1)}, s16[64,2176]{1,0:T(8,128)(2,1)}, u32[]{:S(2)}, u32[]{:S(2)}) collective-permute-start(s16[64,2176]{1,0:T(8,128)(2,1)S(1)} %shard_map.103.refs_4_), channel_id=1, source_target_pairs={{0,2},{1,3},{2,0},{3,1},{4,6},{5,7},{6,4},{7,5},{8,10},{9,11},{10,... | collective-permute-start | bytes 835592 | tf_op jit(solution)/shard_map/ppermute | solution.py:28
  165.4 21.5 %collective-permute-start.22 = (s16[64,1152]{1,0:T(8,128)(2,1)}, s16[64,1152]{1,0:T(8,128)(2,1)}, u32[]{:S(2)}, u32[]{:S(2)}) collective-permute-start(s16[64,1152]{1,0:T(8,128)(2,1)} %shard_map.108.refs_9_), channel_id=1, source_target_pairs={{0,2},{1,3},{2,0},{3,1},{4,6},{5,7},{6,4},{7,5},{8,10},{9,11},{10,... | collective-permute-start | bytes 442376 | tf_op jit(solution)/shard_map/ppermute | solution.py:28
  167.8 19.2 %collective-permute-start.20 = (s16[64,1152]{1,0:T(8,128)(2,1)}, s16[64,1152]{1,0:T(8,128)(2,1)}, u32[]{:S(2)}, u32[]{:S(2)}) collective-permute-start(s16[64,1152]{1,0:T(8,128)(2,1)} %shard_map.107), channel_id=1, source_target_pairs={{0,1},{1,0},{2,3},{3,2},{4,5},{5,4},{6,7},{7,6},{8,9},{9,8},{10,11... | collective-permute-start | bytes 442376 | tf_op jit(solution)/shard_map/ppermute | solution.py:28
  190.2 1.3 collective-permute-start.27
  191.6 4.0 %collective-permute-start.28 = (f32[64,128]{1,0:T(8,128)S(1)}, f32[64,128]{1,0:T(8,128)S(1)}, u32[]{:S(2)}, u32[]{:S(2)}) collective-permute-start(f32[64,128]{1,0:T(8,128)S(1)} %shard_map.112.own), channel_id=1, source_target_pairs={{0,8},{4,12},{8,0},{12,4},{16,24},{20,28},{24,16},{28,20},{1,9},{5... | collective-permute-start | bytes 98312 | tf_op jit(solution)/shard_map/ppermute | solution.py:28
  195.6 4.9 %collective-permute-start.29 = (f32[64,128]{1,0:T(8,128)S(1)}, f32[64,128]{1,0:T(8,128)S(1)}, u32[]{:S(2)}, u32[]{:S(2)}) collective-permute-start(f32[64,128]{1,0:T(8,128)S(1)} %shard_map.113.own), channel_id=1, source_target_pairs={{0,16},{4,20},{8,24},{12,28},{16,0},{20,4},{24,8},{28,12},{1,17},{... | collective-permute-start | bytes 98312 | tf_op jit(solution)/shard_map/ppermute | solution.py:28
  (23 other events, 196.6 us)

commit v6 on v5

--- a/solution.py
+++ b/solution.py
@@ -13,7 +13,7 @@
 CODE_BITS = 14
 VMEM_LIMIT = 4 * MIB
 HEAD_LIMIT = 24 * MIB
-VOCAB_LIMIT = 20 * MIB
+VOCAB_LIMIT = 24 * MIB
 
 
 def together(*arrays):
@@ -77,6 +77,35 @@
     return pltpu.SemaphoreType.DMA((max(1, count), width // widest(512, width), WAYS))
 
 
+def stream(source, held, sems, first, tile):
+    depth, width = held.shape
+    share = depth // WAYS
+
+    def copies(n):
+        at = n * tile if isinstance(n, int) else pl.multiple_of(n * tile, tile)
+        return [
+            pltpu.make_async_copy(
+                source.at[pl.ds(way * share, share), pl.ds(first + at, tile)],
+                held.at[pl.ds(way * share, share), pl.ds(at, tile)],
+                sems.at[n, way],
+            )
+            for way in range(WAYS)
+        ]
+
+    def begin(n, carry):
+        for copy in copies(n):
+            copy.start()
+        return carry
+
+    lax.fori_loop(0, width // tile, begin, 0)
+
+    def wait(n):
+        for copy in copies(n):
+            copy.wait()
+
+    return wait
+
+
 def start_group(group):
     for copy in group:
         copy.start()
@@ -112,24 +141,24 @@
     )(info, weight, *after)
 
 
-def head_body(info, came, source, *refs, height, held, firsts):
-    weights, refs = refs[:held], refs[held:]
-    out, targets, (rows, sems) = refs[0], refs[1:-2], refs[-2:]
-    groups = copy_groups(source.at[info[0]], targets, sems, firsts)
+def head_body(info, came, *refs, height, tile, streams):
+    if streams:
+        source, out, rows, held, sems = refs
+        wait = stream(source.at[info[0]], held, sems, 0, tile)
+        weights = [held]
+    else:
+        weights, (out, rows) = refs[:-2], refs[-2:]
     for unit in range(came.shape[0] // height):
         start = pl.multiple_of(info[1 + unit] * height, height)
         rows[pl.ds(start, height), :] = came[unit * height : (unit + 1) * height, :]
-    waiting = list(groups)
     first = 0
     for weight in weights:
         width = weight.shape[1]
-        tile = widest(512, width)
-        for group in waiting[: width // tile]:
-            start_group(group)
-        waiting = waiting[width // tile :]
-
-        def step(n, carry, weight=weight, tile=tile, first=first):
+
+        def step(n, carry, weight=weight, first=first):
             at = pl.multiple_of(n * tile, tile)
+            if streams:
+                wait(n)
             total = jnp.dot(
                 rows[...], weight[:, pl.ds(at, tile)], preferred_element_type=jnp.float32
             )
@@ -138,28 +167,35 @@
 
         lax.fori_loop(0, width // tile, step, 0)
         first += width
-    wait_groups(groups)
-
-
-def head_matmul(info, came, head_weight, weights, height, out_type, firsts):
+
+
+def head_matmul(info, came, weights, height, out_type):
     count, depth = came.shape
-    wide = weights[0].shape[1]
-    width = wide * len(weights)
-    return pl.pallas_call(
-        functools.partial(head_body, height=height, held=len(weights), firsts=firsts),
-        in_specs=[pl.BlockSpec(memory_space=pltpu.SMEM), VMEM, ANY] + [VMEM] * len(weights),
-        out_specs=[VMEM] * (1 + len(firsts)),
-        out_shape=[jax.ShapeDtypeStruct((count, width), out_type)]
-        + [jax.ShapeDtypeStruct((depth, wide), head_weight.dtype)] * len(firsts),
-        scratch_shapes=[
-            pltpu.VMEM((count, depth), jnp.bfloat16),
-            group_sems(len(firsts), wide),
-        ],
-        compiler_params=pltpu.CompilerParams(vmem_limit_bytes=VMEM_LIMIT),
+    streams = not isinstance(weights, list)
+    if streams:
+        width = weights.shape[2]
+        weights, weight_spec = [weights], ANY
+    else:
+        width = sum(weight.shape[1] for weight in weights)
+        weight_spec = VMEM
+    tile = widest(512, width // 4)
+    scratch = [pltpu.VMEM((count, depth), jnp.bfloat16)]
+    if streams:
+        scratch.append(pltpu.VMEM((depth, width), jnp.bfloat16))
+        scratch.append(pltpu.SemaphoreType.DMA((width // tile, WAYS)))
+    return pl.pallas_call(
+        functools.partial(head_body, height=height, tile=tile, streams=streams),
+        in_specs=[pl.BlockSpec(memory_space=pltpu.SMEM), VMEM] + [weight_spec] * len(weights),
+        out_specs=VMEM,
+        out_shape=jax.ShapeDtypeStruct((count, width), out_type),
+        scratch_shapes=scratch,
+        compiler_params=pltpu.CompilerParams(
+            vmem_limit_bytes=HEAD_LIMIT if streams else VMEM_LIMIT
+        ),
         cost_estimate=pl.CostEstimate(
-            flops=2 * count * depth * width, bytes_accessed=count * width, transcendentals=0
+            flops=2 * count * depth * width, bytes_accessed=2 * depth * width, transcendentals=0
         ),
-    )(info, came, head_weight, *weights)
+    )(info, came, *weights)
 
 
 def encode(value):
@@ -207,68 +243,53 @@
     )(spots, *parts)
 
 
-def vocab_body(rows, *refs, order, tile, waits):
-    weights, (keep, send, powers) = refs[:WAYS], refs[WAYS + waits :]
-    step = pl.program_id(0)
-    share = rows.shape[1] // WAYS
-    total = None
-    for way in range(WAYS):
-        term = jnp.dot(
-            rows[:, way * share : (way + 1) * share],
-            weights[way][...],
-            preferred_element_type=jnp.float32,
-        )
-        total = term if total is None else total + term
+def vocab_body(rows, source, *refs, order, tile, first, waits):
+    keep, send, held, powers, sems = refs[waits:]
+    wait = stream(source, held, sems, first, tile)
     height = rows.shape[0] // len(order)
     half = len(order) // 2
-    sorted_rows = [total[g * height : (g + 1) * height] for g in order]
-    for spot, value in enumerate(sorted_rows[:half]):
-        keep[spot * height : (spot + 1) * height, :] = value
-    code, power = encode(jnp.concatenate(sorted_rows[half:], axis=0))
-    send[:, pl.ds(pl.multiple_of(step * tile, tile), tile)] = code
+    width = held.shape[1]
     lane = lax.broadcasted_iota(jnp.int32, powers.shape, 1)
-
-    @pl.when(step == 0)
-    def _():
-        powers[...] = jnp.where(lane == 0, power, jnp.zeros_like(powers))
-
-    @pl.when(step > 0)
-    def _():
-        powers[...] = jnp.where(lane == step, power, powers[...])
-
-    @pl.when(step == pl.num_programs(0) - 1)
-    def _():
-        send[:, send.shape[1] - LANES :] = powers[...].astype(jnp.int32).astype(jnp.int16)
+    powers[...] = jnp.zeros_like(powers)
+
+    def step(n, carry):
+        at = pl.ds(pl.multiple_of(n * tile, tile), tile)
+        wait(n)
+        total = jnp.dot(rows[...], held[:, at], preferred_element_type=jnp.float32)
+        sorted_rows = [total[g * height : (g + 1) * height] for g in order]
+        for spot, value in enumerate(sorted_rows[:half]):
+            keep[spot * height : (spot + 1) * height, at] = value
+        code, power = encode(jnp.concatenate(sorted_rows[half:], axis=0))
+        send[:, at] = code
+        powers[...] = jnp.where(lane == n, power, powers[...])
+        return carry
+
+    lax.fori_loop(0, width // tile, step, 0)
+    send[:, width:] = powers[...].astype(jnp.int32).astype(jnp.int16)
 
 
 def vocab_matmul(rows, vocab_weight, first, width, order, tile, after):
     depth = vocab_weight.shape[0]
     count = rows.shape[0]
     half = count // 2
-    base = first // tile
-    share = depth // WAYS
-    weight_specs = [
-        pl.BlockSpec((share, tile), functools.partial(lambda way, n: (way, base + n), way))
-        for way in range(WAYS)
-    ]
-    return pl.pallas_call(
-        functools.partial(vocab_body, order=order, tile=tile, waits=len(after)),
-        grid=(width // tile,),
-        in_specs=[VMEM] + weight_specs + [ANY] * len(after),
-        out_specs=[
-            pl.BlockSpec((half, tile), lambda n: (0, n)),
-            pl.BlockSpec((half, width + LANES), lambda n: (0, 0)),
-        ],
+    return pl.pallas_call(
+        functools.partial(vocab_body, order=order, tile=tile, first=first, waits=len(after)),
+        in_specs=[VMEM] + [ANY] * (1 + len(after)),
+        out_specs=[VMEM] * 2,
         out_shape=[
             jax.ShapeDtypeStruct((half, width), jnp.float32),
             jax.ShapeDtypeStruct((half, width + LANES), jnp.int16),
         ],
-        scratch_shapes=[pltpu.VMEM((half, LANES), jnp.float32)],
+        scratch_shapes=[
+            pltpu.VMEM((depth, width), jnp.bfloat16),
+            pltpu.VMEM((half, LANES), jnp.float32),
+            pltpu.SemaphoreType.DMA((width // tile, WAYS)),
+        ],
         compiler_params=pltpu.CompilerParams(vmem_limit_bytes=VOCAB_LIMIT),
         cost_estimate=pl.CostEstimate(
             flops=2 * count * depth * width, bytes_accessed=2 * depth * width, transcendentals=0
         ),
-    )(rows, *[vocab_weight] * WAYS, *after)
+    )(rows, vocab_weight, *after)
 
 
 def fold_body(keep, came, *refs, tile):
@@ -506,22 +527,15 @@
         for j in range(mp):
             perm.append((i * mp + j, (j * pieces + i % pieces) * mp + ((i // pieces) ^ j)))
     head_first = (1 - core).astype(jnp.int32).reshape(1)
-    head_then = core.astype(jnp.int32).reshape(1)
     part = feat // 2
     head_first = (1 - core).astype(jnp.int32).reshape(1)
-    head_then = core.astype(jnp.int32).reshape(1)
     part = feat // 4
     firsts = [part * i for i in range(4)]
     weights_first = fetch(head_first, head_weight, firsts, part, [sent], HEAD_LIMIT)
-    weights_then = []
     block = lax.ppermute(sent, ("batch", "mp"), perm)
     block, *weights_first = together(block, *weights_first)
     for bit in mp_bits:
-        came = swap(block, "mp", lambda i: i ^ bit)
-        if not weights_then:
-            fetched = fetch(head_then, head_weight, firsts[:2], part, [block], HEAD_LIMIT)
-            came, *weights_then = together(came, *fetched)
-        block = jnp.concatenate([block, came], axis=0)
+        block = jnp.concatenate([block, swap(block, "mp", lambda i: i ^ bit)], axis=0)
 
     square_sum = jnp.sum(chosen * chosen, axis=1, keepdims=True)
     for bit in mp_bits:
@@ -534,12 +548,9 @@
         source = (m ^ (unit // pieces) ^ (b // pieces)) * pieces + unit % pieces
         spots.append(((source // 2) ^ pair) * 2 + source % 2)
     info = jnp.stack([core] + spots).astype(jnp.int32)
-    send, *fetched = head_matmul(
-        info, block, head_weight, weights_first, rows, jnp.bfloat16, firsts[2:]
-    )
-    weights_then = list(weights_then) + fetched
+    send = head_matmul(info, block, weights_first, rows, jnp.bfloat16)
     came = swap(send, "batch", lambda i: i ^ 1)
-    (keep,) = head_matmul(info, block, head_weight, weights_then, rows, jnp.float32, [])
+    keep = head_matmul(info, block, head_weight, rows, jnp.float32)
     units = batch // 2
     share = feat // 2
     tall = 2 * rows
@@ -623,26 +634,30 @@
         keeps[block] = keep
         return send
 
+    def finish_blocks(group, earlier, after):
+        return finish(
+            wanted,
+            [(keeps[block], arrivals[block]) for block in group],
+            tile,
+            choices,
+            plan[group[0]][0],
+            vocab_width,
+            earlier,
+            after,
+        )
+
     begin(0, [])
     begin(1, [sends[0]])
     begin(2, [sends[1]])
     last = go_on(0, [sends[2]])
     begin(3, [last])
     last = go_on(1, [sends[3]])
-    begin(4, [last])
-    lasts = [go_on(block, [sends[4]]) for block in (2, 3, 4)]
-    joined = None
-    for group in (range(0, 3), range(3, 5)):
-        joined = finish(
-            wanted,
-            [(keeps[block], arrivals[block]) for block in group],
-            tile,
-            choices,
-            plan[group[0]][0],
-            vocab_width,
-            joined,
-            lasts[2:] if joined is None else [],
-        )
+    begin(4, [last, arrivals[0][-1], arrivals[2][0], arrivals[3][0]])
+    last = go_on(2, [sends[4]])
+    last = go_on(3, [last])
+    joined = finish_blocks((0, 1), None, [last])
+    go_on(4, [joined[1]])
+    joined = finish_blocks((2, 3, 4), joined, [])
     logits, stats = joined
 
     for bit in bits_of(batch):

time: 203 us -> 209 us (1.030)
  waiting for transfers between devices: 60.2 us -> 78.3 us
  Pallas kernels: 80.1 us -> 67.5 us
  local copies, waits for them, and re-layouts: 20.6 us -> 25.1 us
  starting transfers between devices: 36.8 us -> 32.9 us
    ppermute x29, waiting for transfers between devices: 60.2 us -> 78.3 us  [swap(): lax.ppermute(array, axis, [(i, partner(i)) for i in range(lax.axis_size(a...]
    unnamed x51 -> x59, local copies, waits for them, and re-layouts: 19.3 us -> 23.7 us
    ppermute x29, starting transfers between devices: 36.1 us -> 32.2 us  [swap(): lax.ppermute(array, axis, [(i, partner(i)) for i in range(lax.axis_size(a...]
    pallas_call x5, Pallas kernels: 9.5 us -> 5.74 us  [fold(): pl.pallas_call(functools.partial(fold_body, tile=tile), in_specs=[VMEM] *...]
    pallas_call x2 -> x1, Pallas kernels: 9.75 us -> 6.18 us  [fetch(): pl.pallas_call(functools.partial(fetch_body, firsts=firsts), in_specs=[pl...]
    pallas_call x7, Pallas kernels: 48.9 us -> 46.1 us  [the longest x5 34.6 us: vocab_matmul(): pl.pallas_call(functools.partial(vocab_body, order=order, tile=tile, firs...]
    pallas_call x2, Pallas kernels: 9.02 us -> 6.56 us  [finish(): pl.pallas_call(functools.partial(finish_body, tile=tile, choices=choices,...]
  transfers between devices with their start and end apart: 30 -> 30, of which waited for: 16 -> 18; matrix products, arithmetic and copies ran while one was open for 1% -> 1% of each run, Pallas kernels for 30% -> 20%
where the time goes in v6:
time: 209 us
  waiting for transfers between devices  78.3 us (37%)
  Pallas kernels  67.5 us (32%)
  starting transfers between devices  32.9 us (16%)
  local copies, waits for them, and re-layouts  25.1 us (12%)
  other arithmetic  3.48 us (2%)
    ppermute x29, waiting for transfers between devices, swap(): lax.ppermute(array, axis, [(i, partner(i)) for i in range(lax.axis_size(a...  78.3 us
    pallas_call x5, Pallas kernels, vocab_matmul(): pl.pallas_call(functools.partial(vocab_body, order=order, tile=tile, firs...  34.6 us
    ppermute x29, starting transfers between devices, swap(): lax.ppermute(array, axis, [(i, partner(i)) for i in range(lax.axis_size(a...  32.2 us
    unnamed x59, local copies, waits for them, and re-layouts  23.7 us
    pallas_call x2, Pallas kernels, head_matmul(): pl.pallas_call(functools.partial(head_body, height=height, tile=tile, str...  11.5 us
    pallas_call x2, Pallas kernels, finish(): pl.pallas_call(functools.partial(finish_body, tile=tile, choices=choices,...  6.56 us
    pallas_call x1, Pallas kernels, fetch(): pl.pallas_call(functools.partial(fetch_body, firsts=firsts), in_specs=[pl...  6.18 us
    pallas_call x5, Pallas kernels, fold(): pl.pallas_call(functools.partial(fold_body, tile=tile), in_specs=[VMEM] *...  5.74 us
  transfers between devices with their start and end apart: 30, of which 18 were waited for; matrix products, arithmetic and copies ran while one was open for 1% of the time, Pallas kernels for 20%

profile of v6, /device:TPU:0, one launch (start us, length us, event | category | flops | bytes accessed | tf_op | source)
XLA Modules:
  0.0 208.7 jit_solution(1080325577868814379)
XLA Ops:
  5.3 6.2 %shard_map.95 = (bf16[2048,1024]{1,0:T(8,128)(2,1)S(1)}, bf16[2048,1024]{1,0:T(8,128)(2,1)S(1)}, bf16[2048,1024]{1,0:T(8,128)(2,1)S(1)}, bf16[2048,1024]{1,0:T(8,128)(2,1)S(1)}) custom-call(s32[1]{0:T(128)} %bitcast.32.info, bf16[2,2048,4096]{2,1,0:T(8,128)(2,1)} %refs_0_.1, bf16[32,2048]{1,0:T(8,128)(2,1)S(1)} %multiply_convert_fusion.1.refs_0_), custom_call_target="tpu_custom_call" | custom-call | flops 5872025600 | tf_op jit(solution)/shard_map/pallas_call | solution.py:131
  15.5 2.1 copy-done.12
  19.5 5.7 %collective-permute-start.4 = (bf16[32,2048]{1,0:T(8,128)(2,1)S(1)}, bf16[32,2048]{1,0:T(8,128)(2,1)S(1)}, u32[]{:S(2)}, u32[]{:S(2)}) collective-permute-start(bf16[32,2048]{1,0:T(8,128)(2,1)S(1)} %collective-permute-done.3), channel_id=1, source_target_pairs={{0,1},{1,0},{2,3},{3,2},{4,5},{5,4},{6,7},{7,6},{8,9},{9,8},{10,11... | collective-permute-start | bytes 393224 | tf_op jit(solution)/shard_map/ppermute | solution.py:28
  25.2 3.4 %collective-permute-done.4 = bf16[32,2048]{1,0:T(8,128)(2,1)S(1)} collective-permute-done((bf16[32,2048]{1,0:T(8,128)(2,1)S(1)}, bf16[32,2048]{1,0:T(8,128)(2,1)S(1)}, u32[]{:S(2)}, u32[]{:S(2)}) %collective-permute-start.4) | collective-permute-done | bytes 131104 | tf_op jit(solution)/shard_map/ppermute | solution.py:28
  28.7 3.6 %collective-permute-start.5 = (bf16[64,2048]{1,0:T(8,128)(2,1)S(1)}, bf16[64,2048]{1,0:T(8,128)(2,1)S(1)}, u32[]{:S(2)}, u32[]{:S(2)}) collective-permute-start(bf16[64,2048]{1,0:T(8,128)(2,1)S(1)} %pad_maximum_fusion), channel_id=1, source_target_pairs={{0,2},{1,3},{2,0},{3,1},{4,6},{5,7},{6,4},{7,5},{8,10},{9,11},{10,... | collective-permute-start | bytes 786440 | tf_op jit(solution)/shard_map/ppermute | solution.py:28
  32.3 5.8 %collective-permute-done.5 = bf16[64,2048]{1,0:T(8,128)(2,1)S(1)} collective-permute-done((bf16[64,2048]{1,0:T(8,128)(2,1)S(1)}, bf16[64,2048]{1,0:T(8,128)(2,1)S(1)}, u32[]{:S(2)}, u32[]{:S(2)}) %collective-permute-start.5) | collective-permute-done | bytes 262176 | tf_op jit(solution)/shard_map/ppermute | solution.py:28
  38.1 2.2 %copy-done.9 = bf16[2048,1024]{1,0:T(8,128)(2,1)S(1)} copy-done((bf16[2048,1024]{1,0:T(8,128)(2,1)S(1)}, bf16[2048,1024]{1,0:T(8,128)(2,1)}, u32[]{:S(2)}) %copy-start.9) | copy-done | bytes 4194328
  40.3 2.2 %copy-done.11 = bf16[2048,1024]{1,0:T(8,128)(2,1)S(1)} copy-done((bf16[2048,1024]{1,0:T(8,128)(2,1)S(1)}, bf16[2048,1024]{1,0:T(8,128)(2,1)}, u32[]{:S(2)}) %copy-start.11) | copy-done | bytes 4194328
  42.5 2.2 %copy-done.13 = bf16[2048,1024]{1,0:T(8,128)(2,1)S(1)} copy-done((bf16[2048,1024]{1,0:T(8,128)(2,1)S(1)}, bf16[2048,1024]{1,0:T(8,128)(2,1)}, u32[]{:S(2)}) %copy-start.13) | copy-done | bytes 4194328
  44.7 2.2 %copy-done.15 = bf16[2048,1024]{1,0:T(8,128)(2,1)S(1)} copy-done((bf16[2048,1024]{1,0:T(8,128)(2,1)S(1)}, bf16[2048,1024]{1,0:T(8,128)(2,1)}, u32[]{:S(2)}) %copy-start.15) | copy-done | bytes 4194328
  46.9 4.3 %shard_map.97 = bf16[128,4096]{1,0:T(8,128)(2,1)S(1)} custom-call(s32[9]{0:T(128)S(1)} %stack.123.info, bf16[128,2048]{1,0:T(8,128)(2,1)S(1)} %constant_dynamic-update-slice_fusion.came, bf16[2048,1024]{1,0:T(8,128)(2,1)S(1)} %copy-done.9, bf16[2048,1024]{1,0:T(8,128)(2,1)S(1)} %copy-done.11, bf16[2048,1024]{1,0:T(8,128)(2,1)S(1)} %copy-done.13, ...), custom_call_target="tpu_custom_call" | custom-call | flops 2147483648 | bytes 16777216 | tf_op jit(solution)/shard_map/pallas_call | solution.py:186
  52.9 7.2 %shard_map.96 = f32[128,4096]{1,0:T(8,128)S(1)} custom-call(s32[9]{0:T(128)S(1)} %stack.123.info, bf16[128,2048]{1,0:T(8,128)(2,1)S(1)} %constant_dynamic-update-slice_fusion.came, bf16[2,2048,4096]{2,1,0:T(8,128)(2,1)} %refs_0_.1), custom_call_target="tpu_custom_call" | custom-call | flops 2147483648 | bytes 16777216 | tf_op jit(solution)/shard_map/pallas_call | solution.py:186
  63.6 10.1 %collective-permute-done.7 = bf16[64,2048]{1,0:T(8,128)(2,1)S(1)} collective-permute-done((bf16[64,2048]{1,0:T(8,128)(2,1)S(1)}, bf16[64,2048]{1,0:T(8,128)(2,1)S(1)}, u32[]{:S(2)}, u32[]{:S(2)}) %collective-permute-start.7) | collective-permute-done | bytes 262176 | tf_op jit(solution)/shard_map/ppermute | solution.py:28
  73.6 2.3 %collective-permute-done.9 = bf16[64,2048]{1,0:T(8,128)(2,1)S(1)} collective-permute-done((bf16[64,2048]{1,0:T(8,128)(2,1)S(1)}, bf16[64,2048]{1,0:T(8,128)(2,1)S(1)}, u32[]{:S(2)}, u32[]{:S(2)}) %collective-permute-start.9) | collective-permute-done | bytes 262176 | tf_op jit(solution)/shard_map/ppermute | solution.py:28
  76.1 2.1 collective-permute-start.8
  78.1 4.4 %collective-permute-done.10 = bf16[32,2048]{1,0:T(8,128)(2,1)S(1)} collective-permute-done((bf16[32,2048]{1,0:T(8,128)(2,1)S(1)}, bf16[32,2048]{1,0:T(8,128)(2,1)S(1)}, u32[]{:S(2)}, u32[]{:S(2)}) %collective-permute-start.10) | collective-permute-done | bytes 131104 | tf_op jit(solution)/shard_map/ppermute | solution.py:28
  87.1 4.8 %collective-permute-done.11 = bf16[32,2048]{1,0:T(8,128)(2,1)S(1)} collective-permute-done((bf16[32,2048]{1,0:T(8,128)(2,1)S(1)}, bf16[32,2048]{1,0:T(8,128)(2,1)S(1)}, u32[]{:S(2)}, u32[]{:S(2)}) %collective-permute-start.11) | collective-permute-done | bytes 131104 | tf_op jit(solution)/shard_map/ppermute | solution.py:28
  94.5 7.6 %collective-permute-done.13 = bf16[64,2048]{1,0:T(8,128)(2,1)S(1)} collective-permute-done((bf16[64,2048]{1,0:T(8,128)(2,1)S(1)}, bf16[64,2048]{1,0:T(8,128)(2,1)S(1)}, u32[]{:S(2)}, u32[]{:S(2)}) %collective-permute-start.13) | collective-permute-done | bytes 262176 | tf_op jit(solution)/shard_map/ppermute | solution.py:28
  102.1 2.7 %collective-permute-done.14 = bf16[64,2048]{1,0:T(8,128)(2,1)S(1)} collective-permute-done((bf16[64,2048]{1,0:T(8,128)(2,1)S(1)}, bf16[64,2048]{1,0:T(8,128)(2,1)S(1)}, u32[]{:S(2)}, u32[]{:S(2)}) %collective-permute-start.14) | collective-permute-done | bytes 262176 | tf_op jit(solution)/shard_map/ppermute | solution.py:28
  107.5 7.9 %shard_map.99 = (f32[128,2048]{1,0:T(8,128)S(1)}, s16[128,2176]{1,0:T(8,128)(2,1)S(1)}) custom-call(bf16[256,4096]{1,0:T(8,128)(2,1)S(1)} %shard_map.98.rows, bf16[4096,8192]{1,0:T(8,128)(2,1)} %source.9), custom_call_target="tpu_custom_call" | custom-call | flops 4294967296 | bytes 16777216 | tf_op jit(solution)/shard_map/pallas_call | solution.py:275
  116.3 7.9 %shard_map.100 = (f32[128,2048]{1,0:T(8,128)S(1)}, s16[128,2176]{1,0:T(8,128)(2,1)S(1)}) custom-call(bf16[256,4096]{1,0:T(8,128)(2,1)S(1)} %shard_map.98.rows, bf16[4096,8192]{1,0:T(8,128)(2,1)} %source.9, s16[128,2176]{1,0:T(8,128)(2,1)S(1)} %get-tuple-element.34.refs_0_), custom_call_target="tpu_custom_call" | custom-call | flops 4294967296 | bytes 16777216 | tf_op jit(solution)/shard_map/pallas_call | solution.py:275
  125.6 7.9 %shard_map.101 = (f32[128,2048]{1,0:T(8,128)S(1)}, s16[128,2176]{1,0:T(8,128)(2,1)S(1)}) custom-call(bf16[256,4096]{1,0:T(8,128)(2,1)S(1)} %shard_map.98.rows, bf16[4096,8192]{1,0:T(8,128)(2,1)} %source.9, s16[128,2176]{1,0:T(8,128)(2,1)S(1)} %get-tuple-element.35.refs_0_), custom_call_target="tpu_custom_call" | custom-call | flops 4294967296 | bytes 16777216 | tf_op jit(solution)/shard_map/pallas_call | solution.py:275
  136.0 5.1 %shard_map.103 = (f32[128,1024]{1,0:T(8,128)S(1)}, s16[128,1152]{1,0:T(8,128)(2,1)S(1)}) custom-call(bf16[256,4096]{1,0:T(8,128)(2,1)S(1)} %shard_map.98.rows, bf16[4096,8192]{1,0:T(8,128)(2,1)} %source.9, s16[64,2176]{1,0:T(8,128)(2,1)S(1)} %shard_map.102.refs_0_), custom_call_target="tpu_custom_call" | custom-call | flops 2147483648 | bytes 8388608 | tf_op jit(solution)/shard_map/pallas_call | solution.py:275
  144.8 2.9 %collective-permute-done.17.refs_2_.came.refs_1_ = s16[128,2176]{1,0:T(8,128)(2,1)S(1)} collective-permute-done((s16[128,2176]{1,0:T(8,128)(2,1)S(1)}, s16[128,2176]{1,0:T(8,128)(2,1)S(1)}, u32[]{:S(2)}, u32[]{:S(2)}) %collective-permute-start.17) | collective-permute-done | bytes 557088 | tf_op jit(solution)/shard_map/ppermute | solution.py:28
  147.8 7.6 %collective-permute-done.20.refs_1_.refs_2_ = s16[64,2176]{1,0:T(8,128)(2,1)S(1)} collective-permute-done((s16[64,2176]{1,0:T(8,128)(2,1)S(1)}, s16[64,2176]{1,0:T(8,128)(2,1)S(1)}, u32[]{:S(2)}, u32[]{:S(2)}) %collective-permute-start.20) | collective-permute-done | bytes 278560 | tf_op jit(solution)/shard_map/ppermute | solution.py:28
  155.4 5.8 %shard_map.105 = (f32[128,1024]{1,0:T(8,128)S(1)}, s16[128,1152]{1,0:T(8,128)(2,1)}) custom-call(bf16[256,4096]{1,0:T(8,128)(2,1)S(1)} %shard_map.98.rows, bf16[4096,8192]{1,0:T(8,128)(2,1)} %source.9, s16[64,2176]{1,0:T(8,128)(2,1)} %shard_map.104.refs_0_, s16[64,2176]{1,0:T(8,128)(2,1)S(1)} %collective-permute-done.20.refs_1_.refs_2_, ...), custom_call_target="tpu_custom_call" | custom-call | flops 2147483648 | bytes 8388608 | tf_op jit(solution)/shard_map/pallas_call | solution.py:275
  167.5 9.6 %collective-permute-done.25.refs_5_ = s16[64,2176]{1,0:T(8,128)(2,1)S(1)} collective-permute-done((s16[64,2176]{1,0:T(8,128)(2,1)}, s16[64,2176]{1,0:T(8,128)(2,1)S(1)}, u32[]{:S(2)}, u32[]{:S(2)}) %collective-permute-start.25) | collective-permute-done | bytes 278560 | tf_op jit(solution)/shard_map/ppermute | solution.py:28
  183.2 2.8 %shard_map.108 = (f32[64,8192]{1,0:T(8,128)S(1)}, f32[64,128]{1,0:T(8,128)S(1)}) custom-call(s32[64,128]{1,0:T(8,128)S(1)} %pad.4.wanted, f32[128,2048]{1,0:T(8,128)S(1)} %copy-done.3, s16[128,2176]{1,0:T(8,128)(2,1)S(1)} %collective-permute-done.19.came.refs_1_, s16[64,2176]{1,0:T(8,128)(2,1)S(1)} %copy-done.23, f32[128,2048]{1,0:T(8,128)S(1)} %copy-done.7, ...), custom_call_target="tpu_custom_call" | custom-call | tf_op jit(solution)/shard_map/pallas_call | solution.py:416
  188.3 4.2 %collective-permute-done.26.refs_8_ = s16[64,1152]{1,0:T(8,128)(2,1)S(1)} collective-permute-done((s16[64,1152]{1,0:T(8,128)(2,1)S(1)}, s16[64,1152]{1,0:T(8,128)(2,1)S(1)}, u32[]{:S(2)}, u32[]{:S(2)}) %collective-permute-start.26) | collective-permute-done | bytes 147488 | tf_op jit(solution)/shard_map/ppermute | solution.py:28
  192.5 3.8 %shard_map.110 = (f32[64,8192]{1,0:T(8,128)S(1)}, f32[64,128]{1,0:T(8,128)S(1)}) custom-call(s32[64,128]{1,0:T(8,128)S(1)} %pad.4.wanted, f32[128,2048]{1,0:T(8,128)S(1)} %copy-done.5, s16[128,2176]{1,0:T(8,128)(2,1)S(1)} %collective-permute-done.17.refs_2_.came.refs_1_, ...), custom_call_target="tpu_custom_call", output_to_operand_aliasing={{0}: (11, {})} | custom-call | tf_op jit(solution)/shard_map/pallas_call | solution.py:416
  197.8 3.9 %collective-permute-done.28.came = f32[64,128]{1,0:T(8,128)S(1)} collective-permute-done((f32[64,128]{1,0:T(8,128)S(1)}, f32[64,128]{1,0:T(8,128)S(1)}, u32[]{:S(2)}, u32[]{:S(2)}) %collective-permute-start.28) | collective-permute-done | bytes 32800 | tf_op jit(solution)/shard_map/ppermute | solution.py:28
  202.4 4.3 %collective-permute-done.29.came = f32[64,128]{1,0:T(8,128)S(1)} collective-permute-done((f32[64,128]{1,0:T(8,128)S(1)}, f32[64,128]{1,0:T(8,128)S(1)}, u32[]{:S(2)}, u32[]{:S(2)}) %collective-permute-start.29) | collective-permute-done | bytes 32800 | tf_op jit(solution)/shard_map/ppermute | solution.py:28
  (138 shorter events, 52.7 us)
Async XLA Ops:
  0.6 62.1 %copy-start = (f32[2,4096]{1,0:T(2,128)S(1)}, f32[2,4096]{1,0:T(2,128)}, u32[]{:S(2)}) copy-start(f32[2,4096]{1,0:T(2,128)} %param.12) | copy-start | bytes 98308
  3.0 1.5 collective-permute-start
  4.6 14.9 %collective-permute-start.3 = (bf16[32,2048]{1,0:T(8,128)(2,1)S(1)}, bf16[32,2048]{1,0:T(8,128)(2,1)S(1)}, u32[]{:S(2)}, u32[]{:S(2)}) collective-permute-start(bf16[32,2048]{1,0:T(8,128)(2,1)S(1)} %multiply_convert_fusion.1.refs_0_), channel_id=1, source_target_pairs={{0,0},{1,9},{2,18},{3,27},{4,4},{5,13},{6,22},{7,31},{8,1},{9,8},{... | collective-permute-start | bytes 393224 | tf_op jit(solution)/shard_map/ppermute | solution.py:535
  19.5 9.2 %collective-permute-start.4 = (bf16[32,2048]{1,0:T(8,128)(2,1)S(1)}, bf16[32,2048]{1,0:T(8,128)(2,1)S(1)}, u32[]{:S(2)}, u32[]{:S(2)}) collective-permute-start(bf16[32,2048]{1,0:T(8,128)(2,1)S(1)} %collective-permute-done.3), channel_id=1, source_target_pairs={{0,1},{1,0},{2,3},{3,2},{4,5},{5,4},{6,7},{7,6},{8,9},{9,8},{10,11... | collective-permute-start | bytes 393224 | tf_op jit(solution)/shard_map/ppermute | solution.py:28
  28.7 9.4 %collective-permute-start.5 = (bf16[64,2048]{1,0:T(8,128)(2,1)S(1)}, bf16[64,2048]{1,0:T(8,128)(2,1)S(1)}, u32[]{:S(2)}, u32[]{:S(2)}) collective-permute-start(bf16[64,2048]{1,0:T(8,128)(2,1)S(1)} %pad_maximum_fusion), channel_id=1, source_target_pairs={{0,2},{1,3},{2,0},{3,1},{4,6},{5,7},{6,4},{7,5},{8,10},{9,11},{10,... | collective-permute-start | bytes 786440 | tf_op jit(solution)/shard_map/ppermute | solution.py:28
  51.2 8.9 %collective-permute-start.6 = (bf16[128,4096]{1,0:T(8,128)(2,1)S(1)}, bf16[128,4096]{1,0:T(8,128)(2,1)S(1)}, u32[]{:S(2)}, u32[]{:S(2)}) collective-permute-start(bf16[128,4096]{1,0:T(8,128)(2,1)S(1)} %shard_map.97), channel_id=1, source_target_pairs={{0,4},{4,0},{8,12},{12,8},{16,20},{20,16},{24,28},{28,24},{1,5},{5... | collective-permute-start | bytes 3145736 | tf_op jit(solution)/shard_map/ppermute | solution.py:28
  51.4 11.3 %collective-permute-start.1 = (f32[32,1]{0,1:T(1,128)S(1)}, f32[32,1]{0,1:T(1,128)S(1)}, u32[]{:S(2)}, u32[]{:S(2)}) collective-permute-start(f32[32,1]{0,1:T(1,128)S(1)} %bitcast.43), channel_id=1, source_target_pairs={{0,1},{1,0},{2,3},{3,2},{4,5},{5,4},{6,7},{7,6},{8,9},{9,8},{10,11... | collective-permute-start | bytes 392 | tf_op jit(solution)/shard_map/ppermute | solution.py:28
  60.6 13.0 %collective-permute-start.7 = (bf16[64,2048]{1,0:T(8,128)(2,1)S(1)}, bf16[64,2048]{1,0:T(8,128)(2,1)S(1)}, u32[]{:S(2)}, u32[]{:S(2)}) collective-permute-start(bf16[64,2048]{1,0:T(8,128)(2,1)S(1)} %pad_maximum_fusion.1), channel_id=1, source_target_pairs={{0,8},{4,12},{8,0},{12,4},{16,24},{20,28},{24,16},{28,20},{1,9},{5... | collective-permute-start | bytes 786440 | tf_op jit(solution)/shard_map/ppermute | solution.py:28
  61.2 14.7 %collective-permute-start.9 = (bf16[64,2048]{1,0:T(8,128)(2,1)S(1)}, bf16[64,2048]{1,0:T(8,128)(2,1)S(1)}, u32[]{:S(2)}, u32[]{:S(2)}) collective-permute-start(bf16[64,2048]{1,0:T(8,128)(2,1)S(1)} %concatenate.38), channel_id=1, source_target_pairs={{0,16},{4,20},{8,24},{12,28},{16,0},{20,4},{24,8},{28,12},{1,17},{... | collective-permute-start | bytes 786440 | tf_op jit(solution)/shard_map/ppermute | solution.py:28
  62.8 15.4 %collective-permute-start.2 = (f32[32,1]{0,1:T(1,128)S(1)}, f32[32,1]{0,1:T(1,128)S(1)}, u32[]{:S(2)}, u32[]{:S(2)}) collective-permute-start(f32[32,1]{0,1:T(1,128)S(1)} %bitcast_add_fusion), channel_id=1, source_target_pairs={{0,2},{1,3},{2,0},{3,1},{4,6},{5,7},{6,4},{7,5},{8,10},{9,11},{10,... | collective-permute-start | bytes 392 | tf_op jit(solution)/shard_map/ppermute | solution.py:28
  76.0 6.6 %collective-permute-start.10 = (bf16[32,2048]{1,0:T(8,128)(2,1)S(1)}, bf16[32,2048]{1,0:T(8,128)(2,1)S(1)}, u32[]{:S(2)}, u32[]{:S(2)}) collective-permute-start(bf16[32,2048]{1,0:T(8,128)(2,1)S(1)} %get-tuple-element.53), channel_id=1, source_target_pairs={{0,8},{4,12},{8,0},{12,4},{16,24},{20,28},{24,16},{28,20},{1,9},{5... | collective-permute-start | bytes 393224 | tf_op jit(solution)/shard_map/ppermute | solution.py:28
  76.1 8.3 %collective-permute-start.8 = (bf16[32,2048]{1,0:T(8,128)(2,1)S(1)}, bf16[32,2048]{1,0:T(8,128)(2,1)S(1)}, u32[]{:S(2)}, u32[]{:S(2)}) collective-permute-start(bf16[32,2048]{1,0:T(8,128)(2,1)S(1)} %get-tuple-element.52), channel_id=1, source_target_pairs={{0,16},{4,20},{8,24},{12,28},{16,0},{20,4},{24,8},{28,12},{1,17},{... | collective-permute-start | bytes 393224 | tf_op jit(solution)/shard_map/ppermute | solution.py:28
  84.8 7.1 %collective-permute-start.11 = (bf16[32,2048]{1,0:T(8,128)(2,1)S(1)}, bf16[32,2048]{1,0:T(8,128)(2,1)S(1)}, u32[]{:S(2)}, u32[]{:S(2)}) collective-permute-start(bf16[32,2048]{1,0:T(8,128)(2,1)S(1)} %get-tuple-element.58), channel_id=1, source_target_pairs={{0,16},{4,20},{8,24},{12,28},{16,0},{20,4},{24,8},{28,12},{1,17},{... | collective-permute-start | bytes 393224 | tf_op jit(solution)/shard_map/ppermute | solution.py:28
  85.0 6.9 %collective-permute-start.12 = (bf16[32,2048]{1,0:T(8,128)(2,1)S(1)}, bf16[32,2048]{1,0:T(8,128)(2,1)S(1)}, u32[]{:S(2)}, u32[]{:S(2)}) collective-permute-start(bf16[32,2048]{1,0:T(8,128)(2,1)S(1)} %get-tuple-element.59), channel_id=1, source_target_pairs={{0,8},{4,12},{8,0},{12,4},{16,24},{20,28},{24,16},{28,20},{1,9},{5... | collective-permute-start | bytes 393224 | tf_op jit(solution)/shard_map/ppermute | solution.py:28
  92.0 10.1 %collective-permute-start.13 = (bf16[64,2048]{1,0:T(8,128)(2,1)S(1)}, bf16[64,2048]{1,0:T(8,128)(2,1)S(1)}, u32[]{:S(2)}, u32[]{:S(2)}) collective-permute-start(bf16[64,2048]{1,0:T(8,128)(2,1)S(1)} %get-tuple-element.57), channel_id=1, source_target_pairs={{0,8},{4,12},{8,0},{12,4},{16,24},{20,28},{24,16},{28,20},{1,9},{5... | collective-permute-start | bytes 786440 | tf_op jit(solution)/shard_map/ppermute | solution.py:28
  93.0 11.8 %collective-permute-start.14 = (bf16[64,2048]{1,0:T(8,128)(2,1)S(1)}, bf16[64,2048]{1,0:T(8,128)(2,1)S(1)}, u32[]{:S(2)}, u32[]{:S(2)}) collective-permute-start(bf16[64,2048]{1,0:T(8,128)(2,1)S(1)} %get-tuple-element.56), channel_id=1, source_target_pairs={{0,16},{4,20},{8,24},{12,28},{16,0},{20,4},{24,8},{28,12},{1,17},{... | collective-permute-start | bytes 786440 | tf_op jit(solution)/shard_map/ppermute | solution.py:28
  94.5 10.8 %collective-permute-start.15 = (bf16[64,4096]{1,0:T(8,128)(2,1)S(1)}, bf16[64,4096]{1,0:T(8,128)(2,1)S(1)}, u32[]{:S(2)}, u32[]{:S(2)}) collective-permute-start(bf16[64,4096]{1,0:T(8,128)(2,1)S(1)} %maximum_maximum_fusion.refs_0_), channel_id=1, source_target_pairs={{0,4},{4,0},{8,12},{12,8},{16,20},{20,16},{24,28},{28,24},{1,5},{5... | collective-permute-start | bytes 1572872 | tf_op jit(solution)/shard_map/ppermute | solution.py:28
  104.8 2.0 collective-permute-start.16
  115.4 19.8 %collective-permute-start.19 = (s16[128,2176]{1,0:T(8,128)(2,1)S(1)}, s16[128,2176]{1,0:T(8,128)(2,1)S(1)}, u32[]{:S(2)}, u32[]{:S(2)}) collective-permute-start(s16[128,2176]{1,0:T(8,128)(2,1)S(1)} %get-tuple-element.34.refs_0_), channel_id=1, source_target_pairs={{0,1},{1,0},{2,3},{3,2},{4,5},{5,4},{6,7},{7,6},{8,9},{9,8},{10,11... | collective-permute-start | bytes 1671176 | tf_op jit(solution)/shard_map/ppermute | solution.py:28
  124.2 19.0 %collective-permute-start.18 = (s16[128,2176]{1,0:T(8,128)(2,1)S(1)}, s16[128,2176]{1,0:T(8,128)(2,1)S(1)}, u32[]{:S(2)}, u32[]{:S(2)}) collective-permute-start(s16[128,2176]{1,0:T(8,128)(2,1)S(1)} %get-tuple-element.35.refs_0_), channel_id=1, source_target_pairs={{0,2},{1,3},{2,0},{3,1},{4,6},{5,7},{6,4},{7,5},{8,10},{9,11},{10,... | collective-permute-start | bytes 1671176 | tf_op jit(solution)/shard_map/ppermute | solution.py:28
  133.5 30.6 %copy-start.4 = (f32[128,2048]{1,0:T(8,128)}, f32[128,2048]{1,0:T(8,128)S(1)}, u32[]{:S(2)}) copy-start(f32[128,2048]{1,0:T(8,128)S(1)} %get-tuple-element.36.keep.refs_0_) | copy-start | bytes 3145732
  133.5 14.3 %collective-permute-start.17 = (s16[128,2176]{1,0:T(8,128)(2,1)S(1)}, s16[128,2176]{1,0:T(8,128)(2,1)S(1)}, u32[]{:S(2)}, u32[]{:S(2)}) collective-permute-start(s16[128,2176]{1,0:T(8,128)(2,1)S(1)} %get-tuple-element.37.refs_0_), channel_id=1, source_target_pairs={{0,1},{1,0},{2,3},{3,2},{4,5},{5,4},{6,7},{7,6},{8,9},{9,8},{10,11... | collective-permute-start | bytes 1671176 | tf_op jit(solution)/shard_map/ppermute | solution.py:28
  141.1 14.2 %collective-permute-start.21 = (s16[128,1152]{1,0:T(8,128)(2,1)S(1)}, s16[128,1152]{1,0:T(8,128)(2,1)S(1)}, u32[]{:S(2)}, u32[]{:S(2)}) collective-permute-start(s16[128,1152]{1,0:T(8,128)(2,1)S(1)} %get-tuple-element.40.refs_0_), channel_id=1, source_target_pairs={{0,2},{1,3},{2,0},{3,1},{4,6},{5,7},{6,4},{7,5},{8,10},{9,11},{10,... | collective-permute-start | bytes 884744 | tf_op jit(solution)/shard_map/ppermute | solution.py:28
  141.5 13.9 %collective-permute-start.20 = (s16[64,2176]{1,0:T(8,128)(2,1)S(1)}, s16[64,2176]{1,0:T(8,128)(2,1)S(1)}, u32[]{:S(2)}, u32[]{:S(2)}) collective-permute-start(s16[64,2176]{1,0:T(8,128)(2,1)S(1)} %shard_map.102.refs_0_), channel_id=1, source_target_pairs={{0,2},{1,3},{2,0},{3,1},{4,6},{5,7},{6,4},{7,5},{8,10},{9,11},{10,... | collective-permute-start | bytes 835592 | tf_op jit(solution)/shard_map/ppermute | solution.py:28
  162.0 23.9 %collective-permute-start.24 = (s16[128,1152]{1,0:T(8,128)(2,1)}, s16[128,1152]{1,0:T(8,128)(2,1)}, u32[]{:S(2)}, u32[]{:S(2)}) collective-permute-start(s16[128,1152]{1,0:T(8,128)(2,1)} %get-tuple-element.41.refs_0_), channel_id=1, source_target_pairs={{0,1},{1,0},{2,3},{3,2},{4,5},{5,4},{6,7},{7,6},{8,9},{9,8},{10,11... | collective-permute-start | bytes 884744 | tf_op jit(solution)/shard_map/ppermute | solution.py:28
  162.6 14.5 %collective-permute-start.25 = (s16[64,2176]{1,0:T(8,128)(2,1)}, s16[64,2176]{1,0:T(8,128)(2,1)S(1)}, u32[]{:S(2)}, u32[]{:S(2)}) collective-permute-start(s16[64,2176]{1,0:T(8,128)(2,1)} %shard_map.104.refs_0_), channel_id=1, source_target_pairs={{0,1},{1,0},{2,3},{3,2},{4,5},{5,4},{6,7},{7,6},{8,9},{9,8},{10,11... | collective-permute-start | bytes 835592 | tf_op jit(solution)/shard_map/ppermute | solution.py:28
  165.7 22.6 %collective-permute-start.22 = (s16[64,2176]{1,0:T(8,128)(2,1)}, s16[64,2176]{1,0:T(8,128)(2,1)}, u32[]{:S(2)}, u32[]{:S(2)}) collective-permute-start(s16[64,2176]{1,0:T(8,128)(2,1)} %shard_map.106.refs_0_), channel_id=1, source_target_pairs={{0,2},{1,3},{2,0},{3,1},{4,6},{5,7},{6,4},{7,5},{8,10},{9,11},{10,... | collective-permute-start | bytes 835592 | tf_op jit(solution)/shard_map/ppermute | solution.py:28
  166.9 21.4 %collective-permute-start.23 = (s16[64,1152]{1,0:T(8,128)(2,1)S(1)}, s16[64,1152]{1,0:T(8,128)(2,1)S(1)}, u32[]{:S(2)}, u32[]{:S(2)}) collective-permute-start(s16[64,1152]{1,0:T(8,128)(2,1)S(1)} %shard_map.107.refs_6_), channel_id=1, source_target_pairs={{0,1},{1,0},{2,3},{3,2},{4,5},{5,4},{6,7},{7,6},{8,9},{9,8},{10,11... | collective-permute-start | bytes 442376 | tf_op jit(solution)/shard_map/ppermute | solution.py:28
  187.3 5.2 %collective-permute-start.26 = (s16[64,1152]{1,0:T(8,128)(2,1)S(1)}, s16[64,1152]{1,0:T(8,128)(2,1)S(1)}, u32[]{:S(2)}, u32[]{:S(2)}) collective-permute-start(s16[64,1152]{1,0:T(8,128)(2,1)S(1)} %shard_map.109), channel_id=1, source_target_pairs={{0,2},{1,3},{2,0},{3,1},{4,6},{5,7},{6,4},{7,5},{8,10},{9,11},{10,... | collective-permute-start | bytes 442376 | tf_op jit(solution)/shard_map/ppermute | solution.py:28
  196.3 1.3 collective-permute-start.27
  197.7 4.0 %collective-permute-start.28 = (f32[64,128]{1,0:T(8,128)S(1)}, f32[64,128]{1,0:T(8,128)S(1)}, u32[]{:S(2)}, u32[]{:S(2)}) collective-permute-start(f32[64,128]{1,0:T(8,128)S(1)} %shard_map.111.own), channel_id=1, source_target_pairs={{0,8},{4,12},{8,0},{12,4},{16,24},{20,28},{24,16},{28,20},{1,9},{5... | collective-permute-start | bytes 98312 | tf_op jit(solution)/shard_map/ppermute | solution.py:28
  201.8 4.9 %collective-permute-start.29 = (f32[64,128]{1,0:T(8,128)S(1)}, f32[64,128]{1,0:T(8,128)S(1)}, u32[]{:S(2)}, u32[]{:S(2)}) collective-permute-start(f32[64,128]{1,0:T(8,128)S(1)} %shard_map.112.own), channel_id=1, source_target_pairs={{0,16},{4,20},{8,24},{12,28},{16,0},{20,4},{24,8},{28,12},{1,17},{... | collective-permute-start | bytes 98312 | tf_op jit(solution)/shard_map/ppermute | solution.py:28
  (27 other events, 208.4 us)

commit v7 on v6

--- a/solution.py
+++ b/solution.py
@@ -12,12 +12,8 @@
 LANES = 128
 CODE_BITS = 14
 VMEM_LIMIT = 4 * MIB
-HEAD_LIMIT = 24 * MIB
 VOCAB_LIMIT = 24 * MIB
-
-
-def together(*arrays):
-    return lax.optimization_barrier(arrays)
+FINISH_LIMIT = 10 * MIB
 
 
 def bits_of(count):
@@ -52,29 +48,7 @@
 VMEM = pl.BlockSpec(memory_space=pltpu.VMEM)
 ANY = pl.BlockSpec(memory_space=pl.ANY)
 WAYS = 4
-
-
-def copy_groups(source, targets, sems, firsts):
-    groups = []
-    for index, target in enumerate(targets):
-        depth, width = target.shape
-        share, tile = depth // WAYS, widest(512, width)
-        for step in range(width // tile):
-            groups.append(
-                [
-                    pltpu.make_async_copy(
-                        source.at[pl.ds(way * share, share), pl.ds(firsts[index] + step * tile, tile)],
-                        target.at[pl.ds(way * share, share), pl.ds(step * tile, tile)],
-                        sems.at[index, step, way],
-                    )
-                    for way in range(WAYS)
-                ]
-            )
-    return groups
-
-
-def group_sems(count, width):
-    return pltpu.SemaphoreType.DMA((max(1, count), width // widest(512, width), WAYS))
+UNIT_COST = pl.CostEstimate(flops=1, bytes_accessed=1, transcendentals=0)
 
 
 def stream(source, held, sems, first, tile):
@@ -106,96 +80,39 @@
     return wait
 
 
-def start_group(group):
-    for copy in group:
-        copy.start()
-
-
-def wait_groups(groups):
-    for group in groups:
-        for copy in group:
-            copy.wait()
-
-
-def fetch_body(info, weight, *refs, firsts):
-    targets, sems = refs[-1 - len(firsts) : -1], refs[-1]
-    source = weight.at[info[0]] if len(weight.shape) == 3 else weight
-    groups = copy_groups(source, targets, sems, firsts)
-    for group in groups:
-        start_group(group)
-    wait_groups(groups)
-
-
-def fetch(info, weight, firsts, width, after, limit=VMEM_LIMIT):
-    depth = weight.shape[-2]
-    return pl.pallas_call(
-        functools.partial(fetch_body, firsts=firsts),
-        in_specs=[pl.BlockSpec(memory_space=pltpu.SMEM), ANY] + [ANY] * len(after),
-        out_specs=[VMEM] * len(firsts),
-        out_shape=[jax.ShapeDtypeStruct((depth, width), weight.dtype)] * len(firsts),
-        scratch_shapes=[group_sems(len(firsts), width)],
-        compiler_params=pltpu.CompilerParams(vmem_limit_bytes=limit),
-        cost_estimate=pl.CostEstimate(
-            flops=700 * depth * width * len(firsts), bytes_accessed=0, transcendentals=0
-        ),
-    )(info, weight, *after)
-
-
-def head_body(info, came, *refs, height, tile, streams):
-    if streams:
-        source, out, rows, held, sems = refs
-        wait = stream(source.at[info[0]], held, sems, 0, tile)
-        weights = [held]
-    else:
-        weights, (out, rows) = refs[:-2], refs[-2:]
+def head_body(info, came, source, out, rows, held, sems, *, height, tile):
+    wait = stream(source.at[info[0]], held, sems, 0, tile)
     for unit in range(came.shape[0] // height):
         start = pl.multiple_of(info[1 + unit] * height, height)
         rows[pl.ds(start, height), :] = came[unit * height : (unit + 1) * height, :]
-    first = 0
-    for weight in weights:
-        width = weight.shape[1]
-
-        def step(n, carry, weight=weight, first=first):
-            at = pl.multiple_of(n * tile, tile)
-            if streams:
-                wait(n)
-            total = jnp.dot(
-                rows[...], weight[:, pl.ds(at, tile)], preferred_element_type=jnp.float32
-            )
-            out[:, pl.ds(pl.multiple_of(first + at, tile), tile)] = total.astype(out.dtype)
-            return carry
-
-        lax.fori_loop(0, width // tile, step, 0)
-        first += width
-
-
-def head_matmul(info, came, weights, height, out_type):
+
+    def step(n, carry):
+        at = pl.ds(pl.multiple_of(n * tile, tile), tile)
+        wait(n)
+        total = jnp.dot(rows[...], held[:, at], preferred_element_type=jnp.float32)
+        out[:, at] = total.astype(out.dtype)
+        return carry
+
+    lax.fori_loop(0, held.shape[1] // tile, step, 0)
+
+
+def head_matmul(info, came, head_weight, height, out_type):
     count, depth = came.shape
-    streams = not isinstance(weights, list)
-    if streams:
-        width = weights.shape[2]
-        weights, weight_spec = [weights], ANY
-    else:
-        width = sum(weight.shape[1] for weight in weights)
-        weight_spec = VMEM
-    tile = widest(512, width // 4)
-    scratch = [pltpu.VMEM((count, depth), jnp.bfloat16)]
-    if streams:
-        scratch.append(pltpu.VMEM((depth, width), jnp.bfloat16))
-        scratch.append(pltpu.SemaphoreType.DMA((width // tile, WAYS)))
-    return pl.pallas_call(
-        functools.partial(head_body, height=height, tile=tile, streams=streams),
-        in_specs=[pl.BlockSpec(memory_space=pltpu.SMEM), VMEM] + [weight_spec] * len(weights),
+    width = head_weight.shape[2]
+    tile = widest(512, width // 2)
+    return pl.pallas_call(
+        functools.partial(head_body, height=height, tile=tile),
+        in_specs=[pl.BlockSpec(memory_space=pltpu.SMEM), VMEM, ANY],
         out_specs=VMEM,
         out_shape=jax.ShapeDtypeStruct((count, width), out_type),
-        scratch_shapes=scratch,
-        compiler_params=pltpu.CompilerParams(
-            vmem_limit_bytes=HEAD_LIMIT if streams else VMEM_LIMIT
-        ),
-        cost_estimate=pl.CostEstimate(
-            flops=2 * count * depth * width, bytes_accessed=2 * depth * width, transcendentals=0
-        ),
-    )(info, came, *weights)
+        scratch_shapes=[
+            pltpu.VMEM((count, depth), jnp.bfloat16),
+            pltpu.VMEM((depth, width), jnp.bfloat16),
+            pltpu.SemaphoreType.DMA((width // tile, WAYS)),
+        ],
+        cost_estimate=UNIT_COST,
+        compiler_params=pltpu.CompilerParams(vmem_limit_bytes=VOCAB_LIMIT),
+    )(info, came, head_weight)
 
 
 def encode(value):
@@ -239,6 +156,7 @@
         in_specs=[pl.BlockSpec(memory_space=pltpu.SMEM)] + [VMEM] * len(parts),
         out_specs=VMEM,
         out_shape=jax.ShapeDtypeStruct((count, parts[0].shape[1]), parts[0].dtype),
+        cost_estimate=UNIT_COST,
         compiler_params=pltpu.CompilerParams(vmem_limit_bytes=VMEM_LIMIT),
     )(spots, *parts)
 
@@ -286,9 +204,7 @@
             pltpu.SemaphoreType.DMA((width // tile, WAYS)),
         ],
         compiler_params=pltpu.CompilerParams(vmem_limit_bytes=VOCAB_LIMIT),
-        cost_estimate=pl.CostEstimate(
-            flops=2 * count * depth * width, bytes_accessed=2 * depth * width, transcendentals=0
-        ),
+        cost_estimate=UNIT_COST,
     )(rows, vocab_weight, *after)
 
 
@@ -316,6 +232,7 @@
         in_specs=[VMEM] * 2 + [ANY] * len(after),
         out_specs=VMEM,
         out_shape=jax.ShapeDtypeStruct((rows // 2, width + LANES), jnp.int16),
+        cost_estimate=UNIT_COST,
         compiler_params=pltpu.CompilerParams(vmem_limit_bytes=VMEM_LIMIT),
     )(keep, came, *after)
 
@@ -337,6 +254,7 @@
         in_specs=[VMEM] * 2,
         out_specs=VMEM,
         out_shape=jax.ShapeDtypeStruct((rows // 2, width), jnp.float32),
+        cost_estimate=UNIT_COST,
         compiler_params=pltpu.CompilerParams(vmem_limit_bytes=VMEM_LIMIT),
     )(keep, came)
 
@@ -433,7 +351,8 @@
             pltpu.SemaphoreType.DMA((rows // 16,)),
         ],
         input_output_aliases={len(operands): 0} if earlier else {},
-        compiler_params=pltpu.CompilerParams(vmem_limit_bytes=VOCAB_LIMIT),
+        cost_estimate=UNIT_COST,
+        compiler_params=pltpu.CompilerParams(vmem_limit_bytes=FINISH_LIMIT),
     )(*operands, *buffer, *after)
 
 
@@ -449,6 +368,7 @@
         in_specs=[pl.BlockSpec(memory_space=pltpu.SMEM), VMEM, VMEM],
         out_specs=VMEM,
         out_shape=jax.ShapeDtypeStruct(own.shape, own.dtype),
+        cost_estimate=UNIT_COST,
         compiler_params=pltpu.CompilerParams(vmem_limit_bytes=VMEM_LIMIT),
     )(low, own, came)
 
@@ -487,6 +407,7 @@
             jax.ShapeDtypeStruct((out_rows, paths), jnp.float32),
         ],
         scratch_shapes=[pltpu.VMEM(own.shape, own.dtype)],
+        cost_estimate=UNIT_COST,
         compiler_params=pltpu.CompilerParams(vmem_limit_bytes=VMEM_LIMIT),
     )(low, own, came, tree, logits)
 
@@ -526,14 +447,7 @@
     for i in range(batch):
         for j in range(mp):
             perm.append((i * mp + j, (j * pieces + i % pieces) * mp + ((i // pieces) ^ j)))
-    head_first = (1 - core).astype(jnp.int32).reshape(1)
-    part = feat // 2
-    head_first = (1 - core).astype(jnp.int32).reshape(1)
-    part = feat // 4
-    firsts = [part * i for i in range(4)]
-    weights_first = fetch(head_first, head_weight, firsts, part, [sent], HEAD_LIMIT)
     block = lax.ppermute(sent, ("batch", "mp"), perm)
-    block, *weights_first = together(block, *weights_first)
     for bit in mp_bits:
         block = jnp.concatenate([block, swap(block, "mp", lambda i: i ^ bit)], axis=0)
 
@@ -547,10 +461,11 @@
     for unit in range(batch):
         source = (m ^ (unit // pieces) ^ (b // pieces)) * pieces + unit % pieces
         spots.append(((source // 2) ^ pair) * 2 + source % 2)
-    info = jnp.stack([core] + spots).astype(jnp.int32)
-    send = head_matmul(info, block, weights_first, rows, jnp.bfloat16)
+    first = jnp.stack([1 - core] + spots).astype(jnp.int32)
+    then = jnp.stack([core] + spots).astype(jnp.int32)
+    send = head_matmul(first, block, head_weight, rows, jnp.bfloat16)
     came = swap(send, "batch", lambda i: i ^ 1)
-    keep = head_matmul(info, block, head_weight, rows, jnp.float32)
+    keep = head_matmul(then, block, head_weight, rows, jnp.float32)
     units = batch // 2
     share = feat // 2
     tall = 2 * rows
@@ -608,7 +523,7 @@
     wanted = jnp.pad(wanted, ((0, 0), (0, LANES - choices)), constant_values=-1)
 
     unit_width = vocab_width // 8
-    plan = [(0, 2), (2, 2), (4, 2), (6, 1), (7, 1)]
+    plan = [(0, 1), (1, 2), (3, 2), (5, 2), (7, 1)]
     plan = [(first * unit_width, count * unit_width) for first, count in plan]
     tile = widest(512, unit_width)
     blocks = len(plan)
@@ -652,12 +567,13 @@
     last = go_on(0, [sends[2]])
     begin(3, [last])
     last = go_on(1, [sends[3]])
-    begin(4, [last, arrivals[0][-1], arrivals[2][0], arrivals[3][0]])
-    last = go_on(2, [sends[4]])
-    last = go_on(3, [last])
+    begin(4, [last, arrivals[2][0]])
+    last = go_on(2, [sends[4], arrivals[0][-1]])
     joined = finish_blocks((0, 1), None, [last])
-    go_on(4, [joined[1]])
-    joined = finish_blocks((2, 3, 4), joined, [])
+    last = go_on(3, [joined[1]])
+    last = go_on(4, [last])
+    joined = finish_blocks((2,), joined, [last])
+    joined = finish_blocks((3, 4), joined, [])
     logits, stats = joined
 
     for bit in bits_of(batch):

time: 209 us -> 187 us (0.89)
  waiting for transfers between devices: 78.3 us -> 59.9 us
  local copies, waits for them, and re-layouts: 25.1 us -> 12.5 us
  starting transfers between devices: 32.9 us -> 42.3 us
    ppermute x29, waiting for transfers between devices: 78.3 us -> 59.9 us  [swap(): lax.ppermute(array, axis, [(i, partner(i)) for i in range(lax.axis_size(a...]
    unnamed x59 -> x49, local copies, waits for them, and re-layouts: 23.7 us -> 11.1 us
    ppermute x29, starting transfers between devices: 32.2 us -> 41.6 us  [swap(): lax.ppermute(array, axis, [(i, partner(i)) for i in range(lax.axis_size(a...]
    pallas_call x3 -> x2, Pallas kernels: 17.7 us -> 14.4 us  [head_matmul(): pl.pallas_call(functools.partial(head_body, height=height, tile=tile), in...]
    pallas_call x2 -> x3, Pallas kernels: 6.56 us -> 8.82 us  [finish(): pl.pallas_call(functools.partial(finish_body, tile=tile, choices=choices,...]
  transfers between devices with their start and end apart: 30 -> 30, of which waited for: 18 -> 17; matrix products, arithmetic and copies ran while one was open for 1% -> 1% of each run, Pallas kernels for 20% -> 26%
where the time goes in v7:
time: 187 us
  Pallas kernels  67 us (36%)
  waiting for transfers between devices  59.9 us (32%)
  starting transfers between devices  42.3 us (23%)
  local copies, waits for them, and re-layouts  12.5 us (7%)
  other arithmetic  3.48 us (2%)
    ppermute x29, waiting for transfers between devices, swap(): lax.ppermute(array, axis, [(i, partner(i)) for i in range(lax.axis_size(a...  59.9 us
    ppermute x29, starting transfers between devices, swap(): lax.ppermute(array, axis, [(i, partner(i)) for i in range(lax.axis_size(a...  41.6 us
    pallas_call x5, Pallas kernels, vocab_matmul(): pl.pallas_call(functools.partial(vocab_body, order=order, tile=tile, firs...  36.2 us
    pallas_call x2, Pallas kernels, head_matmul(): pl.pallas_call(functools.partial(head_body, height=height, tile=tile), in...  14.4 us
    unnamed x49, local copies, waits for them, and re-layouts  11.1 us
    pallas_call x3, Pallas kernels, finish(): pl.pallas_call(functools.partial(finish_body, tile=tile, choices=choices,...  8.82 us
    pallas_call x5, Pallas kernels, fold(): pl.pallas_call(functools.partial(fold_body, tile=tile), in_specs=[VMEM] *...  4.72 us
  transfers between devices with their start and end apart: 30, of which 17 were waited for; matrix products, arithmetic and copies ran while one was open for 1% of the time, Pallas kernels for 26%

profile of v7, /device:TPU:0, one launch (start us, length us, event | category | flops | bytes accessed | tf_op | source)
XLA Modules:
  0.0 186.6 jit_solution(3873801532975387567)
XLA Ops:
  5.3 16.1 %collective-permute-start.4 = (bf16[32,2048]{1,0:T(8,128)(2,1)S(1)}, bf16[32,2048]{1,0:T(8,128)(2,1)S(1)}, u32[]{:S(2)}, u32[]{:S(2)}) collective-permute-start(bf16[32,2048]{1,0:T(8,128)(2,1)S(1)} %collective-permute-done.3), channel_id=1, source_target_pairs={{0,1},{1,0},{2,3},{3,2},{4,5},{5,4},{6,7},{7,6},{8,9},{9,8},{10,11... | collective-permute-start | bytes 393224 | tf_op jit(solution)/shard_map/ppermute | solution.py:24
  21.5 2.9 %collective-permute-done.4 = bf16[32,2048]{1,0:T(8,128)(2,1)S(1)} collective-permute-done((bf16[32,2048]{1,0:T(8,128)(2,1)S(1)}, bf16[32,2048]{1,0:T(8,128)(2,1)S(1)}, u32[]{:S(2)}, u32[]{:S(2)}) %collective-permute-start.4) | collective-permute-done | bytes 131104 | tf_op jit(solution)/shard_map/ppermute | solution.py:24
  24.7 6.4 %collective-permute-done.5 = bf16[64,2048]{1,0:T(8,128)(2,1)S(1)} collective-permute-done((bf16[64,2048]{1,0:T(8,128)(2,1)S(1)}, bf16[64,2048]{1,0:T(8,128)(2,1)S(1)}, u32[]{:S(2)}, u32[]{:S(2)}) %collective-permute-start.5) | collective-permute-done | bytes 262176 | tf_op jit(solution)/shard_map/ppermute | solution.py:24
  31.1 7.2 %shard_map.96 = bf16[128,4096]{1,0:T(8,128)(2,1)S(1)} custom-call(s32[9]{0:T(128)S(1)} %stack.139.info, bf16[128,2048]{1,0:T(8,128)(2,1)S(1)} %constant_dynamic-update-slice_fusion.came, bf16[2,2048,4096]{2,1,0:T(8,128)(2,1)} %source.8), custom_call_target="tpu_custom_call" | custom-call | flops 1 | bytes 1 | tf_op jit(solution)/shard_map/pallas_call | solution.py:103
  38.7 1.8 collective-permute-start.1
  40.5 7.2 %shard_map.95 = f32[128,4096]{1,0:T(8,128)S(1)} custom-call(s32[9]{0:T(128)S(1)} %stack.137.info, bf16[128,2048]{1,0:T(8,128)(2,1)S(1)} %constant_dynamic-update-slice_fusion.came, bf16[2,2048,4096]{2,1,0:T(8,128)(2,1)} %source.8), custom_call_target="tpu_custom_call" | custom-call | flops 1 | bytes 1 | tf_op jit(solution)/shard_map/pallas_call | solution.py:103
  48.2 4.2 %collective-permute-start.9 = (bf16[64,2048]{1,0:T(8,128)(2,1)S(1)}, bf16[64,2048]{1,0:T(8,128)(2,1)S(1)}, u32[]{:S(2)}, u32[]{:S(2)}) collective-permute-start(bf16[64,2048]{1,0:T(8,128)(2,1)S(1)} %concatenate.38), channel_id=1, source_target_pairs={{0,16},{4,20},{8,24},{12,28},{16,0},{20,4},{24,8},{28,12},{1,17},{... | collective-permute-start | bytes 786440 | tf_op jit(solution)/shard_map/ppermute | solution.py:24
  52.8 9.2 %collective-permute-done.7 = bf16[64,2048]{1,0:T(8,128)(2,1)S(1)} collective-permute-done((bf16[64,2048]{1,0:T(8,128)(2,1)S(1)}, bf16[64,2048]{1,0:T(8,128)(2,1)S(1)}, u32[]{:S(2)}, u32[]{:S(2)}) %collective-permute-start.7) | collective-permute-done | bytes 262176 | tf_op jit(solution)/shard_map/ppermute | solution.py:24
  62.0 2.4 %collective-permute-done.9 = bf16[64,2048]{1,0:T(8,128)(2,1)S(1)} collective-permute-done((bf16[64,2048]{1,0:T(8,128)(2,1)S(1)}, bf16[64,2048]{1,0:T(8,128)(2,1)S(1)}, u32[]{:S(2)}, u32[]{:S(2)}) %collective-permute-start.9) | collective-permute-done | bytes 262176 | tf_op jit(solution)/shard_map/ppermute | solution.py:24
  64.9 2.7 %collective-permute-start.8 = (bf16[32,2048]{1,0:T(8,128)(2,1)S(1)}, bf16[32,2048]{1,0:T(8,128)(2,1)S(1)}, u32[]{:S(2)}, u32[]{:S(2)}) collective-permute-start(bf16[32,2048]{1,0:T(8,128)(2,1)S(1)} %get-tuple-element.38), channel_id=1, source_target_pairs={{0,16},{4,20},{8,24},{12,28},{16,0},{20,4},{24,8},{28,12},{1,17},{... | collective-permute-start | bytes 393224 | tf_op jit(solution)/shard_map/ppermute | solution.py:24
  67.6 4.0 %collective-permute-done.10 = bf16[32,2048]{1,0:T(8,128)(2,1)S(1)} collective-permute-done((bf16[32,2048]{1,0:T(8,128)(2,1)S(1)}, bf16[32,2048]{1,0:T(8,128)(2,1)S(1)}, u32[]{:S(2)}, u32[]{:S(2)}) %collective-permute-start.10) | collective-permute-done | bytes 131104 | tf_op jit(solution)/shard_map/ppermute | solution.py:24
  71.6 1.8 collective-permute-done.8
  74.2 2.5 %collective-permute-start.12 = (bf16[32,2048]{1,0:T(8,128)(2,1)S(1)}, bf16[32,2048]{1,0:T(8,128)(2,1)S(1)}, u32[]{:S(2)}, u32[]{:S(2)}) collective-permute-start(bf16[32,2048]{1,0:T(8,128)(2,1)S(1)} %get-tuple-element.45), channel_id=1, source_target_pairs={{0,8},{4,12},{8,0},{12,4},{16,24},{20,28},{24,16},{28,20},{1,9},{5... | collective-permute-start | bytes 393224 | tf_op jit(solution)/shard_map/ppermute | solution.py:24
  76.7 4.4 %collective-permute-done.11 = bf16[32,2048]{1,0:T(8,128)(2,1)S(1)} collective-permute-done((bf16[32,2048]{1,0:T(8,128)(2,1)S(1)}, bf16[32,2048]{1,0:T(8,128)(2,1)S(1)}, u32[]{:S(2)}, u32[]{:S(2)}) %collective-permute-start.11) | collective-permute-done | bytes 131104 | tf_op jit(solution)/shard_map/ppermute | solution.py:24
  81.8 1.9 %collective-permute-start.14 = (bf16[64,2048]{1,0:T(8,128)(2,1)S(1)}, bf16[64,2048]{1,0:T(8,128)(2,1)S(1)}, u32[]{:S(2)}, u32[]{:S(2)}) collective-permute-start(bf16[64,2048]{1,0:T(8,128)(2,1)S(1)} %get-tuple-element.42), channel_id=1, source_target_pairs={{0,16},{4,20},{8,24},{12,28},{16,0},{20,4},{24,8},{28,12},{1,17},{... | collective-permute-start | bytes 786440 | tf_op jit(solution)/shard_map/ppermute | solution.py:24
  83.7 7.7 %collective-permute-done.13 = bf16[64,2048]{1,0:T(8,128)(2,1)S(1)} collective-permute-done((bf16[64,2048]{1,0:T(8,128)(2,1)S(1)}, bf16[64,2048]{1,0:T(8,128)(2,1)S(1)}, u32[]{:S(2)}, u32[]{:S(2)}) %collective-permute-start.13) | collective-permute-done | bytes 262176 | tf_op jit(solution)/shard_map/ppermute | solution.py:24
  91.4 2.5 %collective-permute-done.14 = bf16[64,2048]{1,0:T(8,128)(2,1)S(1)} collective-permute-done((bf16[64,2048]{1,0:T(8,128)(2,1)S(1)}, bf16[64,2048]{1,0:T(8,128)(2,1)S(1)}, u32[]{:S(2)}, u32[]{:S(2)}) %collective-permute-start.14) | collective-permute-done | bytes 262176 | tf_op jit(solution)/shard_map/ppermute | solution.py:24
  99.5 5.0 %shard_map.98 = (f32[128,1024]{1,0:T(8,128)S(1)}, s16[128,1152]{1,0:T(8,128)(2,1)S(1)}) custom-call(bf16[256,4096]{1,0:T(8,128)(2,1)S(1)} %shard_map.97.rows, bf16[4096,8192]{1,0:T(8,128)(2,1)} %source.13), custom_call_target="tpu_custom_call" | custom-call | flops 1 | bytes 1 | tf_op jit(solution)/shard_map/pallas_call | solution.py:193
  105.0 7.9 %shard_map.99 = (f32[128,2048]{1,0:T(8,128)S(1)}, s16[128,2176]{1,0:T(8,128)(2,1)S(1)}) custom-call(bf16[256,4096]{1,0:T(8,128)(2,1)S(1)} %shard_map.97.rows, bf16[4096,8192]{1,0:T(8,128)(2,1)} %source.13, s16[128,1152]{1,0:T(8,128)(2,1)S(1)} %get-tuple-element.19.refs_0_), custom_call_target="tpu_custom_call" | custom-call | flops 1 | bytes 1 | tf_op jit(solution)/shard_map/pallas_call | solution.py:193
  113.3 8.7 %shard_map.100 = (f32[128,2048]{1,0:T(8,128)S(1)}, s16[128,2176]{1,0:T(8,128)(2,1)}) custom-call(bf16[256,4096]{1,0:T(8,128)(2,1)S(1)} %shard_map.97.rows, bf16[4096,8192]{1,0:T(8,128)(2,1)} %source.13, s16[128,2176]{1,0:T(8,128)(2,1)S(1)} %get-tuple-element.20.refs_0_), custom_call_target="tpu_custom_call" | custom-call | flops 1 | bytes 1 | tf_op jit(solution)/shard_map/pallas_call | solution.py:193
  123.0 1.7 collective-permute-start.22
  125.7 8.7 %shard_map.102 = (f32[128,2048]{1,0:T(8,128)S(1)}, s16[128,2176]{1,0:T(8,128)(2,1)}) custom-call(bf16[256,4096]{1,0:T(8,128)(2,1)S(1)} %shard_map.97.rows, bf16[4096,8192]{1,0:T(8,128)(2,1)} %source.13, s16[64,1152]{1,0:T(8,128)(2,1)} %shard_map.101.refs_0_), custom_call_target="tpu_custom_call" | custom-call | flops 1 | bytes 1 | tf_op jit(solution)/shard_map/pallas_call | solution.py:193
  134.4 1.8 collective-permute-start.18
  138.5 5.8 %shard_map.104 = (f32[128,1024]{1,0:T(8,128)S(1)}, s16[128,1152]{1,0:T(8,128)(2,1)}) custom-call(bf16[256,4096]{1,0:T(8,128)(2,1)S(1)} %shard_map.97.rows, bf16[4096,8192]{1,0:T(8,128)(2,1)} %source.13, s16[64,2176]{1,0:T(8,128)(2,1)} %shard_map.103.refs_0_, s16[128,2176]{1,0:T(8,128)(2,1)S(1)} %collective-permute-done.22.refs_1_.came), custom_call_target="tpu_custom_call" | custom-call | flops 1 | bytes 1 | tf_op jit(solution)/shard_map/pallas_call | solution.py:193
  147.0 5.1 %collective-permute-done.19.refs_1_.refs_2_ = s16[64,1152]{1,0:T(8,128)(2,1)} collective-permute-done((s16[64,1152]{1,0:T(8,128)(2,1)}, s16[64,1152]{1,0:T(8,128)(2,1)}, u32[]{:S(2)}, u32[]{:S(2)}) %collective-permute-start.19) | collective-permute-done | bytes 147488 | tf_op jit(solution)/shard_map/ppermute | solution.py:24
  160.0 3.8 %shard_map.106 = (f32[64,8192]{1,0:T(8,128)S(1)}, f32[64,128]{1,0:T(8,128)S(1)}) custom-call(s32[64,128]{1,0:T(8,128)S(1)} %pad.4.wanted, f32[128,1024]{1,0:T(8,128)S(1)} %copy-done.14, s16[128,1152]{1,0:T(8,128)(2,1)S(1)} %copy-done.16, s16[64,1152]{1,0:T(8,128)(2,1)} %collective-permute-done.19.refs_1_.refs_2_, f32[128,2048]{1,0:T(8,128)S(1)} %copy-done.3, ...), custom_call_target="tpu_custom_call" | custom-call | flops 1 | bytes 1 | tf_op jit(solution)/shard_map/pallas_call | solution.py:334
  166.3 2.2 %shard_map.109 = (f32[64,8192]{1,0:T(8,128)S(1)}, f32[64,128]{1,0:T(8,128)S(1)}) custom-call(s32[64,128]{1,0:T(8,128)S(1)} %pad.4.wanted, f32[128,2048]{1,0:T(8,128)S(1)} %copy-done.8, s16[128,2176]{1,0:T(8,128)(2,1)S(1)} %collective-permute-done.22.refs_1_.came, ...), custom_call_target="tpu_custom_call", output_to_operand_aliasing={{0}: (5, {})} | custom-call | flops 1 | bytes 1 | tf_op jit(solution)/shard_map/pallas_call | solution.py:334
  168.5 2.3 %collective-permute-done.25.refs_5_ = s16[64,1152]{1,0:T(8,128)(2,1)S(1)} collective-permute-done((s16[64,1152]{1,0:T(8,128)(2,1)S(1)}, s16[64,1152]{1,0:T(8,128)(2,1)S(1)}, u32[]{:S(2)}, u32[]{:S(2)}) %collective-permute-start.25) | collective-permute-done | bytes 147488 | tf_op jit(solution)/shard_map/ppermute | solution.py:24
  171.4 2.8 %shard_map.110 = (f32[64,8192]{1,0:T(8,128)S(1)}, f32[64,128]{1,0:T(8,128)S(1)}) custom-call(s32[64,128]{1,0:T(8,128)S(1)} %pad.4.wanted, f32[128,2048]{1,0:T(8,128)S(1)} %copy-done.5, s16[128,2176]{1,0:T(8,128)(2,1)S(1)} %collective-permute-done.18.came.refs_1_, ...), custom_call_target="tpu_custom_call", output_to_operand_aliasing={{0}: (8, {})} | custom-call | flops 1 | bytes 1 | tf_op jit(solution)/shard_map/pallas_call | solution.py:334
  175.7 3.9 %collective-permute-done.28.came = f32[64,128]{1,0:T(8,128)S(1)} collective-permute-done((f32[64,128]{1,0:T(8,128)S(1)}, f32[64,128]{1,0:T(8,128)S(1)}, u32[]{:S(2)}, u32[]{:S(2)}) %collective-permute-start.28) | collective-permute-done | bytes 32800 | tf_op jit(solution)/shard_map/ppermute | solution.py:24
  180.1 4.5 %collective-permute-done.29.came = f32[64,128]{1,0:T(8,128)S(1)} collective-permute-done((f32[64,128]{1,0:T(8,128)S(1)}, f32[64,128]{1,0:T(8,128)S(1)}, u32[]{:S(2)}, u32[]{:S(2)}) %collective-permute-start.29) | collective-permute-done | bytes 32800 | tf_op jit(solution)/shard_map/ppermute | solution.py:24
  184.6 2.0 %shard_map.113 = (f32[32,2,8192]{2,1,0:T(2,128)}, f32[32,64]{1,0:T(8,128)}) custom-call(s32[1]{0:T(128)} %bitcast.low, f32[64,128]{1,0:T(8,128)S(1)} %shard_map.112.own, f32[64,128]{1,0:T(8,128)S(1)} %collective-permute-done.29.came, s32[2,64]{1,0:T(2,128)S(1)} %bitcast.40, f32[64,8192]{1,0:T(8,128)S(1)} %get-tuple-element.33.logits), custom_call_target="tpu_custom_call" | custom-call | flops 1 | bytes 1 | tf_op jit(solution)/shard_map/pallas_call | solution.py:401
  (129 shorter events, 34.0 us)
Async XLA Ops:
  0.6 51.8 %copy-start = (f32[2,4096]{1,0:T(2,128)S(1)}, f32[2,4096]{1,0:T(2,128)}, u32[]{:S(2)}) copy-start(f32[2,4096]{1,0:T(2,128)} %param.12) | copy-start | bytes 98308
  3.0 1.5 collective-permute-start
  4.6 0.7 collective-permute-start.3
  5.3 19.1 %collective-permute-start.4 = (bf16[32,2048]{1,0:T(8,128)(2,1)S(1)}, bf16[32,2048]{1,0:T(8,128)(2,1)S(1)}, u32[]{:S(2)}, u32[]{:S(2)}) collective-permute-start(bf16[32,2048]{1,0:T(8,128)(2,1)S(1)} %collective-permute-done.3), channel_id=1, source_target_pairs={{0,1},{1,0},{2,3},{3,2},{4,5},{5,4},{6,7},{7,6},{8,9},{9,8},{10,11... | collective-permute-start | bytes 393224 | tf_op jit(solution)/shard_map/ppermute | solution.py:24
  24.4 6.7 %collective-permute-start.5 = (bf16[64,2048]{1,0:T(8,128)(2,1)S(1)}, bf16[64,2048]{1,0:T(8,128)(2,1)S(1)}, u32[]{:S(2)}, u32[]{:S(2)}) collective-permute-start(bf16[64,2048]{1,0:T(8,128)(2,1)S(1)} %pad_maximum_fusion), channel_id=1, source_target_pairs={{0,2},{1,3},{2,0},{3,1},{4,6},{5,7},{6,4},{7,5},{8,10},{9,11},{10,... | collective-permute-start | bytes 786440 | tf_op jit(solution)/shard_map/ppermute | solution.py:24
  38.3 9.4 %collective-permute-start.6 = (bf16[128,4096]{1,0:T(8,128)(2,1)S(1)}, bf16[128,4096]{1,0:T(8,128)(2,1)S(1)}, u32[]{:S(2)}, u32[]{:S(2)}) collective-permute-start(bf16[128,4096]{1,0:T(8,128)(2,1)S(1)} %shard_map.96), channel_id=1, source_target_pairs={{0,4},{4,0},{8,12},{12,8},{16,20},{20,16},{24,28},{28,24},{1,5},{5... | collective-permute-start | bytes 3145736 | tf_op jit(solution)/shard_map/ppermute | solution.py:24
  38.7 13.7 %collective-permute-start.1 = (f32[32,1]{0,1:T(1,128)S(1)}, f32[32,1]{0,1:T(1,128)S(1)}, u32[]{:S(2)}, u32[]{:S(2)}) collective-permute-start(f32[32,1]{0,1:T(1,128)S(1)} %bitcast.43), channel_id=1, source_target_pairs={{0,1},{1,0},{2,3},{3,2},{4,5},{5,4},{6,7},{7,6},{8,9},{9,8},{10,11... | collective-permute-start | bytes 392 | tf_op jit(solution)/shard_map/ppermute | solution.py:24
  48.1 25.4 %dynamic-slice-start = ((f32[16384]{0:T(1024)}, s32[]{:T(128)}), f32[4096]{0:T(1024)S(1)}, s32[]{:S(2)}) async-start(f32[16384]{0:T(1024)} %param.10, s32[]{:T(128)} %select_n.264), calls=%async_computation | async-start | bytes 33280 | tf_op jit(solution)/shard_map/dynamic_slice | solution.py:437
  48.2 13.9 %collective-permute-start.7 = (bf16[64,2048]{1,0:T(8,128)(2,1)S(1)}, bf16[64,2048]{1,0:T(8,128)(2,1)S(1)}, u32[]{:S(2)}, u32[]{:S(2)}) collective-permute-start(bf16[64,2048]{1,0:T(8,128)(2,1)S(1)} %pad_maximum_fusion.1), channel_id=1, source_target_pairs={{0,8},{4,12},{8,0},{12,4},{16,24},{20,28},{24,16},{28,20},{1,9},{5... | collective-permute-start | bytes 786440 | tf_op jit(solution)/shard_map/ppermute | solution.py:24
  48.2 16.2 %collective-permute-start.9 = (bf16[64,2048]{1,0:T(8,128)(2,1)S(1)}, bf16[64,2048]{1,0:T(8,128)(2,1)S(1)}, u32[]{:S(2)}, u32[]{:S(2)}) collective-permute-start(bf16[64,2048]{1,0:T(8,128)(2,1)S(1)} %concatenate.38), channel_id=1, source_target_pairs={{0,16},{4,20},{8,24},{12,28},{16,0},{20,4},{24,8},{28,12},{1,17},{... | collective-permute-start | bytes 786440 | tf_op jit(solution)/shard_map/ppermute | solution.py:24
  52.4 15.1 %collective-permute-start.2 = (f32[32,1]{0,1:T(1,128)S(1)}, f32[32,1]{0,1:T(1,128)S(1)}, u32[]{:S(2)}, u32[]{:S(2)}) collective-permute-start(f32[32,1]{0,1:T(1,128)S(1)} %bitcast_add_fusion), channel_id=1, source_target_pairs={{0,2},{1,3},{2,0},{3,1},{4,6},{5,7},{6,4},{7,5},{8,10},{9,11},{10,... | collective-permute-start | bytes 392 | tf_op jit(solution)/shard_map/ppermute | solution.py:24
  64.5 7.1 %collective-permute-start.10 = (bf16[32,2048]{1,0:T(8,128)(2,1)S(1)}, bf16[32,2048]{1,0:T(8,128)(2,1)S(1)}, u32[]{:S(2)}, u32[]{:S(2)}) collective-permute-start(bf16[32,2048]{1,0:T(8,128)(2,1)S(1)} %get-tuple-element.39), channel_id=1, source_target_pairs={{0,8},{4,12},{8,0},{12,4},{16,24},{20,28},{24,16},{28,20},{1,9},{5... | collective-permute-start | bytes 393224 | tf_op jit(solution)/shard_map/ppermute | solution.py:24
  64.9 8.5 %collective-permute-start.8 = (bf16[32,2048]{1,0:T(8,128)(2,1)S(1)}, bf16[32,2048]{1,0:T(8,128)(2,1)S(1)}, u32[]{:S(2)}, u32[]{:S(2)}) collective-permute-start(bf16[32,2048]{1,0:T(8,128)(2,1)S(1)} %get-tuple-element.38), channel_id=1, source_target_pairs={{0,16},{4,20},{8,24},{12,28},{16,0},{20,4},{24,8},{28,12},{1,17},{... | collective-permute-start | bytes 393224 | tf_op jit(solution)/shard_map/ppermute | solution.py:24
  73.8 7.3 %collective-permute-start.11 = (bf16[32,2048]{1,0:T(8,128)(2,1)S(1)}, bf16[32,2048]{1,0:T(8,128)(2,1)S(1)}, u32[]{:S(2)}, u32[]{:S(2)}) collective-permute-start(bf16[32,2048]{1,0:T(8,128)(2,1)S(1)} %get-tuple-element.44), channel_id=1, source_target_pairs={{0,16},{4,20},{8,24},{12,28},{16,0},{20,4},{24,8},{28,12},{1,17},{... | collective-permute-start | bytes 393224 | tf_op jit(solution)/shard_map/ppermute | solution.py:24
  74.2 6.9 %collective-permute-start.12 = (bf16[32,2048]{1,0:T(8,128)(2,1)S(1)}, bf16[32,2048]{1,0:T(8,128)(2,1)S(1)}, u32[]{:S(2)}, u32[]{:S(2)}) collective-permute-start(bf16[32,2048]{1,0:T(8,128)(2,1)S(1)} %get-tuple-element.45), channel_id=1, source_target_pairs={{0,8},{4,12},{8,0},{12,4},{16,24},{20,28},{24,16},{28,20},{1,9},{5... | collective-permute-start | bytes 393224 | tf_op jit(solution)/shard_map/ppermute | solution.py:24
  81.2 10.2 %collective-permute-start.13 = (bf16[64,2048]{1,0:T(8,128)(2,1)S(1)}, bf16[64,2048]{1,0:T(8,128)(2,1)S(1)}, u32[]{:S(2)}, u32[]{:S(2)}) collective-permute-start(bf16[64,2048]{1,0:T(8,128)(2,1)S(1)} %get-tuple-element.43), channel_id=1, source_target_pairs={{0,8},{4,12},{8,0},{12,4},{16,24},{20,28},{24,16},{28,20},{1,9},{5... | collective-permute-start | bytes 786440 | tf_op jit(solution)/shard_map/ppermute | solution.py:24
  81.8 12.1 %collective-permute-start.14 = (bf16[64,2048]{1,0:T(8,128)(2,1)S(1)}, bf16[64,2048]{1,0:T(8,128)(2,1)S(1)}, u32[]{:S(2)}, u32[]{:S(2)}) collective-permute-start(bf16[64,2048]{1,0:T(8,128)(2,1)S(1)} %get-tuple-element.42), channel_id=1, source_target_pairs={{0,16},{4,20},{8,24},{12,28},{16,0},{20,4},{24,8},{28,12},{1,17},{... | collective-permute-start | bytes 786440 | tf_op jit(solution)/shard_map/ppermute | solution.py:24
  83.7 10.7 %collective-permute-start.15 = (bf16[64,4096]{1,0:T(8,128)(2,1)S(1)}, bf16[64,4096]{1,0:T(8,128)(2,1)S(1)}, u32[]{:S(2)}, u32[]{:S(2)}) collective-permute-start(bf16[64,4096]{1,0:T(8,128)(2,1)S(1)} %maximum_maximum_fusion.refs_0_), channel_id=1, source_target_pairs={{0,4},{4,0},{8,12},{12,8},{16,20},{20,16},{24,28},{28,24},{1,5},{5... | collective-permute-start | bytes 1572872 | tf_op jit(solution)/shard_map/ppermute | solution.py:24
  94.0 2.0 %collective-permute-start.16 = (bf16[64,4096]{1,0:T(8,128)(2,1)S(1)}, bf16[64,4096]{1,0:T(8,128)(2,1)S(1)}, u32[]{:S(2)}, u32[]{:S(2)}) collective-permute-start(bf16[64,4096]{1,0:T(8,128)(2,1)S(1)} %constant_dynamic-update-slice_fusion.3.refs_1_), channel_id=1, source_target_pairs={{0,4},{4,0},{8,12},{12,8},{16,20},{20,16},{24,28},{28,24},{1,5},{5... | collective-permute-start | bytes 1572872 | tf_op jit(solution)/shard_map/ppermute | solution.py:24
  104.6 20.1 %collective-permute-start.17 = (s16[128,1152]{1,0:T(8,128)(2,1)S(1)}, s16[128,1152]{1,0:T(8,128)(2,1)S(1)}, u32[]{:S(2)}, u32[]{:S(2)}) collective-permute-start(s16[128,1152]{1,0:T(8,128)(2,1)S(1)} %get-tuple-element.19.refs_0_), channel_id=1, source_target_pairs={{0,1},{1,0},{2,3},{3,2},{4,5},{5,4},{6,7},{7,6},{8,9},{9,8},{10,11... | collective-permute-start | bytes 884744 | tf_op jit(solution)/shard_map/ppermute | solution.py:24
  112.9 23.3 %collective-permute-start.20 = (s16[128,2176]{1,0:T(8,128)(2,1)S(1)}, s16[128,2176]{1,0:T(8,128)(2,1)S(1)}, u32[]{:S(2)}, u32[]{:S(2)}) collective-permute-start(s16[128,2176]{1,0:T(8,128)(2,1)S(1)} %get-tuple-element.20.refs_0_), channel_id=1, source_target_pairs={{0,2},{1,3},{2,0},{3,1},{4,6},{5,7},{6,4},{7,5},{8,10},{9,11},{10,... | collective-permute-start | bytes 1671176 | tf_op jit(solution)/shard_map/ppermute | solution.py:24
  123.0 15.5 %collective-permute-start.22 = (s16[128,2176]{1,0:T(8,128)(2,1)}, s16[128,2176]{1,0:T(8,128)(2,1)S(1)}, u32[]{:S(2)}, u32[]{:S(2)}) collective-permute-start(s16[128,2176]{1,0:T(8,128)(2,1)} %get-tuple-element.21.refs_0_), channel_id=1, source_target_pairs={{0,1},{1,0},{2,3},{3,2},{4,5},{5,4},{6,7},{7,6},{8,9},{9,8},{10,11... | collective-permute-start | bytes 1671176 | tf_op jit(solution)/shard_map/ppermute | solution.py:24
  134.4 29.5 %collective-permute-start.18 = (s16[128,2176]{1,0:T(8,128)(2,1)}, s16[128,2176]{1,0:T(8,128)(2,1)S(1)}, u32[]{:S(2)}, u32[]{:S(2)}) collective-permute-start(s16[128,2176]{1,0:T(8,128)(2,1)} %get-tuple-element.23.refs_0_), channel_id=1, source_target_pairs={{0,2},{1,3},{2,0},{3,1},{4,6},{5,7},{6,4},{7,5},{8,10},{9,11},{10,... | collective-permute-start | bytes 1671176 | tf_op jit(solution)/shard_map/ppermute | solution.py:24
  137.9 17.9 %collective-permute-start.21 = (s16[64,2176]{1,0:T(8,128)(2,1)}, s16[64,2176]{1,0:T(8,128)(2,1)}, u32[]{:S(2)}, u32[]{:S(2)}) collective-permute-start(s16[64,2176]{1,0:T(8,128)(2,1)} %shard_map.103.refs_0_), channel_id=1, source_target_pairs={{0,1},{1,0},{2,3},{3,2},{4,5},{5,4},{6,7},{7,6},{8,9},{9,8},{10,11... | collective-permute-start | bytes 835592 | tf_op jit(solution)/shard_map/ppermute | solution.py:24
  138.2 13.9 %collective-permute-start.19 = (s16[64,1152]{1,0:T(8,128)(2,1)}, s16[64,1152]{1,0:T(8,128)(2,1)}, u32[]{:S(2)}, u32[]{:S(2)}) collective-permute-start(s16[64,1152]{1,0:T(8,128)(2,1)} %shard_map.101.refs_0_), channel_id=1, source_target_pairs={{0,2},{1,3},{2,0},{3,1},{4,6},{5,7},{6,4},{7,5},{8,10},{9,11},{10,... | collective-permute-start | bytes 442376 | tf_op jit(solution)/shard_map/ppermute | solution.py:24
  145.1 20.2 %collective-permute-start.24 = (s16[128,1152]{1,0:T(8,128)(2,1)}, s16[128,1152]{1,0:T(8,128)(2,1)S(1)}, u32[]{:S(2)}, u32[]{:S(2)}) collective-permute-start(s16[128,1152]{1,0:T(8,128)(2,1)} %get-tuple-element.26.refs_0_), channel_id=1, source_target_pairs={{0,1},{1,0},{2,3},{3,2},{4,5},{5,4},{6,7},{7,6},{8,9},{9,8},{10,11... | collective-permute-start | bytes 884744 | tf_op jit(solution)/shard_map/ppermute | solution.py:24
  154.3 12.0 %collective-permute-start.26 = (s16[64,2176]{1,0:T(8,128)(2,1)S(1)}, s16[64,2176]{1,0:T(8,128)(2,1)S(1)}, u32[]{:S(2)}, u32[]{:S(2)}) collective-permute-start(s16[64,2176]{1,0:T(8,128)(2,1)S(1)} %shard_map.105.refs_6_), channel_id=1, source_target_pairs={{0,2},{1,3},{2,0},{3,1},{4,6},{5,7},{6,4},{7,5},{8,10},{9,11},{10,... | collective-permute-start | bytes 835592 | tf_op jit(solution)/shard_map/ppermute | solution.py:24
  164.8 6.6 %collective-permute-start.23 = (s16[64,2176]{1,0:T(8,128)(2,1)S(1)}, s16[64,2176]{1,0:T(8,128)(2,1)S(1)}, u32[]{:S(2)}, u32[]{:S(2)}) collective-permute-start(s16[64,2176]{1,0:T(8,128)(2,1)S(1)} %shard_map.107.refs_0_), channel_id=1, source_target_pairs={{0,1},{1,0},{2,3},{3,2},{4,5},{5,4},{6,7},{7,6},{8,9},{9,8},{10,11... | collective-permute-start | bytes 835592 | tf_op jit(solution)/shard_map/ppermute | solution.py:24
  165.6 5.2 %collective-permute-start.25 = (s16[64,1152]{1,0:T(8,128)(2,1)S(1)}, s16[64,1152]{1,0:T(8,128)(2,1)S(1)}, u32[]{:S(2)}, u32[]{:S(2)}) collective-permute-start(s16[64,1152]{1,0:T(8,128)(2,1)S(1)} %shard_map.108.refs_5_), channel_id=1, source_target_pairs={{0,2},{1,3},{2,0},{3,1},{4,6},{5,7},{6,4},{7,5},{8,10},{9,11},{10,... | collective-permute-start | bytes 442376 | tf_op jit(solution)/shard_map/ppermute | solution.py:24
  174.2 1.3 collective-permute-start.27
  175.6 4.0 %collective-permute-start.28 = (f32[64,128]{1,0:T(8,128)S(1)}, f32[64,128]{1,0:T(8,128)S(1)}, u32[]{:S(2)}, u32[]{:S(2)}) collective-permute-start(f32[64,128]{1,0:T(8,128)S(1)} %shard_map.111.own), channel_id=1, source_target_pairs={{0,8},{4,12},{8,0},{12,4},{16,24},{20,28},{24,16},{28,20},{1,9},{5... | collective-permute-start | bytes 98312 | tf_op jit(solution)/shard_map/ppermute | solution.py:24
  179.7 4.9 %collective-permute-start.29 = (f32[64,128]{1,0:T(8,128)S(1)}, f32[64,128]{1,0:T(8,128)S(1)}, u32[]{:S(2)}, u32[]{:S(2)}) collective-permute-start(f32[64,128]{1,0:T(8,128)S(1)} %shard_map.112.own), channel_id=1, source_target_pairs={{0,16},{4,20},{8,24},{12,28},{16,0},{20,4},{24,8},{28,12},{1,17},{... | collective-permute-start | bytes 98312 | tf_op jit(solution)/shard_map/ppermute | solution.py:24
  (22 other events, 131.0 us)

commit v8 on v7

--- a/solution.py
+++ b/solution.py
@@ -162,7 +162,7 @@
 
 
 def vocab_body(rows, source, *refs, order, tile, first, waits):
-    keep, send, held, powers, sems = refs[waits:]
+    stay, go, send, held, powers, sems = refs[waits:]
     wait = stream(source, held, sems, first, tile)
     height = rows.shape[0] // len(order)
     half = len(order) // 2
@@ -175,8 +175,8 @@
         wait(n)
         total = jnp.dot(rows[...], held[:, at], preferred_element_type=jnp.float32)
         sorted_rows = [total[g * height : (g + 1) * height] for g in order]
-        for spot, value in enumerate(sorted_rows[:half]):
-            keep[spot * height : (spot + 1) * height, at] = value
+        stay[:, at] = jnp.concatenate(sorted_rows[: half // 2], axis=0)
+        go[:, at] = jnp.concatenate(sorted_rows[half // 2 : half], axis=0)
         code, power = encode(jnp.concatenate(sorted_rows[half:], axis=0))
         send[:, at] = code
         powers[...] = jnp.where(lane == n, power, powers[...])
@@ -193,9 +193,10 @@
     return pl.pallas_call(
         functools.partial(vocab_body, order=order, tile=tile, first=first, waits=len(after)),
         in_specs=[VMEM] + [ANY] * (1 + len(after)),
-        out_specs=[VMEM] * 2,
+        out_specs=[VMEM] * 3,
         out_shape=[
-            jax.ShapeDtypeStruct((half, width), jnp.float32),
+            jax.ShapeDtypeStruct((half // 2, width), jnp.float32),
+            jax.ShapeDtypeStruct((half // 2, width), jnp.float32),
             jax.ShapeDtypeStruct((half, width + LANES), jnp.int16),
         ],
         scratch_shapes=[
@@ -212,13 +213,15 @@
     send = refs[-1]
     half = send.shape[0]
     width = keep.shape[1]
+    skip = keep.shape[0] - half
     for row in range(half, 2 * half, 16):
         here, there = slice(row, row + 16), slice(row - half, row - half + 16)
+        held = slice(row - half + skip, row - half + skip + 16)
         marks = came[here, width:].astype(jnp.int32).astype(jnp.float32)
         powers = []
         for step in range(width // tile):
             block = slice(step * tile, (step + 1) * tile)
-            value = keep[here, block] + decode(came[here, block], marks[:, step : step + 1])
+            value = keep[held, block] + decode(came[here, block], marks[:, step : step + 1])
             code, power = encode(value)
             send[there, block] = code
             powers.append(power)
@@ -226,7 +229,7 @@
 
 
 def fold(keep, came, tile, after):
-    rows, width = keep.shape
+    rows, width = came.shape[0], keep.shape[1]
     return pl.pallas_call(
         functools.partial(fold_body, tile=tile),
         in_specs=[VMEM] * 2 + [ANY] * len(after),
@@ -248,7 +251,7 @@
 
 
 def add_kept(keep, came, tile):
-    rows, width = keep.shape
+    rows, width = came.shape[0], keep.shape[1]
     return pl.pallas_call(
         functools.partial(add_body, tile=tile),
         in_specs=[VMEM] * 2,
@@ -528,23 +531,24 @@
     tile = widest(512, unit_width)
     blocks = len(plan)
     stages = [mp_bits if block % 2 == 0 else mp_bits[::-1] for block in range(blocks)]
-    keeps, sends, arrivals = [], [], [[] for _ in plan]
+    keeps, goes, sends, arrivals = [], [], [], [[] for _ in plan]
 
     def begin(block, after):
         first, width = plan[block]
         order = sorted(range(mp), key=lambda g: place(g, stages[block]))
-        keep, send = vocab_matmul(all_rows, vocab_weight, first, width, order, tile, after)
-        keeps.append(keep)
+        stay, go, send = vocab_matmul(all_rows, vocab_weight, first, width, order, tile, after)
+        keeps.append(stay)
+        goes.append(go)
         sends.append(send)
         arrivals[block].append(swap(send, "mp", lambda i: i ^ stages[block][0]))
 
     def go_on(block, after):
-        keep = keeps[block]
+        keep, go = keeps[block], goes[block]
         for bit in stages[block][1:]:
             while len(arrivals[block]) > 1:
                 rest = arrivals[block].pop(0)
-                keep = add_kept(keep, rest, tile)
-            send = fold(keep, arrivals[block][-1], tile, after)
+                keep = go = add_kept(keep, rest, tile)
+            send = fold(go, arrivals[block][-1], tile, after)
             arrivals[block].append(swap(send, "mp", lambda i: i ^ bit))
         keeps[block] = keep
         return send
@@ -568,7 +572,7 @@
     begin(3, [last])
     last = go_on(1, [sends[3]])
     begin(4, [last, arrivals[2][0]])
-    last = go_on(2, [sends[4], arrivals[0][-1]])
+    last = go_on(2, [sends[4]])
     joined = finish_blocks((0, 1), None, [last])
     last = go_on(3, [joined[1]])
     last = go_on(4, [last])

time: 187 us -> 185 us (0.989)
  waiting for transfers between devices: 59.9 us -> 55 us
  Pallas kernels: 67 us -> 69.6 us
    ppermute x29, waiting for transfers between devices: 59.9 us -> 55 us  [swap(): lax.ppermute(array, axis, [(i, partner(i)) for i in range(lax.axis_size(a...]
    unnamed x49 -> x53, local copies, waits for them, and re-layouts: 11.1 us -> 9.78 us
  transfers between devices with their start and end apart: 30 -> 30, of which waited for: 17 -> 16; matrix products, arithmetic and copies ran while one was open for 1% -> 1% of each run, Pallas kernels for 26% -> 27%
where the time goes in v8:
time: 185 us; the launch traced here: 184 us
  Pallas kernels  69.6 us (38%)
  waiting for transfers between devices  55 us (30%)
  starting transfers between devices  43.6 us (24%)
  local copies, waits for them, and re-layouts  11.2 us (6%)
  other arithmetic  3.48 us (2%)
    ppermute x29, waiting for transfers between devices, swap(): lax.ppermute(array, axis, [(i, partner(i)) for i in range(lax.axis_size(a...  55 us
    ppermute x29, starting transfers between devices, swap(): lax.ppermute(array, axis, [(i, partner(i)) for i in range(lax.axis_size(a...  42.9 us
    pallas_call x5, Pallas kernels, vocab_matmul(): pl.pallas_call(functools.partial(vocab_body, order=order, tile=tile, firs...  36.2 us
    pallas_call x2, Pallas kernels, head_matmul(): pl.pallas_call(functools.partial(head_body, height=height, tile=tile), in...  14.4 us
    pallas_call x3, Pallas kernels, finish(): pl.pallas_call(functools.partial(finish_body, tile=tile, choices=choices,...  10 us
    unnamed x53, local copies, waits for them, and re-layouts  9.78 us
    pallas_call x5, Pallas kernels, fold(): pl.pallas_call(functools.partial(fold_body, tile=tile), in_specs=[VMEM] *...  6.14 us
  transfers between devices with their start and end apart: 30, of which 16 were waited for; matrix products, arithmetic and copies ran while one was open for 1% of the time, Pallas kernels for 27%

profile of v8, /device:TPU:0, one launch (start us, length us, event | category | flops | bytes accessed | tf_op | source)
XLA Modules:
  0.0 184.3 jit_solution(9565808293893685456)
XLA Ops:
  5.3 16.1 %collective-permute-start.4 = (bf16[32,2048]{1,0:T(8,128)(2,1)S(1)}, bf16[32,2048]{1,0:T(8,128)(2,1)S(1)}, u32[]{:S(2)}, u32[]{:S(2)}) collective-permute-start(bf16[32,2048]{1,0:T(8,128)(2,1)S(1)} %collective-permute-done.3), channel_id=1, source_target_pairs={{0,1},{1,0},{2,3},{3,2},{4,5},{5,4},{6,7},{7,6},{8,9},{9,8},{10,11... | collective-permute-start | bytes 393224 | tf_op jit(solution)/shard_map/ppermute | solution.py:24
  21.5 2.9 %collective-permute-done.4 = bf16[32,2048]{1,0:T(8,128)(2,1)S(1)} collective-permute-done((bf16[32,2048]{1,0:T(8,128)(2,1)S(1)}, bf16[32,2048]{1,0:T(8,128)(2,1)S(1)}, u32[]{:S(2)}, u32[]{:S(2)}) %collective-permute-start.4) | collective-permute-done | bytes 131104 | tf_op jit(solution)/shard_map/ppermute | solution.py:24
  24.7 6.4 %collective-permute-done.5 = bf16[64,2048]{1,0:T(8,128)(2,1)S(1)} collective-permute-done((bf16[64,2048]{1,0:T(8,128)(2,1)S(1)}, bf16[64,2048]{1,0:T(8,128)(2,1)S(1)}, u32[]{:S(2)}, u32[]{:S(2)}) %collective-permute-start.5) | collective-permute-done | bytes 262176 | tf_op jit(solution)/shard_map/ppermute | solution.py:24
  31.1 7.2 %shard_map.96 = bf16[128,4096]{1,0:T(8,128)(2,1)S(1)} custom-call(s32[9]{0:T(128)S(1)} %stack.139.info, bf16[128,2048]{1,0:T(8,128)(2,1)S(1)} %constant_dynamic-update-slice_fusion.came, bf16[2,2048,4096]{2,1,0:T(8,128)(2,1)} %source.8), custom_call_target="tpu_custom_call" | custom-call | flops 1 | bytes 1 | tf_op jit(solution)/shard_map/pallas_call | solution.py:103
  38.7 1.8 collective-permute-start.1
  40.5 7.2 %shard_map.95 = f32[128,4096]{1,0:T(8,128)S(1)} custom-call(s32[9]{0:T(128)S(1)} %stack.137.info, bf16[128,2048]{1,0:T(8,128)(2,1)S(1)} %constant_dynamic-update-slice_fusion.came, bf16[2,2048,4096]{2,1,0:T(8,128)(2,1)} %source.8), custom_call_target="tpu_custom_call" | custom-call | flops 1 | bytes 1 | tf_op jit(solution)/shard_map/pallas_call | solution.py:103
  48.2 4.2 %collective-permute-start.9 = (bf16[64,2048]{1,0:T(8,128)(2,1)S(1)}, bf16[64,2048]{1,0:T(8,128)(2,1)S(1)}, u32[]{:S(2)}, u32[]{:S(2)}) collective-permute-start(bf16[64,2048]{1,0:T(8,128)(2,1)S(1)} %concatenate.38), channel_id=1, source_target_pairs={{0,16},{4,20},{8,24},{12,28},{16,0},{20,4},{24,8},{28,12},{1,17},{... | collective-permute-start | bytes 786440 | tf_op jit(solution)/shard_map/ppermute | solution.py:24
  52.8 9.2 %collective-permute-done.7 = bf16[64,2048]{1,0:T(8,128)(2,1)S(1)} collective-permute-done((bf16[64,2048]{1,0:T(8,128)(2,1)S(1)}, bf16[64,2048]{1,0:T(8,128)(2,1)S(1)}, u32[]{:S(2)}, u32[]{:S(2)}) %collective-permute-start.7) | collective-permute-done | bytes 262176 | tf_op jit(solution)/shard_map/ppermute | solution.py:24
  62.0 2.4 %collective-permute-done.9 = bf16[64,2048]{1,0:T(8,128)(2,1)S(1)} collective-permute-done((bf16[64,2048]{1,0:T(8,128)(2,1)S(1)}, bf16[64,2048]{1,0:T(8,128)(2,1)S(1)}, u32[]{:S(2)}, u32[]{:S(2)}) %collective-permute-start.9) | collective-permute-done | bytes 262176 | tf_op jit(solution)/shard_map/ppermute | solution.py:24
  64.9 2.7 %collective-permute-start.8 = (bf16[32,2048]{1,0:T(8,128)(2,1)S(1)}, bf16[32,2048]{1,0:T(8,128)(2,1)S(1)}, u32[]{:S(2)}, u32[]{:S(2)}) collective-permute-start(bf16[32,2048]{1,0:T(8,128)(2,1)S(1)} %get-tuple-element.48), channel_id=1, source_target_pairs={{0,16},{4,20},{8,24},{12,28},{16,0},{20,4},{24,8},{28,12},{1,17},{... | collective-permute-start | bytes 393224 | tf_op jit(solution)/shard_map/ppermute | solution.py:24
  67.6 4.0 %collective-permute-done.10 = bf16[32,2048]{1,0:T(8,128)(2,1)S(1)} collective-permute-done((bf16[32,2048]{1,0:T(8,128)(2,1)S(1)}, bf16[32,2048]{1,0:T(8,128)(2,1)S(1)}, u32[]{:S(2)}, u32[]{:S(2)}) %collective-permute-start.10) | collective-permute-done | bytes 131104 | tf_op jit(solution)/shard_map/ppermute | solution.py:24
  71.6 1.8 collective-permute-done.8
  74.2 2.5 %collective-permute-start.12 = (bf16[32,2048]{1,0:T(8,128)(2,1)S(1)}, bf16[32,2048]{1,0:T(8,128)(2,1)S(1)}, u32[]{:S(2)}, u32[]{:S(2)}) collective-permute-start(bf16[32,2048]{1,0:T(8,128)(2,1)S(1)} %get-tuple-element.55), channel_id=1, source_target_pairs={{0,8},{4,12},{8,0},{12,4},{16,24},{20,28},{24,16},{28,20},{1,9},{5... | collective-permute-start | bytes 393224 | tf_op jit(solution)/shard_map/ppermute | solution.py:24
  76.7 4.4 %collective-permute-done.11 = bf16[32,2048]{1,0:T(8,128)(2,1)S(1)} collective-permute-done((bf16[32,2048]{1,0:T(8,128)(2,1)S(1)}, bf16[32,2048]{1,0:T(8,128)(2,1)S(1)}, u32[]{:S(2)}, u32[]{:S(2)}) %collective-permute-start.11) | collective-permute-done | bytes 131104 | tf_op jit(solution)/shard_map/ppermute | solution.py:24
  81.8 1.9 %collective-permute-start.14 = (bf16[64,2048]{1,0:T(8,128)(2,1)S(1)}, bf16[64,2048]{1,0:T(8,128)(2,1)S(1)}, u32[]{:S(2)}, u32[]{:S(2)}) collective-permute-start(bf16[64,2048]{1,0:T(8,128)(2,1)S(1)} %get-tuple-element.52), channel_id=1, source_target_pairs={{0,16},{4,20},{8,24},{12,28},{16,0},{20,4},{24,8},{28,12},{1,17},{... | collective-permute-start | bytes 786440 | tf_op jit(solution)/shard_map/ppermute | solution.py:24
  83.7 7.7 %collective-permute-done.13 = bf16[64,2048]{1,0:T(8,128)(2,1)S(1)} collective-permute-done((bf16[64,2048]{1,0:T(8,128)(2,1)S(1)}, bf16[64,2048]{1,0:T(8,128)(2,1)S(1)}, u32[]{:S(2)}, u32[]{:S(2)}) %collective-permute-start.13) | collective-permute-done | bytes 262176 | tf_op jit(solution)/shard_map/ppermute | solution.py:24
  91.4 2.5 %collective-permute-done.14 = bf16[64,2048]{1,0:T(8,128)(2,1)S(1)} collective-permute-done((bf16[64,2048]{1,0:T(8,128)(2,1)S(1)}, bf16[64,2048]{1,0:T(8,128)(2,1)S(1)}, u32[]{:S(2)}, u32[]{:S(2)}) %collective-permute-start.14) | collective-permute-done | bytes 262176 | tf_op jit(solution)/shard_map/ppermute | solution.py:24
  99.5 5.0 %shard_map.98 = (f32[64,1024]{1,0:T(8,128)S(1)}, f32[64,1024]{1,0:T(8,128)S(1)}, s16[128,1152]{1,0:T(8,128)(2,1)S(1)}) custom-call(bf16[256,4096]{1,0:T(8,128)(2,1)S(1)} %shard_map.97.rows, bf16[4096,8192]{1,0:T(8,128)(2,1)} %source.13), custom_call_target="tpu_custom_call" | custom-call | flops 1 | bytes 1 | tf_op jit(solution)/shard_map/pallas_call | solution.py:193
  105.0 7.9 %shard_map.99 = (f32[64,2048]{1,0:T(8,128)S(1)}, f32[64,2048]{1,0:T(8,128)S(1)}, s16[128,2176]{1,0:T(8,128)(2,1)S(1)}) custom-call(bf16[256,4096]{1,0:T(8,128)(2,1)S(1)} %shard_map.97.rows, bf16[4096,8192]{1,0:T(8,128)(2,1)} %source.13, s16[128,1152]{1,0:T(8,128)(2,1)S(1)} %get-tuple-element.24.refs_0_), custom_call_target="tpu_custom_call" | custom-call | flops 1 | bytes 1 | tf_op jit(solution)/shard_map/pallas_call | solution.py:193
  113.3 8.7 %shard_map.100 = (f32[64,2048]{1,0:T(8,128)S(1)}, f32[64,2048]{1,0:T(8,128)S(1)}, s16[128,2176]{1,0:T(8,128)(2,1)}) custom-call(bf16[256,4096]{1,0:T(8,128)(2,1)S(1)} %shard_map.97.rows, bf16[4096,8192]{1,0:T(8,128)(2,1)} %source.13, s16[128,2176]{1,0:T(8,128)(2,1)S(1)} %get-tuple-element.25.refs_0_), custom_call_target="tpu_custom_call" | custom-call | flops 1 | bytes 1 | tf_op jit(solution)/shard_map/pallas_call | solution.py:193
  124.8 8.8 %shard_map.102 = (f32[64,2048]{1,0:T(8,128)S(1)}, f32[64,2048]{1,0:T(8,128)S(1)}, s16[128,2176]{1,0:T(8,128)(2,1)}) custom-call(bf16[256,4096]{1,0:T(8,128)(2,1)S(1)} %shard_map.97.rows, bf16[4096,8192]{1,0:T(8,128)(2,1)} %source.13, s16[64,1152]{1,0:T(8,128)(2,1)S(1)} %shard_map.101.refs_0_), custom_call_target="tpu_custom_call" | custom-call | flops 1 | bytes 1 | tf_op jit(solution)/shard_map/pallas_call | solution.py:193
  134.4 1.7 collective-permute-start.18
  138.4 5.7 %shard_map.104 = (f32[64,1024]{1,0:T(8,128)S(1)}, f32[64,1024]{1,0:T(8,128)S(1)}, s16[128,1152]{1,0:T(8,128)(2,1)}) custom-call(bf16[256,4096]{1,0:T(8,128)(2,1)S(1)} %shard_map.97.rows, bf16[4096,8192]{1,0:T(8,128)(2,1)} %source.13, s16[64,2176]{1,0:T(8,128)(2,1)} %shard_map.103.refs_0_, s16[128,2176]{1,0:T(8,128)(2,1)S(1)} %collective-permute-done.22.refs_1_.came), custom_call_target="tpu_custom_call" | custom-call | flops 1 | bytes 1 | tf_op jit(solution)/shard_map/pallas_call | solution.py:193
  149.4 1.8 collective-permute-start.26
  151.2 1.9 %collective-permute-done.19.refs_2_ = s16[64,1152]{1,0:T(8,128)(2,1)} collective-permute-done((s16[64,1152]{1,0:T(8,128)(2,1)}, s16[64,1152]{1,0:T(8,128)(2,1)}, u32[]{:S(2)}, u32[]{:S(2)}) %collective-permute-start.19) | collective-permute-done | bytes 147488 | tf_op jit(solution)/shard_map/ppermute | solution.py:24
  155.1 3.9 %shard_map.106 = (f32[64,8192]{1,0:T(8,128)S(1)}, f32[64,128]{1,0:T(8,128)S(1)}) custom-call(s32[64,128]{1,0:T(8,128)S(1)} %pad.4.wanted, f32[64,1024]{1,0:T(8,128)S(1)} %copy-done.18, s16[128,1152]{1,0:T(8,128)(2,1)S(1)} %collective-permute-done.17.came.refs_1_, s16[64,1152]{1,0:T(8,128)(2,1)} %collective-permute-done.19.refs_2_, ...), custom_call_target="tpu_custom_call" | custom-call | flops 1 | bytes 1 | tf_op jit(solution)/shard_map/pallas_call | solution.py:337
  159.0 1.9 %shard_map.107.refs_0_ = s16[64,2176]{1,0:T(8,128)(2,1)S(1)} custom-call(f32[64,2048]{1,0:T(8,128)S(1)} %copy-done.12, s16[128,2176]{1,0:T(8,128)(2,1)} %collective-permute-done.18.came.refs_1_, f32[64,128]{1,0:T(8,128)S(1)} %get-tuple-element.35.refs_0_.refs_3_), custom_call_target="tpu_custom_call" | custom-call | flops 1 | bytes 1 | tf_op jit(solution)/shard_map/pallas_call | solution.py:233
  164.5 2.2 %shard_map.109 = (f32[64,8192]{1,0:T(8,128)S(1)}, f32[64,128]{1,0:T(8,128)S(1)}) custom-call(s32[64,128]{1,0:T(8,128)S(1)} %pad.4.wanted, f32[64,2048]{1,0:T(8,128)S(1)} %copy-done.8, s16[128,2176]{1,0:T(8,128)(2,1)S(1)} %collective-permute-done.22.refs_1_.came, ...), custom_call_target="tpu_custom_call", output_to_operand_aliasing={{0}: (5, {})} | custom-call | flops 1 | bytes 1 | tf_op jit(solution)/shard_map/pallas_call | solution.py:337
  168.0 3.9 %shard_map.110 = (f32[64,8192]{1,0:T(8,128)S(1)}, f32[64,128]{1,0:T(8,128)S(1)}) custom-call(s32[64,128]{1,0:T(8,128)S(1)} %pad.4.wanted, f32[64,2048]{1,0:T(8,128)S(1)} %copy-done.16, s16[128,2176]{1,0:T(8,128)(2,1)} %collective-permute-done.18.came.refs_1_, s16[64,2176]{1,0:T(8,128)(2,1)S(1)} %collective-permute-done.23.refs_2_, ...), custom_call_target="tpu_custom_call", output_to_operand_aliasing={{0}: (8, {})} | custom-call | flops 1 | bytes 1 | tf_op jit(solution)/shard_map/pallas_call | solution.py:337
  173.4 3.9 %collective-permute-done.28.came = f32[64,128]{1,0:T(8,128)S(1)} collective-permute-done((f32[64,128]{1,0:T(8,128)S(1)}, f32[64,128]{1,0:T(8,128)S(1)}, u32[]{:S(2)}, u32[]{:S(2)}) %collective-permute-start.28) | collective-permute-done | bytes 32800 | tf_op jit(solution)/shard_map/ppermute | solution.py:24
  177.8 4.5 %collective-permute-done.29.came = f32[64,128]{1,0:T(8,128)S(1)} collective-permute-done((f32[64,128]{1,0:T(8,128)S(1)}, f32[64,128]{1,0:T(8,128)S(1)}, u32[]{:S(2)}, u32[]{:S(2)}) %collective-permute-start.29) | collective-permute-done | bytes 32800 | tf_op jit(solution)/shard_map/ppermute | solution.py:24
  182.3 2.0 %shard_map.113 = (f32[32,2,8192]{2,1,0:T(2,128)}, f32[32,64]{1,0:T(8,128)}) custom-call(s32[1]{0:T(128)} %bitcast.low, f32[64,128]{1,0:T(8,128)S(1)} %shard_map.112.own, f32[64,128]{1,0:T(8,128)S(1)} %collective-permute-done.29.came, s32[2,64]{1,0:T(2,128)S(1)} %bitcast.40, f32[64,8192]{1,0:T(8,128)S(1)} %get-tuple-element.43.logits), custom_call_target="tpu_custom_call" | custom-call | flops 1 | bytes 1 | tf_op jit(solution)/shard_map/pallas_call | solution.py:404
  (133 shorter events, 34.0 us)
Async XLA Ops:
  0.6 51.8 %copy-start = (f32[2,4096]{1,0:T(2,128)S(1)}, f32[2,4096]{1,0:T(2,128)}, u32[]{:S(2)}) copy-start(f32[2,4096]{1,0:T(2,128)} %param.12) | copy-start | bytes 98308
  3.0 1.5 collective-permute-start
  4.6 0.7 collective-permute-start.3
  5.3 19.1 %collective-permute-start.4 = (bf16[32,2048]{1,0:T(8,128)(2,1)S(1)}, bf16[32,2048]{1,0:T(8,128)(2,1)S(1)}, u32[]{:S(2)}, u32[]{:S(2)}) collective-permute-start(bf16[32,2048]{1,0:T(8,128)(2,1)S(1)} %collective-permute-done.3), channel_id=1, source_target_pairs={{0,1},{1,0},{2,3},{3,2},{4,5},{5,4},{6,7},{7,6},{8,9},{9,8},{10,11... | collective-permute-start | bytes 393224 | tf_op jit(solution)/shard_map/ppermute | solution.py:24
  24.4 6.7 %collective-permute-start.5 = (bf16[64,2048]{1,0:T(8,128)(2,1)S(1)}, bf16[64,2048]{1,0:T(8,128)(2,1)S(1)}, u32[]{:S(2)}, u32[]{:S(2)}) collective-permute-start(bf16[64,2048]{1,0:T(8,128)(2,1)S(1)} %pad_maximum_fusion), channel_id=1, source_target_pairs={{0,2},{1,3},{2,0},{3,1},{4,6},{5,7},{6,4},{7,5},{8,10},{9,11},{10,... | collective-permute-start | bytes 786440 | tf_op jit(solution)/shard_map/ppermute | solution.py:24
  38.3 9.4 %collective-permute-start.6 = (bf16[128,4096]{1,0:T(8,128)(2,1)S(1)}, bf16[128,4096]{1,0:T(8,128)(2,1)S(1)}, u32[]{:S(2)}, u32[]{:S(2)}) collective-permute-start(bf16[128,4096]{1,0:T(8,128)(2,1)S(1)} %shard_map.96), channel_id=1, source_target_pairs={{0,4},{4,0},{8,12},{12,8},{16,20},{20,16},{24,28},{28,24},{1,5},{5... | collective-permute-start | bytes 3145736 | tf_op jit(solution)/shard_map/ppermute | solution.py:24
  38.7 13.7 %collective-permute-start.1 = (f32[32,1]{0,1:T(1,128)S(1)}, f32[32,1]{0,1:T(1,128)S(1)}, u32[]{:S(2)}, u32[]{:S(2)}) collective-permute-start(f32[32,1]{0,1:T(1,128)S(1)} %bitcast.43), channel_id=1, source_target_pairs={{0,1},{1,0},{2,3},{3,2},{4,5},{5,4},{6,7},{7,6},{8,9},{9,8},{10,11... | collective-permute-start | bytes 392 | tf_op jit(solution)/shard_map/ppermute | solution.py:24
  48.1 25.4 %dynamic-slice-start = ((f32[16384]{0:T(1024)}, s32[]{:T(128)}), f32[4096]{0:T(1024)S(1)}, s32[]{:S(2)}) async-start(f32[16384]{0:T(1024)} %param.10, s32[]{:T(128)} %select_n.264), calls=%async_computation | async-start | bytes 33280 | tf_op jit(solution)/shard_map/dynamic_slice | solution.py:440
  48.2 13.9 %collective-permute-start.7 = (bf16[64,2048]{1,0:T(8,128)(2,1)S(1)}, bf16[64,2048]{1,0:T(8,128)(2,1)S(1)}, u32[]{:S(2)}, u32[]{:S(2)}) collective-permute-start(bf16[64,2048]{1,0:T(8,128)(2,1)S(1)} %pad_maximum_fusion.1), channel_id=1, source_target_pairs={{0,8},{4,12},{8,0},{12,4},{16,24},{20,28},{24,16},{28,20},{1,9},{5... | collective-permute-start | bytes 786440 | tf_op jit(solution)/shard_map/ppermute | solution.py:24
  48.2 16.2 %collective-permute-start.9 = (bf16[64,2048]{1,0:T(8,128)(2,1)S(1)}, bf16[64,2048]{1,0:T(8,128)(2,1)S(1)}, u32[]{:S(2)}, u32[]{:S(2)}) collective-permute-start(bf16[64,2048]{1,0:T(8,128)(2,1)S(1)} %concatenate.38), channel_id=1, source_target_pairs={{0,16},{4,20},{8,24},{12,28},{16,0},{20,4},{24,8},{28,12},{1,17},{... | collective-permute-start | bytes 786440 | tf_op jit(solution)/shard_map/ppermute | solution.py:24
  52.4 15.1 %collective-permute-start.2 = (f32[32,1]{0,1:T(1,128)S(1)}, f32[32,1]{0,1:T(1,128)S(1)}, u32[]{:S(2)}, u32[]{:S(2)}) collective-permute-start(f32[32,1]{0,1:T(1,128)S(1)} %bitcast_add_fusion), channel_id=1, source_target_pairs={{0,2},{1,3},{2,0},{3,1},{4,6},{5,7},{6,4},{7,5},{8,10},{9,11},{10,... | collective-permute-start | bytes 392 | tf_op jit(solution)/shard_map/ppermute | solution.py:24
  64.5 7.1 %collective-permute-start.10 = (bf16[32,2048]{1,0:T(8,128)(2,1)S(1)}, bf16[32,2048]{1,0:T(8,128)(2,1)S(1)}, u32[]{:S(2)}, u32[]{:S(2)}) collective-permute-start(bf16[32,2048]{1,0:T(8,128)(2,1)S(1)} %get-tuple-element.49), channel_id=1, source_target_pairs={{0,8},{4,12},{8,0},{12,4},{16,24},{20,28},{24,16},{28,20},{1,9},{5... | collective-permute-start | bytes 393224 | tf_op jit(solution)/shard_map/ppermute | solution.py:24
  64.9 8.5 %collective-permute-start.8 = (bf16[32,2048]{1,0:T(8,128)(2,1)S(1)}, bf16[32,2048]{1,0:T(8,128)(2,1)S(1)}, u32[]{:S(2)}, u32[]{:S(2)}) collective-permute-start(bf16[32,2048]{1,0:T(8,128)(2,1)S(1)} %get-tuple-element.48), channel_id=1, source_target_pairs={{0,16},{4,20},{8,24},{12,28},{16,0},{20,4},{24,8},{28,12},{1,17},{... | collective-permute-start | bytes 393224 | tf_op jit(solution)/shard_map/ppermute | solution.py:24
  73.8 7.3 %collective-permute-start.11 = (bf16[32,2048]{1,0:T(8,128)(2,1)S(1)}, bf16[32,2048]{1,0:T(8,128)(2,1)S(1)}, u32[]{:S(2)}, u32[]{:S(2)}) collective-permute-start(bf16[32,2048]{1,0:T(8,128)(2,1)S(1)} %get-tuple-element.54), channel_id=1, source_target_pairs={{0,16},{4,20},{8,24},{12,28},{16,0},{20,4},{24,8},{28,12},{1,17},{... | collective-permute-start | bytes 393224 | tf_op jit(solution)/shard_map/ppermute | solution.py:24
  74.2 6.9 %collective-permute-start.12 = (bf16[32,2048]{1,0:T(8,128)(2,1)S(1)}, bf16[32,2048]{1,0:T(8,128)(2,1)S(1)}, u32[]{:S(2)}, u32[]{:S(2)}) collective-permute-start(bf16[32,2048]{1,0:T(8,128)(2,1)S(1)} %get-tuple-element.55), channel_id=1, source_target_pairs={{0,8},{4,12},{8,0},{12,4},{16,24},{20,28},{24,16},{28,20},{1,9},{5... | collective-permute-start | bytes 393224 | tf_op jit(solution)/shard_map/ppermute | solution.py:24
  81.2 10.2 %collective-permute-start.13 = (bf16[64,2048]{1,0:T(8,128)(2,1)S(1)}, bf16[64,2048]{1,0:T(8,128)(2,1)S(1)}, u32[]{:S(2)}, u32[]{:S(2)}) collective-permute-start(bf16[64,2048]{1,0:T(8,128)(2,1)S(1)} %get-tuple-element.53), channel_id=1, source_target_pairs={{0,8},{4,12},{8,0},{12,4},{16,24},{20,28},{24,16},{28,20},{1,9},{5... | collective-permute-start | bytes 786440 | tf_op jit(solution)/shard_map/ppermute | solution.py:24
  81.8 12.1 %collective-permute-start.14 = (bf16[64,2048]{1,0:T(8,128)(2,1)S(1)}, bf16[64,2048]{1,0:T(8,128)(2,1)S(1)}, u32[]{:S(2)}, u32[]{:S(2)}) collective-permute-start(bf16[64,2048]{1,0:T(8,128)(2,1)S(1)} %get-tuple-element.52), channel_id=1, source_target_pairs={{0,16},{4,20},{8,24},{12,28},{16,0},{20,4},{24,8},{28,12},{1,17},{... | collective-permute-start | bytes 786440 | tf_op jit(solution)/shard_map/ppermute | solution.py:24
  83.7 10.7 %collective-permute-start.15 = (bf16[64,4096]{1,0:T(8,128)(2,1)S(1)}, bf16[64,4096]{1,0:T(8,128)(2,1)S(1)}, u32[]{:S(2)}, u32[]{:S(2)}) collective-permute-start(bf16[64,4096]{1,0:T(8,128)(2,1)S(1)} %maximum_maximum_fusion.refs_0_), channel_id=1, source_target_pairs={{0,4},{4,0},{8,12},{12,8},{16,20},{20,16},{24,28},{28,24},{1,5},{5... | collective-permute-start | bytes 1572872 | tf_op jit(solution)/shard_map/ppermute | solution.py:24
  94.0 2.0 %collective-permute-start.16 = (bf16[64,4096]{1,0:T(8,128)(2,1)S(1)}, bf16[64,4096]{1,0:T(8,128)(2,1)S(1)}, u32[]{:S(2)}, u32[]{:S(2)}) collective-permute-start(bf16[64,4096]{1,0:T(8,128)(2,1)S(1)} %constant_dynamic-update-slice_fusion.3.refs_1_), channel_id=1, source_target_pairs={{0,4},{4,0},{8,12},{12,8},{16,20},{20,16},{24,28},{28,24},{1,5},{5... | collective-permute-start | bytes 1572872 | tf_op jit(solution)/shard_map/ppermute | solution.py:24
  104.5 19.9 %collective-permute-start.17 = (s16[128,1152]{1,0:T(8,128)(2,1)S(1)}, s16[128,1152]{1,0:T(8,128)(2,1)S(1)}, u32[]{:S(2)}, u32[]{:S(2)}) collective-permute-start(s16[128,1152]{1,0:T(8,128)(2,1)S(1)} %get-tuple-element.24.refs_0_), channel_id=1, source_target_pairs={{0,1},{1,0},{2,3},{3,2},{4,5},{5,4},{6,7},{7,6},{8,9},{9,8},{10,11... | collective-permute-start | bytes 884744 | tf_op jit(solution)/shard_map/ppermute | solution.py:24
  112.9 23.2 %collective-permute-start.20 = (s16[128,2176]{1,0:T(8,128)(2,1)S(1)}, s16[128,2176]{1,0:T(8,128)(2,1)S(1)}, u32[]{:S(2)}, u32[]{:S(2)}) collective-permute-start(s16[128,2176]{1,0:T(8,128)(2,1)S(1)} %get-tuple-element.25.refs_0_), channel_id=1, source_target_pairs={{0,2},{1,3},{2,0},{3,1},{4,6},{5,7},{6,4},{7,5},{8,10},{9,11},{10,... | collective-permute-start | bytes 1671176 | tf_op jit(solution)/shard_map/ppermute | solution.py:24
  122.8 15.7 %collective-permute-start.22 = (s16[128,2176]{1,0:T(8,128)(2,1)}, s16[128,2176]{1,0:T(8,128)(2,1)S(1)}, u32[]{:S(2)}, u32[]{:S(2)}) collective-permute-start(s16[128,2176]{1,0:T(8,128)(2,1)} %get-tuple-element.26.refs_0_), channel_id=1, source_target_pairs={{0,1},{1,0},{2,3},{3,2},{4,5},{5,4},{6,7},{7,6},{8,9},{9,8},{10,11... | collective-permute-start | bytes 1671176 | tf_op jit(solution)/shard_map/ppermute | solution.py:24
  134.4 24.6 %collective-permute-start.18 = (s16[128,2176]{1,0:T(8,128)(2,1)}, s16[128,2176]{1,0:T(8,128)(2,1)}, u32[]{:S(2)}, u32[]{:S(2)}) collective-permute-start(s16[128,2176]{1,0:T(8,128)(2,1)} %get-tuple-element.28.refs_0_), channel_id=1, source_target_pairs={{0,2},{1,3},{2,0},{3,1},{4,6},{5,7},{6,4},{7,5},{8,10},{9,11},{10,... | collective-permute-start | bytes 1671176 | tf_op jit(solution)/shard_map/ppermute | solution.py:24
  137.8 15.3 %collective-permute-start.21 = (s16[64,2176]{1,0:T(8,128)(2,1)}, s16[64,2176]{1,0:T(8,128)(2,1)}, u32[]{:S(2)}, u32[]{:S(2)}) collective-permute-start(s16[64,2176]{1,0:T(8,128)(2,1)} %shard_map.103.refs_0_), channel_id=1, source_target_pairs={{0,1},{1,0},{2,3},{3,2},{4,5},{5,4},{6,7},{7,6},{8,9},{9,8},{10,11... | collective-permute-start | bytes 835592 | tf_op jit(solution)/shard_map/ppermute | solution.py:24
  138.1 15.0 %collective-permute-start.19 = (s16[64,1152]{1,0:T(8,128)(2,1)}, s16[64,1152]{1,0:T(8,128)(2,1)}, u32[]{:S(2)}, u32[]{:S(2)}) collective-permute-start(s16[64,1152]{1,0:T(8,128)(2,1)} %copy-done.2), channel_id=1, source_target_pairs={{0,2},{1,3},{2,0},{3,1},{4,6},{5,7},{6,4},{7,5},{8,10},{9,11},{10,... | collective-permute-start | bytes 442376 | tf_op jit(solution)/shard_map/ppermute | solution.py:24
  145.6 15.9 %collective-permute-start.24 = (s16[128,1152]{1,0:T(8,128)(2,1)}, s16[128,1152]{1,0:T(8,128)(2,1)}, u32[]{:S(2)}, u32[]{:S(2)}) collective-permute-start(s16[128,1152]{1,0:T(8,128)(2,1)} %get-tuple-element.34.refs_0_), channel_id=1, source_target_pairs={{0,1},{1,0},{2,3},{3,2},{4,5},{5,4},{6,7},{7,6},{8,9},{9,8},{10,11... | collective-permute-start | bytes 884744 | tf_op jit(solution)/shard_map/ppermute | solution.py:24
  149.4 15.0 %collective-permute-start.26 = (s16[64,2176]{1,0:T(8,128)(2,1)S(1)}, s16[64,2176]{1,0:T(8,128)(2,1)S(1)}, u32[]{:S(2)}, u32[]{:S(2)}) collective-permute-start(s16[64,2176]{1,0:T(8,128)(2,1)S(1)} %shard_map.105.refs_6_), channel_id=1, source_target_pairs={{0,2},{1,3},{2,0},{3,1},{4,6},{5,7},{6,4},{7,5},{8,10},{9,11},{10,... | collective-permute-start | bytes 835592 | tf_op jit(solution)/shard_map/ppermute | solution.py:24
  161.0 7.0 %collective-permute-start.23 = (s16[64,2176]{1,0:T(8,128)(2,1)S(1)}, s16[64,2176]{1,0:T(8,128)(2,1)S(1)}, u32[]{:S(2)}, u32[]{:S(2)}) collective-permute-start(s16[64,2176]{1,0:T(8,128)(2,1)S(1)} %shard_map.107.refs_0_), channel_id=1, source_target_pairs={{0,1},{1,0},{2,3},{3,2},{4,5},{5,4},{6,7},{7,6},{8,9},{9,8},{10,11... | collective-permute-start | bytes 835592 | tf_op jit(solution)/shard_map/ppermute | solution.py:24
  162.8 5.2 %collective-permute-start.25 = (s16[64,1152]{1,0:T(8,128)(2,1)S(1)}, s16[64,1152]{1,0:T(8,128)(2,1)S(1)}, u32[]{:S(2)}, u32[]{:S(2)}) collective-permute-start(s16[64,1152]{1,0:T(8,128)(2,1)S(1)} %shard_map.108.refs_5_), channel_id=1, source_target_pairs={{0,2},{1,3},{2,0},{3,1},{4,6},{5,7},{6,4},{7,5},{8,10},{9,11},{10,... | collective-permute-start | bytes 442376 | tf_op jit(solution)/shard_map/ppermute | solution.py:24
  172.0 1.3 collective-permute-start.27
  173.3 4.0 %collective-permute-start.28 = (f32[64,128]{1,0:T(8,128)S(1)}, f32[64,128]{1,0:T(8,128)S(1)}, u32[]{:S(2)}, u32[]{:S(2)}) collective-permute-start(f32[64,128]{1,0:T(8,128)S(1)} %shard_map.111.own), channel_id=1, source_target_pairs={{0,8},{4,12},{8,0},{12,4},{16,24},{20,28},{24,16},{28,20},{1,9},{5... | collective-permute-start | bytes 98312 | tf_op jit(solution)/shard_map/ppermute | solution.py:24
  177.4 4.9 %collective-permute-start.29 = (f32[64,128]{1,0:T(8,128)S(1)}, f32[64,128]{1,0:T(8,128)S(1)}, u32[]{:S(2)}, u32[]{:S(2)}) collective-permute-start(f32[64,128]{1,0:T(8,128)S(1)} %shard_map.112.own), channel_id=1, source_target_pairs={{0,16},{4,20},{8,24},{12,28},{16,0},{20,4},{24,8},{28,12},{1,17},{... | collective-permute-start | bytes 98312 | tf_op jit(solution)/shard_map/ppermute | solution.py:24
  (24 other events, 135.8 us)

commit v9 on v8

--- a/solution.py
+++ b/solution.py
@@ -163,7 +163,8 @@
 
 def vocab_body(rows, source, *refs, order, tile, first, waits):
     stay, go, send, held, powers, sems = refs[waits:]
-    wait = stream(source, held, sems, first, tile)
+    part = widest(256, tile)
+    wait = stream(source, held, sems, first, part)
     height = rows.shape[0] // len(order)
     half = len(order) // 2
     width = held.shape[1]
@@ -172,8 +173,14 @@
 
     def step(n, carry):
         at = pl.ds(pl.multiple_of(n * tile, tile), tile)
-        wait(n)
-        total = jnp.dot(rows[...], held[:, at], preferred_element_type=jnp.float32)
+        terms = []
+        for index in range(tile // part):
+            wait(n * (tile // part) + index)
+            columns = pl.ds(pl.multiple_of(n * tile + index * part, part), part)
+            terms.append(
+                jnp.dot(rows[...], held[:, columns], preferred_element_type=jnp.float32)
+            )
+        total = jnp.concatenate(terms, axis=1)
         sorted_rows = [total[g * height : (g + 1) * height] for g in order]
         stay[:, at] = jnp.concatenate(sorted_rows[: half // 2], axis=0)
         go[:, at] = jnp.concatenate(sorted_rows[half // 2 : half], axis=0)
@@ -202,7 +209,7 @@
         scratch_shapes=[
             pltpu.VMEM((depth, width), jnp.bfloat16),
             pltpu.VMEM((half, LANES), jnp.float32),
-            pltpu.SemaphoreType.DMA((width // tile, WAYS)),
+            pltpu.SemaphoreType.DMA((width // widest(256, tile), WAYS)),
         ],
         compiler_params=pltpu.CompilerParams(vmem_limit_bytes=VOCAB_LIMIT),
         cost_estimate=UNIT_COST,

time: 185 us -> 200 us (1.081)
  Pallas kernels: 69.6 us -> 86.1 us
    pallas_call x5, Pallas kernels: 36.2 us -> 52.9 us  [vocab_matmul(): pl.pallas_call(functools.partial(vocab_body, order=order, tile=tile, firs...]
  transfers between devices with their start and end apart: 30 -> 30, of which waited for: 16 -> 15; matrix products, arithmetic and copies ran while one was open for 1% -> 1% of each run, Pallas kernels for 27% -> 33%
where the time goes in v9:
time: 200 us; the launch traced here: 199 us
  Pallas kernels  86.1 us (43%)
  waiting for transfers between devices  54.4 us (27%)
  starting transfers between devices  42.3 us (21%)
  local copies, waits for them, and re-layouts  11.2 us (6%)
  other arithmetic  3.48 us (2%)
    ppermute x29, waiting for transfers between devices, swap(): lax.ppermute(array, axis, [(i, partner(i)) for i in range(lax.axis_size(a...  54.3 us
    pallas_call x5, Pallas kernels, vocab_matmul(): pl.pallas_call(functools.partial(vocab_body, order=order, tile=tile, firs...  52.9 us
    ppermute x29, starting transfers between devices, swap(): lax.ppermute(array, axis, [(i, partner(i)) for i in range(lax.axis_size(a...  41.6 us
    pallas_call x2, Pallas kernels, head_matmul(): pl.pallas_call(functools.partial(head_body, height=height, tile=tile), in...  14.4 us
    pallas_call x3, Pallas kernels, finish(): pl.pallas_call(functools.partial(finish_body, tile=tile, choices=choices,...  9.83 us
    unnamed x53, local copies, waits for them, and re-layouts  9.78 us
    pallas_call x5, Pallas kernels, fold(): pl.pallas_call(functools.partial(fold_body, tile=tile), in_specs=[VMEM] *...  6.14 us
  transfers between devices with their start and end apart: 30, of which 15 were waited for; matrix products, arithmetic and copies ran while one was open for 1% of the time, Pallas kernels for 33%

profile of v9, /device:TPU:0, one launch (start us, length us, event | category | flops | bytes accessed | tf_op | source)
XLA Modules:
  0.0 199.0 jit_solution(18433195701871359098)
XLA Ops:
  5.3 16.1 %collective-permute-start.4 = (bf16[32,2048]{1,0:T(8,128)(2,1)S(1)}, bf16[32,2048]{1,0:T(8,128)(2,1)S(1)}, u32[]{:S(2)}, u32[]{:S(2)}) collective-permute-start(bf16[32,2048]{1,0:T(8,128)(2,1)S(1)} %collective-permute-done.3), channel_id=1, source_target_pairs={{0,1},{1,0},{2,3},{3,2},{4,5},{5,4},{6,7},{7,6},{8,9},{9,8},{10,11... | collective-permute-start | bytes 393224 | tf_op jit(solution)/shard_map/ppermute | solution.py:24
  21.5 2.9 %collective-permute-done.4 = bf16[32,2048]{1,0:T(8,128)(2,1)S(1)} collective-permute-done((bf16[32,2048]{1,0:T(8,128)(2,1)S(1)}, bf16[32,2048]{1,0:T(8,128)(2,1)S(1)}, u32[]{:S(2)}, u32[]{:S(2)}) %collective-permute-start.4) | collective-permute-done | bytes 131104 | tf_op jit(solution)/shard_map/ppermute | solution.py:24
  24.7 6.4 %collective-permute-done.5 = bf16[64,2048]{1,0:T(8,128)(2,1)S(1)} collective-permute-done((bf16[64,2048]{1,0:T(8,128)(2,1)S(1)}, bf16[64,2048]{1,0:T(8,128)(2,1)S(1)}, u32[]{:S(2)}, u32[]{:S(2)}) %collective-permute-start.5) | collective-permute-done | bytes 262176 | tf_op jit(solution)/shard_map/ppermute | solution.py:24
  31.1 7.2 %shard_map.96 = bf16[128,4096]{1,0:T(8,128)(2,1)S(1)} custom-call(s32[9]{0:T(128)S(1)} %stack.139.info, bf16[128,2048]{1,0:T(8,128)(2,1)S(1)} %constant_dynamic-update-slice_fusion.came, bf16[2,2048,4096]{2,1,0:T(8,128)(2,1)} %source.8), custom_call_target="tpu_custom_call" | custom-call | flops 1 | bytes 1 | tf_op jit(solution)/shard_map/pallas_call | solution.py:103
  38.7 1.8 collective-permute-start.1
  40.5 7.2 %shard_map.95 = f32[128,4096]{1,0:T(8,128)S(1)} custom-call(s32[9]{0:T(128)S(1)} %stack.137.info, bf16[128,2048]{1,0:T(8,128)(2,1)S(1)} %constant_dynamic-update-slice_fusion.came, bf16[2,2048,4096]{2,1,0:T(8,128)(2,1)} %source.8), custom_call_target="tpu_custom_call" | custom-call | flops 1 | bytes 1 | tf_op jit(solution)/shard_map/pallas_call | solution.py:103
  48.2 4.2 %collective-permute-start.9 = (bf16[64,2048]{1,0:T(8,128)(2,1)S(1)}, bf16[64,2048]{1,0:T(8,128)(2,1)S(1)}, u32[]{:S(2)}, u32[]{:S(2)}) collective-permute-start(bf16[64,2048]{1,0:T(8,128)(2,1)S(1)} %concatenate.38), channel_id=1, source_target_pairs={{0,16},{4,20},{8,24},{12,28},{16,0},{20,4},{24,8},{28,12},{1,17},{... | collective-permute-start | bytes 786440 | tf_op jit(solution)/shard_map/ppermute | solution.py:24
  52.8 9.2 %collective-permute-done.7 = bf16[64,2048]{1,0:T(8,128)(2,1)S(1)} collective-permute-done((bf16[64,2048]{1,0:T(8,128)(2,1)S(1)}, bf16[64,2048]{1,0:T(8,128)(2,1)S(1)}, u32[]{:S(2)}, u32[]{:S(2)}) %collective-permute-start.7) | collective-permute-done | bytes 262176 | tf_op jit(solution)/shard_map/ppermute | solution.py:24
  62.0 2.4 %collective-permute-done.9 = bf16[64,2048]{1,0:T(8,128)(2,1)S(1)} collective-permute-done((bf16[64,2048]{1,0:T(8,128)(2,1)S(1)}, bf16[64,2048]{1,0:T(8,128)(2,1)S(1)}, u32[]{:S(2)}, u32[]{:S(2)}) %collective-permute-start.9) | collective-permute-done | bytes 262176 | tf_op jit(solution)/shard_map/ppermute | solution.py:24
  64.9 2.7 %collective-permute-start.8 = (bf16[32,2048]{1,0:T(8,128)(2,1)S(1)}, bf16[32,2048]{1,0:T(8,128)(2,1)S(1)}, u32[]{:S(2)}, u32[]{:S(2)}) collective-permute-start(bf16[32,2048]{1,0:T(8,128)(2,1)S(1)} %get-tuple-element.48), channel_id=1, source_target_pairs={{0,16},{4,20},{8,24},{12,28},{16,0},{20,4},{24,8},{28,12},{1,17},{... | collective-permute-start | bytes 393224 | tf_op jit(solution)/shard_map/ppermute | solution.py:24
  67.6 4.0 %collective-permute-done.10 = bf16[32,2048]{1,0:T(8,128)(2,1)S(1)} collective-permute-done((bf16[32,2048]{1,0:T(8,128)(2,1)S(1)}, bf16[32,2048]{1,0:T(8,128)(2,1)S(1)}, u32[]{:S(2)}, u32[]{:S(2)}) %collective-permute-start.10) | collective-permute-done | bytes 131104 | tf_op jit(solution)/shard_map/ppermute | solution.py:24
  71.6 1.8 collective-permute-done.8
  74.2 2.5 %collective-permute-start.12 = (bf16[32,2048]{1,0:T(8,128)(2,1)S(1)}, bf16[32,2048]{1,0:T(8,128)(2,1)S(1)}, u32[]{:S(2)}, u32[]{:S(2)}) collective-permute-start(bf16[32,2048]{1,0:T(8,128)(2,1)S(1)} %get-tuple-element.55), channel_id=1, source_target_pairs={{0,8},{4,12},{8,0},{12,4},{16,24},{20,28},{24,16},{28,20},{1,9},{5... | collective-permute-start | bytes 393224 | tf_op jit(solution)/shard_map/ppermute | solution.py:24
  76.7 4.4 %collective-permute-done.11 = bf16[32,2048]{1,0:T(8,128)(2,1)S(1)} collective-permute-done((bf16[32,2048]{1,0:T(8,128)(2,1)S(1)}, bf16[32,2048]{1,0:T(8,128)(2,1)S(1)}, u32[]{:S(2)}, u32[]{:S(2)}) %collective-permute-start.11) | collective-permute-done | bytes 131104 | tf_op jit(solution)/shard_map/ppermute | solution.py:24
  81.8 1.9 collective-permute-start.14
  83.7 7.7 %collective-permute-done.13 = bf16[64,2048]{1,0:T(8,128)(2,1)S(1)} collective-permute-done((bf16[64,2048]{1,0:T(8,128)(2,1)S(1)}, bf16[64,2048]{1,0:T(8,128)(2,1)S(1)}, u32[]{:S(2)}, u32[]{:S(2)}) %collective-permute-start.13) | collective-permute-done | bytes 262176 | tf_op jit(solution)/shard_map/ppermute | solution.py:24
  91.4 2.5 %collective-permute-done.14 = bf16[64,2048]{1,0:T(8,128)(2,1)S(1)} collective-permute-done((bf16[64,2048]{1,0:T(8,128)(2,1)S(1)}, bf16[64,2048]{1,0:T(8,128)(2,1)S(1)}, u32[]{:S(2)}, u32[]{:S(2)}) %collective-permute-start.14) | collective-permute-done | bytes 262176 | tf_op jit(solution)/shard_map/ppermute | solution.py:24
  99.5 6.9 %shard_map.98 = (f32[64,1024]{1,0:T(8,128)S(1)}, f32[64,1024]{1,0:T(8,128)S(1)}, s16[128,1152]{1,0:T(8,128)(2,1)S(1)}) custom-call(bf16[256,4096]{1,0:T(8,128)(2,1)S(1)} %shard_map.97.rows, bf16[4096,8192]{1,0:T(8,128)(2,1)} %source.13), custom_call_target="tpu_custom_call" | custom-call | flops 1 | bytes 1 | tf_op jit(solution)/shard_map/pallas_call | solution.py:200
  106.8 12.3 %shard_map.99 = (f32[64,2048]{1,0:T(8,128)S(1)}, f32[64,2048]{1,0:T(8,128)S(1)}, s16[128,2176]{1,0:T(8,128)(2,1)S(1)}) custom-call(bf16[256,4096]{1,0:T(8,128)(2,1)S(1)} %shard_map.97.rows, bf16[4096,8192]{1,0:T(8,128)(2,1)} %source.13, s16[128,1152]{1,0:T(8,128)(2,1)S(1)} %get-tuple-element.24.refs_0_), custom_call_target="tpu_custom_call" | custom-call | flops 1 | bytes 1 | tf_op jit(solution)/shard_map/pallas_call | solution.py:200
  119.4 13.0 %shard_map.100 = (f32[64,2048]{1,0:T(8,128)S(1)}, f32[64,2048]{1,0:T(8,128)S(1)}, s16[128,2176]{1,0:T(8,128)(2,1)}) custom-call(bf16[256,4096]{1,0:T(8,128)(2,1)S(1)} %shard_map.97.rows, bf16[4096,8192]{1,0:T(8,128)(2,1)} %source.13, s16[128,2176]{1,0:T(8,128)(2,1)S(1)} %get-tuple-element.25.refs_0_), custom_call_target="tpu_custom_call" | custom-call | flops 1 | bytes 1 | tf_op jit(solution)/shard_map/pallas_call | solution.py:200
  135.3 13.1 %shard_map.102 = (f32[64,2048]{1,0:T(8,128)S(1)}, f32[64,2048]{1,0:T(8,128)S(1)}, s16[128,2176]{1,0:T(8,128)(2,1)}) custom-call(bf16[256,4096]{1,0:T(8,128)(2,1)S(1)} %shard_map.97.rows, bf16[4096,8192]{1,0:T(8,128)(2,1)} %source.13, s16[64,1152]{1,0:T(8,128)(2,1)S(1)} %shard_map.101.refs_0_), custom_call_target="tpu_custom_call" | custom-call | flops 1 | bytes 1 | tf_op jit(solution)/shard_map/pallas_call | solution.py:200
  149.2 1.7 collective-permute-start.18
  153.2 7.6 %shard_map.104 = (f32[64,1024]{1,0:T(8,128)S(1)}, f32[64,1024]{1,0:T(8,128)S(1)}, s16[128,1152]{1,0:T(8,128)(2,1)}) custom-call(bf16[256,4096]{1,0:T(8,128)(2,1)S(1)} %shard_map.97.rows, bf16[4096,8192]{1,0:T(8,128)(2,1)} %source.13, s16[64,2176]{1,0:T(8,128)(2,1)} %shard_map.103.refs_0_, s16[128,2176]{1,0:T(8,128)(2,1)S(1)} %collective-permute-done.22.refs_1_.came), custom_call_target="tpu_custom_call" | custom-call | flops 1 | bytes 1 | tf_op jit(solution)/shard_map/pallas_call | solution.py:200
  166.1 1.8 collective-permute-start.26
  169.9 3.7 %shard_map.106 = (f32[64,8192]{1,0:T(8,128)S(1)}, f32[64,128]{1,0:T(8,128)S(1)}) custom-call(s32[64,128]{1,0:T(8,128)S(1)} %pad.4.wanted, f32[64,1024]{1,0:T(8,128)S(1)} %copy-done.18, s16[128,1152]{1,0:T(8,128)(2,1)S(1)} %collective-permute-done.17.came.refs_1_, s16[64,1152]{1,0:T(8,128)(2,1)} %collective-permute-done.19.refs_2_, ...), custom_call_target="tpu_custom_call" | custom-call | flops 1 | bytes 1 | tf_op jit(solution)/shard_map/pallas_call | solution.py:344
  173.6 1.9 shard_map.107.refs_0_
  177.9 2.2 %shard_map.109 = (f32[64,8192]{1,0:T(8,128)S(1)}, f32[64,128]{1,0:T(8,128)S(1)}) custom-call(s32[64,128]{1,0:T(8,128)S(1)} %pad.4.wanted, f32[64,2048]{1,0:T(8,128)S(1)} %copy-done.8, s16[128,2176]{1,0:T(8,128)(2,1)S(1)} %collective-permute-done.22.refs_1_.came, ...), custom_call_target="tpu_custom_call", output_to_operand_aliasing={{0}: (5, {})} | custom-call | flops 1 | bytes 1 | tf_op jit(solution)/shard_map/pallas_call | solution.py:344
  180.1 2.6 %collective-permute-done.25.refs_5_ = s16[64,1152]{1,0:T(8,128)(2,1)S(1)} collective-permute-done((s16[64,1152]{1,0:T(8,128)(2,1)S(1)}, s16[64,1152]{1,0:T(8,128)(2,1)S(1)}, u32[]{:S(2)}, u32[]{:S(2)}) %collective-permute-start.25) | collective-permute-done | bytes 147488 | tf_op jit(solution)/shard_map/ppermute | solution.py:24
  182.6 3.9 %shard_map.110 = (f32[64,8192]{1,0:T(8,128)S(1)}, f32[64,128]{1,0:T(8,128)S(1)}) custom-call(s32[64,128]{1,0:T(8,128)S(1)} %pad.4.wanted, f32[64,2048]{1,0:T(8,128)S(1)} %copy-done.16, s16[128,2176]{1,0:T(8,128)(2,1)} %collective-permute-done.18.came.refs_1_, s16[64,2176]{1,0:T(8,128)(2,1)S(1)} %collective-permute-done.23.refs_2_, ...), custom_call_target="tpu_custom_call", output_to_operand_aliasing={{0}: (8, {})} | custom-call | flops 1 | bytes 1 | tf_op jit(solution)/shard_map/pallas_call | solution.py:344
  188.1 3.9 %collective-permute-done.28.came = f32[64,128]{1,0:T(8,128)S(1)} collective-permute-done((f32[64,128]{1,0:T(8,128)S(1)}, f32[64,128]{1,0:T(8,128)S(1)}, u32[]{:S(2)}, u32[]{:S(2)}) %collective-permute-start.28) | collective-permute-done | bytes 32800 | tf_op jit(solution)/shard_map/ppermute | solution.py:24
  192.5 4.5 %collective-permute-done.29.came = f32[64,128]{1,0:T(8,128)S(1)} collective-permute-done((f32[64,128]{1,0:T(8,128)S(1)}, f32[64,128]{1,0:T(8,128)S(1)}, u32[]{:S(2)}, u32[]{:S(2)}) %collective-permute-start.29) | collective-permute-done | bytes 32800 | tf_op jit(solution)/shard_map/ppermute | solution.py:24
  196.9 2.0 %shard_map.113 = (f32[32,2,8192]{2,1,0:T(2,128)}, f32[32,64]{1,0:T(8,128)}) custom-call(s32[1]{0:T(128)} %bitcast.low, f32[64,128]{1,0:T(8,128)S(1)} %shard_map.112.own, f32[64,128]{1,0:T(8,128)S(1)} %collective-permute-done.29.came, s32[2,64]{1,0:T(2,128)S(1)} %bitcast.40, f32[64,8192]{1,0:T(8,128)S(1)} %get-tuple-element.43.logits), custom_call_target="tpu_custom_call" | custom-call | flops 1 | bytes 1 | tf_op jit(solution)/shard_map/pallas_call | solution.py:411
  (133 shorter events, 31.4 us)
Async XLA Ops:
  0.6 51.8 %copy-start = (f32[2,4096]{1,0:T(2,128)S(1)}, f32[2,4096]{1,0:T(2,128)}, u32[]{:S(2)}) copy-start(f32[2,4096]{1,0:T(2,128)} %param.12) | copy-start | bytes 98308
  3.0 1.5 collective-permute-start
  4.6 0.7 collective-permute-start.3
  5.3 19.1 %collective-permute-start.4 = (bf16[32,2048]{1,0:T(8,128)(2,1)S(1)}, bf16[32,2048]{1,0:T(8,128)(2,1)S(1)}, u32[]{:S(2)}, u32[]{:S(2)}) collective-permute-start(bf16[32,2048]{1,0:T(8,128)(2,1)S(1)} %collective-permute-done.3), channel_id=1, source_target_pairs={{0,1},{1,0},{2,3},{3,2},{4,5},{5,4},{6,7},{7,6},{8,9},{9,8},{10,11... | collective-permute-start | bytes 393224 | tf_op jit(solution)/shard_map/ppermute | solution.py:24
  24.4 6.7 %collective-permute-start.5 = (bf16[64,2048]{1,0:T(8,128)(2,1)S(1)}, bf16[64,2048]{1,0:T(8,128)(2,1)S(1)}, u32[]{:S(2)}, u32[]{:S(2)}) collective-permute-start(bf16[64,2048]{1,0:T(8,128)(2,1)S(1)} %pad_maximum_fusion), channel_id=1, source_target_pairs={{0,2},{1,3},{2,0},{3,1},{4,6},{5,7},{6,4},{7,5},{8,10},{9,11},{10,... | collective-permute-start | bytes 786440 | tf_op jit(solution)/shard_map/ppermute | solution.py:24
  38.3 9.4 %collective-permute-start.6 = (bf16[128,4096]{1,0:T(8,128)(2,1)S(1)}, bf16[128,4096]{1,0:T(8,128)(2,1)S(1)}, u32[]{:S(2)}, u32[]{:S(2)}) collective-permute-start(bf16[128,4096]{1,0:T(8,128)(2,1)S(1)} %shard_map.96), channel_id=1, source_target_pairs={{0,4},{4,0},{8,12},{12,8},{16,20},{20,16},{24,28},{28,24},{1,5},{5... | collective-permute-start | bytes 3145736 | tf_op jit(solution)/shard_map/ppermute | solution.py:24
  38.7 13.7 %collective-permute-start.1 = (f32[32,1]{0,1:T(1,128)S(1)}, f32[32,1]{0,1:T(1,128)S(1)}, u32[]{:S(2)}, u32[]{:S(2)}) collective-permute-start(f32[32,1]{0,1:T(1,128)S(1)} %bitcast.43), channel_id=1, source_target_pairs={{0,1},{1,0},{2,3},{3,2},{4,5},{5,4},{6,7},{7,6},{8,9},{9,8},{10,11... | collective-permute-start | bytes 392 | tf_op jit(solution)/shard_map/ppermute | solution.py:24
  48.1 25.4 %dynamic-slice-start = ((f32[16384]{0:T(1024)}, s32[]{:T(128)}), f32[4096]{0:T(1024)S(1)}, s32[]{:S(2)}) async-start(f32[16384]{0:T(1024)} %param.10, s32[]{:T(128)} %select_n.264), calls=%async_computation | async-start | bytes 33280 | tf_op jit(solution)/shard_map/dynamic_slice | solution.py:447
  48.2 13.9 %collective-permute-start.7 = (bf16[64,2048]{1,0:T(8,128)(2,1)S(1)}, bf16[64,2048]{1,0:T(8,128)(2,1)S(1)}, u32[]{:S(2)}, u32[]{:S(2)}) collective-permute-start(bf16[64,2048]{1,0:T(8,128)(2,1)S(1)} %pad_maximum_fusion.1), channel_id=1, source_target_pairs={{0,8},{4,12},{8,0},{12,4},{16,24},{20,28},{24,16},{28,20},{1,9},{5... | collective-permute-start | bytes 786440 | tf_op jit(solution)/shard_map/ppermute | solution.py:24
  48.2 16.2 %collective-permute-start.9 = (bf16[64,2048]{1,0:T(8,128)(2,1)S(1)}, bf16[64,2048]{1,0:T(8,128)(2,1)S(1)}, u32[]{:S(2)}, u32[]{:S(2)}) collective-permute-start(bf16[64,2048]{1,0:T(8,128)(2,1)S(1)} %concatenate.38), channel_id=1, source_target_pairs={{0,16},{4,20},{8,24},{12,28},{16,0},{20,4},{24,8},{28,12},{1,17},{... | collective-permute-start | bytes 786440 | tf_op jit(solution)/shard_map/ppermute | solution.py:24
  52.4 15.1 %collective-permute-start.2 = (f32[32,1]{0,1:T(1,128)S(1)}, f32[32,1]{0,1:T(1,128)S(1)}, u32[]{:S(2)}, u32[]{:S(2)}) collective-permute-start(f32[32,1]{0,1:T(1,128)S(1)} %bitcast_add_fusion), channel_id=1, source_target_pairs={{0,2},{1,3},{2,0},{3,1},{4,6},{5,7},{6,4},{7,5},{8,10},{9,11},{10,... | collective-permute-start | bytes 392 | tf_op jit(solution)/shard_map/ppermute | solution.py:24
  64.5 7.1 %collective-permute-start.10 = (bf16[32,2048]{1,0:T(8,128)(2,1)S(1)}, bf16[32,2048]{1,0:T(8,128)(2,1)S(1)}, u32[]{:S(2)}, u32[]{:S(2)}) collective-permute-start(bf16[32,2048]{1,0:T(8,128)(2,1)S(1)} %get-tuple-element.49), channel_id=1, source_target_pairs={{0,8},{4,12},{8,0},{12,4},{16,24},{20,28},{24,16},{28,20},{1,9},{5... | collective-permute-start | bytes 393224 | tf_op jit(solution)/shard_map/ppermute | solution.py:24
  64.9 8.5 %collective-permute-start.8 = (bf16[32,2048]{1,0:T(8,128)(2,1)S(1)}, bf16[32,2048]{1,0:T(8,128)(2,1)S(1)}, u32[]{:S(2)}, u32[]{:S(2)}) collective-permute-start(bf16[32,2048]{1,0:T(8,128)(2,1)S(1)} %get-tuple-element.48), channel_id=1, source_target_pairs={{0,16},{4,20},{8,24},{12,28},{16,0},{20,4},{24,8},{28,12},{1,17},{... | collective-permute-start | bytes 393224 | tf_op jit(solution)/shard_map/ppermute | solution.py:24
  73.8 7.3 %collective-permute-start.11 = (bf16[32,2048]{1,0:T(8,128)(2,1)S(1)}, bf16[32,2048]{1,0:T(8,128)(2,1)S(1)}, u32[]{:S(2)}, u32[]{:S(2)}) collective-permute-start(bf16[32,2048]{1,0:T(8,128)(2,1)S(1)} %get-tuple-element.54), channel_id=1, source_target_pairs={{0,16},{4,20},{8,24},{12,28},{16,0},{20,4},{24,8},{28,12},{1,17},{... | collective-permute-start | bytes 393224 | tf_op jit(solution)/shard_map/ppermute | solution.py:24
  74.2 6.9 %collective-permute-start.12 = (bf16[32,2048]{1,0:T(8,128)(2,1)S(1)}, bf16[32,2048]{1,0:T(8,128)(2,1)S(1)}, u32[]{:S(2)}, u32[]{:S(2)}) collective-permute-start(bf16[32,2048]{1,0:T(8,128)(2,1)S(1)} %get-tuple-element.55), channel_id=1, source_target_pairs={{0,8},{4,12},{8,0},{12,4},{16,24},{20,28},{24,16},{28,20},{1,9},{5... | collective-permute-start | bytes 393224 | tf_op jit(solution)/shard_map/ppermute | solution.py:24
  81.2 10.2 %collective-permute-start.13 = (bf16[64,2048]{1,0:T(8,128)(2,1)S(1)}, bf16[64,2048]{1,0:T(8,128)(2,1)S(1)}, u32[]{:S(2)}, u32[]{:S(2)}) collective-permute-start(bf16[64,2048]{1,0:T(8,128)(2,1)S(1)} %get-tuple-element.53), channel_id=1, source_target_pairs={{0,8},{4,12},{8,0},{12,4},{16,24},{20,28},{24,16},{28,20},{1,9},{5... | collective-permute-start | bytes 786440 | tf_op jit(solution)/shard_map/ppermute | solution.py:24
  81.8 12.1 %collective-permute-start.14 = (bf16[64,2048]{1,0:T(8,128)(2,1)S(1)}, bf16[64,2048]{1,0:T(8,128)(2,1)S(1)}, u32[]{:S(2)}, u32[]{:S(2)}) collective-permute-start(bf16[64,2048]{1,0:T(8,128)(2,1)S(1)} %get-tuple-element.52), channel_id=1, source_target_pairs={{0,16},{4,20},{8,24},{12,28},{16,0},{20,4},{24,8},{28,12},{1,17},{... | collective-permute-start | bytes 786440 | tf_op jit(solution)/shard_map/ppermute | solution.py:24
  83.7 10.7 %collective-permute-start.15 = (bf16[64,4096]{1,0:T(8,128)(2,1)S(1)}, bf16[64,4096]{1,0:T(8,128)(2,1)S(1)}, u32[]{:S(2)}, u32[]{:S(2)}) collective-permute-start(bf16[64,4096]{1,0:T(8,128)(2,1)S(1)} %maximum_maximum_fusion.refs_0_), channel_id=1, source_target_pairs={{0,4},{4,0},{8,12},{12,8},{16,20},{20,16},{24,28},{28,24},{1,5},{5... | collective-permute-start | bytes 1572872 | tf_op jit(solution)/shard_map/ppermute | solution.py:24
  94.0 2.0 collective-permute-start.16
  106.4 28.6 %collective-permute-start.17 = (s16[128,1152]{1,0:T(8,128)(2,1)S(1)}, s16[128,1152]{1,0:T(8,128)(2,1)S(1)}, u32[]{:S(2)}, u32[]{:S(2)}) collective-permute-start(s16[128,1152]{1,0:T(8,128)(2,1)S(1)} %get-tuple-element.24.refs_0_), channel_id=1, source_target_pairs={{0,1},{1,0},{2,3},{3,2},{4,5},{5,4},{6,7},{7,6},{8,9},{9,8},{10,11... | collective-permute-start | bytes 884744 | tf_op jit(solution)/shard_map/ppermute | solution.py:24
  119.1 31.9 %collective-permute-start.20 = (s16[128,2176]{1,0:T(8,128)(2,1)S(1)}, s16[128,2176]{1,0:T(8,128)(2,1)S(1)}, u32[]{:S(2)}, u32[]{:S(2)}) collective-permute-start(s16[128,2176]{1,0:T(8,128)(2,1)S(1)} %get-tuple-element.25.refs_0_), channel_id=1, source_target_pairs={{0,2},{1,3},{2,0},{3,1},{4,6},{5,7},{6,4},{7,5},{8,10},{9,11},{10,... | collective-permute-start | bytes 1671176 | tf_op jit(solution)/shard_map/ppermute | solution.py:24
  133.3 20.0 %collective-permute-start.22 = (s16[128,2176]{1,0:T(8,128)(2,1)}, s16[128,2176]{1,0:T(8,128)(2,1)S(1)}, u32[]{:S(2)}, u32[]{:S(2)}) collective-permute-start(s16[128,2176]{1,0:T(8,128)(2,1)} %get-tuple-element.26.refs_0_), channel_id=1, source_target_pairs={{0,1},{1,0},{2,3},{3,2},{4,5},{5,4},{6,7},{7,6},{8,9},{9,8},{10,11... | collective-permute-start | bytes 1671176 | tf_op jit(solution)/shard_map/ppermute | solution.py:24
  149.2 24.4 %collective-permute-start.18 = (s16[128,2176]{1,0:T(8,128)(2,1)}, s16[128,2176]{1,0:T(8,128)(2,1)}, u32[]{:S(2)}, u32[]{:S(2)}) collective-permute-start(s16[128,2176]{1,0:T(8,128)(2,1)} %get-tuple-element.28.refs_0_), channel_id=1, source_target_pairs={{0,2},{1,3},{2,0},{3,1},{4,6},{5,7},{6,4},{7,5},{8,10},{9,11},{10,... | collective-permute-start | bytes 1671176 | tf_op jit(solution)/shard_map/ppermute | solution.py:24
  152.6 15.3 %collective-permute-start.21 = (s16[64,2176]{1,0:T(8,128)(2,1)}, s16[64,2176]{1,0:T(8,128)(2,1)}, u32[]{:S(2)}, u32[]{:S(2)}) collective-permute-start(s16[64,2176]{1,0:T(8,128)(2,1)} %shard_map.103.refs_0_), channel_id=1, source_target_pairs={{0,1},{1,0},{2,3},{3,2},{4,5},{5,4},{6,7},{7,6},{8,9},{9,8},{10,11... | collective-permute-start | bytes 835592 | tf_op jit(solution)/shard_map/ppermute | solution.py:24
  153.0 14.9 %collective-permute-start.19 = (s16[64,1152]{1,0:T(8,128)(2,1)}, s16[64,1152]{1,0:T(8,128)(2,1)}, u32[]{:S(2)}, u32[]{:S(2)}) collective-permute-start(s16[64,1152]{1,0:T(8,128)(2,1)} %copy-done.2), channel_id=1, source_target_pairs={{0,2},{1,3},{2,0},{3,1},{4,6},{5,7},{6,4},{7,5},{8,10},{9,11},{10,... | collective-permute-start | bytes 442376 | tf_op jit(solution)/shard_map/ppermute | solution.py:24
  162.2 13.8 %collective-permute-start.24 = (s16[128,1152]{1,0:T(8,128)(2,1)}, s16[128,1152]{1,0:T(8,128)(2,1)}, u32[]{:S(2)}, u32[]{:S(2)}) collective-permute-start(s16[128,1152]{1,0:T(8,128)(2,1)} %get-tuple-element.34.refs_0_), channel_id=1, source_target_pairs={{0,1},{1,0},{2,3},{3,2},{4,5},{5,4},{6,7},{7,6},{8,9},{9,8},{10,11... | collective-permute-start | bytes 884744 | tf_op jit(solution)/shard_map/ppermute | solution.py:24
  166.1 11.8 %collective-permute-start.26 = (s16[64,2176]{1,0:T(8,128)(2,1)S(1)}, s16[64,2176]{1,0:T(8,128)(2,1)S(1)}, u32[]{:S(2)}, u32[]{:S(2)}) collective-permute-start(s16[64,2176]{1,0:T(8,128)(2,1)S(1)} %shard_map.105.refs_6_), channel_id=1, source_target_pairs={{0,2},{1,3},{2,0},{3,1},{4,6},{5,7},{6,4},{7,5},{8,10},{9,11},{10,... | collective-permute-start | bytes 835592 | tf_op jit(solution)/shard_map/ppermute | solution.py:24
  175.6 7.0 %collective-permute-start.23 = (s16[64,2176]{1,0:T(8,128)(2,1)S(1)}, s16[64,2176]{1,0:T(8,128)(2,1)S(1)}, u32[]{:S(2)}, u32[]{:S(2)}) collective-permute-start(s16[64,2176]{1,0:T(8,128)(2,1)S(1)} %shard_map.107.refs_0_), channel_id=1, source_target_pairs={{0,1},{1,0},{2,3},{3,2},{4,5},{5,4},{6,7},{7,6},{8,9},{9,8},{10,11... | collective-permute-start | bytes 835592 | tf_op jit(solution)/shard_map/ppermute | solution.py:24
  177.4 5.2 %collective-permute-start.25 = (s16[64,1152]{1,0:T(8,128)(2,1)S(1)}, s16[64,1152]{1,0:T(8,128)(2,1)S(1)}, u32[]{:S(2)}, u32[]{:S(2)}) collective-permute-start(s16[64,1152]{1,0:T(8,128)(2,1)S(1)} %shard_map.108.refs_5_), channel_id=1, source_target_pairs={{0,2},{1,3},{2,0},{3,1},{4,6},{5,7},{6,4},{7,5},{8,10},{9,11},{10,... | collective-permute-start | bytes 442376 | tf_op jit(solution)/shard_map/ppermute | solution.py:24
  186.6 1.3 collective-permute-start.27
  188.0 4.0 %collective-permute-start.28 = (f32[64,128]{1,0:T(8,128)S(1)}, f32[64,128]{1,0:T(8,128)S(1)}, u32[]{:S(2)}, u32[]{:S(2)}) collective-permute-start(f32[64,128]{1,0:T(8,128)S(1)} %shard_map.111.own), channel_id=1, source_target_pairs={{0,8},{4,12},{8,0},{12,4},{16,24},{20,28},{24,16},{28,20},{1,9},{5... | collective-permute-start | bytes 98312 | tf_op jit(solution)/shard_map/ppermute | solution.py:24
  192.1 4.9 %collective-permute-start.29 = (f32[64,128]{1,0:T(8,128)S(1)}, f32[64,128]{1,0:T(8,128)S(1)}, u32[]{:S(2)}, u32[]{:S(2)}) collective-permute-start(f32[64,128]{1,0:T(8,128)S(1)} %shard_map.112.own), channel_id=1, source_target_pairs={{0,16},{4,20},{8,24},{12,28},{16,0},{20,4},{24,8},{28,12},{1,17},{... | collective-permute-start | bytes 98312 | tf_op jit(solution)/shard_map/ppermute | solution.py:24
  (24 other events, 149.5 us)
